TPU v7x, 32 devices: a whole 2x2x4 slice. The times are simulated.
32 devices in a mesh: section: 2 (over x), space: 8 (over z, y), dp: 2 (over core).
Axes of the slice: x: 2, y: 2, z: 4, core: 2. Of those that a mesh axis runs over, the one named last changes fastest.
Arguments:
- features: bfloat16 [2, 2, 4, 512, 256], P(None, 'dp', None, 'space'), may hold values from -6 to 6
- coords: float32 [2, 2, 3, 512], P(None, 'dp', None, 'space'), as said below
- neighbours: int32 [2, 2, 32, 512], P(None, 'dp', None, 'space'), may hold values from 0 to 95, as said below
- counts: int32 [2, 2, 512], P(None, 'dp', 'space'), may hold values from 1 to 32, as said below
- shifts: int32 [2, 2, 2, 32, 512], P(None, 'dp', None, None, 'space'), may hold values from -1 to 1
- norm_gain: bfloat16 [2, 256], P('section'), may hold values from 0.25 to 1.75
- norm_bias: bfloat16 [2, 256], P('section'), may hold values from -3 to 3
- qkv_weight: bfloat16 [2, 256, 1280], P('section'), may hold values from -0.375 to 0.375
- vector_weight: bfloat16 [2, 256, 768], P('section'), may hold values from -0.375 to 0.375
- filter_weight: bfloat16 [2, 32, 1024], P('section'), may hold values from -3 to 3
- out_weight: bfloat16 [2, 256, 768], P('section'), may hold values from -0.75 to 0.75
- cotangent: bfloat16 [2, 2, 4, 512, 256], P(None, 'dp', None, 'space'), may hold values from -6 to 6
Outputs:
- layer_outputs: bfloat16 [2, 2, 2, 4, 512, 256], P('section', None, 'dp', None, 'space')
- input_grads: float32 [2, 2, 2, 4, 512, 256], P('section', None, 'dp', None, 'space')
- gain_grad: float32 [2, 256], P('section', 'space')
- bias_grad: float32 [2, 256], P('section', 'space')
- qkv_grad: float32 [2, 256, 1280], P('section', None, 'space')
- vector_weight_gradient: float32 [2, 256, 768], P('section', None, 'space')
- filter_grad: float32 [2, 32, 1024], P('section', None, 'space')
- out_grad: float32 [2, 256, 768], P('section', None, 'space')
- coords_grad: float32 [2, 2, 3, 512], P(None, 'dp', None, 'space')
Inputs may be any that keep to these rules, and one draw needn't show every extreme that they name: `neighbours`: slot n of the atom in row r of its slab (r = i mod 64) holds r + 16 + o with 1 <= |o| <= 16; the 32 offsets o of an atom are distinct. Every slab of 64 atoms of every box holds an atom with 32 live slots; the slabs' mean counts differ. `coords`: component 0 of atom i lies within 1.8 / 16 of 4 i / 16; components 1 and 2 lie in [0, 2.5).
All inputs are finite; a program needn't handle non-finite values.
Results may differ from a plain program's by a relative error of at most 0.015.
The roundings to bfloat16 on the way count: a program that leaves them out, or rounds other values in their place, can miss the bound.
Values may be sent and summed in bfloat16 or wider, within the bound.
No kernel may reach another device: no remote copies, remote signals or barrier semaphores. Data moves between devices by JAX's collectives and lax.ppermute only.
A program may use at most 256 MiB of HBM per device.

v0:
```python
import functools
import math

import jax
import jax.numpy as jnp
from jax import lax
from jax.sharding import PartitionSpec as P

HEADS = 8


CUTOFF = 5.0
LN_EPS = 1e-05
SOFTEN = 0.25
CROSS = 2.5


def shifted(block, axis, distance):
    devices = range(lax.axis_size(axis))
    route = [((i - distance) % len(devices), i) for i in devices]
    return lax.ppermute(block, axis, route)


def extended(cells, sides, width):
    for axis, dim in sides:
        count = lax.axis_size(axis)
        head = lax.slice_in_dim(cells, 0, width, axis=dim)
        tail = lax.slice_in_dim(cells, cells.shape[dim] - width, cells.shape[dim], axis=dim)
        cells = jnp.concatenate(
            [
                lax.ppermute(tail, axis, [(i, (i + 1) % count) for i in range(count)]),
                cells,
                lax.ppermute(head, axis, [((i + 1) % count, i) for i in range(count)]),
            ],
            axis=dim,
        )
    return cells


def from_behind(value, axis, steps):
    count = lax.axis_size(axis)
    leading, last = (max(0, -steps), min(count, count - steps))
    return lax.ppermute(value, axis, [(source, source + steps) for source in range(leading, last)])


def layer_norm(scalars, norm_gain, norm_bias):
    centre = jnp.mean(scalars, axis=-1, keepdims=True)
    centred = scalars - centre
    spread = jnp.mean(centred * centred, axis=-1, keepdims=True)
    return centred * lax.rsqrt(spread + LN_EPS) * norm_gain + norm_bias


def edge_terms(separation, live_slot, basis_count):
    distance = jnp.sqrt(jnp.sum(separation * separation, axis=0) + SOFTEN)
    unit_vec = separation / distance
    inside = distance < CUTOFF
    cutoff = jnp.where(inside, 0.5 * (jnp.cos(math.pi * distance / CUTOFF) + 1.0), 0.0) * live_slot
    centres = jnp.linspace(math.exp(-CUTOFF), 1.0, basis_count, dtype=jnp.float32)
    sharpness = (2.0 / basis_count * (1.0 - math.exp(-CUTOFF))) ** (-2)
    shrink = jnp.exp(-distance)
    smearing = cutoff[None] * jnp.exp(-sharpness * (shrink[None] - centres[:, None, None]) ** 2)
    return (unit_vec, cutoff, smearing)


def edge_core(
    filter_pre, queries, key_value, vector_features, unit_vec, cutoff, source, head_count
):
    feature_width = queries.shape[1]
    slot_count = source.shape[0]
    row_count = source.shape[1]
    head_dim = feature_width // head_count
    filters = jax.nn.silu(filter_pre).reshape(slot_count, row_count, 4 * feature_width)
    gathered = key_value[source]
    neighbour_vec = vector_features[:, source]
    product = queries[None] * gathered[..., :feature_width] * filters[..., :feature_width]
    score_values = jnp.sum(product.reshape(slot_count, row_count, head_count, head_dim), axis=-1)
    attention = jax.nn.silu(score_values) * cutoff[..., None]
    values = gathered[..., feature_width:] * filters[..., feature_width:]
    scalar_msg = (
        values[..., :feature_width].reshape(slot_count, row_count, head_count, head_dim)
        * attention[..., None]
    ).reshape(slot_count, row_count, feature_width)
    vector_msg = (
        neighbour_vec * values[None, ..., feature_width : 2 * feature_width]
        + values[None, ..., 2 * feature_width :] * unit_vec[..., None]
    )
    return (jnp.sum(scalar_msg, axis=0), jnp.sum(vector_msg, axis=1))


def combine(out_proj, vector_projection, vector_agg):
    feature_width = out_proj.shape[1] // 3
    vec_dot = jnp.sum(
        vector_projection[..., :feature_width]
        * vector_projection[..., feature_width : 2 * feature_width],
        axis=0,
    )
    scalar_delta = (
        vec_dot * out_proj[:, feature_width : 2 * feature_width] + out_proj[:, 2 * feature_width :]
    )
    vector_delta = (
        vector_projection[..., 2 * feature_width :] * out_proj[None, :, :feature_width] + vector_agg
    )
    return (scalar_delta, vector_delta)


def tile_edges(
    coords_all,
    wrap_image,
    neighbour_tile,
    shift_tile,
    count_tile,
    first_row,
    halo_rows,
    length_x,
    basis_count,
):
    tile_rows = neighbour_tile.shape[1]
    own_coords = lax.slice_in_dim(
        coords_all, halo_rows + first_row, halo_rows + first_row + tile_rows, axis=1
    )
    others = coords_all[:, neighbour_tile]
    offset = jnp.stack(
        [
            wrap_image[neighbour_tile] * length_x,
            shift_tile[0].astype(jnp.float32) * CROSS,
            shift_tile[1].astype(jnp.float32) * CROSS,
        ]
    )
    separation = others - own_coords[:, None, :] + offset
    slot_count = neighbour_tile.shape[0]
    live_slot = (jnp.arange(slot_count, dtype=jnp.int32)[:, None] < count_tile[None, :]).astype(
        jnp.float32
    )
    return edge_terms(separation, live_slot, basis_count)


def filter_product(smearing, filter_weight):
    flat = smearing.reshape(smearing.shape[0], -1).astype(jnp.bfloat16)
    filter_pre = lax.dot_general(
        flat, filter_weight, (((0,), (0,)), ((), ())), preferred_element_type=jnp.float32
    )
    return (flat, filter_pre)


def layer_forward(weights, haloed, geometry, wrap_image, halo_rows, length_x):
    norm_gain, norm_bias, qkv_weight, vector_weight, filter_weight, out_weight = weights
    coords_all, neighbour_ids, cell_shifts, live_counts = geometry
    feature_width = haloed.shape[2]
    atom_count = haloed.shape[1] - 2 * halo_rows
    basis_count = filter_weight.shape[0]
    normed = layer_norm(haloed[0].astype(jnp.float32), norm_gain, norm_bias).astype(jnp.bfloat16)
    projected = jnp.dot(normed, qkv_weight, preferred_element_type=jnp.float32)
    local_vector = haloed[1:, halo_rows : halo_rows + atom_count]
    vector_projection = jnp.einsum(
        "smv,va->sma", local_vector, vector_weight, preferred_element_type=jnp.float32
    )
    vectors_all = haloed[1:].astype(jnp.float32)
    key_value = projected[:, feature_width:]
    tile_rows = math.gcd(atom_count, 128)
    unit_vec, cutoff, smearing = tile_edges(
        coords_all,
        wrap_image,
        neighbour_ids,
        cell_shifts,
        live_counts,
        0,
        halo_rows,
        length_x,
        basis_count,
    )
    flat, filter_pre = filter_product(smearing, filter_weight)
    query_tile = projected[halo_rows : halo_rows + tile_rows, :feature_width]
    scalar_tile, vector_tile = edge_core(
        filter_pre, query_tile, key_value, vectors_all, unit_vec, cutoff, neighbour_ids, HEADS
    )
    scalar_low = scalar_tile.astype(jnp.bfloat16)
    out_proj = jnp.dot(scalar_low, out_weight, preferred_element_type=jnp.float32)
    scalar_delta, vector_delta = combine(out_proj, vector_projection, vector_tile)
    own_feats = haloed[:, halo_rows : halo_rows + atom_count].astype(jnp.float32)
    fresh = jnp.concatenate(
        [(own_feats[0] + scalar_delta)[None], own_feats[1:] + vector_delta], axis=0
    )
    return (
        fresh,
        (haloed, normed, projected, vector_projection, vector_tile, scalar_low, out_proj),
    )


def fold_rims(whole, from_lower, from_upper, halo_rows, atom_count, axis_pos):
    middle = lax.slice_in_dim(whole, halo_rows, halo_rows + atom_count, axis=axis_pos)
    filler_shape = list(from_lower.shape)
    filler_shape[axis_pos] = atom_count - 2 * halo_rows
    padded = jnp.concatenate(
        [from_lower, jnp.zeros(filler_shape, jnp.float32), from_upper], axis=axis_pos
    )
    return middle + padded


def layer_backward(weights, kept, incoming, geometry, wrap_image, halo_rows, length_x):
    norm_gain, norm_bias, qkv_weight, vector_weight, filter_weight, out_weight = weights
    haloed, normed, projected, vector_projection, vector_agg, scalar_low, out_proj = kept
    coords_all, neighbour_ids, cell_shifts, live_counts = geometry
    feature_width = haloed.shape[2]
    total_rows = haloed.shape[1]
    atom_count = total_rows - 2 * halo_rows
    basis_count = filter_weight.shape[0]
    combined, combine_back = jax.vjp(combine, out_proj, vector_projection, vector_agg)
    g_out_proj, vector_projection_gradient, g_vector_agg = combine_back((incoming[0], incoming[1:]))
    g_out_proj = g_out_proj.astype(jnp.bfloat16)
    vector_projection_gradient = vector_projection_gradient.astype(jnp.bfloat16)
    g_scalar = lax.dot_general(
        g_out_proj, out_weight, (((1,), (1,)), ((), ())), preferred_element_type=jnp.float32
    )
    out_grad = lax.dot_general(
        scalar_low, g_out_proj, (((0,), (0,)), ((), ())), preferred_element_type=jnp.float32
    )
    local_vector = haloed[1:, halo_rows : halo_rows + atom_count]
    g_vec_back = jnp.einsum(
        "sei,ti->set", vector_projection_gradient, vector_weight, preferred_element_type=jnp.float32
    )
    vector_weight_gradient = jnp.einsum(
        "ivn,ive->ne", local_vector, vector_projection_gradient, preferred_element_type=jnp.float32
    )
    vectors_all = haloed[1:].astype(jnp.float32)
    key_value = projected[:, feature_width:]
    tile_rows = math.gcd(atom_count, 128)
    geometry_fn = functools.partial(
        tile_edges,
        wrap_image=wrap_image,
        neighbour_tile=neighbour_ids,
        shift_tile=cell_shifts,
        count_tile=live_counts,
        first_row=0,
        halo_rows=halo_rows,
        length_x=length_x,
        basis_count=basis_count,
    )
    (unit_vec, cutoff, smearing), geometry_back = jax.vjp(geometry_fn, coords_all)
    flat, filter_pre = filter_product(smearing, filter_weight)
    query_tile = projected[halo_rows : halo_rows + tile_rows, :feature_width]
    core_fn = functools.partial(edge_core, source=neighbour_ids, head_count=HEADS)
    core_out, core_back = jax.vjp(
        core_fn, filter_pre, query_tile, key_value, vectors_all, unit_vec, cutoff
    )
    g_filter, g_query, g_kv_tile, g_vec_tile, g_unit, g_cutoff = core_back((g_scalar, g_vector_agg))
    g_filter = g_filter.astype(jnp.bfloat16)
    g_smearing = lax.dot_general(
        filter_weight, g_filter, (((1,), (1,)), ((), ())), preferred_element_type=jnp.float32
    ).reshape(smearing.shape)
    filter_grad = lax.dot_general(
        flat, g_filter, (((1,), (0,)), ((), ())), preferred_element_type=jnp.float32
    )
    g_coords = geometry_back((g_unit, g_cutoff, g_smearing))[0]
    lower_rim = (g_kv_tile[:halo_rows], g_vec_tile[:, :halo_rows], g_coords[:, :halo_rows])
    upper_rim = (
        g_kv_tile[halo_rows + atom_count :],
        g_vec_tile[:, halo_rows + atom_count :],
        g_coords[:, halo_rows + atom_count :],
    )
    from_upper = (
        shifted(lower_rim[0].astype(jnp.bfloat16), "space", -1).astype(jnp.float32),
        shifted(lower_rim[1].astype(jnp.bfloat16), "space", -1).astype(jnp.float32),
        shifted(lower_rim[2].astype(jnp.bfloat16), "space", -1).astype(jnp.float32),
    )
    from_lower = (
        shifted(upper_rim[0].astype(jnp.bfloat16), "space", 1).astype(jnp.float32),
        shifted(upper_rim[1].astype(jnp.bfloat16), "space", 1).astype(jnp.float32),
        shifted(upper_rim[2].astype(jnp.bfloat16), "space", 1).astype(jnp.float32),
    )
    g_kv_own = fold_rims(g_kv_tile, from_lower[0], from_upper[0], halo_rows, atom_count, 0)
    g_vec_own = fold_rims(g_vec_tile, from_lower[1], from_upper[1], halo_rows, atom_count, 1)
    g_coords_own = fold_rims(g_coords, from_lower[2], from_upper[2], halo_rows, atom_count, 1)
    g_projected = jnp.concatenate([g_query, g_kv_own], axis=1).astype(jnp.bfloat16)
    own_normed = normed[halo_rows : halo_rows + atom_count]
    qkv_grad = lax.dot_general(
        own_normed, g_projected, (((0,), (0,)), ((), ())), preferred_element_type=jnp.float32
    )
    g_normed = lax.dot_general(
        g_projected, qkv_weight, (((1,), (1,)), ((), ())), preferred_element_type=jnp.float32
    )
    own_scalars = haloed[0, halo_rows : halo_rows + atom_count].astype(jnp.float32)
    norm_value, norm_back = jax.vjp(layer_norm, own_scalars, norm_gain, norm_bias)
    g_scalars, gain_grad, bias_grad = norm_back(g_normed)
    input_grad = jnp.concatenate(
        [(incoming[0] + g_scalars)[None], incoming[1:] + g_vec_back + g_vec_own], axis=0
    )
    return (
        input_grad,
        (gain_grad, bias_grad, qkv_grad, vector_weight_gradient, filter_grad, out_grad),
        g_coords_own,
    )


def stack_all(*arrays):
    return jnp.stack(arrays)


def take_row(stacked, index):
    return stacked[index]


def add_all(first_tuple, second_tuple):
    return tuple((left + right for left, right in zip(first_tuple, second_tuple)))


def on_device(
    features,
    coords,
    neighbours,
    counts,
    shifts,
    norm_gain,
    norm_bias,
    qkv_weight,
    vector_weight,
    filter_weight,
    out_weight,
    cotangent,
):
    micro_count = features.shape[0]
    atom_count = features.shape[3]
    halo_rows = atom_count // 4
    space_count = lax.axis_size("space")
    section_index = lax.axis_index("section")
    space_index = lax.axis_index("space")
    length_x = space_count * atom_count * 4.0 / halo_rows
    weights = (
        norm_gain[0].astype(jnp.float32),
        norm_bias[0].astype(jnp.float32),
        qkv_weight[0],
        vector_weight[0],
        filter_weight[0],
        out_weight[0],
    )
    coords_halo = extended(coords[:, 0], (("space", 2),), halo_rows)
    row_index = jnp.arange(atom_count + 2 * halo_rows, dtype=jnp.int32)
    wrap_image = (
        jnp.where((row_index < halo_rows) & (space_index == 0), -1.0, 0.0)
        + jnp.where(
            (row_index >= atom_count + halo_rows) & (space_index == space_count - 1), 1.0, 0.0
        )
    ).astype(jnp.float32)

    def pick_micro(index):
        return (coords_halo[index], neighbours[index, 0], shifts[index, 0], counts[index, 0])

    received = jnp.zeros(features.shape[2:], jnp.bfloat16)
    outputs = jnp.zeros(features.shape[:1] + features.shape[2:], jnp.bfloat16)
    kept_list = []
    for moment in range(micro_count + 1):
        micro_index = jnp.clip(moment - section_index, 0, micro_count - 1)
        valid = (moment - section_index >= 0) & (moment - section_index < micro_count)
        current = jnp.where(section_index == 0, features[min(moment, micro_count - 1), 0], received)
        haloed = extended(current, (("space", 1),), halo_rows)
        fresh, kept = layer_forward(
            weights, haloed, pick_micro(micro_index), wrap_image, halo_rows, length_x
        )
        fresh_low = fresh.astype(jnp.bfloat16)
        outputs = outputs.at[micro_index].set(jnp.where(valid, fresh_low, outputs[micro_index]))
        kept_list.append(kept)
        if moment < micro_count:
            received = from_behind(fresh_low, "section", 1)
    kept_stack = jax.tree.map(stack_all, *kept_list)
    received_grad = jnp.zeros(features.shape[2:], jnp.bfloat16)
    input_total = jnp.zeros(features.shape[:1] + features.shape[2:], jnp.float32)
    coords_total = jnp.zeros(coords[:, 0].shape, jnp.float32)
    totals = None
    for moment in range(micro_count + 1):
        micro_index = jnp.clip(micro_count - moment - section_index, 0, micro_count - 1)
        valid = (micro_count - moment - section_index >= 0) & (
            micro_count - moment - section_index < micro_count
        )
        incoming = jnp.where(
            section_index == 1,
            cotangent[max(micro_count - 1 - moment, 0), 0].astype(jnp.float32),
            received_grad.astype(jnp.float32),
        )
        kept = jax.tree.map(
            functools.partial(take_row, index=micro_index + section_index), kept_stack
        )
        input_grad, weight_grads, coords_part = layer_backward(
            weights, kept, incoming, pick_micro(micro_index), wrap_image, halo_rows, length_x
        )
        input_total = input_total.at[micro_index].set(
            jnp.where(valid, input_grad, input_total[micro_index])
        )
        coords_total = coords_total.at[micro_index].add(jnp.where(valid, coords_part, 0.0))
        if moment < micro_count:
            received_grad = from_behind(input_grad.astype(jnp.bfloat16), "section", -1)
        weight_on = valid.astype(jnp.float32)
        gain_term, bias_term, qkv_term, vec_term, filter_term, out_term = tuple(
            (grad_part * weight_on for grad_part in weight_grads)
        )
        shares = (gain_term, bias_term, qkv_term, vec_term, filter_term, out_term)
        if totals is None:
            totals = tuple(shares)
        else:
            totals = add_all(totals, shares)
    local_parts = (
        lax.psum_scatter(totals[0], "space", scatter_dimension=0, tiled=True),
        lax.psum_scatter(totals[1], "space", scatter_dimension=0, tiled=True),
        lax.psum_scatter(totals[2], "space", scatter_dimension=1, tiled=True),
        lax.psum_scatter(totals[3], "space", scatter_dimension=1, tiled=True),
        lax.psum_scatter(totals[4], "space", scatter_dimension=1, tiled=True),
        lax.psum_scatter(totals[5], "space", scatter_dimension=1, tiled=True),
    )
    totals = lax.psum(
        (
            local_parts[0],
            local_parts[1],
            local_parts[2],
            local_parts[3],
            local_parts[4],
            local_parts[5],
        ),
        "dp",
    )
    coords_sum = lax.psum(coords_total, "section")
    return (
        outputs[None, :, None],
        input_total[None, :, None],
        totals[0][None],
        totals[1][None],
        totals[2][None],
        totals[3][None],
        totals[4][None],
        totals[5][None],
        coords_sum[:, None],
    )


def solution(mesh):
    return jax.shard_map(
        on_device,
        mesh=mesh,
        in_specs=(
            P(None, "dp", None, "space", None),
            P(None, "dp", None, "space"),
            P(None, "dp", None, "space"),
            P(None, "dp", "space"),
            P(None, "dp", None, None, "space"),
            P("section", None),
            P("section", None),
            P("section", None, None),
            P("section", None, None),
            P("section", None, None),
            P("section", None, None),
            P(None, "dp", None, "space", None),
        ),
        out_specs=(
            P("section", None, "dp", None, "space", None),
            P("section", None, "dp", None, "space", None),
            P("section", "space"),
            P("section", "space"),
            P("section", None, "space"),
            P("section", None, "space"),
            P("section", None, "space"),
            P("section", None, "space"),
            P(None, "dp", None, "space"),
        ),
        check_vma=False,
    )
```

profile of v0, /device:TPU:0, one launch (start us, length us, event | category | flops | bytes accessed | tf_op | source)
XLA Modules:
  0.0 1600.3 jit_solution(15299632231153224285)
XLA Ops:
  8.9 6.0 collective-permute-start.1
  15.7 4.7 collective-permute-start.3
  26.5 12.6 gather_fusion.2
  39.4 12.6 gather_fusion.10
  52.1 12.6 gather_fusion.6
  70.2 7.6 gather_fusion.1
  77.9 5.5 gather_fusion.9
  83.4 7.6 gather_fusion.5
  98.0 7.0 fusion.14
  105.1 7.0 fusion.13
  112.2 7.1 fusion.12
  123.5 18.6 %gather_fusion.3 = f32[2048,3,256]{2,1,0:T(4,128)} fusion(f32[3,96,256]{2,0,1:T(4,128)S(1)} %copy.969, s32[2048]{0:T(1024)S(1)} %broadcast_clamp_fusion.2), kind=kCustom, calls=%fused_computation.3 | custom fusion | bytes 12591104 | tf_op jit(solution)/shard_map/gather | solution.py:74
  142.1 9.8 gather_fusion
  151.9 8.3 slice_multiply_fusion.2
  177.4 6.5 fusion.22
  184.3 6.4 fusion.11
  198.1 4.7 collective-permute-start.6
  204.5 5.0 collective-permute-done.5
  211.2 18.6 %gather_fusion.7 = f32[2048,3,256]{2,1,0:T(4,128)} fusion(f32[3,96,256]{2,0,1:T(4,128)S(1)} %copy.978, s32[2048]{0:T(1024)S(1)} %broadcast_clamp_fusion.1), kind=kCustom, calls=%fused_computation.7 | custom fusion | bytes 12591104 | tf_op jit(solution)/shard_map/gather | solution.py:74
  229.8 9.8 gather_fusion.4
  239.5 8.3 slice_multiply_fusion.1
  264.9 6.5 fusion.20
  271.8 6.4 fusion.10
  299.8 10.0 gather_fusion.8
  309.9 9.8 gather_fusion.12
  319.6 10.1 slice_multiply_fusion
  332.8 18.5 %gather_fusion.13 = f32[2048,3,256]{2,1,0:T(4,128)} fusion(f32[3,96,256]{2,0,1:T(4,128)S(1)} %copy.998, s32[2048]{0:T(1024)S(1)} %broadcast_clamp_fusion), kind=kCustom, calls=%fused_computation.13 | custom fusion | bytes 12591104 | tf_op jit(solution)/shard_map/jvp()/gather | solution.py:74
  374.2 8.2 fusion.23
  395.6 18.6 %gather_fusion.11 = f32[2048,3,256]{2,1,0:T(4,128)} fusion(f32[3,96,256]{2,0,1:T(4,128)S(1)} %copy.987, s32[2048]{0:T(1024)S(1)} %broadcast_clamp_fusion), kind=kCustom, calls=%fused_computation.11 | custom fusion | bytes 12591104 | tf_op jit(solution)/shard_map/gather | solution.py:74
  414.3 6.6 fusion.18
  421.6 30.7 %multiply_reduce_fusion.2 = (f32[3,32,64]{0,2,1:T(8,128)}, f32[32,64,256]{2,1,0:T(8,128)}, f32[3,64,256]{2,0,1:T(4,128)S(1)}, f32[32,64,256]{2,1,0:T(8,128)}, f32[3,32,64,256]{3,0,2,1:T(4,128)}) fusion(f32[32,64,256]{2,1,0:T(8,128)} %get-tuple-element.339, f32[3,64,256]{2,0,1:T(4,128)S(1)} %copy-done.52, f32[3,32,64,256]{3,0,2,1:T(4,128)} %bitcast.620, ...), kind=kLoop, calls=%fused_computation.53 | loop fusion | flops 16197632 | bytes 31899648 | tf_op jit(solution)/shard_map/transpose(jvp())/reduce_sum | solution.py:85
  453.7 151.8 %scatter_fusion = f32[3,96,256]{2,0,1:T(4,128)S(1)} fusion(f32[3,96,256]{2,0,1:T(4,128)S(1)} %broadcast.1237.clone, s32[2048]{0:T(1024)S(1)} %copy-done.129, f32[2048,3,256]{2,1,0:T(4,128)} %bitcast.622), kind=kCustom, calls=%fused_computation.19 | custom fusion | flops 1572864 | bytes 18882560 | tf_op jit(solution)/shard_map/transpose(jvp())/scatter-add | solution.py:74
  619.3 9.6 slice_multiply_fusion.7
  633.5 19.1 %scatter_custom_fusion = f32[96,1024]{1,0:T(8,128)S(1)} fusion(s32[2048]{0:T(1024)S(1)} %copy-done.129, f32[2048,1024]{1,0:T(8,128)} %bitcast.638, f32[]{:T(128)} %constant.298.clone.1), kind=kCustom, calls=%fused_computation.312 | custom fusion | flops 2097152 | bytes 393728 | tf_op jit(solution)/shard_map/transpose(jvp())/scatter-add | solution.py:73
  658.1 9.9 gather_fusion.14
  668.0 5.5 slice_multiply_fusion.6
  690.5 9.8 gather_fusion.16
  700.3 5.5 slice_multiply_fusion.4
  726.1 6.1 fusion.2
  756.7 18.5 %gather_fusion.15 = f32[2048,3,256]{2,1,0:T(4,128)} fusion(f32[3,96,256]{2,0,1:T(4,128)S(1)} %copy.1009, s32[2048]{0:T(1024)S(1)} %copy-done.47), kind=kCustom, calls=%fused_computation.15 | custom fusion | bytes 12591104 | tf_op jit(solution)/shard_map/jvp()/gather | solution.py:74
  779.4 18.5 %gather_fusion.17 = f32[2048,3,256]{2,1,0:T(4,128)} fusion(f32[3,96,256]{2,0,1:T(4,128)S(1)} %copy.1020, s32[2048]{0:T(1024)S(1)} %copy-done.45), kind=kCustom, calls=%fused_computation.17 | custom fusion | bytes 12591104 | tf_op jit(solution)/shard_map/jvp()/gather | solution.py:74
  807.8 28.9 %multiply_reduce_fusion.1 = (f32[3,32,64]{0,2,1:T(8,128)}, f32[32,64,256]{2,1,0:T(8,128)}, f32[32,64,256]{2,1,0:T(8,128)}, f32[3,32,64,256]{3,0,2,1:T(4,128)}) fusion(f32[32,64,256]{2,1,0:T(8,128)} %get-tuple-element.335, f32[3,64,256]{2,0,1:T(4,128)S(1)} %copy.1008, f32[3,32,64,256]{3,0,2,1:T(4,128)} %bitcast.624, f32[3,32,64]{0,2,1:T(8,128)S(1)} %copy-done.9, ...), kind=kLoop, calls=%fused_computation.52 | loop fusion | flops 9955328 | bytes 21217280 | tf_op jit(solution)/shard_map/transpose(jvp())/reduce_sum | solution.py:85
  836.8 151.8 %scatter_fusion.1 = f32[3,96,256]{2,0,1:T(4,128)S(1)} fusion(f32[3,96,256]{2,0,1:T(4,128)S(1)} %broadcast.1237.clone.1, s32[2048]{0:T(1024)S(1)} %copy-done.127, f32[2048,3,256]{2,1,0:T(4,128)} %bitcast.627), kind=kCustom, calls=%fused_computation.21 | custom fusion | flops 1572864 | bytes 18882560 | tf_op jit(solution)/shard_map/transpose(jvp())/scatter-add | solution.py:74
  990.1 4.7 collective-permute-start.18
  1005.7 6.5 fusion.25
  1020.1 9.6 slice_multiply_fusion.5
  1034.3 19.1 %scatter_custom_fusion.2 = f32[96,1024]{1,0:T(8,128)S(1)} fusion(s32[2048]{0:T(1024)S(1)} %copy-done.127, f32[2048,1024]{1,0:T(8,128)} %bitcast.639, f32[]{:T(128)} %constant.298.clone.1), kind=kCustom, calls=%fused_computation.310 | custom fusion | flops 2097152 | bytes 393728 | tf_op jit(solution)/shard_map/transpose(jvp())/scatter-add | solution.py:73
  1063.2 6.1 fusion.5
  1099.3 28.9 %multiply_reduce_fusion = (f32[3,32,64]{0,2,1:T(8,128)}, f32[32,64,256]{2,1,0:T(8,128)}, f32[32,64,256]{2,1,0:T(8,128)}, f32[3,32,64,256]{3,0,2,1:T(4,128)}) fusion(f32[32,64,256]{2,1,0:T(8,128)S(1)} %copy-done.13, f32[3,64,256]{2,0,1:T(4,128)S(1)} %copy.1019, f32[3,32,64,256]{3,0,2,1:T(4,128)} %bitcast.623, f32[3,32,64]{0,2,1:T(8,128)S(1)} %copy-done.7, ...), kind=kLoop, calls=%fused_computation.51 | loop fusion | flops 9955328 | bytes 21217280 | tf_op jit(solution)/shard_map/transpose(jvp())/reduce_sum | solution.py:85
  1128.3 151.9 %scatter_fusion.2 = f32[3,96,256]{2,0,1:T(4,128)S(1)} fusion(f32[3,96,256]{2,0,1:T(4,128)S(1)} %broadcast.1237, s32[2048]{0:T(1024)S(1)} %copy-done.125, f32[2048,3,256]{2,1,0:T(4,128)} %bitcast.628), kind=kCustom, calls=%fused_computation.23 | custom fusion | flops 1572864 | bytes 18882560 | tf_op jit(solution)/shard_map/transpose(jvp())/scatter-add | solution.py:74
  1281.6 4.7 collective-permute-start.23
  1309.3 10.1 slice_multiply_fusion.3
  1319.5 4.9 fusion.27
  1329.0 19.1 %scatter_custom_fusion.4 = f32[96,1024]{1,0:T(8,128)S(1)} fusion(s32[2048]{0:T(1024)S(1)} %copy-done.125, f32[2048,1024]{1,0:T(8,128)} %bitcast.640, f32[]{:T(128)} %constant.298.clone.1), kind=kCustom, calls=%fused_computation.308 | custom fusion | flops 2097152 | bytes 393728 | tf_op jit(solution)/shard_map/transpose(jvp())/scatter-add | solution.py:73
  1355.9 7.6 pad_add_fusion
  1363.7 9.0 fusion.8
  1384.8 11.9 scatter_fusion.3
  1406.0 11.8 scatter_fusion.4
  1428.6 11.5 scatter_fusion.5
  1459.3 7.4 psum.55
  1472.8 17.6 %all-reduce.44 = (f32[256]{0:T(256)S(1)}, f32[256]{0:T(256)S(1)}) all-reduce(f32[256]{0:T(256)S(1)} %multiply_add_fusion.1, f32[256]{0:T(256)S(1)} %multiply_add_fusion), channel_id=2, replica_groups=mesh['section'=2,'space'=8,'dp'=2] {'space'}, use_global_device_ids=true, to_apply=%region_66.68.clone | all-reduce | flops 512 | bytes 4096
  1490.5 14.1 reduce-scatter.5.cloned.1.call-done
  1506.5 62.2 %reduce-scatter.9.cloned.1.call-done = f32[32,128]{1,0:T(8,128)} async-done(((f32[32,1024]{1,0:T(8,128)}), f32[32,128]{1,0:T(8,128)}) %reduce-scatter.9.cloned.1.call-update) | async-done | bytes 16400 | tf_op jit(solution)/shard_map/reduce_scatter | solution.py:404
  1573.2 15.4 all-reduce.49.cloned.1.call-done
  (831 shorter events, 401.1 us)
Async XLA Ops:
  7.2 115.1 %copy-start = (bf16[1,256,1280]{2,1,0:T(8,128)(2,1)S(1)}, bf16[1,256,1280]{2,1,0:T(8,128)(2,1)}, u32[]{:S(2)}) copy-start(bf16[1,256,1280]{2,1,0:T(8,128)(2,1)} %param.39) | copy-start | bytes 1966084
  7.2 1483.3 %reduce-scatter.7.cloned.1.call-start = ((), (), s32[]{:S(2)}) async-start(), calls=%async_computation.5 | async-start | bytes 884736 | tf_op jit(solution)/shard_map/reduce_scatter | solution.py:403
  8.9 112.1 %collective-permute-start.1 = (bf16[4,16,256]{2,1,0:T(8,128)(2,1)S(1)}, bf16[4,16,256]{2,1,0:T(8,128)(2,1)S(1)}, u32[]{:S(2)}, u32[]{:S(2)}) collective-permute-start(bf16[4,16,256]{2,1,0:T(8,128)(2,1)S(1)} %get-tuple-element.430), channel_id=1, source_target_pairs={{2,0},{4,2},{6,4},{8,6},{10,8},{12,10},{14,12},{0,14},{3,1},{5,3},... | collective-permute-start | bytes 98312 | tf_op jit(solution)/shard_map/ppermute | solution.py:33
  14.9 106.1 %collective-permute-start = (bf16[4,16,256]{2,1,0:T(8,128)(2,1)S(1)}, bf16[4,16,256]{2,1,0:T(8,128)(2,1)S(1)}, u32[]{:S(2)}, u32[]{:S(2)}) collective-permute-start(bf16[4,16,256]{2,1,0:T(8,128)(2,1)S(1)} %get-tuple-element.429), channel_id=1, source_target_pairs={{0,2},{2,4},{4,6},{6,8},{8,10},{10,12},{12,14},{14,0},{1,3},{3,5},... | collective-permute-start | bytes 98312 | tf_op jit(solution)/shard_map/ppermute | solution.py:31
  15.7 54.3 %collective-permute-start.3 = (f32[2,3,16]{2,0,1:T(2,128)S(1)}, f32[2,3,16]{2,0,1:T(2,128)S(1)}, u32[]{:S(2)}, u32[]{:S(2)}) collective-permute-start(f32[2,3,16]{2,0,1:T(2,128)S(1)} %get-tuple-element.462), channel_id=1, source_target_pairs={{2,0},{4,2},{6,4},{8,6},{10,8},{12,10},{14,12},{0,14},{3,1},{5,3},... | collective-permute-start | bytes 1160 | tf_op jit(solution)/shard_map/ppermute | solution.py:33
  20.4 49.5 %collective-permute-start.2 = (f32[2,3,16]{2,0,1:T(2,128)S(1)}, f32[2,3,16]{2,0,1:T(2,128)S(1)}, u32[]{:S(2)}, u32[]{:S(2)}) collective-permute-start(f32[2,3,16]{2,0,1:T(2,128)S(1)} %get-tuple-element.461), channel_id=1, source_target_pairs={{0,2},{2,4},{4,6},{6,8},{8,10},{10,12},{12,14},{14,0},{1,3},{3,5},... | collective-permute-start | bytes 1160 | tf_op jit(solution)/shard_map/ppermute | solution.py:31
  21.4 268.3 %copy-start.14 = (f32[1,1,4,64,256]{4,3,2,1,0:T(8,128)}, f32[1,1,4,64,256]{4,3,2,1,0:T(8,128)S(1)}, u32[]{:S(2)}) copy-start(f32[1,1,4,64,256]{4,3,2,1,0:T(8,128)S(1)} %convert_select_fusion.2) | copy-start | bytes 786436
  25.1 117.0 %copy-start.44 = (s32[2048]{0:T(1024)}, s32[2048]{0:T(1024)S(1)}, u32[]{:S(2)}) copy-start(s32[2048]{0:T(1024)S(1)} %broadcast_clamp_fusion.2) | copy-start | bytes 24580
  25.8 96.3 %copy-start.181 = (f32[1,256]{1,0:T(1,128)}, f32[1,256]{1,0:T(1,128)S(1)}, u32[]{:S(2)}) copy-start(f32[1,256]{1,0:T(1,128)S(1)} %add.788) | copy-start | bytes 3076
  26.5 95.7 %copy-start.157 = (f32[1,256]{1,0:T(1,128)}, f32[1,256]{1,0:T(1,128)S(1)}, u32[]{:S(2)}) copy-start(f32[1,256]{1,0:T(1,128)S(1)} %mul.1867) | copy-start | bytes 3076
  39.2 53.5 %copy-start.190 = (s32[64]{0:T(128)}, s32[64]{0:T(128)S(1)}, u32[]{:S(2)}) copy-start(s32[64]{0:T(128)S(1)} %get-tuple-element.464) | copy-start | bytes 772
  39.2 57.1 %copy-start.191 = (s32[64]{0:T(128)}, s32[64]{0:T(128)S(1)}, u32[]{:S(2)}) copy-start(s32[64]{0:T(128)S(1)} %get-tuple-element.465) | copy-start | bytes 772
  39.2 57.9 %copy-start.192 = (s32[64]{0:T(128)}, s32[64]{0:T(128)S(1)}, u32[]{:S(2)}) copy-start(s32[64]{0:T(128)S(1)} %get-tuple-element.463) | copy-start | bytes 772
  39.3 190.4 %copy-start.46 = (s32[2048]{0:T(1024)}, s32[2048]{0:T(1024)S(1)}, u32[]{:S(2)}) copy-start(s32[2048]{0:T(1024)S(1)} %broadcast_clamp_fusion.1) | copy-start | bytes 24580
  64.8 33.2 %copy-start.131 = (bf16[1,32,1024]{2,1,0:T(8,128)(2,1)S(1)}, bf16[1,32,1024]{2,1,0:T(8,128)(2,1)}, u32[]{:S(2)}) copy-start(bf16[1,32,1024]{2,1,0:T(8,128)(2,1)} %param.41) | copy-start | bytes 196612
  69.3 42.9 %copy-start.184 = (f32[32]{0:T(128)}, f32[32]{0:T(128)S(1)}, u32[]{:S(2)}) copy-start(f32[32]{0:T(128)S(1)} %pad_maximum_fusion.23) | copy-start | bytes 388
  119.7 64.5 %copy-start.6 = (f32[3,32,64]{0,2,1:T(8,128)}, f32[3,32,64]{0,2,1:T(8,128)S(1)}, u32[]{:S(2)}) copy-start(f32[3,32,64]{0,2,1:T(8,128)S(1)} %copy.970) | copy-start | bytes 73732
  191.5 5.9 collective-permute-start.4
  198.1 6.3 collective-permute-start.6
  202.9 6.6 collective-permute-start.5
  278.4 6.8 collective-permute-start.7
  286.2 5.2 collective-permute-start.9
  286.3 6.7 collective-permute-start.8
  421.6 32.1 %copy-start.129 = (s32[2048]{0:T(1024)S(1)}, s32[2048]{0:T(1024)}, u32[]{:S(2)}) copy-start(s32[2048]{0:T(1024)} %copy-done.128) | copy-start | bytes 24580
  607.0 133.5 %collective-permute-start.13 = (bf16[3,16,256]{2,1,0:T(8,128)(2,1)}, bf16[3,16,256]{2,1,0:T(8,128)(2,1)}, u32[]{:S(2)}, u32[]{:S(2)}) collective-permute-start(bf16[3,16,256]{2,1,0:T(8,128)(2,1)} %get-tuple-element.424), channel_id=1, source_target_pairs={{2,0},{4,2},{6,4},{8,6},{10,8},{12,10},{14,12},{0,14},{3,1},{5,3},... | collective-permute-start | bytes 73736 | tf_op jit(solution)/shard_map/ppermute | solution.py:21
  608.3 132.9 %collective-permute-start.12 = (bf16[3,16,256]{2,1,0:T(8,128)(2,1)}, bf16[3,16,256]{2,1,0:T(8,128)(2,1)}, u32[]{:S(2)}, u32[]{:S(2)}) collective-permute-start(bf16[3,16,256]{2,1,0:T(8,128)(2,1)} %get-tuple-element.423), channel_id=1, source_target_pairs={{14,0},{0,2},{2,4},{4,6},{6,8},{8,10},{10,12},{12,14},{15,1},{1,3}... | collective-permute-start | bytes 73736 | tf_op jit(solution)/shard_map/ppermute | solution.py:21
  653.2 88.7 %collective-permute-start.11 = (bf16[16,1024]{1,0:T(8,128)(2,1)}, bf16[16,1024]{1,0:T(8,128)(2,1)}, u32[]{:S(2)}, u32[]{:S(2)}) collective-permute-start(bf16[16,1024]{1,0:T(8,128)(2,1)} %get-tuple-element.409), channel_id=1, source_target_pairs={{2,0},{4,2},{6,4},{8,6},{10,8},{12,10},{14,12},{0,14},{3,1},{5,3},... | collective-permute-start | bytes 98312 | tf_op jit(solution)/shard_map/ppermute | solution.py:21
  657.2 85.5 %collective-permute-start.10 = (bf16[16,1024]{1,0:T(8,128)(2,1)}, bf16[16,1024]{1,0:T(8,128)(2,1)}, u32[]{:S(2)}, u32[]{:S(2)}) collective-permute-start(bf16[16,1024]{1,0:T(8,128)(2,1)} %get-tuple-element.408), channel_id=1, source_target_pairs={{14,0},{0,2},{2,4},{4,6},{6,8},{8,10},{10,12},{12,14},{15,1},{1,3}... | collective-permute-start | bytes 98312 | tf_op jit(solution)/shard_map/ppermute | solution.py:21
  753.1 50.9 %collective-permute-start.14 = (bf16[4,64,256]{2,1,0:T(8,128)(2,1)}, bf16[4,64,256]{2,1,0:T(8,128)(2,1)}, u32[]{:S(2)}, u32[]{:S(2)}) collective-permute-start(bf16[4,64,256]{2,1,0:T(8,128)(2,1)} %pad_maximum_fusion.14), channel_id=1, source_target_pairs={{16,0},{17,1},{18,2},{19,3},{20,4},{21,5},{22,6},{23,7},{24,8},{25... | collective-permute-start | bytes 393224 | tf_op jit(solution)/shard_map/ppermute | solution.py:43
  836.8 158.0 %copy-start.91 = (f32[64,256]{1,0:T(8,128)S(1)}, f32[64,256]{1,0:T(8,128)}, u32[]{:S(2)}) copy-start(f32[64,256]{1,0:T(8,128)} %slice_bitcast_fusion.4) | copy-start | bytes 196612
  990.1 88.4 %collective-permute-start.18 = (bf16[3,16,256]{2,1,0:T(8,128)(2,1)}, bf16[3,16,256]{2,1,0:T(8,128)(2,1)}, u32[]{:S(2)}, u32[]{:S(2)}) collective-permute-start(bf16[3,16,256]{2,1,0:T(8,128)(2,1)} %get-tuple-element.422), channel_id=1, source_target_pairs={{2,0},{4,2},{6,4},{8,6},{10,8},{12,10},{14,12},{0,14},{3,1},{5,3},... | collective-permute-start | bytes 73736 | tf_op jit(solution)/shard_map/ppermute | solution.py:21
  994.8 84.4 %collective-permute-start.17 = (bf16[3,16,256]{2,1,0:T(8,128)(2,1)}, bf16[3,16,256]{2,1,0:T(8,128)(2,1)}, u32[]{:S(2)}, u32[]{:S(2)}) collective-permute-start(bf16[3,16,256]{2,1,0:T(8,128)(2,1)} %get-tuple-element.421), channel_id=1, source_target_pairs={{14,0},{0,2},{2,4},{4,6},{6,8},{8,10},{10,12},{12,14},{15,1},{1,3}... | collective-permute-start | bytes 73736 | tf_op jit(solution)/shard_map/ppermute | solution.py:21
  1054.0 27.4 %collective-permute-start.16 = (bf16[16,1024]{1,0:T(8,128)(2,1)}, bf16[16,1024]{1,0:T(8,128)(2,1)}, u32[]{:S(2)}, u32[]{:S(2)}) collective-permute-start(bf16[16,1024]{1,0:T(8,128)(2,1)} %get-tuple-element.405), channel_id=1, source_target_pairs={{2,0},{4,2},{6,4},{8,6},{10,8},{12,10},{14,12},{0,14},{3,1},{5,3},... | collective-permute-start | bytes 98312 | tf_op jit(solution)/shard_map/ppermute | solution.py:21
  1058.7 23.4 %collective-permute-start.15 = (bf16[16,1024]{1,0:T(8,128)(2,1)}, bf16[16,1024]{1,0:T(8,128)(2,1)}, u32[]{:S(2)}, u32[]{:S(2)}) collective-permute-start(bf16[16,1024]{1,0:T(8,128)(2,1)} %get-tuple-element.404), channel_id=1, source_target_pairs={{14,0},{0,2},{2,4},{4,6},{6,8},{8,10},{10,12},{12,14},{15,1},{1,3}... | collective-permute-start | bytes 98312 | tf_op jit(solution)/shard_map/ppermute | solution.py:21
  1090.6 7.5 collective-permute-start.19
  1098.2 188.1 %copy-start.26 = (f32[4,64,256]{2,1,0:T(8,128)}, f32[4,64,256]{2,1,0:T(8,128)S(1)}, u32[]{:S(2)}) copy-start(f32[4,64,256]{2,1,0:T(8,128)S(1)} %convert_select_fusion) | copy-start | bytes 786436
  1098.2 188.1 %copy-start.90 = (f32[64,256]{1,0:T(8,128)}, f32[64,256]{1,0:T(8,128)S(1)}, u32[]{:S(2)}) copy-start(f32[64,256]{1,0:T(8,128)S(1)} %slice_bitcast_fusion.3) | copy-start | bytes 196612
  1099.2 187.2 %copy-start.82 = (f32[64,256]{1,0:T(8,128)}, f32[64,256]{1,0:T(8,128)S(1)}, u32[]{:S(2)}) copy-start(f32[64,256]{1,0:T(8,128)S(1)} %get-tuple-element.237) | copy-start | bytes 196612
  1281.6 185.7 %collective-permute-start.23 = (bf16[3,16,256]{2,1,0:T(8,128)(2,1)}, bf16[3,16,256]{2,1,0:T(8,128)(2,1)}, u32[]{:S(2)}, u32[]{:S(2)}) collective-permute-start(bf16[3,16,256]{2,1,0:T(8,128)(2,1)} %get-tuple-element.420), channel_id=1, source_target_pairs={{2,0},{4,2},{6,4},{8,6},{10,8},{12,10},{14,12},{0,14},{3,1},{5,3},... | collective-permute-start | bytes 73736 | tf_op jit(solution)/shard_map/ppermute | solution.py:21
  1286.3 181.7 %collective-permute-start.22 = (bf16[3,16,256]{2,1,0:T(8,128)(2,1)}, bf16[3,16,256]{2,1,0:T(8,128)(2,1)}, u32[]{:S(2)}, u32[]{:S(2)}) collective-permute-start(bf16[3,16,256]{2,1,0:T(8,128)(2,1)} %get-tuple-element.419), channel_id=1, source_target_pairs={{14,0},{0,2},{2,4},{4,6},{6,8},{8,10},{10,12},{12,14},{15,1},{1,3}... | collective-permute-start | bytes 73736 | tf_op jit(solution)/shard_map/ppermute | solution.py:21
  1309.3 181.2 %reduce-scatter.11.cloned.1.call-start = ((), (), s32[]{:S(2)}) async-start(), calls=%async_computation.7 | async-start | bytes 884736 | tf_op jit(solution)/shard_map/reduce_scatter | solution.py:405
  1348.7 24.0 %collective-permute-start.21 = (bf16[16,1024]{1,0:T(8,128)(2,1)}, bf16[16,1024]{1,0:T(8,128)(2,1)}, u32[]{:S(2)}, u32[]{:S(2)}) collective-permute-start(bf16[16,1024]{1,0:T(8,128)(2,1)} %get-tuple-element.401), channel_id=1, source_target_pairs={{2,0},{4,2},{6,4},{8,6},{10,8},{12,10},{14,12},{0,14},{3,1},{5,3},... | collective-permute-start | bytes 98312 | tf_op jit(solution)/shard_map/ppermute | solution.py:21
  1353.4 20.1 %collective-permute-start.20 = (bf16[16,1024]{1,0:T(8,128)(2,1)}, bf16[16,1024]{1,0:T(8,128)(2,1)}, u32[]{:S(2)}, u32[]{:S(2)}) collective-permute-start(bf16[16,1024]{1,0:T(8,128)(2,1)} %get-tuple-element.400), channel_id=1, source_target_pairs={{14,0},{0,2},{2,4},{4,6},{6,8},{8,10},{10,12},{12,14},{15,1},{1,3}... | collective-permute-start | bytes 98312 | tf_op jit(solution)/shard_map/ppermute | solution.py:21
  1363.6 141.1 %reduce-scatter.5.cloned.1.call-start = ((), (), s32[]{:S(2)}) async-start(), calls=%async_computation.4 | async-start | bytes 1474560 | tf_op jit(solution)/shard_map/reduce_scatter | solution.py:402
  1378.0 45.1 %copy-start.24 = (f32[3,32,64]{0,2,1:T(8,128)S(1)}, f32[3,32,64]{0,2,1:T(8,128)}, u32[]{:S(2)}) copy-start(f32[3,32,64]{0,2,1:T(8,128)} %get-tuple-element.255) | copy-start | bytes 73732
  1378.1 47.0 %copy-start.63 = (f32[3,32,64]{2,1,0:T(8,128)S(1)}, f32[3,32,64]{2,1,0:T(8,128)}, u32[]{:S(2)}) copy-start(f32[3,32,64]{2,1,0:T(8,128)} %copy-done.62) | copy-start | bytes 73732
  1378.1 48.6 %copy-start.146 = (f32[32,64]{1,0:T(8,128)S(1)}, f32[32,64]{1,0:T(8,128)}, u32[]{:S(2)}) copy-start(f32[32,64]{1,0:T(8,128)} %copy-done.145) | copy-start | bytes 24580
  1378.1 190.6 %reduce-scatter.9.cloned.1.call-start = ((), (), s32[]{:S(2)}) async-start(), calls=%async_computation.6 | async-start | bytes 147456 | tf_op jit(solution)/shard_map/reduce_scatter | solution.py:404
  1384.8 84.0 %copy-start.27 = (f32[4,64,256]{2,1,0:T(8,128)S(1)}, f32[4,64,256]{2,1,0:T(8,128)}, u32[]{:S(2)}) copy-start(f32[4,64,256]{2,1,0:T(8,128)} %copy-done.26) | copy-start | bytes 786436
  1384.8 84.0 %copy-start.33 = (f32[3,64,256]{2,1,0:T(8,128)S(1)}, f32[3,64,256]{2,1,0:T(8,128)}, u32[]{:S(2)}) copy-start(f32[3,64,256]{2,1,0:T(8,128)} %get-tuple-element.368) | copy-start | bytes 589828
  1384.8 84.0 %copy-start.35 = (f32[3,64,256]{2,1,0:T(8,128)S(1)}, f32[3,64,256]{2,1,0:T(8,128)}, u32[]{:S(2)}) copy-start(f32[3,64,256]{2,1,0:T(8,128)} %get-tuple-element.369) | copy-start | bytes 589828
  1384.8 84.0 %copy-start.36 = (f32[3,64,256]{2,1,0:T(8,128)S(1)}, f32[3,64,256]{2,1,0:T(8,128)}, u32[]{:S(2)}) copy-start(f32[3,64,256]{2,1,0:T(8,128)} %get-tuple-element.392) | copy-start | bytes 589828
  1397.3 46.7 %collective-permute-start.25 = (bf16[3,16]{0,1:T(8,128)(2,1)}, bf16[3,16]{0,1:T(8,128)(2,1)}, u32[]{:S(2)}, u32[]{:S(2)}) collective-permute-start(bf16[3,16]{0,1:T(8,128)(2,1)} %get-tuple-element.445), channel_id=1, source_target_pairs={{2,0},{4,2},{6,4},{8,6},{10,8},{12,10},{14,12},{0,14},{3,1},{5,3},... | collective-permute-start | bytes 296 | tf_op jit(solution)/shard_map/ppermute | solution.py:21
  1402.1 42.7 %collective-permute-start.24 = (bf16[3,16]{0,1:T(8,128)(2,1)}, bf16[3,16]{0,1:T(8,128)(2,1)}, u32[]{:S(2)}, u32[]{:S(2)}) collective-permute-start(bf16[3,16]{0,1:T(8,128)(2,1)} %get-tuple-element.444), channel_id=1, source_target_pairs={{14,0},{0,2},{2,4},{4,6},{6,8},{8,10},{10,12},{12,14},{15,1},{1,3}... | collective-permute-start | bytes 296 | tf_op jit(solution)/shard_map/ppermute | solution.py:21
  1403.7 66.4 %copy-start.56 = (bf16[4,96,256]{2,1,0:T(8,128)(2,1)S(1)}, bf16[4,96,256]{2,1,0:T(8,128)(2,1)}, u32[]{:S(2)}) copy-start(bf16[4,96,256]{2,1,0:T(8,128)(2,1)} %get-tuple-element.362) | copy-start | bytes 589828
  1417.8 53.4 %copy-start.161 = (f32[1,256]{1,0:T(1,128)S(1)}, f32[1,256]{1,0:T(1,128)}, u32[]{:S(2)}) copy-start(f32[1,256]{1,0:T(1,128)} %copy-done.157) | copy-start | bytes 3076
  1417.8 53.4 %copy-start.187 = (f32[64]{0:T(128)S(1)}, f32[64]{0:T(128)}, u32[]{:S(2)}) copy-start(f32[64]{0:T(128)} %broadcast_multiply_fusion.18) | copy-start | bytes 772
  1418.4 33.1 %collective-permute-start.27 = (bf16[3,16]{0,1:T(8,128)(2,1)}, bf16[3,16]{0,1:T(8,128)(2,1)}, u32[]{:S(2)}, u32[]{:S(2)}) collective-permute-start(bf16[3,16]{0,1:T(8,128)(2,1)} %get-tuple-element.443), channel_id=1, source_target_pairs={{2,0},{4,2},{6,4},{8,6},{10,8},{12,10},{14,12},{0,14},{3,1},{5,3},... | collective-permute-start | bytes 296 | tf_op jit(solution)/shard_map/ppermute | solution.py:21
  1440.1 64.7 %copy-start.107 = (f32[1,2,1,4,64,256]{5,4,3,1,2,0:T(8,128)S(1)}, f32[1,2,1,4,64,256]{5,4,3,1,2,0:T(8,128)}, u32[]{:S(2)}) copy-start(f32[1,2,1,4,64,256]{5,4,3,1,2,0:T(8,128)} %copy.1077) | copy-start | bytes 1572868
  1444.0 144.6 %all-reduce.49.cloned.1.call-start = ((), (), s32[]{:S(2)}) async-start(), calls=%async_computation.8 | async-start | bytes 720896 | tf_op jit(solution)/shard_map/psum | solution.py:407
  1444.1 8.3 collective-permute-start.26
  1444.8 8.9 collective-permute-start.29
  1451.6 6.4 collective-permute-start.28
  1506.4 86.8 %copy-start.108 = (f32[1,2,1,4,64,256]{5,4,3,1,2,0:T(8,128)}, f32[1,2,1,4,64,256]{5,4,3,1,2,0:T(8,128)S(1)}, u32[]{:S(2)}) copy-start(f32[1,2,1,4,64,256]{5,4,3,1,2,0:T(8,128)S(1)} %fusion.106) | copy-start | bytes 1572868
  (172 other events, 1885.4 us)
Sparse Core Ops, SparseCore 0:
  1309.4 63.1 reduce-scatter.6
  1376.3 61.4 reduce-scatter.10
  1441.1 63.4 reduce-scatter.4
  1508.4 60.2 reduce-scatter.8
  1571.0 17.5 all-reduce.48
where the time goes:
time: 1630 us; the launch traced here: 1600 us
  other arithmetic  933 us (57%)
  local copies, waits for them, and re-layouts  374 us (23%)
  waiting for transfers between devices  108 us (7%)
  matrix products  69.3 us (4%)
  starting transfers between devices  67.5 us (4%)
  blocking collectives  29.6 us (2%)
  between operations  18.1 us (1%)
    scatter-add x3, other arithmetic, edge_core(): neighbour_vec = vector_features[:, source]  456 us
    gather x6, local copies, waits for them, and re-layouts, edge_core(): neighbour_vec = vector_features[:, source]  111 us
    reduce_sum x3, other arithmetic, edge_core(): values[None, ..., 2 * feature_width:] * unit_vec[..., None]  88.5 us
    mul x8, other arithmetic, edge_core(): values = gathered[..., feature_width:] * filters[..., feature_width:]  67.2 us
    reduce_scatter x1, waiting for transfers between devices, on_device(): lax.psum_scatter(totals[4], 'space', scatter_dimension=1, tiled=True)  62.2 us
    gather x6, local copies, waits for them, and re-layouts, edge_core(): gathered = key_value[source]  59 us
    scatter-add x3, other arithmetic, edge_core(): gathered = key_value[source]  57.2 us
    mul x8, other arithmetic, edge_core(): queries[None] * gathered[..., :feature_width] * filters[..., :feature_width]  39.6 us
  transfers between devices with their start and end apart: 35, of which 10 were waited for; matrix products, arithmetic and copies ran while one was open for 33% of the time, Pallas kernels for 0%

commit v1 on v0

v1 whole, which is shorter than its diff:
```python
import math
from types import SimpleNamespace

import jax
import jax.numpy as jnp
from jax import lax
from jax.experimental import pallas as pl
from jax.experimental.pallas import tpu as pltpu
from jax.sharding import PartitionSpec as P

HEADS = 8
CUTOFF = 5.0
LN_EPS = 1e-05
SOFTEN = 0.25
CROSS = 2.5
GROUP = 4
LANES = 128
SUBLANES = 8
FIRST, SECOND = 0, 1

F32 = jnp.float32
BF16 = jnp.bfloat16
VMEM = pl.BlockSpec(memory_space=pltpu.VMEM)
SMEM = pl.BlockSpec(memory_space=pltpu.SMEM)
HBM = pl.BlockSpec(memory_space=pltpu.HBM)


def dot(left, right, left_dim=1, right_dim=0):
    return lax.dot_general(
        left, right, (((left_dim,), (right_dim,)), ((), ())), preferred_element_type=F32
    )


def iota(shape, dim):
    return lax.broadcasted_iota(jnp.int32, shape, dim)


def packed_places(parts, width):
    row = jnp.concatenate(parts, axis=1)
    high = row.astype(BF16).astype(F32)
    rest = row - high
    middle = rest.astype(BF16).astype(F32)
    rows = jnp.concatenate([high, middle, rest - middle, jnp.zeros((13, row.shape[1]), F32)], axis=0)
    return jnp.concatenate([rows, jnp.zeros((16, width - row.shape[1]), F32)], axis=1).astype(BF16)


def unpacked_places(block, c, count):
    rows = block[:, c * count : (c + 1) * count].astype(F32)
    return rows[0:1] + rows[1:2] + rows[2:3]


class Sizes:
    def __init__(self, atoms, width, basis, slots, space):
        self.atoms, self.width, self.basis, self.slots, self.space = atoms, width, basis, slots, space
        self.halo = atoms // 4
        self.rows = atoms + 2 * self.halo
        self.blocks = slots // GROUP
        self.edges = GROUP * atoms
        self.halves = width // LANES
        self.window = atoms + SUBLANES
        self.sent = 3 * self.halo
        self.widths = (5 * width // space, 3 * width // space, 3 * width // space)
        self.spare = sum(self.widths)
        self.packed = -(-(self.spare + basis) // LANES) * LANES
        self.factors = -(-(self.rows + 4 * atoms) // LANES) * LANES


def halves_of(sz):
    return [slice(cg * LANES, (cg + 1) * LANES) for cg in range(sz.halves)]


def first_row(b):
    return GROUP * b + jnp.where(b >= 4, 1, 0)


def sharpness_of(basis):
    return (2.0 / basis * (1.0 - math.exp(-CUTOFF))) ** (-2)


def write_centres(ref, basis):
    low_end = math.exp(-CUTOFF)
    step = iota(ref.shape, 0).astype(F32) / (basis - 1)
    ref[...] = low_end * (1.0 - step) + step


def edge_geometry(r, sz, m, coords, nbr, counts, shifts):
    A, H, E, EB = sz.atoms, sz.halo, sz.rows, sz.edges
    lane = iota((8, LANES), 1)
    row = iota((8, LANES), 0)
    slab, last = r.scal[1], r.scal[3]
    spot = iota((1, LANES), 1)
    length_x = (last + 1).astype(F32) * (A * 4.0 / H)
    places = []
    for c in range(3):
        places.append(
            jnp.concatenate(
                [
                    unpacked_places(r.pack_low[m, 4], c, H),
                    coords[c],
                    unpacked_places(r.pack_high[m, 4], c, H),
                    jnp.zeros((1, LANES - E), F32),
                ],
                axis=1,
            )
        )
    places.append(
        jnp.where((spot < H) & (slab == 0), -length_x, 0.0)
        + jnp.where((spot >= H + A) & (slab == last), length_x, 0.0)
    )
    near = []
    for c in range(4):
        y = jnp.broadcast_to(places[c], (8, LANES))
        for bit in range(3):
            y = jnp.where((row >> bit) & 1 == 1, pltpu.roll(y, LANES - GROUP * 2**bit, 1), y)
        y = jnp.where(row >= 4, pltpu.roll(y, LANES - 1, 1), y)
        first = jnp.where(lane < A, y, pltpu.roll(y, A - 1, 1))
        other = jnp.where(lane < A, pltpu.roll(y, LANES - 2, 1), pltpu.roll(y, A - 3, 1))
        near.append(jnp.concatenate([first, other], axis=1))
    wide_lane = iota((8, EB), 1)
    wide_row = iota((8, EB), 0)
    wanted = GROUP * wide_row + wide_lane // A + jnp.where(wide_row >= 4, 1, 0) + wide_lane % A
    alive = iota((sz.slots, A), 0) < counts[...]
    code = jnp.where(alive, 16, 0) + (shifts[0] + 1) * 4 + (shifts[1] + 1)
    code = jnp.concatenate([code] * GROUP, axis=1)
    named = jnp.concatenate([nbr[...]] * GROUP, axis=1)
    found = jnp.zeros((8, EB), jnp.int32)
    for n in range(sz.slots):
        found = found + jnp.where(named[n : n + 1, :] == wanted, code[n : n + 1, :], 0)
    live = (found >> 4).astype(F32)
    offsets = (
        near[3],
        (((found >> 2) & 3) - 1).astype(F32) * CROSS,
        ((found & 3) - 1).astype(F32) * CROSS,
    )
    sep = []
    for c in range(3):
        mine = coords[c]
        sep.append(near[c] - jnp.concatenate([mine] * GROUP, axis=1) + offsets[c])
    distance = jnp.sqrt(sep[0] * sep[0] + sep[1] * sep[1] + sep[2] * sep[2] + SOFTEN)
    inside = distance < CUTOFF
    cut = jnp.where(inside, 0.5 * (jnp.cos(math.pi * distance / CUTOFF) + 1.0), 0.0) * live
    for index, value in enumerate(
        sep + [distance, live, cut, jnp.exp(-distance)] + [part / distance for part in sep]
    ):
        r.geo[index] = value


DISTANCE, LIVE, CUT, SHRINK, UNIT = 3, 4, 5, 6, 7


def bell_of(r, sz, b):
    delta = r.geo[SHRINK, pl.ds(b, 1), :] - r.centres[...]
    return delta, jnp.exp(-sharpness_of(sz.basis) * delta * delta)


def write_edge_tables(r, sz, b, wide_kind):
    A, EB = sz.atoms, sz.edges
    cut = r.geo[CUT, pl.ds(b, 1), :]
    _, bell = bell_of(r, sz, b)
    smear = cut * bell
    if hasattr(r, "smear"):
        r.smear[b] = smear.astype(BF16)
    r.smear_t[b] = jnp.transpose(smear).astype(BF16)
    coarse = cut.astype(BF16).astype(F32)
    which = iota((16, EB), 0)
    pair = jnp.where(which == 0, coarse, jnp.where(which == 1, cut - coarse, 0.0)).astype(BF16)
    r.cut_wide[b] = dot(pair, jnp.ones((16, LANES), BF16), 0, 0).astype(wide_kind)
    for c in range(3):
        r.units[b, c * A : (c + 1) * A, :] = (
            r.diag[...] * r.geo[UNIT + c, pl.ds(b, 1), :]
        ).astype(BF16)


def write_constants(r, sz):
    A, EB, F = sz.atoms, sz.edges, sz.width
    if hasattr(r, "centres"):
        write_centres(r.centres, sz.basis)
    if hasattr(r, "diag"):
        r.diag[...] = jnp.where(iota((A, EB), 1) % A == iota((A, EB), 0), 1.0, 0.0)
    if hasattr(r, "fold"):
        r.fold[...] = jnp.where(iota((A, EB), 1) % A == iota((A, EB), 0), 1.0, 0.0).astype(BF16)
    if hasattr(r, "heads"):
        r.heads[...] = jnp.where(
            iota((F, F), 0) // (F // HEADS) == iota((F, F), 1) // (F // HEADS), 0.5, 0.0
        ).astype(BF16)


def node_part(r, sz, own, low, high, wqkv):
    A, H, E, F, CG = sz.atoms, sz.halo, sz.rows, sz.width, sz.halves
    halves = halves_of(sz)
    scalars = jnp.concatenate([low[0, 0:H], own[0], high[0, 0:H]], axis=0).astype(F32)
    centred = scalars - jnp.mean(scalars, axis=-1, keepdims=True)
    spread = jnp.mean(centred * centred, axis=-1, keepdims=True)
    scale = lax.rsqrt(spread + LN_EPS)
    normed = (centred * scale * r.norms[0:1, :] + r.norms[1:2, :]).astype(BF16)
    left = r.left
    left[0:E, :] = normed
    left[E : E + 3 * A, :] = own[1:4].reshape(3 * A, F)
    left[E + 4 * A :, :] = jnp.zeros((sz.factors - E - 4 * A, F), BF16)
    for part in range(5):
        projected = dot(normed, wqkv[:, part * F : (part + 1) * F])
        for cg in range(CG):
            if part == 0:
                r.query[cg] = projected[H : H + A, halves[cg]]
            else:
                r.kv[(part - 1) * CG + cg] = projected[:, halves[cg]]
    for c in range(3):
        for cg in range(CG):
            r.vec[c * CG + cg, 0:H, :] = low[c + 1, 0:H, halves[cg]].astype(F32)
            r.vec[c * CG + cg, H : H + A, :] = own[c + 1][:, halves[cg]].astype(F32)
            r.vec[c * CG + cg, H + A : E, :] = high[c + 1, 0:H, halves[cg]].astype(F32)
    return centred * scale, scale


def tiles(sz, first):
    A = sz.atoms
    for kk in range(GROUP):
        for cg in range(sz.halves):
            yield (
                cg,
                slice(kk * A, (kk + 1) * A),
                slice(cg * LANES, (cg + 1) * LANES),
                pl.ds(first + kk, A),
            )


def vector_dot(r, sz):
    A, F, vp = sz.atoms, sz.width, r.vproj
    return sum(
        vp[c * A : (c + 1) * A, 0:F] * vp[c * A : (c + 1) * A, F : 2 * F] for c in range(3)
    )


def write_layer_output(r, sz, own, out_proj, vec_dot, vector_agg):
    A, H, F, vp = sz.atoms, sz.halo, sz.width, r.vproj
    for index in range(4):
        if index == 0:
            fresh = vec_dot * out_proj[:, F : 2 * F] + out_proj[:, 2 * F :]
        else:
            rows = slice((index - 1) * A, index * A)
            fresh = vp[rows, 2 * F :] * out_proj[:, 0:F] + vector_agg[index - 1]
        fresh = (own[index].astype(F32) + fresh).astype(BF16)
        r.fresh[index] = fresh
        if hasattr(r, "head"):
            r.head[index, 0:H, :] = fresh[:H]
            r.tail[index, 0:H, :] = fresh[A - H :]


def first_forward(r, sz, m):
    A, H, E, F, EB = sz.atoms, sz.halo, sz.rows, sz.width, sz.edges
    CG = sz.halves
    early = [
        (r.coords.at[m], r.s_coords),
        (r.nbr.at[m, 0], r.s_nbr),
        (r.counts.at[m], r.s_counts),
        (r.shifts.at[m, 0], r.s_shifts),
        (r.features.at[m, 0], r.s_own),
        (r.wqkv.at[0], r.s_wqkv),
    ]
    late = [(r.wfilt.at[0], r.s_wfilt), (r.wvec.at[0], r.s_wvec), (r.wout.at[0], r.s_wout)]
    copies = [
        pltpu.make_async_copy(source, target, r.sems.at[i])
        for i, (source, target) in enumerate(early + late)
    ]
    for copy in copies:
        copy.start()
    write_constants(r, sz)
    r.sagg[...] = jnp.zeros_like(r.sagg)
    r.vagg[...] = jnp.zeros_like(r.vagg)
    for copy in copies[: len(early)]:
        copy.wait()
    edge_geometry(r, sz, m, r.s_coords, r.s_nbr, r.s_counts, r.s_shifts)

    def tables(b, carry):
        write_edge_tables(r, sz, b, F32)
        return carry

    lax.fori_loop(0, sz.blocks, tables, 0, unroll=2)
    own = r.s_own
    node_part(r, sz, own, r.pack_low.at[m], r.pack_high.at[m], r.s_wqkv)
    for copy in copies[len(early) :]:
        copy.wait()
    r.wh[...] = (r.s_wfilt[...].astype(F32) * 0.5).astype(BF16)
    r.vproj[...] = dot(r.left[E : E + 3 * A, :], r.s_wvec[...])

    def filter_part(b, part):
        return dot(r.smear_t[b], r.wh[:, part * F : (part + 1) * F])

    def block(b, carry):
        first = first_row(b)
        half = filter_part(b, 0)
        for cg, at, cols, near_rows in tiles(sz, first):
            h = half[at, cols]
            product = r.query[cg] * r.kv[cg, near_rows, :] * (h + h * jnp.tanh(h))
            coarse = product.astype(BF16)
            r.pack1[at, cols] = coarse
            r.pack2[at, cols] = (product - coarse.astype(F32)).astype(BF16)
        score = dot(r.pack1[...], r.heads[...]) + dot(r.pack2[...], r.heads[...])
        r.score[b] = score.astype(BF16)
        half = filter_part(b, 2)
        for cg, at, cols, near_rows in tiles(sz, first):
            h = half[at, cols]
            value = r.kv[2 * CG + cg, near_rows, :] * (h + h * jnp.tanh(h))
            for c in range(3):
                r.vagg[c * CG + cg] += r.vec[c * CG + cg, near_rows, :] * value
        half = filter_part(b, 3)
        for cg, at, cols, near_rows in tiles(sz, first):
            h = half[at, cols]
            value = r.kv[3 * CG + cg, near_rows, :] * (h + h * jnp.tanh(h))
            r.third[b, at, cols] = value.astype(BF16)
        half = filter_part(b, 1)
        for cg, at, cols, near_rows in tiles(sz, first):
            h = half[at, cols]
            s = score[at, cols]
            attention = (s + s * jnp.tanh(s)) * r.cut_wide[b, at, :]
            r.sagg[cg] += attention * (r.kv[CG + cg, near_rows, :] * (h + h * jnp.tanh(h)))
        return carry

    lax.fori_loop(0, sz.blocks, block, 0)
    third = sum(dot(r.units[b], r.third[b]) for b in range(sz.blocks))
    scalar_low = jnp.concatenate([r.sagg[cg] for cg in range(CG)], axis=1).astype(BF16)
    r.scalar_out[...] = scalar_low
    out_proj = dot(scalar_low, r.s_wout[...])
    vector_agg = [
        jnp.concatenate([r.vagg[c * CG + cg] for cg in range(CG)], axis=1)
        + third[c * A : (c + 1) * A, :]
        for c in range(3)
    ]
    write_layer_output(r, sz, own, out_proj, vector_dot(r, sz), vector_agg)


def edge_filters(r, sz, m):
    F = sz.width
    write_constants(r, sz)
    edge_geometry(r, sz, m, r.coords.at[m], r.nbr.at[m, 0], r.counts.at[m], r.shifts.at[m, 0])
    r.wh[...] = (r.wfilt[0].astype(F32) * 0.5).astype(BF16)

    def block(b, carry):
        write_edge_tables(r, sz, b, BF16)
        for part in range(4):
            cols = slice(part * F, (part + 1) * F)
            h = dot(r.smear_t[b], r.wh[:, cols])
            t = jnp.tanh(h)
            up = 1.0 + t
            f = h * up
            r.silu[b, :, cols] = f.astype(BF16)
            r.slope[b, :, cols] = (up + f * (1.0 - t)).astype(BF16)
        return carry

    lax.fori_loop(0, sz.blocks, block, 0)


def both_ways(r, sz, m, fwd):
    A, H, E, F = sz.atoms, sz.halo, sz.rows, sz.width
    EB, CG, NB, W = sz.edges, sz.halves, sz.blocks, sz.window
    lane = iota((8, LANES), 1)
    row = iota((8, LANES), 0)
    halves = halves_of(sz)
    if fwd:
        own, low, high = r.own, r.low, r.high
    else:
        own, low, high = r.features.at[m, 0], r.pack_low.at[m], r.pack_high.at[m]
    wqkv, wvec, wout = r.wqkv.at[0], r.wvec.at[0], r.wout.at[0]
    write_constants(r, sz)
    xhat, scale = node_part(r, sz, own, low, high, wqkv)
    gain = r.norms[0:1, :]
    left = r.left
    vp = r.vproj
    vp[...] = dot(left[E : E + 3 * A, :], wvec[...])
    r.wh[...] = (r.wfilt[0].astype(F32) * 0.5).astype(BF16)
    for cg in range(CG):
        r.query_low[:, halves[cg]] = r.query[cg].astype(BF16)

    if fwd:
        r.sagg[...] = jnp.zeros_like(r.sagg)
        r.vagg[...] = jnp.zeros_like(r.vagg)

        def forward_block(b, carry):
            first = first_row(b)
            for cg, at, cols, near_rows in tiles(sz, first):
                product = r.query[cg] * r.kv[cg, near_rows, :] * r.silu[b, at, cols].astype(F32)
                coarse = product.astype(BF16)
                r.pack1[at, cols] = coarse
                r.pack2[at, cols] = (product - coarse.astype(F32)).astype(BF16)
            score = dot(r.pack1[...], r.heads[...]) + dot(r.pack2[...], r.heads[...])
            for cg, at, cols, near_rows in tiles(sz, first):
                f = r.silu[b, at, slice(2 * F + cg * LANES, 2 * F + (cg + 1) * LANES)]
                value = r.kv[2 * CG + cg, near_rows, :].astype(BF16) * f
                for c in range(3):
                    r.spread[1 + c, at, cols] = (
                        r.vec[c * CG + cg, near_rows, :].astype(BF16) * value
                    )
            for cg, at, cols, near_rows in tiles(sz, first):
                f = r.silu[b, at, slice(3 * F + cg * LANES, 3 * F + (cg + 1) * LANES)]
                r.pack3[at, cols] = r.kv[3 * CG + cg, near_rows, :].astype(BF16) * f
            for cg, at, cols, near_rows in tiles(sz, first):
                f = r.silu[b, at, slice(F + cg * LANES, F + (cg + 1) * LANES)]
                s = score[at, cols].astype(BF16)
                r.score[b, at, cols] = s
                attention = s * (1.0 + jnp.tanh(s)) * r.cut_wide[b, at, :]
                r.spread[0, at, cols] = attention * (
                    r.kv[CG + cg, near_rows, :].astype(BF16) * f
                )
            r.sagg[...] += dot(r.fold[...], r.spread[0])
            for c in range(3):
                r.vagg[c] += dot(r.fold[...], r.spread[1 + c]) + dot(
                    r.units[b, c * A : (c + 1) * A, :], r.pack3[...]
                )
            return carry

        lax.fori_loop(0, NB, forward_block, 0)
        scalar_low = r.sagg[...].astype(BF16)
    else:
        scalar_low = r.scalar_in[...]
    left[E + 3 * A : E + 4 * A, :] = scalar_low
    out_proj = dot(scalar_low, wout[...])
    vec_dot = vector_dot(r, sz)
    if fwd:
        write_layer_output(r, sz, own, out_proj, vec_dot, [r.vagg[c] for c in range(3)])

    def incoming(index):
        if fwd:
            return r.cotangent[m, 0, index].astype(F32)
        gap = jnp.zeros((A - 2 * H, F), F32)
        edge = [r.inc_low[index, 0:H].astype(F32), gap, r.inc_high[index, 0:H].astype(F32)]
        value = r.inc[index].astype(F32) + jnp.concatenate(edge, axis=0)
        return value.astype(BF16).astype(F32)

    g_x = incoming(0)
    r.gx[0] = g_x
    g_first = jnp.zeros((A, F), F32)
    g_mid = g_x * out_proj[:, F : 2 * F]
    for c in range(3):
        g_vec = incoming(c + 1)
        r.gx[c + 1] = g_vec
        rows = slice(c * A, (c + 1) * A)
        r.gvlow[rows, :] = g_vec.astype(BF16)
        g_first = g_first + g_vec * vp[rows, 2 * F :]
        r.gvproj[rows, 0:F] = (g_mid * vp[rows, F : 2 * F]).astype(BF16)
        r.gvproj[rows, F : 2 * F] = (g_mid * vp[rows, 0:F]).astype(BF16)
        r.gvproj[rows, 2 * F :] = (g_vec * out_proj[:, 0:F]).astype(BF16)
    r.gout[:, 0:F] = g_first.astype(BF16)
    r.gout[:, F : 2 * F] = (g_x * vec_dot).astype(BF16)
    r.gout[:, 2 * F :] = g_x.astype(BF16)
    r.gs[...] = dot(r.gout[...], wout[...], 1, 1).astype(BF16)
    for total in (r.gnear, r.gq, r.gfilt):
        total[...] = jnp.zeros_like(total)

    def backward_block(b, carry):
        first = first_row(b)
        base = pl.multiple_of(first // SUBLANES * SUBLANES, SUBLANES)

        def filters(part, cg, at):
            cols = slice(part * F + cg * LANES, part * F + (cg + 1) * LANES)
            return r.silu[b, at, cols], r.slope[b, at, cols], cols

        for cg, at, cols, near_rows in tiles(sz, first):
            f, _, _ = filters(1, cg, at)
            value = r.kv[CG + cg, near_rows, :].astype(BF16)
            r.pack2[at, cols] = r.gs[:, cols] * (value * f)
            r.keep4[at, cols] = value
        g_att = dot(r.pack2[...], r.heads[...])
        for cg, at, cols, near_rows in tiles(sz, first):
            f, slope, part_cols = filters(2, cg, at)
            value = r.kv[2 * CG + cg, near_rows, :].astype(BF16)
            message = value * f
            for c in range(3):
                g_vec = r.gvlow[c * A : (c + 1) * A, cols]
                term = g_vec * r.vec[c * CG + cg, near_rows, :].astype(BF16)
                g_edge = term if c == 0 else g_edge + term
                r.spread[4 + c, at, cols] = g_vec * message
            r.spread[2, at, cols] = g_edge * f
            r.gpre[at, part_cols] = g_edge * (value * slope)
        g_third = dot(r.units[b], r.gvlow[...], 0, 0)
        for cg, at, cols, near_rows in tiles(sz, first):
            f, slope, part_cols = filters(3, cg, at)
            value = r.kv[3 * CG + cg, near_rows, :].astype(BF16)
            r.pack3[at, cols] = value * f
            g_edge = g_third[at, cols].astype(BF16)
            r.spread[3, at, cols] = g_edge * f
            r.gpre[at, part_cols] = g_edge * (value * slope)
        for cg, at, cols, near_rows in tiles(sz, first):
            s = r.score[b, at, cols]
            t = jnp.tanh(s)
            up = 1.0 + t
            act = s * up
            wide = r.cut_wide[b, at, :]
            ga = g_att[at, cols].astype(BF16)
            r.pack1[at, cols] = ga * act
            g_score = ga * wide * (up + act * (1.0 - t))
            g_edge = r.gs[:, cols] * (act * wide)
            f, slope, part_cols = filters(0, cg, at)
            key = r.kv[cg, near_rows, :].astype(BF16)
            middle = g_score * f
            steep = g_score * slope
            r.spread[7, at, cols] = middle * key
            r.spread[0, at, cols] = middle * r.query_low[:, cols]
            r.gpre[at, part_cols] = steep * (key * r.query_low[:, cols])
            f, slope, part_cols = filters(1, cg, at)
            r.spread[1, at, cols] = g_edge * f
            r.gpre[at, part_cols] = g_edge * (r.keep4[at, cols] * slope)
        lanes = iota((W, EB), 1)
        place = jnp.where(
            lanes % A + lanes // A + (first - base) == iota((W, EB), 0), 1.0, 0.0
        ).astype(BF16)
        for index in range(7):
            r.gnear[index, pl.ds(base, W), :] += dot(place, r.spread[index])
        r.gq[...] += dot(r.fold[...], r.spread[7])
        g_unit = dot(r.gvlow[...], r.pack3[...], 1, 1)
        for c in range(3):
            r.gunit[c, pl.ds(b, 1), :] = jnp.sum(
                g_unit[c * A : (c + 1) * A, :] * r.diag[...], axis=0, keepdims=True
            )
        g_cut = dot(jnp.ones((16, F), BF16), r.pack1[...], 1, 1)[0:1, :] * (2.0 * HEADS / F)
        g_smear = dot(r.wh[...], r.gpre[...], 1, 1)
        r.gfilt[...] += dot(r.smear[b], r.gpre[...])
        delta, bell = bell_of(r, sz, b)
        through = g_smear * bell
        r.gcut[pl.ds(b, 1), :] = g_cut + jnp.sum(through, axis=0, keepdims=True)
        r.gshrink[pl.ds(b, 1), :] = r.geo[CUT, pl.ds(b, 1), :] * jnp.sum(
            through * delta, axis=0, keepdims=True
        ) * (-2.0 * sharpness_of(sz.basis))
        return carry

    lax.fori_loop(0, NB, backward_block, 0)

    distance = r.geo[DISTANCE]
    g_dist = r.gcut[...] * r.geo[LIVE] * jnp.where(
        distance < CUTOFF,
        (-0.5 * math.pi / CUTOFF) * jnp.sin(math.pi * distance / CUTOFF),
        0.0,
    ) - r.gshrink[...] * r.geo[SHRINK]
    inverse = 1.0 / distance
    g_unit = [r.gunit[c] for c in range(3)]
    sep = [r.geo[c] for c in range(3)]
    along = g_unit[0] * sep[0] + g_unit[1] * sep[1] + g_unit[2] * sep[2]
    radial = (g_dist - along * inverse * inverse) * inverse
    r.gplaces[...] = jnp.zeros_like(r.gplaces)
    for c in range(3):
        g_sep = g_unit[c] * inverse + radial * sep[c]
        first, other = g_sep[:, :LANES], g_sep[:, LANES:]
        z = (
            jnp.where(lane < A, first, 0.0)
            + pltpu.roll(jnp.where(lane < A, 0.0, first), A + 1, 1)
            + pltpu.roll(jnp.where(lane < A, other, 0.0), 2, 1)
            + pltpu.roll(jnp.where(lane < A, 0.0, other), A + 3, 1)
        )
        for bit in range(3):
            z = jnp.where((row >> bit) & 1 == 1, pltpu.roll(z, GROUP * 2**bit, 1), z)
        z = jnp.where(row >= 4, pltpu.roll(z, 1, 1), z)
        total = jnp.sum(g_sep, axis=0, keepdims=True)
        mine = total[:, 0:A] + total[:, A : 2 * A] + total[:, 2 * A : 3 * A] + total[:, 3 * A :]
        mine = jnp.concatenate(
            [jnp.zeros((1, H), F32), mine, jnp.zeros((1, LANES - H - A), F32)], axis=1
        )
        r.gplaces[c : c + 1, :] = jnp.sum(z, axis=0, keepdims=True) - mine

    gproj = r.gproj
    gproj[:, 0:F] = jnp.zeros((E, F), BF16)
    gproj[H : H + A, 0:F] = r.gq[...].astype(BF16)
    for part in range(4):
        gproj[:, (part + 1) * F : (part + 2) * F] = r.gnear[part].astype(BF16)
    g_normed = dot(gproj[...], wqkv[...], 1, 1)
    u = gain * g_normed
    g_scalars = scale * (
        u
        - jnp.mean(u, axis=-1, keepdims=True)
        - xhat * jnp.mean(u * xhat, axis=-1, keepdims=True)
    )
    r.gnorm[...] = jnp.zeros_like(r.gnorm)
    r.gnorm[0:1, :] = jnp.sum(g_normed * xhat, axis=0, keepdims=True)
    r.gnorm[1:2, :] = jnp.sum(g_normed, axis=0, keepdims=True)
    vec_back = dot(r.gvproj[...], wvec[...], 1, 1)
    for index in range(4):
        if index == 0:
            whole = g_scalars
            middle = whole[H : H + A] + r.gx[0]
        else:
            c = index - 1
            whole = r.gnear[4 + c]
            middle = whole[H : H + A] + r.gx[index] + vec_back[c * A : (c + 1) * A, :]
        r.back[index] = middle
        r.back_low[index] = middle.astype(BF16)
        r.rim_low[index] = whole[0:H].astype(BF16)
        r.rim_high[index] = whole[H + A :].astype(BF16)


FACTORS = ("left", "gproj", "gvproj", "gout", "gfilt", "gnorm", "rim_low", "rim_high", "gplaces")


def call(body, arrays, outs, scratch, role=None, grant_mb=24):
    arrays, outs = vars(arrays), vars(outs)
    names = list(arrays) + list(outs) + list(scratch)

    def kernel(*args):
        refs = SimpleNamespace(**dict(zip(names, args, strict=True)))
        if role is None:
            body(refs)
        else:
            pl.when(refs.scal[0] == role)(lambda: body(refs))

    results = pl.pallas_call(
        kernel,
        out_shape=list(outs.values()),
        in_specs=[spec for _, spec in arrays.values()],
        out_specs=[VMEM for _ in outs],
        scratch_shapes=[
            pltpu.VMEM(*s) if isinstance(s, tuple) else s for s in scratch.values()
        ],
        compiler_params=pltpu.CompilerParams(vmem_limit_bytes=grant_mb * 2**20),
    )(*[array for array, _ in arrays.values()])
    return SimpleNamespace(**dict(zip(outs, results, strict=True)))


def first_call(sz, m, arrays):
    A, H, E, F = sz.atoms, sz.halo, sz.rows, sz.width
    EB, CG, NB = sz.edges, sz.halves, sz.blocks
    shape = jax.ShapeDtypeStruct
    outs = SimpleNamespace(
        fresh=shape((4, A, F), BF16),
        head=shape((4, sz.sent, F), BF16),
        tail=shape((4, sz.sent, F), BF16),
        scalar_out=shape((A, F), BF16),
        score=shape((NB, EB, F), BF16),
    )
    scratch = dict(
        s_own=((4, A, F), BF16),
        s_coords=((3, 1, A), F32),
        s_nbr=((sz.slots, A), jnp.int32),
        s_counts=((1, A), jnp.int32),
        s_shifts=((2, sz.slots, A), jnp.int32),
        s_wqkv=((F, 5 * F), BF16),
        s_wvec=((F, 3 * F), BF16),
        s_wfilt=((sz.basis, 4 * F), BF16),
        s_wout=((F, 3 * F), BF16),
        sems=pltpu.SemaphoreType.DMA((9,)),
        left=((sz.factors, F), BF16),
        query=((CG, A, LANES), F32),
        kv=((4 * CG, E, LANES), F32),
        vec=((3 * CG, E, LANES), F32),
        vproj=((3 * A, 3 * F), F32),
        wh=((sz.basis, 4 * F), BF16),
        heads=((F, F), BF16),
        diag=((A, EB), F32),
        geo=((10, 8, EB), F32),
        centres=((sz.basis, EB), F32),
        smear_t=((NB, EB, sz.basis), BF16),
        cut_wide=((NB, EB, LANES), F32),
        units=((NB, 3 * A, EB), BF16),
        pack1=((EB, F), BF16),
        pack2=((EB, F), BF16),
        sagg=((CG, A, LANES), F32),
        vagg=((3 * CG, A, LANES), F32),
        third=((NB, EB, F), BF16),
    )
    return call(lambda r: first_forward(r, sz, m), arrays, outs, scratch, FIRST, grant_mb=54)


def filter_call(sz, m, arrays):
    A, F = sz.atoms, sz.width
    EB, NB = sz.edges, sz.blocks
    shape = jax.ShapeDtypeStruct
    outs = SimpleNamespace(
        geo=shape((10, 8, EB), F32),
        smear=shape((NB, sz.basis, EB), BF16),
        cut_wide=shape((NB, EB, LANES), BF16),
        units=shape((NB, 3 * A, EB), BF16),
        silu=shape((NB, EB, 4 * F), BF16),
        slope=shape((NB, EB, 4 * F), BF16),
    )
    scratch = dict(
        wh=((sz.basis, 4 * F), BF16),
        diag=((A, EB), F32),
        centres=((sz.basis, EB), F32),
        smear_t=((NB, EB, sz.basis), BF16),
    )
    return call(lambda r: edge_filters(r, sz, m), arrays, outs, scratch)


def both_call(sz, m, fwd, arrays):
    A, H, E, F = sz.atoms, sz.halo, sz.rows, sz.width
    EB, CG, NB = sz.edges, sz.halves, sz.blocks
    shape = jax.ShapeDtypeStruct
    outs = SimpleNamespace(
        back=shape((4, A, F), F32),
        back_low=shape((4, A, F), BF16),
        rim_low=shape((4, H, F), BF16),
        rim_high=shape((4, H, F), BF16),
        gplaces=shape((8, LANES), F32),
        left=shape((sz.factors, F), BF16),
        gproj=shape((E, 5 * F), BF16),
        gvproj=shape((3 * A, 3 * F), BF16),
        gout=shape((A, 3 * F), BF16),
        gfilt=shape((sz.basis, 4 * F), F32),
        gnorm=shape((8, F), F32),
    )
    scratch = dict(
        query=((CG, A, LANES), F32),
        query_low=((A, F), BF16),
        kv=((4 * CG, E, LANES), F32),
        vec=((3 * CG, E, LANES), F32),
        vproj=((3 * A, 3 * F), F32),
        wh=((sz.basis, 4 * F), BF16),
        heads=((F, F), BF16),
        diag=((A, EB), F32),
        fold=((A, EB), BF16),
        centres=((sz.basis, EB), F32),
        pack1=((EB, F), BF16),
        pack2=((EB, F), BF16),
        pack3=((EB, F), BF16),
        keep4=((EB, F), BF16),
        gx=((4, A, F), F32),
        gvlow=((3 * A, F), BF16),
        gs=((A, F), BF16),
        spread=((8, EB, F), BF16),
        gpre=((EB, 4 * F), BF16),
        gq=((A, F), F32),
        gnear=((7, E, F), F32),
        gunit=((3, 8, EB), F32),
        gcut=((8, EB), F32),
        gshrink=((8, EB), F32),
    )
    if fwd:
        outs.fresh = shape((4, A, F), BF16)
        scratch.update(
            score=((NB, EB, F), BF16), sagg=((A, F), F32), vagg=((3, A, F), F32)
        )
    role = SECOND if fwd else FIRST
    return call(lambda r: both_ways(r, sz, m, fwd), arrays, outs, scratch, role)


def border_call(sz, features, coords):
    A, H, F = sz.atoms, sz.halo, sz.width
    count = features.shape[0]

    def body(r):
        copies = [pltpu.make_async_copy(r.coords, r.s_coords, r.sems.at[2 * count])]
        for m in range(count):
            copies.append(
                pltpu.make_async_copy(
                    r.features.at[m, 0, :, A - H : A, :], r.up.at[m, 0:4], r.sems.at[2 * m]
                )
            )
            copies.append(
                pltpu.make_async_copy(
                    r.features.at[m, 0, :, 0:H, :], r.down.at[m, 0:4], r.sems.at[2 * m + 1]
                )
            )
        for copy in copies:
            copy.start()
        copies[0].wait()
        for m in range(count):
            r.up[m, 4] = packed_places([r.s_coords[m, c][:, A - H :] for c in range(3)], F)
            r.down[m, 4] = packed_places([r.s_coords[m, c][:, :H] for c in range(3)], F)
        for copy in copies[1:]:
            copy.wait()

    shape = jax.ShapeDtypeStruct((count, 5, H, F), BF16)
    return call(
        body,
        SimpleNamespace(features=(features, HBM), coords=(coords, HBM)),
        SimpleNamespace(up=shape, down=shape),
        dict(s_coords=(coords.shape, F32), sems=pltpu.SemaphoreType.DMA((2 * count + 1,))),
        grant_mb=54,
    )


def gradient_call(sz, scal, sets):
    A, H, E, F = sz.atoms, sz.halo, sz.rows, sz.width
    count = len(sets[0])
    K = sz.factors
    w1, w2, w3 = sz.widths
    w4, w5 = 4 * F // sz.space, F // sz.space
    half = F // 2
    arrays = SimpleNamespace(scal=(scal, SMEM))
    for role in (FIRST, SECOND):
        for m in range(count):
            for name in FACTORS:
                setattr(arrays, f"{name}_{role}_{m}", (getattr(sets[role][m], name), VMEM))

    def body(r, role):
        def get(name, m):
            return getattr(r, f"{name}_{role}_{m}")

        for m in range(count):
            r.up[m, 0:4] = get("rim_high", m)[...]
            r.down[m, 0:4] = get("rim_low", m)[...]
            places = get("gplaces", m)
            r.up[m, 4] = packed_places([places[c : c + 1, H + A : E] for c in range(3)], F)
            r.down[m, 4] = packed_places([places[c : c + 1, 0:H] for c in range(3)], F)
            for c in range(3):
                r.mine[m, c] = places[c : c + 1, H : H + A]
            r.left[:, m * K : (m + 1) * K] = jnp.transpose(get("left", m)[...])
        filt = jnp.transpose(sum(get("gfilt", m)[...] for m in range(count)) * 0.5)
        norm = sum(get("gnorm", m)[...] for m in range(count))
        r.right[...] = jnp.zeros_like(r.right)
        core = r.scal[2]
        for k in range(sz.space):
            for m in range(count):
                at = m * K
                r.right[at : at + E, 0:w1] = get("gproj", m)[:, k * w1 : (k + 1) * w1]
                at += E
                r.right[at : at + 3 * A, w1 : w1 + w2] = get("gvproj", m)[:, k * w2 : (k + 1) * w2]
                at += 3 * A
                r.right[at : at + A, w1 + w2 : sz.spare] = get("gout", m)[:, k * w3 : (k + 1) * w3]
            r.packed[...] = dot(r.left[...], r.right[...])
            spare = slice(sz.spare, sz.spare + sz.basis)
            r.packed[0:w4, spare] = filt[k * w4 : (k + 1) * w4, :]
            narrow = slice(sz.spare, sz.spare + w5)
            r.packed[half : half + 1, narrow] = norm[0:1, k * w5 : (k + 1) * w5]
            r.packed[half + 8 : half + 9, narrow] = norm[1:2, k * w5 : (k + 1) * w5]
            r.send[k] = r.packed[pl.ds(pl.multiple_of((1 - core) * half, half), half), :].astype(BF16)
            r.stay[k] = r.packed[pl.ds(pl.multiple_of(core * half, half), half), :]

    def both(r):
        for role in (FIRST, SECOND):
            pl.when(r.scal[0] == role)(lambda role=role: body(r, role))

    shape = jax.ShapeDtypeStruct
    return call(
        both,
        arrays,
        SimpleNamespace(
            up=shape((count, 5, H, F), BF16),
            down=shape((count, 5, H, F), BF16),
            mine=shape((count, 3, 1, A), F32),
            send=shape((sz.space, half, sz.packed), BF16),
            stay=shape((sz.space, half, sz.packed), F32),
        ),
        dict(
            left=((F, count * K), BF16),
            right=((count * K, sz.packed), BF16),
            packed=((F, sz.packed), F32),
        ),
    )


def result_call(sz, scal, fresh, back, from_low, from_high, mine):
    A, H, F = sz.atoms, sz.halo, sz.width
    count = len(back[0])
    arrays = SimpleNamespace(
        scal=(scal, SMEM), low=(from_low, VMEM), high=(from_high, VMEM), mine=(mine, VMEM)
    )
    for role in (FIRST, SECOND):
        for m in range(count):
            setattr(arrays, f"fresh_{role}_{m}", (fresh[role][m], VMEM))
            setattr(arrays, f"back_{role}_{m}", (back[role][m], VMEM))

    def body(r, role):
        for m in range(count):
            r.outputs[0, m, 0] = getattr(r, f"fresh_{role}_{m}")[...]
            whole = getattr(r, f"back_{role}_{m}")
            r.grads[0, m, 0, :, 0:H, :] = whole[:, 0:H, :] + r.low[m, 0:4].astype(F32)
            r.grads[0, m, 0, :, H : A - H, :] = whole[:, H : A - H, :]
            r.grads[0, m, 0, :, A - H :, :] = whole[:, A - H :, :] + r.high[m, 0:4].astype(F32)
            for c in range(3):
                edge = [
                    unpacked_places(r.low[m, 4], c, H),
                    jnp.zeros((1, A - 2 * H), F32),
                    unpacked_places(r.high[m, 4], c, H),
                ]
                r.places[m, c] = r.mine[m, c] + jnp.concatenate(edge, axis=1)

    def both(r):
        for role in (FIRST, SECOND):
            pl.when(r.scal[0] == role)(lambda role=role: body(r, role))

    shape = jax.ShapeDtypeStruct
    return call(
        both,
        arrays,
        SimpleNamespace(
            outputs=shape((1, count, 1, 4, A, F), BF16),
            grads=shape((1, count, 1, 4, A, F), F32),
            places=shape((count, 3, 1, A), F32),
        ),
        {},
    )


def share_call(sz, scal, total, other):
    F = sz.width
    w1, w2, w3 = sz.widths
    w4, w5 = 4 * F // sz.space, F // sz.space
    half = F // 2

    def body(r, first, second):
        for at, part in ((0, first), (half, second)):
            r.qkv[0, at : at + half, :] = part[:, :w1]
            r.vector[0, at : at + half, :] = part[:, w1 : w1 + w2]
            r.out[0, at : at + half, :] = part[:, w1 + w2 : sz.spare]
        r.filt[0] = jnp.transpose(first[:w4, sz.spare : sz.spare + sz.basis])
        r.gain[...] = second[0:1, sz.spare : sz.spare + w5]
        r.bias[...] = second[8:9, sz.spare : sz.spare + w5]

    def both(r):
        pl.when(r.scal[2] == 0)(lambda: body(r, r.total, r.other))
        pl.when(r.scal[2] == 1)(lambda: body(r, r.other, r.total))

    shape = jax.ShapeDtypeStruct
    return call(
        both,
        SimpleNamespace(scal=(scal, SMEM), total=(total, VMEM), other=(other, VMEM)),
        SimpleNamespace(
            gain=shape((1, w5), F32),
            bias=shape((1, w5), F32),
            qkv=shape((1, F, w1), F32),
            vector=shape((1, F, w2), F32),
            filt=shape((1, sz.basis, w4), F32),
            out=shape((1, F, w3), F32),
        ),
        {},
    )


def on_device(
    features,
    coords,
    neighbours,
    counts,
    shifts,
    norm_gain,
    norm_bias,
    qkv_weight,
    vector_weight,
    filter_weight,
    out_weight,
    cotangent,
):
    micro_count = features.shape[0]
    space = lax.axis_size("space")
    section = lax.axis_index("section")
    slab = lax.axis_index("space")
    core = lax.axis_index("dp")
    sz = Sizes(features.shape[3], features.shape[4], filter_weight.shape[1], neighbours.shape[2], space)
    up = [(i, (i + 1) % space) for i in range(space)]
    down = [((i + 1) % space, i) for i in range(space)]

    scal = jnp.stack([section, slab, core, space - 1]).astype(jnp.int32)
    places = jnp.transpose(coords, (0, 2, 1, 3))
    norms = jnp.concatenate([norm_gain, norm_bias], axis=0).astype(F32)
    borders = border_call(sz, features, places)
    pack_low = lax.ppermute(borders.up, "space", up)
    pack_high = lax.ppermute(borders.down, "space", down)
    both = ("section", "space")
    forth = [(k, space + k) for k in range(space)]
    forth_up = [(k, space + (k + 1) % space) for k in range(space)]
    forth_down = [((k + 1) % space, space + k) for k in range(space)]
    back = [(space + k, k) for k in range(space)]
    back_up = [(space + k, (k + 1) % space) for k in range(space)]
    back_down = [(space + (k + 1) % space, k) for k in range(space)]

    def geometry_inputs(place):
        return SimpleNamespace(
            scal=(scal, SMEM),
            pack_low=(pack_low, VMEM),
            pack_high=(pack_high, VMEM),
            coords=(places, place),
            nbr=(neighbours, place),
            counts=(counts, place),
            shifts=(shifts, place),
            wfilt=(filter_weight, place),
        )

    firsts, sent = [], []
    for m in range(micro_count):
        arrays = geometry_inputs(HBM)
        arrays.features = (features, HBM)
        arrays.norms = (norms, VMEM)
        arrays.wqkv, arrays.wvec, arrays.wout = (
            (qkv_weight, HBM), (vector_weight, HBM), (out_weight, HBM)
        )
        first = first_call(sz, m, arrays)
        firsts.append(first)
        sent.append((
            lax.ppermute(first.fresh, both, forth),
            lax.ppermute(first.tail, both, forth_up),
            lax.ppermute(first.head, both, forth_down),
        ))
    filters = [filter_call(sz, m, geometry_inputs(VMEM)) for m in range(micro_count)]
    for made, geo in zip(filters, lax.optimization_barrier([made.geo for made in filters])):
        made.geo = geo

    def both_inputs(m):
        made = filters[m]
        return SimpleNamespace(
            scal=(scal, SMEM),
            norms=(norms, VMEM),
            wqkv=(qkv_weight, VMEM),
            wvec=(vector_weight, VMEM),
            wfilt=(filter_weight, VMEM),
            wout=(out_weight, VMEM),
            geo=(made.geo, VMEM),
            smear=(made.smear, VMEM),
            cut_wide=(made.cut_wide, VMEM),
            units=(made.units, VMEM),
            silu=(made.silu, VMEM),
            slope=(made.slope, VMEM),
        )

    seconds, returned = [], []
    for m in range(micro_count):
        arrays = both_inputs(m)
        own, low, high = sent[m]
        arrays.own, arrays.low, arrays.high = (own, VMEM), (low, VMEM), (high, VMEM)
        arrays.cotangent = (cotangent, VMEM)
        second = both_call(sz, m, True, arrays)
        seconds.append(second)
        back_low, rim_low, rim_high = second.back_low, second.rim_low, second.rim_high
        if m:
            _, inc_low, inc_high = returned[-1]
            inc_low, inc_high, back_low, rim_low, rim_high = lax.optimization_barrier(
                (inc_low, inc_high, back_low, rim_low, rim_high)
            )
            returned[-1] = (returned[-1][0], inc_low, inc_high)
        returned.append((
            lax.ppermute(back_low, both, back),
            lax.ppermute(rim_high, both, back_up),
            lax.ppermute(rim_low, both, back_down),
        ))
    thirds = []
    for m in range(micro_count):
        arrays = both_inputs(m)
        arrays.pack_low, arrays.pack_high = (pack_low, VMEM), (pack_high, VMEM)
        arrays.features = (features, VMEM)
        arrays.scalar_in = (firsts[m].scalar_out, VMEM)
        arrays.score = (firsts[m].score, VMEM)
        inc, inc_low, inc_high = returned[m]
        arrays.inc, arrays.inc_low, arrays.inc_high = (inc, VMEM), (inc_low, VMEM), (inc_high, VMEM)
        thirds.append(both_call(sz, m, False, arrays))

    shares = gradient_call(sz, scal, (thirds, seconds))
    summed = shares.stay + lax.ppermute(shares.send, "dp", [(0, 1), (1, 0)]).astype(F32)
    pieces = summed.astype(BF16)
    total = lax.dynamic_index_in_dim(summed, slab, 0, keepdims=False)
    for hop in range(1, space):
        piece = lax.dynamic_index_in_dim(pieces, (slab + hop) % space, 0, keepdims=False)
        total = total + lax.ppermute(
            piece, "space", [(i, (i + hop) % space) for i in range(space)]
        ).astype(F32)
    from_low = lax.ppermute(shares.up, "space", up)
    from_high = lax.ppermute(shares.down, "space", down)
    results = result_call(
        sz,
        scal,
        ([v.fresh for v in firsts], [v.fresh for v in seconds]),
        ([v.back for v in thirds], [v.back for v in seconds]),
        from_low,
        from_high,
        shares.mine,
    )
    places_sum = results.places + lax.ppermute(results.places, "section", [(0, 1), (1, 0)])
    other = lax.ppermute(total, "dp", [(0, 1), (1, 0)])
    share = share_call(sz, scal, total, other)
    return (
        results.outputs,
        results.grads,
        share.gain,
        share.bias,
        share.qkv,
        share.vector,
        share.filt,
        share.out,
        jnp.transpose(places_sum, (0, 2, 1, 3)),
    )


def solution(mesh):
    return jax.shard_map(
        on_device,
        mesh=mesh,
        in_specs=(
            P(None, "dp", None, "space", None),
            P(None, "dp", None, "space"),
            P(None, "dp", None, "space"),
            P(None, "dp", "space"),
            P(None, "dp", None, None, "space"),
            P("section", None),
            P("section", None),
            P("section", None, None),
            P("section", None, None),
            P("section", None, None),
            P("section", None, None),
            P(None, "dp", None, "space", None),
        ),
        out_specs=(
            P("section", None, "dp", None, "space", None),
            P("section", None, "dp", None, "space", None),
            P("section", "space"),
            P("section", "space"),
            P("section", None, "space"),
            P("section", None, "space"),
            P("section", None, "space"),
            P("section", None, "space"),
            P(None, "dp", None, "space"),
        ),
        check_vma=False,
    )
```

time: 1630 us -> 144 us (0.09); the launches traced: 1600 us -> 144 us
  other arithmetic: 933 us -> 6.2 us
  local copies, waits for them, and re-layouts: 374 us -> 3.06 us
  waiting for transfers between devices: 108 us -> 32.3 us
  matrix products: 69.3 us -> 0 us
  Pallas kernels: 0 us -> 66.4 us
  starting transfers between devices: 67.5 us -> 34.7 us
  blocking collectives: 29.6 us -> 0 us
  between operations: 18.1 us -> 1.14 us
    scatter-add x12 -> x0, other arithmetic: 552 us -> none  [the longest x3 456 us: edge_core(): neighbour_vec = vector_features[:, source]]
    gather x21 -> x0, local copies, waits for them, and re-layouts: 232 us -> none  [the longest x6 111 us: edge_core(): neighbour_vec = vector_features[:, source]]
    reduce_sum x48 -> x0, other arithmetic: 165 us -> none  [the longest x3 88.5 us: edge_core(): values[None, ..., 2 * feature_width:] * unit_vec[..., None]]
    mul x35 -> x0, other arithmetic: 117 us -> none  [the longest x8 67.2 us: edge_core(): values = gathered[..., feature_width:] * filters[..., feature_width:]]
    reduce_scatter x4 -> x0, waiting for transfers between devices: 76.3 us -> none  [the longest x1 62.2 us: on_device(): lax.psum_scatter(totals[4], 'space', scatter_dimension=1, tiled=True)]
    dot_general x36 -> x0, matrix products: 69.3 us -> none  [the longest x3 21.2 us: filter_product(): lax.dot_general(flat, filter_weight, (((0,), (0,)), ((), ())), preferred_...]
    pallas_call x0 -> x12, Pallas kernels: none -> 66.4 us  [call(): pl.pallas_call(kernel, out_shape=list(outs.values()), in_specs=[spec for...]
    mul x24 -> x0, local copies, waits for them, and re-layouts: 60 us -> none  [the longest x12 36.5 us: edge_core(): values[..., :feature_width]]
  transfers between devices with their start and end apart: 35 -> 26, of which waited for: 10 -> 11; matrix products, arithmetic and copies ran while one was open for 33% -> 2% of each run, Pallas kernels for 0% -> 25%
where the time goes in v1:
time: 144 us
  Pallas kernels  66.4 us (46%)
  starting transfers between devices  34.7 us (24%)
  waiting for transfers between devices  32.3 us (22%)
  other arithmetic  6.2 us (4%)
  local copies, waits for them, and re-layouts  3.06 us (2%)
    pallas_call x12, Pallas kernels, call(): pl.pallas_call(kernel, out_shape=list(outs.values()), in_specs=[spec for...  66.4 us
    ppermute x2, waiting for transfers between devices, on_device(): lax.ppermute(rim_high, both, back_up)  15.3 us
    ppermute x7, waiting for transfers between devices, on_device(): lax.ppermute(piece, 'space', [(i, (i + hop) % space) for i in range(space)])  8.19 us
    ppermute x7, starting transfers between devices, on_device(): lax.ppermute(piece, 'space', [(i, (i + hop) % space) for i in range(space)])  8.12 us
    ppermute x1, starting transfers between devices, on_device(): from_high = lax.ppermute(shares.down, 'space', down)  4.1 us
    ppermute x1, waiting for transfers between devices, on_device(): from_low = lax.ppermute(shares.up, 'space', up)  3.33 us
    ppermute x1, starting transfers between devices, on_device(): pack_high = lax.ppermute(borders.down, 'space', down)  3.1 us
    ppermute x1, starting transfers between devices, on_device(): pack_low = lax.ppermute(borders.up, 'space', up)  3.02 us
  transfers between devices with their start and end apart: 26, of which 11 were waited for; matrix products, arithmetic and copies ran while one was open for 2% of the time, Pallas kernels for 25%

profile of v1, /device:TPU:0, one launch (start us, length us, event | category | flops | bytes accessed | tf_op | source)
XLA Modules:
  0.0 143.8 jit_solution(9143841597349207495)
XLA Ops:
  0.6 1.5 %shard_map.187 = (bf16[2,5,16,256]{3,2,1,0:T(8,128)(2,1)}, bf16[2,5,16,256]{3,2,1,0:T(8,128)(2,1)}) custom-call(bf16[2,1,4,64,256]{4,3,2,1,0:T(8,128)(2,1)} %args_14_.3, f32[2,3,1,64]{3,2,1,0:T(1,128)} %bitcast.34), custom_call_target="tpu_custom_call" | custom-call | tf_op jit(solution)/shard_map/pallas_call | solution.py:602
  2.2 3.0 %collective-permute-start = (bf16[2,5,16,256]{3,2,1,0:T(8,128)(2,1)}, bf16[2,5,16,256]{3,2,1,0:T(8,128)(2,1)S(1)}, u32[]{:S(2)}, u32[]{:S(2)}) collective-permute-start(bf16[2,5,16,256]{3,2,1,0:T(8,128)(2,1)} %get-tuple-element.98), channel_id=1, source_target_pairs={{0,2},{2,4},{4,6},{6,8},{8,10},{10,12},{12,14},{14,0},{1,3},{3,5},... | collective-permute-start | bytes 245768 | tf_op jit(solution)/shard_map/ppermute | solution.py:943
  5.2 3.1 %collective-permute-start.1 = (bf16[2,5,16,256]{3,2,1,0:T(8,128)(2,1)}, bf16[2,5,16,256]{3,2,1,0:T(8,128)(2,1)S(1)}, u32[]{:S(2)}, u32[]{:S(2)}) collective-permute-start(bf16[2,5,16,256]{3,2,1,0:T(8,128)(2,1)} %get-tuple-element.99), channel_id=1, source_target_pairs={{2,0},{4,2},{6,4},{8,6},{10,8},{12,10},{14,12},{0,14},{3,1},{5,3},... | collective-permute-start | bytes 245768 | tf_op jit(solution)/shard_map/ppermute | solution.py:944
  8.3 1.3 maximum_convert_fusion.args_9_.args_1_
  9.6 0.7 pad_add_fusion.args_0_
  10.3 0.0 copy-start.21
  10.3 0.7 collective-permute-done.args_1_.args_12_
  11.0 0.6 collective-permute-done.1.args_2_.args_13_
  11.6 0.0 copy-done.5
  11.6 0.6 copy-done.7
  12.3 10.7 %shard_map.190 = (bf16[4,64,256]{2,1,0:T(8,128)(2,1)}, bf16[4,48,256]{2,1,0:T(8,128)(2,1)}, bf16[4,48,256]{2,1,0:T(8,128)(2,1)}, bf16[64,256]{1,0:T(8,128)(2,1)}, bf16[8,256,256]{2,1,0:T(8,128)(2,1)}) custom-call(s32[4]{0:T(128)} %pad_add_fusion.args_0_, bf16[2,5,16,256]{3,2,1,0:T(8,128)(2,1)} %copy-done.5, bf16[2,5,16,256]{3,2,1,0:T(8,128)(2,1)} %copy-done.7, ...), custom_call_target="tpu_custom_call" | custom-call | tf_op jit(solution)/shard_map/pallas_call | solution.py:602
  23.0 0.0 copy-start
  23.0 0.0 copy-start.1
  23.0 0.0 copy-start.2
  23.1 0.0 copy-start.9
  23.1 0.0 copy-start.16
  23.1 1.4 collective-permute-start.3
  24.5 1.3 collective-permute-start.2
  25.8 1.3 collective-permute-start.4
  27.1 10.7 %shard_map.192 = (bf16[4,64,256]{2,1,0:T(8,128)(2,1)}, bf16[4,48,256]{2,1,0:T(8,128)(2,1)}, bf16[4,48,256]{2,1,0:T(8,128)(2,1)}, bf16[64,256]{1,0:T(8,128)(2,1)}, bf16[8,256,256]{2,1,0:T(8,128)(2,1)}) custom-call(s32[4]{0:T(128)} %pad_add_fusion.args_0_, bf16[2,5,16,256]{3,2,1,0:T(8,128)(2,1)} %copy-done.5, bf16[2,5,16,256]{3,2,1,0:T(8,128)(2,1)} %copy-done.7, ...), custom_call_target="tpu_custom_call" | custom-call | tf_op jit(solution)/shard_map/pallas_call | solution.py:602
  37.8 1.3 collective-permute-start.8
  39.1 1.3 collective-permute-start.9
  40.5 1.3 collective-permute-start.10
  41.8 5.3 %shard_map.188 = (f32[10,8,256]{2,1,0:T(8,128)S(1)}, bf16[8,32,256]{2,1,0:T(8,128)(2,1)S(1)}, bf16[8,256,128]{2,1,0:T(8,128)(2,1)S(1)}, bf16[8,192,256]{2,1,0:T(...) custom-call(s32[4]{0:T(128)S(1)} %copy-done.18, ...), custom_call_target="tpu_custom_call" | custom-call | tf_op jit(solution)/shard_map/pallas_call | solution.py:602
  47.2 5.3 %shard_map.189 = (f32[10,8,256]{2,1,0:T(8,128)S(1)}, bf16[8,32,256]{2,1,0:T(8,128)(2,1)S(1)}, bf16[8,256,128]{2,1,0:T(8,128)(2,1)S(1)}, bf16[8,192,256]{2,1,0:T(...) custom-call(s32[4]{0:T(128)S(1)} %copy-done.18, ...), custom_call_target="tpu_custom_call" | custom-call | tf_op jit(solution)/shard_map/pallas_call | solution.py:602
  52.5 0.0 collective-permute-done.4.args_14_
  52.5 0.0 collective-permute-done.2.args_12_
  52.6 0.6 shard_map.191
  53.2 1.3 collective-permute-start.6
  54.5 1.3 collective-permute-start.7
  55.8 1.3 collective-permute-start.5
  57.1 0.0 copy-start.3
  57.1 0.6 shard_map.193
  57.7 9.5 %collective-permute-done.6.args_18_ = bf16[4,16,256]{2,1,0:T(8,128)(2,1)S(1)} collective-permute-done((bf16[4,16,256]{2,1,0:T(8,128)(2,1)S(1)}, bf16[4,16,256]{2,1,0:T(8,128)(2,1)S(1)}, u32[]{:S(2)}, u32[]{:S(2)}) %collective-permute-start.6) | collective-permute-done | bytes 32800 | tf_op jit(solution)/shard_map/ppermute | solution.py:1018
  67.2 0.4 collective-permute-done.7.args_19_
  67.5 1.3 collective-permute-start.11
  68.8 1.3 collective-permute-start.12
  70.1 1.3 collective-permute-start.13
  71.5 12.6 %shard_map.194 = (f32[4,64,256]{2,1,0:T(8,128)S(1)}, bf16[4,64,256]{2,1,0:T(8,128)(2,1)}, bf16[4,16,256]{2,1,0:T(8,128)(2,1)S(1)}, bf16[4,16,256]{2,1,0:T(8,128)...) custom-call(s32[4]{0:T(128)S(1)} %copy-done.18, ...), custom_call_target="tpu_custom_call" | custom-call | tf_op jit(solution)/shard_map/pallas_call | solution.py:602
  84.1 5.8 %collective-permute-done.12.args_18_ = bf16[4,16,256]{2,1,0:T(8,128)(2,1)S(1)} collective-permute-done((bf16[4,16,256]{2,1,0:T(8,128)(2,1)S(1)}, bf16[4,16,256]{2,1,0:T(8,128)(2,1)S(1)}, u32[]{:S(2)}, u32[]{:S(2)}) %collective-permute-start.12) | collective-permute-done | bytes 32800 | tf_op jit(solution)/shard_map/ppermute | solution.py:1018
  90.0 0.4 collective-permute-done.13.args_19_
  90.3 12.5 %shard_map.195 = (f32[4,64,256]{2,1,0:T(8,128)S(1)}, bf16[4,64,256]{2,1,0:T(8,128)(2,1)}, bf16[4,16,256]{2,1,0:T(8,128)(2,1)S(1)}, bf16[4,16,256]{2,1,0:T(8,128)...) custom-call(s32[4]{0:T(128)S(1)} %copy-done.18, ...), custom_call_target="tpu_custom_call" | custom-call | tf_op jit(solution)/shard_map/pallas_call | solution.py:602
  102.8 3.7 %shard_map.196 = (bf16[2,5,16,256]{3,2,1,0:T(8,128)(2,1)S(1)}, bf16[2,5,16,256]{3,2,1,0:T(8,128)(2,1)S(1)}, f32[2,3,1,64]{3,2,1,0:T(1,128)S(1)}, bf16[8,128,384]{2,1,0:T(8,128)(2,1)}, f32[8,128,384]{2,1,0:T(8,128)S(1)}) custom-call(s32[4]{0:T(128)S(1)} %copy-done.18, bf16[384,256]{1,0:T(8,128)(2,1)S(1)} %get-tuple-element.130.args_1_, ...), custom_call_target="tpu_custom_call" | custom-call | tf_op jit(solution)/shard_map/pallas_call | solution.py:602
  106.5 2.6 %collective-permute-done.16 = bf16[8,128,384]{2,1,0:T(8,128)(2,1)} collective-permute-done((bf16[8,128,384]{2,1,0:T(8,128)(2,1)}, bf16[8,128,384]{2,1,0:T(8,128)(2,1)}, u32[]{:S(2)}, u32[]{:S(2)}) %collective-permute-start.16) | collective-permute-done | bytes 786464 | tf_op jit(solution)/shard_map/ppermute | solution.py:1033
  109.1 2.6 %fusion.6 = (bf16[8,128,384]{2,1,0:T(8,128)(2,1)S(1)}, f32[8,128,384]{2,1,0:T(8,128)}) fusion(f32[8,128,384]{2,1,0:T(8,128)S(1)} %get-tuple-element.178, bf16[8,128,384]{2,1,0:T(8,128)(2,1)} %collective-permute-done.16), kind=kLoop, calls=%fused_computation.18 | loop fusion | flops 1179648 | bytes 4718592 | tf_op jit(solution)/shard_map/convert_element_type | solution.py:1034
  111.8 0.1 dynamic-slice_bitcast_fusion.6
  111.8 3.7 %collective-permute-start.23 = (bf16[128,384]{1,0:T(8,128)(2,1)S(1)}, bf16[128,384]{1,0:T(8,128)(2,1)S(1)}, u32[]{:S(2)}, u32[]{:S(2)}) collective-permute-start(bf16[128,384]{1,0:T(8,128)(2,1)S(1)} %get-tuple-element.199), channel_id=1, source_target_pairs={{0,14},{2,0},{4,2},{6,4},{8,6},{10,8},{12,10},{14,12},{1,15},{3,1}... | collective-permute-start | bytes 294920 | tf_op jit(solution)/shard_map/ppermute | solution.py:1038
  115.5 0.6 collective-permute-start.14
  116.2 4.1 %collective-permute-start.15 = (bf16[2,5,16,256]{3,2,1,0:T(8,128)(2,1)S(1)}, bf16[2,5,16,256]{3,2,1,0:T(8,128)(2,1)S(1)}, u32[]{:S(2)}, u32[]{:S(2)}) collective-permute-start(bf16[2,5,16,256]{3,2,1,0:T(8,128)(2,1)S(1)} %get-tuple-element.168), channel_id=1, source_target_pairs={{2,0},{4,2},{6,4},{8,6},{10,8},{12,10},{14,12},{0,14},{3,1},{5,3},... | collective-permute-start | bytes 245768 | tf_op jit(solution)/shard_map/ppermute | solution.py:1042
  120.2 3.3 %collective-permute-done.14.args_1_ = bf16[2,5,16,256]{3,2,1,0:T(8,128)(2,1)S(1)} collective-permute-done((bf16[2,5,16,256]{3,2,1,0:T(8,128)(2,1)S(1)}, bf16[2,5,16,256]{3,2,1,0:T(8,128)(2,1)S(1)}, u32[]{:S(2)}, u32[]{:S(2)}) %collective-permute-start.14) | collective-permute-done | bytes 81952 | tf_op jit(solution)/shard_map/ppermute | solution.py:1041
  123.6 0.0 collective-permute-start.19
  123.6 0.8 collective-permute-start.18
  124.4 3.6 %collective-permute-start.17 = (bf16[128,384]{1,0:T(8,128)(2,1)S(1)}, bf16[128,384]{1,0:T(8,128)(2,1)S(1)}, u32[]{:S(2)}, u32[]{:S(2)}) collective-permute-start(bf16[128,384]{1,0:T(8,128)(2,1)S(1)} %get-tuple-element.198), channel_id=1, source_target_pairs={{0,2},{2,4},{4,6},{6,8},{8,10},{10,12},{12,14},{14,0},{1,3},{3,5},... | collective-permute-start | bytes 294920 | tf_op jit(solution)/shard_map/ppermute | solution.py:1038
  128.0 1.5 %shard_map.197 = (bf16[1,2,1,4,64,256]{5,4,3,2,1,0:T(8,128)(2,1)}, f32[1,2,1,4,64,256]{5,4,3,2,1,0:T(8,128)}, f32[2,3,1,64]{3,2,1,0:T(1,128)S(1)}) custom-call(s32[4]{0:T(128)S(1)} %copy-done.18, bf16[2,5,16,256]{3,2,1,0:T(8,128)(2,1)S(1)} %collective-permute-done.14.args_1_, bf16[2,5,16,256]{3,2,1,0:T(8,128)(2,1)S(1)} %collective-permute-done.15.args_2_, ...), custom_call_target="tpu_custom_call" | custom-call | tf_op jit(solution)/shard_map/pallas_call | solution.py:602
  129.6 4.3 %collective-permute-done.20 = bf16[128,384]{1,0:T(8,128)(2,1)S(1)} collective-permute-done((bf16[128,384]{1,0:T(8,128)(2,1)S(1)}, bf16[128,384]{1,0:T(8,128)(2,1)S(1)}, u32[]{:S(2)}, u32[]{:S(2)}) %collective-permute-start.20) | collective-permute-done | bytes 98336 | tf_op jit(solution)/shard_map/ppermute | solution.py:1038
  133.9 3.9 %collective-permute-done.19 = bf16[128,384]{1,0:T(8,128)(2,1)S(1)} collective-permute-done((bf16[128,384]{1,0:T(8,128)(2,1)S(1)}, bf16[128,384]{1,0:T(8,128)(2,1)S(1)}, u32[]{:S(2)}, u32[]{:S(2)}) %collective-permute-start.19) | collective-permute-done | bytes 98336 | tf_op jit(solution)/shard_map/ppermute | solution.py:1038
  137.7 1.0 fusion.5.args_1_
  138.8 0.1 collective-permute-start.24
  138.9 0.6 add_bitcast_fusion
  139.4 0.8 collective-permute-done.24.args_2_
  140.3 1.3 shard_map.198
  141.6 0.8 copy.21
  142.4 0.7 copy.22
  143.1 0.7 copy.23
  (53 shorter events, 0.1 us)
Async XLA Ops:
  2.2 8.8 %collective-permute-start = (bf16[2,5,16,256]{3,2,1,0:T(8,128)(2,1)}, bf16[2,5,16,256]{3,2,1,0:T(8,128)(2,1)S(1)}, u32[]{:S(2)}, u32[]{:S(2)}) collective-permute-start(bf16[2,5,16,256]{3,2,1,0:T(8,128)(2,1)} %get-tuple-element.98), channel_id=1, source_target_pairs={{0,2},{2,4},{4,6},{6,8},{8,10},{10,12},{12,14},{14,0},{1,3},{3,5},... | collective-permute-start | bytes 245768 | tf_op jit(solution)/shard_map/ppermute | solution.py:943
  5.2 6.4 %collective-permute-start.1 = (bf16[2,5,16,256]{3,2,1,0:T(8,128)(2,1)}, bf16[2,5,16,256]{3,2,1,0:T(8,128)(2,1)S(1)}, u32[]{:S(2)}, u32[]{:S(2)}) collective-permute-start(bf16[2,5,16,256]{3,2,1,0:T(8,128)(2,1)} %get-tuple-element.99), channel_id=1, source_target_pairs={{2,0},{4,2},{6,4},{8,6},{10,8},{12,10},{14,12},{0,14},{3,1},{5,3},... | collective-permute-start | bytes 245768 | tf_op jit(solution)/shard_map/ppermute | solution.py:944
  10.3 31.5 %copy-start.4 = (bf16[1,32,1024]{2,1,0:T(8,128)(2,1)S(1)}, bf16[1,32,1024]{2,1,0:T(8,128)(2,1)}, u32[]{:S(2)}) copy-start(bf16[1,32,1024]{2,1,0:T(8,128)(2,1)} %args_4_.18) | copy-start | bytes 196612
  10.3 31.5 %copy-start.12 = (s32[2,1,2,32,64]{4,3,2,1,0:T(8,128)S(1)}, s32[2,1,2,32,64]{4,3,2,1,0:T(8,128)}, u32[]{:S(2)}) copy-start(s32[2,1,2,32,64]{4,3,2,1,0:T(8,128)} %args_6_.10) | copy-start | bytes 98308
  10.3 31.5 %copy-start.13 = (s32[2,1,32,64]{3,2,1,0:T(8,128)S(1)}, s32[2,1,32,64]{3,2,1,0:T(8,128)}, u32[]{:S(2)}) copy-start(s32[2,1,32,64]{3,2,1,0:T(8,128)} %args_4_.15) | copy-start | bytes 49156
  10.3 31.5 %copy-start.17 = (f32[2,1,3,64]{3,1,2,0:T(1,128)S(1)}, f32[2,1,3,64]{3,1,2,0:T(1,128)}, u32[]{:S(2)}) copy-start(f32[2,1,3,64]{3,1,2,0:T(1,128)} %param.13) | copy-start | bytes 4612
  10.3 31.5 %copy-start.18 = (s32[4]{0:T(128)S(1)}, s32[4]{0:T(128)}, u32[]{:S(2)}) copy-start(s32[4]{0:T(128)} %pad_add_fusion.args_0_) | copy-start | bytes 52
  10.3 31.5 %copy-start.21 = (s32[2,1,64]{2,1,0:T(1,128)S(1)}, s32[2,1,64]{2,1,0:T(1,128)}, u32[]{:S(2)}) copy-start(s32[2,1,64]{2,1,0:T(1,128)} %args_5_.15) | copy-start | bytes 1540
  11.0 0.6 copy-start.5
  11.6 0.6 copy-start.7
  23.0 18.8 %copy-start.6 = (bf16[2,5,16,256]{3,2,1,0:T(8,128)(2,1)S(1)}, bf16[2,5,16,256]{3,2,1,0:T(8,128)(2,1)}, u32[]{:S(2)}) copy-start(bf16[2,5,16,256]{3,2,1,0:T(8,128)(2,1)} %copy-done.5) | copy-start | bytes 245764
  23.0 18.8 %copy-start.8 = (bf16[2,5,16,256]{3,2,1,0:T(8,128)(2,1)S(1)}, bf16[2,5,16,256]{3,2,1,0:T(8,128)(2,1)}, u32[]{:S(2)}) copy-start(bf16[2,5,16,256]{3,2,1,0:T(8,128)(2,1)} %copy-done.7) | copy-start | bytes 245764
  23.0 29.5 %copy-start = (bf16[1,256,1280]{2,1,0:T(8,128)(2,1)S(1)}, bf16[1,256,1280]{2,1,0:T(8,128)(2,1)}, u32[]{:S(2)}) copy-start(bf16[1,256,1280]{2,1,0:T(8,128)(2,1)} %args_2_.10) | copy-start | bytes 1966084
  23.0 29.5 %copy-start.1 = (bf16[1,256,768]{2,1,0:T(8,128)(2,1)S(1)}, bf16[1,256,768]{2,1,0:T(8,128)(2,1)}, u32[]{:S(2)}) copy-start(bf16[1,256,768]{2,1,0:T(8,128)(2,1)} %args_3_.10) | copy-start | bytes 1179652
  23.0 29.5 %copy-start.2 = (bf16[1,256,768]{2,1,0:T(8,128)(2,1)S(1)}, bf16[1,256,768]{2,1,0:T(8,128)(2,1)}, u32[]{:S(2)}) copy-start(bf16[1,256,768]{2,1,0:T(8,128)(2,1)} %args_5_.18) | copy-start | bytes 1179652
  23.1 29.5 %copy-start.9 = (bf16[2,1,4,64,256]{4,3,2,1,0:T(8,128)(2,1)S(1)}, bf16[2,1,4,64,256]{4,3,2,1,0:T(8,128)(2,1)}, u32[]{:S(2)}) copy-start(bf16[2,1,4,64,256]{4,3,2,1,0:T(8,128)(2,1)} %args_15_.3) | copy-start | bytes 786436
  23.1 29.5 %copy-start.16 = (f32[2,256]{1,0:T(2,128)S(1)}, f32[2,256]{1,0:T(2,128)}, u32[]{:S(2)}) copy-start(f32[2,256]{1,0:T(2,128)} %maximum_convert_fusion.args_9_.args_1_) | copy-start | bytes 6148
  23.1 17.4 %collective-permute-start.3 = (bf16[4,48,256]{2,1,0:T(8,128)(2,1)}, bf16[4,48,256]{2,1,0:T(8,128)(2,1)S(1)}, u32[]{:S(2)}, u32[]{:S(2)}) collective-permute-start(bf16[4,48,256]{2,1,0:T(8,128)(2,1)} %get-tuple-element.111), channel_id=1, source_target_pairs={{0,18},{2,20},{4,22},{6,24},{8,26},{10,28},{12,30},{14,16},{1,19},... | collective-permute-start | bytes 294920 | tf_op jit(solution)/shard_map/ppermute | solution.py:977
  24.5 28.0 %collective-permute-start.2 = (bf16[4,64,256]{2,1,0:T(8,128)(2,1)}, bf16[4,64,256]{2,1,0:T(8,128)(2,1)S(1)}, u32[]{:S(2)}, u32[]{:S(2)}) collective-permute-start(bf16[4,64,256]{2,1,0:T(8,128)(2,1)} %get-tuple-element.110.args_4_), channel_id=1, source_target_pairs={{0,16},{2,18},{4,20},{6,22},{8,24},{10,26},{12,28},{14,30},{1,17},... | collective-permute-start | bytes 393224 | tf_op jit(solution)/shard_map/ppermute | solution.py:976
  25.8 26.7 %collective-permute-start.4 = (bf16[4,48,256]{2,1,0:T(8,128)(2,1)}, bf16[4,48,256]{2,1,0:T(8,128)(2,1)S(1)}, u32[]{:S(2)}, u32[]{:S(2)}) collective-permute-start(bf16[4,48,256]{2,1,0:T(8,128)(2,1)} %get-tuple-element.112), channel_id=1, source_target_pairs={{2,16},{4,18},{6,20},{8,22},{10,24},{12,26},{14,28},{0,30},{3,17},... | collective-permute-start | bytes 294920 | tf_op jit(solution)/shard_map/ppermute | solution.py:978
  37.8 19.3 %collective-permute-start.8 = (bf16[4,64,256]{2,1,0:T(8,128)(2,1)}, bf16[4,64,256]{2,1,0:T(8,128)(2,1)S(1)}, u32[]{:S(2)}, u32[]{:S(2)}) collective-permute-start(bf16[4,64,256]{2,1,0:T(8,128)(2,1)} %get-tuple-element.122.args_6_), channel_id=1, source_target_pairs={{0,16},{2,18},{4,20},{6,22},{8,24},{10,26},{12,28},{14,30},{1,17},... | collective-permute-start | bytes 393224 | tf_op jit(solution)/shard_map/ppermute | solution.py:976
  39.1 16.6 %collective-permute-start.9 = (bf16[4,48,256]{2,1,0:T(8,128)(2,1)}, bf16[4,48,256]{2,1,0:T(8,128)(2,1)S(1)}, u32[]{:S(2)}, u32[]{:S(2)}) collective-permute-start(bf16[4,48,256]{2,1,0:T(8,128)(2,1)} %get-tuple-element.123), channel_id=1, source_target_pairs={{0,18},{2,20},{4,22},{6,24},{8,26},{10,28},{12,30},{14,16},{1,19},... | collective-permute-start | bytes 294920 | tf_op jit(solution)/shard_map/ppermute | solution.py:977
  40.5 16.6 %collective-permute-start.10 = (bf16[4,48,256]{2,1,0:T(8,128)(2,1)}, bf16[4,48,256]{2,1,0:T(8,128)(2,1)S(1)}, u32[]{:S(2)}, u32[]{:S(2)}) collective-permute-start(bf16[4,48,256]{2,1,0:T(8,128)(2,1)} %get-tuple-element.124), channel_id=1, source_target_pairs={{2,16},{4,18},{6,20},{8,22},{10,24},{12,26},{14,28},{0,30},{3,17},... | collective-permute-start | bytes 294920 | tf_op jit(solution)/shard_map/ppermute | solution.py:978
  53.2 14.0 %collective-permute-start.6 = (bf16[4,16,256]{2,1,0:T(8,128)(2,1)S(1)}, bf16[4,16,256]{2,1,0:T(8,128)(2,1)S(1)}, u32[]{:S(2)}, u32[]{:S(2)}) collective-permute-start(bf16[4,16,256]{2,1,0:T(8,128)(2,1)S(1)} %get-tuple-element.114.args_26_), channel_id=1, source_target_pairs={{16,2},{18,4},{20,6},{22,8},{24,10},{26,12},{28,14},{30,0},{17,3},... | collective-permute-start | bytes 98312 | tf_op jit(solution)/shard_map/ppermute | solution.py:1018
  54.5 13.1 %collective-permute-start.7 = (bf16[4,16,256]{2,1,0:T(8,128)(2,1)S(1)}, bf16[4,16,256]{2,1,0:T(8,128)(2,1)S(1)}, u32[]{:S(2)}, u32[]{:S(2)}) collective-permute-start(bf16[4,16,256]{2,1,0:T(8,128)(2,1)S(1)} %get-tuple-element.115.args_25_), channel_id=1, source_target_pairs={{18,0},{20,2},{22,4},{24,6},{26,8},{28,10},{30,12},{16,14},{19,1},... | collective-permute-start | bytes 98312 | tf_op jit(solution)/shard_map/ppermute | solution.py:1019
  55.8 15.6 %collective-permute-start.5 = (bf16[4,64,256]{2,1,0:T(8,128)(2,1)S(1)}, bf16[4,64,256]{2,1,0:T(8,128)(2,1)S(1)}, u32[]{:S(2)}, u32[]{:S(2)}) collective-permute-start(bf16[4,64,256]{2,1,0:T(8,128)(2,1)S(1)} %get-tuple-element.113), channel_id=1, source_target_pairs={{16,0},{18,2},{20,4},{22,6},{24,8},{26,10},{28,12},{30,14},{17,1},... | collective-permute-start | bytes 393224 | tf_op jit(solution)/shard_map/ppermute | solution.py:1017
  57.1 14.3 %copy-start.3 = (bf16[2,1,4,64,256]{4,3,2,1,0:T(8,128)(2,1)S(1)}, bf16[2,1,4,64,256]{4,3,2,1,0:T(8,128)(2,1)}, u32[]{:S(2)}) copy-start(bf16[2,1,4,64,256]{4,3,2,1,0:T(8,128)(2,1)} %args_14_.3) | copy-start | bytes 786436
  57.1 14.3 %copy-start.11 = (bf16[8,256,256]{2,1,0:T(8,128)(2,1)S(1)}, bf16[8,256,256]{2,1,0:T(8,128)(2,1)}, u32[]{:S(2)}) copy-start(bf16[8,256,256]{2,1,0:T(8,128)(2,1)} %get-tuple-element.109.args_16_) | copy-start | bytes 3145732
  57.1 14.3 %copy-start.20 = (bf16[64,256]{1,0:T(8,128)(2,1)S(1)}, bf16[64,256]{1,0:T(8,128)(2,1)}, u32[]{:S(2)}) copy-start(bf16[64,256]{1,0:T(8,128)(2,1)} %get-tuple-element.108.args_15_) | copy-start | bytes 98308
  67.5 22.8 %collective-permute-start.11 = (bf16[4,64,256]{2,1,0:T(8,128)(2,1)S(1)}, bf16[4,64,256]{2,1,0:T(8,128)(2,1)S(1)}, u32[]{:S(2)}, u32[]{:S(2)}) collective-permute-start(bf16[4,64,256]{2,1,0:T(8,128)(2,1)S(1)} %get-tuple-element.141), channel_id=1, source_target_pairs={{16,0},{18,2},{20,4},{22,6},{24,8},{26,10},{28,12},{30,14},{17,1},... | collective-permute-start | bytes 393224 | tf_op jit(solution)/shard_map/ppermute | solution.py:1017
  68.8 21.1 %collective-permute-start.12 = (bf16[4,16,256]{2,1,0:T(8,128)(2,1)S(1)}, bf16[4,16,256]{2,1,0:T(8,128)(2,1)S(1)}, u32[]{:S(2)}, u32[]{:S(2)}) collective-permute-start(bf16[4,16,256]{2,1,0:T(8,128)(2,1)S(1)} %get-tuple-element.142.args_35_), channel_id=1, source_target_pairs={{16,2},{18,4},{20,6},{22,8},{24,10},{26,12},{28,14},{30,0},{17,3},... | collective-permute-start | bytes 98312 | tf_op jit(solution)/shard_map/ppermute | solution.py:1018
  70.1 20.2 %collective-permute-start.13 = (bf16[4,16,256]{2,1,0:T(8,128)(2,1)S(1)}, bf16[4,16,256]{2,1,0:T(8,128)(2,1)S(1)}, u32[]{:S(2)}, u32[]{:S(2)}) collective-permute-start(bf16[4,16,256]{2,1,0:T(8,128)(2,1)S(1)} %get-tuple-element.143.args_34_), channel_id=1, source_target_pairs={{18,0},{20,2},{22,4},{24,6},{26,8},{28,10},{30,12},{16,14},{19,1},... | collective-permute-start | bytes 98312 | tf_op jit(solution)/shard_map/ppermute | solution.py:1019
  71.5 18.9 %copy-start.10 = (bf16[8,256,256]{2,1,0:T(8,128)(2,1)S(1)}, bf16[8,256,256]{2,1,0:T(8,128)(2,1)}, u32[]{:S(2)}) copy-start(bf16[8,256,256]{2,1,0:T(8,128)(2,1)} %get-tuple-element.140.args_16_) | copy-start | bytes 3145732
  71.5 18.9 %copy-start.19 = (bf16[64,256]{1,0:T(8,128)(2,1)S(1)}, bf16[64,256]{1,0:T(8,128)(2,1)}, u32[]{:S(2)}) copy-start(bf16[64,256]{1,0:T(8,128)(2,1)} %get-tuple-element.139.args_15_) | copy-start | bytes 98308
  106.5 2.6 %collective-permute-start.16 = (bf16[8,128,384]{2,1,0:T(8,128)(2,1)}, bf16[8,128,384]{2,1,0:T(8,128)(2,1)}, u32[]{:S(2)}, u32[]{:S(2)}) collective-permute-start(bf16[8,128,384]{2,1,0:T(8,128)(2,1)} %get-tuple-element.179), channel_id=1, source_target_pairs={{0,1},{1,0},{2,3},{3,2},{4,5},{5,4},{6,7},{7,6},{8,9},{9,8},{10,11... | collective-permute-start | bytes 2359304 | tf_op jit(solution)/shard_map/ppermute | solution.py:1033
  109.1 18.9 %copy-start.14 = (bf16[4,64,256]{2,1,0:T(8,128)(2,1)S(1)}, bf16[4,64,256]{2,1,0:T(8,128)(2,1)}, u32[]{:S(2)}) copy-start(bf16[4,64,256]{2,1,0:T(8,128)(2,1)} %get-tuple-element.110.args_4_) | copy-start | bytes 393220
  109.1 18.9 %copy-start.15 = (bf16[4,64,256]{2,1,0:T(8,128)(2,1)S(1)}, bf16[4,64,256]{2,1,0:T(8,128)(2,1)}, u32[]{:S(2)}) copy-start(bf16[4,64,256]{2,1,0:T(8,128)(2,1)} %get-tuple-element.122.args_6_) | copy-start | bytes 393220
  111.8 11.8 %collective-permute-start.23 = (bf16[128,384]{1,0:T(8,128)(2,1)S(1)}, bf16[128,384]{1,0:T(8,128)(2,1)S(1)}, u32[]{:S(2)}, u32[]{:S(2)}) collective-permute-start(bf16[128,384]{1,0:T(8,128)(2,1)S(1)} %get-tuple-element.199), channel_id=1, source_target_pairs={{0,14},{2,0},{4,2},{6,4},{8,6},{10,8},{12,10},{14,12},{1,15},{3,1}... | collective-permute-start | bytes 294920 | tf_op jit(solution)/shard_map/ppermute | solution.py:1038
  115.5 8.9 %collective-permute-start.22 = (bf16[128,384]{1,0:T(8,128)(2,1)S(1)}, bf16[128,384]{1,0:T(8,128)(2,1)S(1)}, u32[]{:S(2)}, u32[]{:S(2)}) collective-permute-start(bf16[128,384]{1,0:T(8,128)(2,1)S(1)} %get-tuple-element.200), channel_id=1, source_target_pairs={{0,12},{2,14},{4,0},{6,2},{8,4},{10,6},{12,8},{14,10},{1,13},{3,15... | collective-permute-start | bytes 294920 | tf_op jit(solution)/shard_map/ppermute | solution.py:1038
  115.5 8.1 %collective-permute-start.14 = (bf16[2,5,16,256]{3,2,1,0:T(8,128)(2,1)S(1)}, bf16[2,5,16,256]{3,2,1,0:T(8,128)(2,1)S(1)}, u32[]{:S(2)}, u32[]{:S(2)}) collective-permute-start(bf16[2,5,16,256]{3,2,1,0:T(8,128)(2,1)S(1)} %get-tuple-element.167), channel_id=1, source_target_pairs={{0,2},{2,4},{4,6},{6,8},{8,10},{10,12},{12,14},{14,0},{1,3},{3,5},... | collective-permute-start | bytes 245768 | tf_op jit(solution)/shard_map/ppermute | solution.py:1041
  116.2 7.4 %collective-permute-start.15 = (bf16[2,5,16,256]{3,2,1,0:T(8,128)(2,1)S(1)}, bf16[2,5,16,256]{3,2,1,0:T(8,128)(2,1)S(1)}, u32[]{:S(2)}, u32[]{:S(2)}) collective-permute-start(bf16[2,5,16,256]{3,2,1,0:T(8,128)(2,1)S(1)} %get-tuple-element.168), channel_id=1, source_target_pairs={{2,0},{4,2},{6,4},{8,6},{10,8},{12,10},{14,12},{0,14},{3,1},{5,3},... | collective-permute-start | bytes 245768 | tf_op jit(solution)/shard_map/ppermute | solution.py:1042
  120.2 9.3 %collective-permute-start.21 = (bf16[128,384]{1,0:T(8,128)(2,1)S(1)}, bf16[128,384]{1,0:T(8,128)(2,1)S(1)}, u32[]{:S(2)}, u32[]{:S(2)}) collective-permute-start(bf16[128,384]{1,0:T(8,128)(2,1)S(1)} %get-tuple-element.201), channel_id=1, source_target_pairs={{0,10},{2,12},{4,14},{6,0},{8,2},{10,4},{12,6},{14,8},{1,11},{3,13... | collective-permute-start | bytes 294920 | tf_op jit(solution)/shard_map/ppermute | solution.py:1038
  123.6 10.3 %collective-permute-start.20 = (bf16[128,384]{1,0:T(8,128)(2,1)S(1)}, bf16[128,384]{1,0:T(8,128)(2,1)S(1)}, u32[]{:S(2)}, u32[]{:S(2)}) collective-permute-start(bf16[128,384]{1,0:T(8,128)(2,1)S(1)} %get-tuple-element.202), channel_id=1, source_target_pairs={{0,8},{2,10},{4,12},{6,14},{8,0},{10,2},{12,4},{14,6},{1,9},{3,11}... | collective-permute-start | bytes 294920 | tf_op jit(solution)/shard_map/ppermute | solution.py:1038
  123.6 14.1 %collective-permute-start.19 = (bf16[128,384]{1,0:T(8,128)(2,1)S(1)}, bf16[128,384]{1,0:T(8,128)(2,1)S(1)}, u32[]{:S(2)}, u32[]{:S(2)}) collective-permute-start(bf16[128,384]{1,0:T(8,128)(2,1)S(1)} %get-tuple-element.203), channel_id=1, source_target_pairs={{0,6},{2,8},{4,10},{6,12},{8,14},{10,0},{12,2},{14,4},{1,7},{3,9},... | collective-permute-start | bytes 294920 | tf_op jit(solution)/shard_map/ppermute | solution.py:1038
  123.6 14.1 %collective-permute-start.18 = (bf16[128,384]{1,0:T(8,128)(2,1)S(1)}, bf16[128,384]{1,0:T(8,128)(2,1)S(1)}, u32[]{:S(2)}, u32[]{:S(2)}) collective-permute-start(bf16[128,384]{1,0:T(8,128)(2,1)S(1)} %get-tuple-element.204), channel_id=1, source_target_pairs={{0,4},{2,6},{4,8},{6,10},{8,12},{10,14},{12,0},{14,2},{1,5},{3,7},... | collective-permute-start | bytes 294920 | tf_op jit(solution)/shard_map/ppermute | solution.py:1038
  124.4 13.3 %collective-permute-start.17 = (bf16[128,384]{1,0:T(8,128)(2,1)S(1)}, bf16[128,384]{1,0:T(8,128)(2,1)S(1)}, u32[]{:S(2)}, u32[]{:S(2)}) collective-permute-start(bf16[128,384]{1,0:T(8,128)(2,1)S(1)} %get-tuple-element.198), channel_id=1, source_target_pairs={{0,2},{2,4},{4,6},{6,8},{8,10},{10,12},{12,14},{14,0},{1,3},{3,5},... | collective-permute-start | bytes 294920 | tf_op jit(solution)/shard_map/ppermute | solution.py:1038
  129.6 9.3 %collective-permute-start.25 = (f32[2,3,1,64]{3,2,1,0:T(1,128)S(1)}, f32[2,3,1,64]{3,2,1,0:T(1,128)S(1)}, u32[]{:S(2)}, u32[]{:S(2)}) collective-permute-start(f32[2,3,1,64]{3,2,1,0:T(1,128)S(1)} %get-tuple-element.186), channel_id=1, source_target_pairs={{0,16},{16,0},{1,17},{17,1},{2,18},{18,2},{3,19},{19,3},{4,20},{20... | collective-permute-start | bytes 4616 | tf_op jit(solution)/shard_map/ppermute | solution.py:1052
  138.8 1.5 %collective-permute-start.24 = (f32[128,384]{1,0:T(8,128)S(1)}, f32[128,384]{1,0:T(8,128)S(1)}, u32[]{:S(2)}, u32[]{:S(2)}) collective-permute-start(f32[128,384]{1,0:T(8,128)S(1)} %fusion.5.args_1_), channel_id=1, source_target_pairs={{0,1},{1,0},{2,3},{3,2},{4,5},{5,4},{6,7},{7,6},{8,9},{9,8},{10,11... | collective-permute-start | bytes 589832 | tf_op jit(solution)/shard_map/ppermute | solution.py:1053

commit v2 on v1

--- a/solution.py
+++ b/solution.py
@@ -58,10 +58,10 @@
         self.edges = GROUP * atoms
         self.halves = width // LANES
         self.window = atoms + SUBLANES
-        self.sent = 3 * self.halo
+        self.sent = atoms
         self.widths = (5 * width // space, 3 * width // space, 3 * width // space)
         self.spare = sum(self.widths)
-        self.packed = -(-(self.spare + basis) // LANES) * LANES
+        self.packed = -(-(self.spare + basis) // 16) * 16
         self.factors = -(-(self.rows + 4 * atoms) // LANES) * LANES
 
 
@@ -83,8 +83,8 @@
     ref[...] = low_end * (1.0 - step) + step
 
 
-def edge_geometry(r, sz, m, coords, nbr, counts, shifts):
-    A, H, E, EB = sz.atoms, sz.halo, sz.rows, sz.edges
+def edge_geometry(r, sz, m, coords, slots):
+    A, H, E, EB, K = sz.atoms, sz.halo, sz.rows, sz.edges, sz.slots
     lane = iota((8, LANES), 1)
     row = iota((8, LANES), 0)
     slab, last = r.scal[1], r.scal[3]
@@ -119,12 +119,12 @@
     wide_lane = iota((8, EB), 1)
     wide_row = iota((8, EB), 0)
     wanted = GROUP * wide_row + wide_lane // A + jnp.where(wide_row >= 4, 1, 0) + wide_lane % A
-    alive = iota((sz.slots, A), 0) < counts[...]
-    code = jnp.where(alive, 16, 0) + (shifts[0] + 1) * 4 + (shifts[1] + 1)
+    alive = iota((K, A), 0) < slots[3 * K : 3 * K + 1, :]
+    code = jnp.where(alive, 16, 0) + (slots[K : 2 * K, :] + 1) * 4 + (slots[2 * K : 3 * K, :] + 1)
     code = jnp.concatenate([code] * GROUP, axis=1)
-    named = jnp.concatenate([nbr[...]] * GROUP, axis=1)
+    named = jnp.concatenate([slots[0:K, :]] * GROUP, axis=1)
     found = jnp.zeros((8, EB), jnp.int32)
-    for n in range(sz.slots):
+    for n in range(K):
         found = found + jnp.where(named[n : n + 1, :] == wanted, code[n : n + 1, :], 0)
     live = (found >> 4).astype(F32)
     offsets = (
@@ -212,6 +212,11 @@
     return centred * scale, scale
 
 
+def buffers(r, sz, which):
+    end = str(which)
+    return SimpleNamespace(**{k[:-1]: v for k, v in vars(r).items() if k.endswith(end)})
+
+
 def tiles(sz, first):
     A = sz.atoms
     for kk in range(GROUP):
@@ -222,6 +227,19 @@
                 slice(cg * LANES, (cg + 1) * LANES),
                 pl.ds(first + kk, A),
             )
+
+
+def stacked(sz, first, tile):
+    made = [tile(*where) for where in tiles(sz, first)]
+    CG = sz.halves
+    wholes = []
+    for index in range(len(made[0])):
+        lines = [
+            jnp.concatenate([made[kk * CG + cg][index] for cg in range(CG)], axis=1)
+            for kk in range(GROUP)
+        ]
+        wholes.append(jnp.concatenate(lines, axis=0))
+    return wholes
 
 
 def vector_dot(r, sz):
@@ -246,30 +264,32 @@
             r.tail[index, 0:H, :] = fresh[A - H :]
 
 
-def first_forward(r, sz, m):
+def first_forward(r, sz, m, fetch):
     A, H, E, F, EB = sz.atoms, sz.halo, sz.rows, sz.width, sz.edges
     CG = sz.halves
-    early = [
-        (r.coords.at[m], r.s_coords),
-        (r.nbr.at[m, 0], r.s_nbr),
-        (r.counts.at[m], r.s_counts),
-        (r.shifts.at[m, 0], r.s_shifts),
-        (r.features.at[m, 0], r.s_own),
-        (r.wqkv.at[0], r.s_wqkv),
+    moves = [
+        (r.coords.at[m], "s_coords"),
+        (r.slots.at[m], "s_slots"),
+        (r.features.at[m, 0], "s_own"),
+        (r.wqkv.at[0], "s_wqkv"),
+        (r.wh, "s_wh"),
+        (r.wvec.at[0], "s_wvec"),
+        (r.wout.at[0], "s_wout"),
     ]
-    late = [(r.wfilt.at[0], r.s_wfilt), (r.wvec.at[0], r.s_wvec), (r.wout.at[0], r.s_wout)]
-    copies = [
-        pltpu.make_async_copy(source, target, r.sems.at[i])
-        for i, (source, target) in enumerate(early + late)
-    ]
-    for copy in copies:
-        copy.start()
+    early = moves[:4]
+    copies = []
+    for i, (source, name) in enumerate(moves):
+        if fetch:
+            copies.append(pltpu.make_async_copy(source, getattr(r, name), r.sems.at[i]))
+            copies[-1].start()
+        else:
+            setattr(r, name, source)
     write_constants(r, sz)
     r.sagg[...] = jnp.zeros_like(r.sagg)
     r.vagg[...] = jnp.zeros_like(r.vagg)
     for copy in copies[: len(early)]:
         copy.wait()
-    edge_geometry(r, sz, m, r.s_coords, r.s_nbr, r.s_counts, r.s_shifts)
+    edge_geometry(r, sz, m, r.s_coords, r.s_slots)
 
     def tables(b, carry):
         write_edge_tables(r, sz, b, F32)
@@ -280,23 +300,23 @@
     node_part(r, sz, own, r.pack_low.at[m], r.pack_high.at[m], r.s_wqkv)
     for copy in copies[len(early) :]:
         copy.wait()
-    r.wh[...] = (r.s_wfilt[...].astype(F32) * 0.5).astype(BF16)
     r.vproj[...] = dot(r.left[E : E + 3 * A, :], r.s_wvec[...])
 
     def filter_part(b, part):
-        return dot(r.smear_t[b], r.wh[:, part * F : (part + 1) * F])
-
-    def block(b, carry):
+        return dot(r.smear_t[b], r.s_wh[:, part * F : (part + 1) * F])
+
+    def block(b, w):
         first = first_row(b)
         half = filter_part(b, 0)
         for cg, at, cols, near_rows in tiles(sz, first):
             h = half[at, cols]
             product = r.query[cg] * r.kv[cg, near_rows, :] * (h + h * jnp.tanh(h))
             coarse = product.astype(BF16)
-            r.pack1[at, cols] = coarse
-            r.pack2[at, cols] = (product - coarse.astype(F32)).astype(BF16)
-        score = dot(r.pack1[...], r.heads[...]) + dot(r.pack2[...], r.heads[...])
-        r.score[b] = score.astype(BF16)
+            w.pack1[at, cols] = coarse
+            w.pack2[at, cols] = (product - coarse.astype(F32)).astype(BF16)
+        score = dot(w.pack1[...], r.heads[...]) + dot(w.pack2[...], r.heads[...])
+        for cg in range(CG):
+            r.score[b, cg] = score[:, cg * LANES : (cg + 1) * LANES].astype(BF16)
         half = filter_part(b, 2)
         for cg, at, cols, near_rows in tiles(sz, first):
             h = half[at, cols]
@@ -314,12 +334,16 @@
             s = score[at, cols]
             attention = (s + s * jnp.tanh(s)) * r.cut_wide[b, at, :]
             r.sagg[cg] += attention * (r.kv[CG + cg, near_rows, :] * (h + h * jnp.tanh(h)))
+
+    def pair(i, carry):
+        for which in range(2):
+            block(2 * i + which, buffers(r, sz, which))
         return carry
 
-    lax.fori_loop(0, sz.blocks, block, 0)
+    lax.fori_loop(0, sz.blocks // 2, pair, 0)
     third = sum(dot(r.units[b], r.third[b]) for b in range(sz.blocks))
     scalar_low = jnp.concatenate([r.sagg[cg] for cg in range(CG)], axis=1).astype(BF16)
-    r.scalar_out[...] = scalar_low
+    r.o_scalar[...] = scalar_low
     out_proj = dot(scalar_low, r.s_wout[...])
     vector_agg = [
         jnp.concatenate([r.vagg[c * CG + cg] for cg in range(CG)], axis=1)
@@ -327,27 +351,48 @@
         for c in range(3)
     ]
     write_layer_output(r, sz, own, out_proj, vector_dot(r, sz), vector_agg)
-
-
-def edge_filters(r, sz, m):
+    if not fetch:
+        return
+    copies = [
+        pltpu.make_async_copy(source, target, r.sems.at[i])
+        for i, (source, target) in enumerate([
+            (r.fresh, r.out_fresh),
+            (r.head, r.out_head),
+            (r.tail, r.out_tail),
+            (r.o_scalar, r.out_scalar),
+            (r.score, r.out_score),
+        ])
+    ]
+    for copy in copies:
+        copy.start()
+    for copy in copies:
+        copy.wait()
+
+
+def edge_filters(r, sz, which):
     F = sz.width
     write_constants(r, sz)
-    edge_geometry(r, sz, m, r.coords.at[m], r.nbr.at[m, 0], r.counts.at[m], r.shifts.at[m, 0])
-    r.wh[...] = (r.wfilt[0].astype(F32) * 0.5).astype(BF16)
-
-    def block(b, carry):
-        write_edge_tables(r, sz, b, BF16)
-        for part in range(4):
-            cols = slice(part * F, (part + 1) * F)
-            h = dot(r.smear_t[b], r.wh[:, cols])
-            t = jnp.tanh(h)
-            up = 1.0 + t
-            f = h * up
-            r.silu[b, :, cols] = f.astype(BF16)
-            r.slope[b, :, cols] = (up + f * (1.0 - t)).astype(BF16)
-        return carry
-
-    lax.fori_loop(0, sz.blocks, block, 0)
+    for m in which:
+        w = SimpleNamespace(**vars(r))
+        vars(w).update(vars(buffers(r, sz, m)))
+        edge_geometry(w, sz, m, r.coords.at[m], r.slots.at[m])
+
+        def block(b, carry, w=w):
+            write_edge_tables(w, sz, b, BF16)
+            for part in range(4):
+                cols = slice(part * F, (part + 1) * F)
+                h = dot(r.smear_t[b], r.wh[:, cols])
+                t = jnp.tanh(h)
+                f = h + h * t
+                f, t = f.astype(BF16), t.astype(BF16)
+                slope = (1.0 + t) + f * (1.0 - t)
+                for cg in range(sz.halves):
+                    half = slice(cg * LANES, (cg + 1) * LANES)
+                    w.silu[b, part * sz.halves + cg] = f[:, half]
+                    w.slope[b, part * sz.halves + cg] = slope[:, half]
+            return carry
+
+        lax.fori_loop(0, sz.blocks, block, 0, unroll=2)
 
 
 def both_ways(r, sz, m, fwd):
@@ -367,48 +412,52 @@
     left = r.left
     vp = r.vproj
     vp[...] = dot(left[E : E + 3 * A, :], wvec[...])
-    r.wh[...] = (r.wfilt[0].astype(F32) * 0.5).astype(BF16)
     for cg in range(CG):
         r.query_low[:, halves[cg]] = r.query[cg].astype(BF16)
 
     if fwd:
         r.sagg[...] = jnp.zeros_like(r.sagg)
         r.vagg[...] = jnp.zeros_like(r.vagg)
+        r.uagg[...] = jnp.zeros_like(r.uagg)
 
         def forward_block(b, carry):
             first = first_row(b)
-            for cg, at, cols, near_rows in tiles(sz, first):
-                product = r.query[cg] * r.kv[cg, near_rows, :] * r.silu[b, at, cols].astype(F32)
+
+            def filters(part, cg, at):
+                return r.silu[b, part * CG + cg, at, :]
+
+            def keys(cg, at, cols, near_rows):
+                product = r.query[cg] * r.kv[cg, near_rows, :] * filters(0, cg, at).astype(F32)
                 coarse = product.astype(BF16)
-                r.pack1[at, cols] = coarse
-                r.pack2[at, cols] = (product - coarse.astype(F32)).astype(BF16)
-            score = dot(r.pack1[...], r.heads[...]) + dot(r.pack2[...], r.heads[...])
-            for cg, at, cols, near_rows in tiles(sz, first):
-                f = r.silu[b, at, slice(2 * F + cg * LANES, 2 * F + (cg + 1) * LANES)]
-                value = r.kv[2 * CG + cg, near_rows, :].astype(BF16) * f
-                for c in range(3):
-                    r.spread[1 + c, at, cols] = (
-                        r.vec[c * CG + cg, near_rows, :].astype(BF16) * value
-                    )
-            for cg, at, cols, near_rows in tiles(sz, first):
-                f = r.silu[b, at, slice(3 * F + cg * LANES, 3 * F + (cg + 1) * LANES)]
-                r.pack3[at, cols] = r.kv[3 * CG + cg, near_rows, :].astype(BF16) * f
-            for cg, at, cols, near_rows in tiles(sz, first):
-                f = r.silu[b, at, slice(F + cg * LANES, F + (cg + 1) * LANES)]
-                s = score[at, cols].astype(BF16)
-                r.score[b, at, cols] = s
+                return coarse, (product - coarse.astype(F32)).astype(BF16)
+
+            coarse, fine = stacked(sz, first, keys)
+            score = dot(coarse, r.heads[...]) + dot(fine, r.heads[...])
+            for cg in range(CG):
+                r.score[b, cg] = score[:, halves[cg]].astype(BF16)
+
+            def vectors(cg, at, cols, near_rows):
+                value = r.kv[2 * CG + cg, near_rows, :].astype(BF16) * filters(2, cg, at)
+                return [
+                    r.vec[c * CG + cg, near_rows, :].astype(BF16) * value for c in range(3)
+                ] + [r.kv[3 * CG + cg, near_rows, :].astype(BF16) * filters(3, cg, at)]
+
+            moved = stacked(sz, first, vectors)
+            for c in range(3):
+                r.vagg[c] += dot(r.fold[...], moved[c])
+            r.uagg[...] += dot(r.units[b], moved[3])
+
+            def scalars(cg, at, cols, near_rows):
+                s = r.score[b, cg, at, :]
                 attention = s * (1.0 + jnp.tanh(s)) * r.cut_wide[b, at, :]
-                r.spread[0, at, cols] = attention * (
-                    r.kv[CG + cg, near_rows, :].astype(BF16) * f
-                )
-            r.sagg[...] += dot(r.fold[...], r.spread[0])
-            for c in range(3):
-                r.vagg[c] += dot(r.fold[...], r.spread[1 + c]) + dot(
-                    r.units[b, c * A : (c + 1) * A, :], r.pack3[...]
-                )
+                return [
+                    attention * (r.kv[CG + cg, near_rows, :].astype(BF16) * filters(1, cg, at))
+                ]
+
+            r.sagg[...] += dot(r.fold[...], *stacked(sz, first, scalars))
             return carry
 
-        lax.fori_loop(0, NB, forward_block, 0)
+        lax.fori_loop(0, NB, forward_block, 0, unroll=4)
         scalar_low = r.sagg[...].astype(BF16)
     else:
         scalar_low = r.scalar_in[...]
@@ -416,7 +465,8 @@
     out_proj = dot(scalar_low, wout[...])
     vec_dot = vector_dot(r, sz)
     if fwd:
-        write_layer_output(r, sz, own, out_proj, vec_dot, [r.vagg[c] for c in range(3)])
+        vector_agg = [r.vagg[c] + r.uagg[c * A : (c + 1) * A, :] for c in range(3)]
+        write_layer_output(r, sz, own, out_proj, vec_dot, vector_agg)
 
     def incoming(index):
         if fwd:
@@ -449,71 +499,84 @@
     def backward_block(b, carry):
         first = first_row(b)
         base = pl.multiple_of(first // SUBLANES * SUBLANES, SUBLANES)
+        lanes = iota((W, EB), 1)
+        place = jnp.where(
+            lanes % A + lanes // A + (first - base) == iota((W, EB), 0), 1.0, 0.0
+        ).astype(BF16)
+
+        def collect(index, terms):
+            r.gnear[index, pl.ds(base, W), :] += dot(place, terms)
 
         def filters(part, cg, at):
-            cols = slice(part * F + cg * LANES, part * F + (cg + 1) * LANES)
-            return r.silu[b, at, cols], r.slope[b, at, cols], cols
-
-        for cg, at, cols, near_rows in tiles(sz, first):
-            f, _, _ = filters(1, cg, at)
+            return r.silu[b, part * CG + cg, at, :], r.slope[b, part * CG + cg, at, :]
+
+        def weights(cg, at, cols, near_rows):
             value = r.kv[CG + cg, near_rows, :].astype(BF16)
-            r.pack2[at, cols] = r.gs[:, cols] * (value * f)
-            r.keep4[at, cols] = value
-        g_att = dot(r.pack2[...], r.heads[...])
-        for cg, at, cols, near_rows in tiles(sz, first):
-            f, slope, part_cols = filters(2, cg, at)
+            return [r.gs[:, cols] * (value * filters(1, cg, at)[0])]
+
+        g_att = dot(*stacked(sz, first, weights), r.heads[...])
+
+        def vectors(cg, at, cols, near_rows):
+            f, slope = filters(2, cg, at)
             value = r.kv[2 * CG + cg, near_rows, :].astype(BF16)
             message = value * f
+            moved = []
             for c in range(3):
                 g_vec = r.gvlow[c * A : (c + 1) * A, cols]
                 term = g_vec * r.vec[c * CG + cg, near_rows, :].astype(BF16)
                 g_edge = term if c == 0 else g_edge + term
-                r.spread[4 + c, at, cols] = g_vec * message
-            r.spread[2, at, cols] = g_edge * f
-            r.gpre[at, part_cols] = g_edge * (value * slope)
+                moved.append(g_vec * message)
+            return moved + [g_edge * f, g_edge * (value * slope)]
+
+        *moved, g_value, g_pre = stacked(sz, first, vectors)
+        for c in range(3):
+            collect(4 + c, moved[c])
+        collect(2, g_value)
+        pre = [None, None, g_pre, None]
         g_third = dot(r.units[b], r.gvlow[...], 0, 0)
-        for cg, at, cols, near_rows in tiles(sz, first):
-            f, slope, part_cols = filters(3, cg, at)
+
+        def units(cg, at, cols, near_rows):
+            f, slope = filters(3, cg, at)
             value = r.kv[3 * CG + cg, near_rows, :].astype(BF16)
-            r.pack3[at, cols] = value * f
             g_edge = g_third[at, cols].astype(BF16)
-            r.spread[3, at, cols] = g_edge * f
-            r.gpre[at, part_cols] = g_edge * (value * slope)
-        for cg, at, cols, near_rows in tiles(sz, first):
-            s = r.score[b, at, cols]
+            return value * f, g_edge * f, g_edge * (value * slope)
+
+        message, g_value, pre[3] = stacked(sz, first, units)
+        collect(3, g_value)
+        g_unit = dot(r.gvlow[...], message, 1, 1)
+        for c in range(3):
+            r.gunit[c, pl.ds(b, 1), :] = jnp.sum(
+                g_unit[c * A : (c + 1) * A, :] * r.diag[...], axis=0, keepdims=True
+            )
+
+        def attention(cg, at, cols, near_rows):
+            s = r.score[b, cg, at, :]
             t = jnp.tanh(s)
             up = 1.0 + t
             act = s * up
             wide = r.cut_wide[b, at, :]
             ga = g_att[at, cols].astype(BF16)
-            r.pack1[at, cols] = ga * act
             g_score = ga * wide * (up + act * (1.0 - t))
             g_edge = r.gs[:, cols] * (act * wide)
-            f, slope, part_cols = filters(0, cg, at)
+            f, slope = filters(0, cg, at)
             key = r.kv[cg, near_rows, :].astype(BF16)
+            query = r.query_low[:, cols]
             middle = g_score * f
-            steep = g_score * slope
-            r.spread[7, at, cols] = middle * key
-            r.spread[0, at, cols] = middle * r.query_low[:, cols]
-            r.gpre[at, part_cols] = steep * (key * r.query_low[:, cols])
-            f, slope, part_cols = filters(1, cg, at)
-            r.spread[1, at, cols] = g_edge * f
-            r.gpre[at, part_cols] = g_edge * (r.keep4[at, cols] * slope)
-        lanes = iota((W, EB), 1)
-        place = jnp.where(
-            lanes % A + lanes // A + (first - base) == iota((W, EB), 0), 1.0, 0.0
-        ).astype(BF16)
-        for index in range(7):
-            r.gnear[index, pl.ds(base, W), :] += dot(place, r.spread[index])
-        r.gq[...] += dot(r.fold[...], r.spread[7])
-        g_unit = dot(r.gvlow[...], r.pack3[...], 1, 1)
-        for c in range(3):
-            r.gunit[c, pl.ds(b, 1), :] = jnp.sum(
-                g_unit[c * A : (c + 1) * A, :] * r.diag[...], axis=0, keepdims=True
-            )
-        g_cut = dot(jnp.ones((16, F), BF16), r.pack1[...], 1, 1)[0:1, :] * (2.0 * HEADS / F)
-        g_smear = dot(r.wh[...], r.gpre[...], 1, 1)
-        r.gfilt[...] += dot(r.smear[b], r.gpre[...])
+            made = [ga * act, middle * key, middle * query, (g_score * slope) * (key * query)]
+            f, slope = filters(1, cg, at)
+            value = r.kv[CG + cg, near_rows, :].astype(BF16)
+            return made + [g_edge * f, g_edge * (value * slope)]
+
+        g_act, g_query, g_key, pre[0], g_value, pre[1] = stacked(sz, first, attention)
+        r.gq[...] += dot(r.fold[...], g_query)
+        collect(0, g_key)
+        collect(1, g_value)
+        g_cut = dot(jnp.ones((16, F), BF16), g_act, 1, 1)[0:1, :] * (2.0 * HEADS / F)
+        g_smear = jnp.zeros((sz.basis, EB), F32)
+        for part in range(4):
+            cols = slice(part * F, (part + 1) * F)
+            g_smear = g_smear + dot(r.wh[:, cols], pre[part], 1, 1)
+            r.gfilt[:, cols] += dot(r.smear[b], pre[part])
         delta, bell = bell_of(r, sz, b)
         through = g_smear * bell
         r.gcut[pl.ds(b, 1), :] = g_cut + jnp.sum(through, axis=0, keepdims=True)
@@ -585,10 +648,11 @@
         r.rim_high[index] = whole[H + A :].astype(BF16)
 
 
-FACTORS = ("left", "gproj", "gvproj", "gout", "gfilt", "gnorm", "rim_low", "rim_high", "gplaces")
-
-
-def call(body, arrays, outs, scratch, role=None, grant_mb=24):
+FACTORS = ("left", "gproj", "gvproj", "gout", "gfilt", "gnorm")
+BORDERS = ("rim_low", "rim_high", "gplaces")
+
+
+def call(body, arrays, outs, scratch, role=None, grant_mb=16, place=VMEM):
     arrays, outs = vars(arrays), vars(outs)
     names = list(arrays) + list(outs) + list(scratch)
 
@@ -603,43 +667,44 @@
         kernel,
         out_shape=list(outs.values()),
         in_specs=[spec for _, spec in arrays.values()],
-        out_specs=[VMEM for _ in outs],
+        out_specs=[place for _ in outs],
         scratch_shapes=[
             pltpu.VMEM(*s) if isinstance(s, tuple) else s for s in scratch.values()
         ],
-        compiler_params=pltpu.CompilerParams(vmem_limit_bytes=grant_mb * 2**20),
+        compiler_params=pltpu.CompilerParams(vmem_limit_bytes=int(grant_mb * 2**20)),
     )(*[array for array, _ in arrays.values()])
     return SimpleNamespace(**dict(zip(outs, results, strict=True)))
 
 
-def first_call(sz, m, arrays):
+def first_call(sz, m, fetch, arrays):
     A, H, E, F = sz.atoms, sz.halo, sz.rows, sz.width
     EB, CG, NB = sz.edges, sz.halves, sz.blocks
     shape = jax.ShapeDtypeStruct
-    outs = SimpleNamespace(
-        fresh=shape((4, A, F), BF16),
-        head=shape((4, sz.sent, F), BF16),
-        tail=shape((4, sz.sent, F), BF16),
-        scalar_out=shape((A, F), BF16),
-        score=shape((NB, EB, F), BF16),
-    )
-    scratch = dict(
+    results = dict(
+        fresh=((4, A, F), BF16),
+        head=((4, sz.sent, F), BF16),
+        tail=((4, sz.sent, F), BF16),
+        o_scalar=((A, F), BF16),
+        score=((NB, CG, EB, LANES), BF16),
+    )
+    fetched = dict(
         s_own=((4, A, F), BF16),
         s_coords=((3, 1, A), F32),
-        s_nbr=((sz.slots, A), jnp.int32),
-        s_counts=((1, A), jnp.int32),
-        s_shifts=((2, sz.slots, A), jnp.int32),
+        s_slots=((3 * sz.slots + 8, A), jnp.int32),
         s_wqkv=((F, 5 * F), BF16),
         s_wvec=((F, 3 * F), BF16),
-        s_wfilt=((sz.basis, 4 * F), BF16),
+        s_wh=((sz.basis, 4 * F), BF16),
         s_wout=((F, 3 * F), BF16),
         sems=pltpu.SemaphoreType.DMA((9,)),
+    )
+    named = dict(fresh="out_fresh", head="out_head", tail="out_tail", o_scalar="out_scalar", score="out_score")
+    outs = SimpleNamespace(**{(named[k] if fetch else k): shape(*v) for k, v in results.items()})
+    scratch = dict(
         left=((sz.factors, F), BF16),
         query=((CG, A, LANES), F32),
         kv=((4 * CG, E, LANES), F32),
         vec=((3 * CG, E, LANES), F32),
         vproj=((3 * A, 3 * F), F32),
-        wh=((sz.basis, 4 * F), BF16),
         heads=((F, F), BF16),
         diag=((A, EB), F32),
         geo=((10, 8, EB), F32),
@@ -647,37 +712,58 @@
         smear_t=((NB, EB, sz.basis), BF16),
         cut_wide=((NB, EB, LANES), F32),
         units=((NB, 3 * A, EB), BF16),
-        pack1=((EB, F), BF16),
-        pack2=((EB, F), BF16),
+        pack10=((EB, F), BF16),
+        pack20=((EB, F), BF16),
+        pack11=((EB, F), BF16),
+        pack21=((EB, F), BF16),
         sagg=((CG, A, LANES), F32),
         vagg=((3 * CG, A, LANES), F32),
         third=((NB, EB, F), BF16),
     )
-    return call(lambda r: first_forward(r, sz, m), arrays, outs, scratch, FIRST, grant_mb=54)
-
-
-def filter_call(sz, m, arrays):
+    if fetch:
+        scratch.update(results)
+        scratch.update(fetched)
+    made = call(
+        lambda r: first_forward(r, sz, m, fetch),
+        arrays,
+        outs,
+        scratch,
+        FIRST,
+        grant_mb=54 if fetch else 20,
+        place=HBM if fetch else VMEM,
+    )
+    return SimpleNamespace(**{k: getattr(made, named[k] if fetch else k) for k in results})
+
+
+def filter_call(sz, role, which, arrays):
     A, F = sz.atoms, sz.width
-    EB, NB = sz.edges, sz.blocks
+    EB, CG, NB = sz.edges, sz.halves, sz.blocks
     shape = jax.ShapeDtypeStruct
-    outs = SimpleNamespace(
+    outs = dict(
         geo=shape((10, 8, EB), F32),
         smear=shape((NB, sz.basis, EB), BF16),
         cut_wide=shape((NB, EB, LANES), BF16),
         units=shape((NB, 3 * A, EB), BF16),
-        silu=shape((NB, EB, 4 * F), BF16),
-        slope=shape((NB, EB, 4 * F), BF16),
+        silu=shape((NB, 4 * CG, EB, LANES), BF16),
+        slope=shape((NB, 4 * CG, EB, LANES), BF16),
     )
     scratch = dict(
-        wh=((sz.basis, 4 * F), BF16),
         diag=((A, EB), F32),
         centres=((sz.basis, EB), F32),
         smear_t=((NB, EB, sz.basis), BF16),
     )
-    return call(lambda r: edge_filters(r, sz, m), arrays, outs, scratch)
-
-
-def both_call(sz, m, fwd, arrays):
+    made = call(
+        lambda r: edge_filters(r, sz, which),
+        arrays,
+        SimpleNamespace(**{f"{k}{m}": v for m in which for k, v in outs.items()}),
+        scratch,
+        role,
+        grant_mb=6,
+    )
+    return {m: SimpleNamespace(**{k: getattr(made, f"{k}{m}") for k in outs}) for m in which}
+
+
+def both_call(sz, m, fwd, arrays, border_sets=()):
     A, H, E, F = sz.atoms, sz.halo, sz.rows, sz.width
     EB, CG, NB = sz.edges, sz.halves, sz.blocks
     shape = jax.ShapeDtypeStruct
@@ -700,20 +786,13 @@
         kv=((4 * CG, E, LANES), F32),
         vec=((3 * CG, E, LANES), F32),
         vproj=((3 * A, 3 * F), F32),
-        wh=((sz.basis, 4 * F), BF16),
         heads=((F, F), BF16),
         diag=((A, EB), F32),
         fold=((A, EB), BF16),
         centres=((sz.basis, EB), F32),
-        pack1=((EB, F), BF16),
-        pack2=((EB, F), BF16),
-        pack3=((EB, F), BF16),
-        keep4=((EB, F), BF16),
         gx=((4, A, F), F32),
         gvlow=((3 * A, F), BF16),
         gs=((A, F), BF16),
-        spread=((8, EB, F), BF16),
-        gpre=((EB, 4 * F), BF16),
         gq=((A, F), F32),
         gnear=((7, E, F), F32),
         gunit=((3, 8, EB), F32),
@@ -723,31 +802,66 @@
     if fwd:
         outs.fresh = shape((4, A, F), BF16)
         scratch.update(
-            score=((NB, EB, F), BF16), sagg=((A, F), F32), vagg=((3, A, F), F32)
+            score=((NB, CG, EB, LANES), BF16), sagg=((A, F), F32), vagg=((3, A, F), F32), uagg=((3 * A, F), F32)
         )
-    role = SECOND if fwd else FIRST
-    return call(lambda r: both_ways(r, sz, m, fwd), arrays, outs, scratch, role)
-
-
-def border_call(sz, features, coords):
-    A, H, F = sz.atoms, sz.halo, sz.width
+    if not border_sets:
+        role = SECOND if fwd else FIRST
+        return call(lambda r: both_ways(r, sz, m, fwd), arrays, outs, scratch, role)
+    count = m + 1
+    outs.up, outs.down = shape((count, 4, H, F), BF16), shape((count, 4, H, F), BF16)
+    outs.moved = shape((count, 8, LANES), F32)
+    for role, sets in enumerate(border_sets):
+        for i, made in enumerate(sets):
+            for name in BORDERS:
+                setattr(arrays, f"{name}_{role}_{i}", (getattr(made, name), VMEM))
+
+    def hand_on(r, role):
+        for i in range(count):
+            low, high, places = (
+                getattr(r, f"{name}_{role}_{i}") if i < len(border_sets[role]) else getattr(r, name)
+                for name in BORDERS
+            )
+            r.up[i] = high[...]
+            r.down[i] = low[...]
+            r.moved[i] = places[...]
+
+    def body(r):
+        @pl.when(r.scal[0] == FIRST)
+        def _():
+            both_ways(r, sz, m, fwd)
+            hand_on(r, FIRST)
+
+        pl.when(r.scal[0] == SECOND)(lambda: hand_on(r, SECOND))
+
+    return call(body, arrays, outs, scratch)
+
+
+def border_call(sz, features, coords, neighbours, shifts, counts, gain, bias, filter_weight):
+    A, H, F, K = sz.atoms, sz.halo, sz.width, sz.slots
     count = features.shape[0]
 
     def body(r):
-        copies = [pltpu.make_async_copy(r.coords, r.s_coords, r.sems.at[2 * count])]
+        moves = [(r.coords, r.s_coords)]
         for m in range(count):
-            copies.append(
-                pltpu.make_async_copy(
-                    r.features.at[m, 0, :, A - H : A, :], r.up.at[m, 0:4], r.sems.at[2 * m]
-                )
-            )
-            copies.append(
-                pltpu.make_async_copy(
-                    r.features.at[m, 0, :, 0:H, :], r.down.at[m, 0:4], r.sems.at[2 * m + 1]
-                )
-            )
+            moves += [
+                (r.features.at[m, 0, :, A - H : A, :], r.up.at[m, 0:4]),
+                (r.features.at[m, 0, :, 0:H, :], r.down.at[m, 0:4]),
+                (r.nbr.at[m, 0], r.slots.at[m, 0:K]),
+                (r.shifts.at[m, 0, 0], r.slots.at[m, K : 2 * K]),
+                (r.shifts.at[m, 0, 1], r.slots.at[m, 2 * K : 3 * K]),
+            ]
+        copies = [
+            pltpu.make_async_copy(source, target, r.sems.at[i])
+            for i, (source, target) in enumerate(moves)
+        ]
         for copy in copies:
             copy.start()
+        r.wh[...] = (r.wfilt[0].astype(F32) * 0.5).astype(BF16)
+        r.norms[0:1, :] = r.gain[...].astype(F32)
+        r.norms[1:2, :] = r.bias[...].astype(F32)
+        r.norms[2:, :] = jnp.zeros((6, F), F32)
+        for m in range(count):
+            r.slots[m, 3 * K :, :] = jnp.broadcast_to(r.counts[m], (8, A))
         copies[0].wait()
         for m in range(count):
             r.up[m, 4] = packed_places([r.s_coords[m, c][:, A - H :] for c in range(3)], F)
@@ -755,20 +869,34 @@
         for copy in copies[1:]:
             copy.wait()
 
-    shape = jax.ShapeDtypeStruct((count, 5, H, F), BF16)
+    shape = jax.ShapeDtypeStruct
     return call(
         body,
-        SimpleNamespace(features=(features, HBM), coords=(coords, HBM)),
-        SimpleNamespace(up=shape, down=shape),
-        dict(s_coords=(coords.shape, F32), sems=pltpu.SemaphoreType.DMA((2 * count + 1,))),
+        SimpleNamespace(
+            features=(features, HBM),
+            coords=(coords, HBM),
+            nbr=(neighbours, HBM),
+            shifts=(shifts, HBM),
+            counts=(counts, VMEM),
+            gain=(gain, VMEM),
+            bias=(bias, VMEM),
+            wfilt=(filter_weight, VMEM),
+        ),
+        SimpleNamespace(
+            up=shape((count, 5, H, F), BF16),
+            down=shape((count, 5, H, F), BF16),
+            slots=shape((count, 3 * K + 8, A), jnp.int32),
+            norms=shape((8, F), F32),
+            wh=shape((sz.basis, 4 * F), BF16),
+        ),
+        dict(s_coords=(coords.shape, F32), sems=pltpu.SemaphoreType.DMA((5 * count + 1,))),
         grant_mb=54,
     )
 
 
 def gradient_call(sz, scal, sets):
-    A, H, E, F = sz.atoms, sz.halo, sz.rows, sz.width
+    A, E, F = sz.atoms, sz.rows, sz.width
     count = len(sets[0])
-    K = sz.factors
     w1, w2, w3 = sz.widths
     w4, w5 = 4 * F // sz.space, F // sz.space
     half = F // 2
@@ -782,35 +910,40 @@
         def get(name, m):
             return getattr(r, f"{name}_{role}_{m}")
 
-        for m in range(count):
-            r.up[m, 0:4] = get("rim_high", m)[...]
-            r.down[m, 0:4] = get("rim_low", m)[...]
-            places = get("gplaces", m)
-            r.up[m, 4] = packed_places([places[c : c + 1, H + A : E] for c in range(3)], F)
-            r.down[m, 4] = packed_places([places[c : c + 1, 0:H] for c in range(3)], F)
-            for c in range(3):
-                r.mine[m, c] = places[c : c + 1, H : H + A]
-            r.left[:, m * K : (m + 1) * K] = jnp.transpose(get("left", m)[...])
-        filt = jnp.transpose(sum(get("gfilt", m)[...] for m in range(count)) * 0.5)
-        norm = sum(get("gnorm", m)[...] for m in range(count))
-        r.right[...] = jnp.zeros_like(r.right)
+        every = range(count)
+        e, a = E, A
+        r.qkv[...] = sum(dot(get("gproj", m)[...], get("left", m)[0:e, :], 0, 0) for m in every)
+        r.vector[...] = sum(
+            dot(get("gvproj", m)[...], get("left", m)[e : e + 3 * a, :], 0, 0) for m in every
+        )
+        r.out[...] = sum(
+            dot(get("gout", m)[...], get("left", m)[e + 3 * a : e + 4 * a, :], 0, 0) for m in every
+        )
+        filt = sum(get("gfilt", m)[...] for m in every) * 0.5
+        norm = sum(get("gnorm", m)[...] for m in every)
         core = r.scal[2]
         for k in range(sz.space):
-            for m in range(count):
-                at = m * K
-                r.right[at : at + E, 0:w1] = get("gproj", m)[:, k * w1 : (k + 1) * w1]
-                at += E
-                r.right[at : at + 3 * A, w1 : w1 + w2] = get("gvproj", m)[:, k * w2 : (k + 1) * w2]
-                at += 3 * A
-                r.right[at : at + A, w1 + w2 : sz.spare] = get("gout", m)[:, k * w3 : (k + 1) * w3]
-            r.packed[...] = dot(r.left[...], r.right[...])
-            spare = slice(sz.spare, sz.spare + sz.basis)
-            r.packed[0:w4, spare] = filt[k * w4 : (k + 1) * w4, :]
-            narrow = slice(sz.spare, sz.spare + w5)
-            r.packed[half : half + 1, narrow] = norm[0:1, k * w5 : (k + 1) * w5]
-            r.packed[half + 8 : half + 9, narrow] = norm[1:2, k * w5 : (k + 1) * w5]
-            r.send[k] = r.packed[pl.ds(pl.multiple_of((1 - core) * half, half), half), :].astype(BF16)
-            r.stay[k] = r.packed[pl.ds(pl.multiple_of(core * half, half), half), :]
+            spare = [filt[:, k * w4 : (k + 1) * w4]]
+            if half > w4:
+                spare.append(jnp.zeros((sz.basis, half - w4), F32))
+            left = jnp.concatenate(spare, axis=1)
+            rows = [norm[:, k * w5 : (k + 1) * w5], jnp.zeros((8, half - w5), F32)]
+            right = jnp.concatenate(rows, axis=1)
+            right = jnp.concatenate(
+                [right, jnp.zeros((sz.packed - sz.spare - 8, half), F32)], axis=0
+            )
+            if sz.packed - sz.spare > sz.basis:
+                gap = jnp.zeros((sz.packed - sz.spare - sz.basis, half), F32)
+                left = jnp.concatenate([left, gap], axis=0)
+            parts = [
+                r.qkv[k * w1 : (k + 1) * w1, :],
+                r.vector[k * w2 : (k + 1) * w2, :],
+                r.out[k * w3 : (k + 1) * w3, :],
+            ]
+            first = jnp.concatenate([part[:, :half] for part in parts] + [left], axis=0)
+            second = jnp.concatenate([part[:, half:] for part in parts] + [right], axis=0)
+            r.send[k] = jnp.where(core == 0, second, first).astype(BF16)
+            r.stay[k] = jnp.where(core == 0, first, second)
 
     def both(r):
         for role in (FIRST, SECOND):
@@ -821,18 +954,78 @@
         both,
         arrays,
         SimpleNamespace(
-            up=shape((count, 5, H, F), BF16),
-            down=shape((count, 5, H, F), BF16),
-            mine=shape((count, 3, 1, A), F32),
-            send=shape((sz.space, half, sz.packed), BF16),
-            stay=shape((sz.space, half, sz.packed), F32),
+            send=shape((sz.space, sz.packed, half), BF16),
+            stay=shape((sz.space, sz.packed, half), F32),
         ),
         dict(
-            left=((F, count * K), BF16),
-            right=((count * K, sz.packed), BF16),
-            packed=((F, sz.packed), F32),
+            qkv=((5 * F, F), F32),
+            vector=((3 * F, F), F32),
+            out=((3 * F, F), F32),
         ),
     )
+
+
+def border_rows(sz, m, index):
+    start = sz.packed + (m * 5 + index) * 2 * sz.halo
+    return [slice(start + i * sz.halo, start + (i + 1) * sz.halo) for i in range(2)]
+
+
+def border_block(sz, ref, m, index):
+    return jnp.concatenate([ref[rows, :] for rows in border_rows(sz, m, index)], axis=1)
+
+
+def piece_call(sz, scal, stay, recv, up, down, moved, other):
+    A, H, E, F = sz.atoms, sz.halo, sz.rows, sz.width
+    count = up.shape[0]
+    half = F // 2
+
+    def body(r):
+        slab, space = r.scal[1], sz.space
+        for hop in range(space):
+            k = lax.rem(slab + hop, space)
+            total = r.stay[k] + r.recv[k].astype(F32)
+            target = getattr(r, f"hop{hop}")
+            target[0 : sz.packed, :] = total.astype(target.dtype)
+        for m in range(count):
+            places = r.moved[m] + r.other[m]
+            rows = [places[c : c + 1, :] for c in range(3)]
+            ends = (
+                (r.hop1, r.up, [row[:, H + A : E] for row in rows]),
+                (getattr(r, f"hop{space - 1}"), r.down, [row[:, 0:H] for row in rows]),
+            )
+            for target, border, part in ends:
+                blocks = [border[m, index] for index in range(4)] + [packed_places(part, F)]
+                for index, block in enumerate(blocks):
+                    first, second = border_rows(sz, m, index)
+                    target[first, :] = block[:, :half]
+                    target[second, :] = block[:, half:]
+            for c in range(3):
+                r.mine[m, c] = rows[c][:, H : H + A]
+
+    shape = jax.ShapeDtypeStruct
+    outs = {
+        f"hop{hop}": shape(
+            (sz.packed + (10 * H * count if hop in (1, sz.space - 1) else 0), half),
+            BF16 if hop else F32,
+        )
+        for hop in range(sz.space)
+    }
+    outs.update(mine=shape((count, 3, 1, A), F32))
+    made = call(
+        body,
+        SimpleNamespace(
+            scal=(scal, SMEM),
+            stay=(stay, VMEM),
+            recv=(recv, VMEM),
+            up=(up, VMEM),
+            down=(down, VMEM),
+            moved=(moved, VMEM),
+            other=(other, VMEM),
+        ),
+        SimpleNamespace(**outs),
+        {},
+    )
+    return [getattr(made, f"hop{hop}") for hop in range(sz.space)], made.mine
 
 
 def result_call(sz, scal, fresh, back, from_low, from_high, mine):
@@ -850,14 +1043,17 @@
         for m in range(count):
             r.outputs[0, m, 0] = getattr(r, f"fresh_{role}_{m}")[...]
             whole = getattr(r, f"back_{role}_{m}")
-            r.grads[0, m, 0, :, 0:H, :] = whole[:, 0:H, :] + r.low[m, 0:4].astype(F32)
-            r.grads[0, m, 0, :, H : A - H, :] = whole[:, H : A - H, :]
-            r.grads[0, m, 0, :, A - H :, :] = whole[:, A - H :, :] + r.high[m, 0:4].astype(F32)
+            for index in range(4):
+                low = border_block(sz, r.low, m, index).astype(F32)
+                high = border_block(sz, r.high, m, index).astype(F32)
+                r.grads[0, m, 0, index, 0:H, :] = whole[index, 0:H, :] + low
+                r.grads[0, m, 0, index, H : A - H, :] = whole[index, H : A - H, :]
+                r.grads[0, m, 0, index, A - H :, :] = whole[index, A - H :, :] + high
             for c in range(3):
                 edge = [
-                    unpacked_places(r.low[m, 4], c, H),
+                    unpacked_places(border_block(sz, r.low, m, 4), c, H),
                     jnp.zeros((1, A - 2 * H), F32),
-                    unpacked_places(r.high[m, 4], c, H),
+                    unpacked_places(border_block(sz, r.high, m, 4), c, H),
                 ]
                 r.places[m, c] = r.mine[m, c] + jnp.concatenate(edge, axis=1)
 
@@ -885,13 +1081,13 @@
     half = F // 2
 
     def body(r, first, second):
-        for at, part in ((0, first), (half, second)):
-            r.qkv[0, at : at + half, :] = part[:, :w1]
-            r.vector[0, at : at + half, :] = part[:, w1 : w1 + w2]
-            r.out[0, at : at + half, :] = part[:, w1 + w2 : sz.spare]
-        r.filt[0] = jnp.transpose(first[:w4, sz.spare : sz.spare + sz.basis])
-        r.gain[...] = second[0:1, sz.spare : sz.spare + w5]
-        r.bias[...] = second[8:9, sz.spare : sz.spare + w5]
+        for lanes, part in ((slice(0, half), first), (slice(half, F), second)):
+            r.qkv[0, :, lanes] = part[0:w1, :]
+            r.vector[0, :, lanes] = part[w1 : w1 + w2, :]
+            r.out[0, :, lanes] = part[w1 + w2 : sz.spare, :]
+        r.filt[0] = first[sz.spare : sz.spare + sz.basis, 0:w4]
+        r.gain[...] = second[sz.spare : sz.spare + 1, 0:w5]
+        r.bias[...] = second[sz.spare + 1 : sz.spare + 2, 0:w5]
 
     def both(r):
         pl.when(r.scal[2] == 0)(lambda: body(r, r.total, r.other))
@@ -904,10 +1100,10 @@
         SimpleNamespace(
             gain=shape((1, w5), F32),
             bias=shape((1, w5), F32),
-            qkv=shape((1, F, w1), F32),
-            vector=shape((1, F, w2), F32),
+            qkv=shape((1, w1, F), F32),
+            vector=shape((1, w2, F), F32),
             filt=shape((1, sz.basis, w4), F32),
-            out=shape((1, F, w3), F32),
+            out=shape((1, w3, F), F32),
         ),
         {},
     )
@@ -938,8 +1134,10 @@
 
     scal = jnp.stack([section, slab, core, space - 1]).astype(jnp.int32)
     places = jnp.transpose(coords, (0, 2, 1, 3))
-    norms = jnp.concatenate([norm_gain, norm_bias], axis=0).astype(F32)
-    borders = border_call(sz, features, places)
+    borders = border_call(
+        sz, features, places, neighbours, shifts, counts, norm_gain, norm_bias, filter_weight
+    )
+    slots, norms, half_filter = borders.slots, borders.norms, borders.wh
     pack_low = lax.ppermute(borders.up, "space", up)
     pack_high = lax.ppermute(borders.down, "space", down)
     both = ("section", "space")
@@ -956,13 +1154,11 @@
             pack_low=(pack_low, VMEM),
             pack_high=(pack_high, VMEM),
             coords=(places, place),
-            nbr=(neighbours, place),
-            counts=(counts, place),
-            shifts=(shifts, place),
-            wfilt=(filter_weight, place),
+            slots=(slots, place),
+            wh=(half_filter, place),
         )
 
-    firsts, sent = [], []
+    firsts, sent, filters = [], [], {}
     for m in range(micro_count):
         arrays = geometry_inputs(HBM)
         arrays.features = (features, HBM)
@@ -970,25 +1166,26 @@
         arrays.wqkv, arrays.wvec, arrays.wout = (
             (qkv_weight, HBM), (vector_weight, HBM), (out_weight, HBM)
         )
-        first = first_call(sz, m, arrays)
+        first = first_call(sz, m, True, arrays)
         firsts.append(first)
+        if m == micro_count - 1:
+            made = filters[SECOND] = filter_call(
+                sz, SECOND, range(micro_count), geometry_inputs(VMEM)
+            )
+            first.head, made[0].geo = lax.optimization_barrier((first.head, made[0].geo))
         sent.append((
             lax.ppermute(first.fresh, both, forth),
             lax.ppermute(first.tail, both, forth_up),
             lax.ppermute(first.head, both, forth_down),
         ))
-    filters = [filter_call(sz, m, geometry_inputs(VMEM)) for m in range(micro_count)]
-    for made, geo in zip(filters, lax.optimization_barrier([made.geo for made in filters])):
-        made.geo = geo
-
-    def both_inputs(m):
-        made = filters[m]
+    def both_inputs(m, role):
+        made = filters[role][m]
         return SimpleNamespace(
             scal=(scal, SMEM),
             norms=(norms, VMEM),
             wqkv=(qkv_weight, VMEM),
             wvec=(vector_weight, VMEM),
-            wfilt=(filter_weight, VMEM),
+            wh=(half_filter, VMEM),
             wout=(out_weight, VMEM),
             geo=(made.geo, VMEM),
             smear=(made.smear, VMEM),
@@ -1000,19 +1197,27 @@
 
     seconds, returned = [], []
     for m in range(micro_count):
-        arrays = both_inputs(m)
+        if m == 1:
+            other = filters[FIRST][0]
+            other.geo, filters[SECOND][m].geo = lax.optimization_barrier(
+                (other.geo, filters[SECOND][m].geo)
+            )
+        arrays = both_inputs(m, SECOND)
         own, low, high = sent[m]
         arrays.own, arrays.low, arrays.high = (own, VMEM), (low, VMEM), (high, VMEM)
         arrays.cotangent = (cotangent, VMEM)
         second = both_call(sz, m, True, arrays)
         seconds.append(second)
+        if m == 0:
+            later = geometry_inputs(VMEM)
+            held, second.gplaces = lax.optimization_barrier((slots, second.gplaces))
+            later.slots = (held, VMEM)
+            filters[FIRST] = filter_call(sz, FIRST, range(micro_count), later)
         back_low, rim_low, rim_high = second.back_low, second.rim_low, second.rim_high
         if m:
-            _, inc_low, inc_high = returned[-1]
-            inc_low, inc_high, back_low, rim_low, rim_high = lax.optimization_barrier(
-                (inc_low, inc_high, back_low, rim_low, rim_high)
+            returned[-1], back_low, rim_low, rim_high = lax.optimization_barrier(
+                (returned[-1], back_low, rim_low, rim_high)
             )
-            returned[-1] = (returned[-1][0], inc_low, inc_high)
         returned.append((
             lax.ppermute(back_low, both, back),
             lax.ppermute(rim_high, both, back_up),
@@ -1020,36 +1225,38 @@
         ))
     thirds = []
     for m in range(micro_count):
-        arrays = both_inputs(m)
+        arrays = both_inputs(m, FIRST)
         arrays.pack_low, arrays.pack_high = (pack_low, VMEM), (pack_high, VMEM)
         arrays.features = (features, VMEM)
-        arrays.scalar_in = (firsts[m].scalar_out, VMEM)
+        arrays.scalar_in = (firsts[m].o_scalar, VMEM)
         arrays.score = (firsts[m].score, VMEM)
         inc, inc_low, inc_high = returned[m]
         arrays.inc, arrays.inc_low, arrays.inc_high = (inc, VMEM), (inc_low, VMEM), (inc_high, VMEM)
-        thirds.append(both_call(sz, m, False, arrays))
-
+        sets = (thirds, seconds) if m == micro_count - 1 else ()
+        thirds.append(both_call(sz, m, False, arrays, sets))
+
+    last = thirds[-1]
+    other = lax.ppermute(last.moved, "section", [(0, 1), (1, 0)])
     shares = gradient_call(sz, scal, (thirds, seconds))
-    summed = shares.stay + lax.ppermute(shares.send, "dp", [(0, 1), (1, 0)]).astype(F32)
-    pieces = summed.astype(BF16)
-    total = lax.dynamic_index_in_dim(summed, slab, 0, keepdims=False)
-    for hop in range(1, space):
-        piece = lax.dynamic_index_in_dim(pieces, (slab + hop) % space, 0, keepdims=False)
-        total = total + lax.ppermute(
-            piece, "space", [(i, (i + hop) % space) for i in range(space)]
-        ).astype(F32)
-    from_low = lax.ppermute(shares.up, "space", up)
-    from_high = lax.ppermute(shares.down, "space", down)
+    recv = lax.ppermute(shares.send, "dp", [(0, 1), (1, 0)])
+    (total, *pieces), mine = piece_call(
+        sz, scal, shares.stay, recv, last.up, last.down, last.moved, other
+    )
+    received = [
+        lax.ppermute(piece, "space", [(i, (i + hop) % space) for i in range(space)])
+        for hop, piece in enumerate(pieces, 1)
+    ]
+    for piece in received:
+        total = total + piece[: sz.packed].astype(F32)
     results = result_call(
         sz,
         scal,
         ([v.fresh for v in firsts], [v.fresh for v in seconds]),
         ([v.back for v in thirds], [v.back for v in seconds]),
-        from_low,
-        from_high,
-        shares.mine,
-    )
-    places_sum = results.places + lax.ppermute(results.places, "section", [(0, 1), (1, 0)])
+        received[0],
+        received[-1],
+        mine,
+    )
     other = lax.ppermute(total, "dp", [(0, 1), (1, 0)])
     share = share_call(sz, scal, total, other)
     return (
@@ -1057,11 +1264,11 @@
         results.grads,
         share.gain,
         share.bias,
-        share.qkv,
-        share.vector,
+        jnp.transpose(share.qkv, (0, 2, 1)),
+        jnp.transpose(share.vector, (0, 2, 1)),
         share.filt,
-        share.out,
-        jnp.transpose(places_sum, (0, 2, 1, 3)),
+        jnp.transpose(share.out, (0, 2, 1)),
+        jnp.transpose(results.places, (0, 2, 1, 3)),
     )
 
 

time: 144 us -> 119 us (0.83)
  waiting for transfers between devices: 32.3 us -> 21.7 us
  Pallas kernels: 66.4 us -> 58.8 us
  other arithmetic: 6.2 us -> 0.75 us
  starting transfers between devices: 34.7 us -> 32.2 us
    ppermute x2, waiting for transfers between devices: 15.3 us -> 2.36 us  [on_device(): lax.ppermute(rim_high, both, back_up)]
    pallas_call x12 -> x13, Pallas kernels: 66.4 us -> 58.8 us  [call(): pl.pallas_call(kernel, out_shape=list(outs.values()), in_specs=[spec for...]
    ppermute x7, waiting for transfers between devices: 8.19 us -> 13 us  [on_device(): lax.ppermute(piece, 'space', [(i, (i + hop) % space) for i in range(space)])]
    ppermute x4 -> x2, starting transfers between devices: 4.73 us -> 0.14 us  [the longest x1 0.07 us: on_device(): recv = lax.ppermute(shares.send, 'dp', [(0, 1), (1, 0)])]
    convert_element_type x2 -> x0, other arithmetic: 3.91 us -> none  [the longest x1 2.63 us: on_device(): pieces = summed.astype(BF16)]
    ppermute x4 -> x2, waiting for transfers between devices: 5.96 us -> 3.64 us  [the longest x1 3.64 us: on_device(): other = lax.ppermute(last.moved, 'section', [(0, 1), (1, 0)])]
    ppermute x7, starting transfers between devices: 8.12 us -> 10.3 us  [on_device(): lax.ppermute(piece, 'space', [(i, (i + hop) % space) for i in range(space)])]
    unnamed x47 -> x48, local copies, waits for them, and re-layouts: 2.99 us -> 4 us
  transfers between devices with their start and end apart: 26 -> 24, of which waited for: 11 -> 7; matrix products, arithmetic and copies ran while one was open for 2% -> 1% of each run, Pallas kernels for 25% -> 27%
where the time goes in v2:
time: 119 us
  Pallas kernels  58.8 us (49%)
  starting transfers between devices  32.2 us (27%)
  waiting for transfers between devices  21.7 us (18%)
  local copies, waits for them, and re-layouts  4 us (3%)
  between operations  1.19 us (1%)
    pallas_call x13, Pallas kernels, call(): pl.pallas_call(kernel, out_shape=list(outs.values()), in_specs=[spec for...  58.8 us
    ppermute x7, waiting for transfers between devices, on_device(): lax.ppermute(piece, 'space', [(i, (i + hop) % space) for i in range(space)])  13 us
    ppermute x7, starting transfers between devices, on_device(): lax.ppermute(piece, 'space', [(i, (i + hop) % space) for i in range(space)])  10.3 us
    unnamed x48, local copies, waits for them, and re-layouts  4 us
    ppermute x1, waiting for transfers between devices, on_device(): other = lax.ppermute(last.moved, 'section', [(0, 1), (1, 0)])  3.64 us
    ppermute x1, starting transfers between devices, on_device(): pack_high = lax.ppermute(borders.down, 'space', down)  3.1 us
    ppermute x1, starting transfers between devices, on_device(): pack_low = lax.ppermute(borders.up, 'space', up)  3.02 us
    ppermute x2, starting transfers between devices, on_device(): lax.ppermute(first.tail, both, forth_up)  2.59 us
  transfers between devices with their start and end apart: 24, of which 7 were waited for; matrix products, arithmetic and copies ran while one was open for 1% of the time, Pallas kernels for 27%

profile of v2, /device:TPU:0, one launch (start us, length us, event | category | flops | bytes accessed | tf_op | source)
XLA Modules:
  0.0 118.7 jit_solution(16026396909449902091)
XLA Ops:
  0.6 0.0 copy-start.21
  0.7 0.0 copy-start
  0.7 0.0 copy-start.1
  0.7 0.0 copy-start.2
  0.7 2.7 %shard_map.187 = (bf16[2,5,16,256]{3,2,1,0:T(8,128)(2,1)}, bf16[2,5,16,256]{3,2,1,0:T(8,128)(2,1)}, s32[2,104,64]{2,1,0:T(8,128)}, f32[8,256]{1,0:T(8,128)}, bf16[32,1024]{1,0:T(8,128)(2,1)}) custom-call(bf16[2,1,4,64,256]{4,3,2,1,0:T(8,128)(2,1)} %args_14_.3, f32[2,3,1,64]{3,2,1,0:T(1,128)} %bitcast.8, s32[2,1,32,64]{3,2,1,0:T(8,128)} %args_2_.8, ...), custom_call_target="tpu_custom_call" | custom-call | tf_op jit(solution)/shard_map/pallas_call | solution.py:666
  3.4 0.0 copy-start.16
  3.4 3.0 %collective-permute-start = (bf16[2,5,16,256]{3,2,1,0:T(8,128)(2,1)}, bf16[2,5,16,256]{3,2,1,0:T(8,128)(2,1)S(1)}, u32[]{:S(2)}, u32[]{:S(2)}) collective-permute-start(bf16[2,5,16,256]{3,2,1,0:T(8,128)(2,1)} %get-tuple-element.126), channel_id=1, source_target_pairs={{0,2},{2,4},{4,6},{6,8},{8,10},{10,12},{12,14},{14,0},{1,3},{3,5},... | collective-permute-start | bytes 245768 | tf_op jit(solution)/shard_map/ppermute | solution.py:1141
  6.5 3.1 %collective-permute-start.1 = (bf16[2,5,16,256]{3,2,1,0:T(8,128)(2,1)}, bf16[2,5,16,256]{3,2,1,0:T(8,128)(2,1)S(1)}, u32[]{:S(2)}, u32[]{:S(2)}) collective-permute-start(bf16[2,5,16,256]{3,2,1,0:T(8,128)(2,1)} %get-tuple-element.127), channel_id=1, source_target_pairs={{2,0},{4,2},{6,4},{8,6},{10,8},{12,10},{14,12},{0,14},{3,1},{5,3},... | collective-permute-start | bytes 245768 | tf_op jit(solution)/shard_map/ppermute | solution.py:1142
  9.6 0.7 pad_add_fusion.args_0_
  10.2 2.0 %collective-permute-done.args_1_.args_12_ = bf16[2,5,16,256]{3,2,1,0:T(8,128)(2,1)S(1)} collective-permute-done((bf16[2,5,16,256]{3,2,1,0:T(8,128)(2,1)}, bf16[2,5,16,256]{3,2,1,0:T(8,128)(2,1)S(1)}, u32[]{:S(2)}, u32[]{:S(2)}) %collective-permute-start) | collective-permute-done | bytes 81952 | tf_op jit(solution)/shard_map/ppermute | solution.py:1141
  12.3 0.6 collective-permute-done.1.args_2_.args_13_
  12.9 0.0 copy-done.6
  12.9 0.6 copy-done.9
  13.5 10.1 %shard_map.190 = (bf16[4,64,256]{2,1,0:T(8,128)(2,1)}, bf16[4,64,256]{2,1,0:T(8,128)(2,1)}, bf16[4,64,256]{2,1,0:T(8,128)(2,1)}, bf16[64,256]{1,0:T(8,128)(2,1)}, bf16[8,2,256,128]{3,2,1,0:T(8,128)(2,1)}) custom-call(s32[4]{0:T(128)} %pad_add_fusion.args_0_, bf16[2,5,16,256]{3,2,1,0:T(8,128)(2,1)} %copy-done.6, bf16[2,5,16,256]{3,2,1,0:T(8,128)(2,1)} %copy-done.9, ...), custom_call_target="tpu_custom_call" | custom-call | tf_op jit(solution)/shard_map/pallas_call | solution.py:666
  23.6 1.3 %collective-permute-start.2 = (bf16[4,64,256]{2,1,0:T(8,128)(2,1)}, bf16[4,64,256]{2,1,0:T(8,128)(2,1)S(1)}, u32[]{:S(2)}, u32[]{:S(2)}) collective-permute-start(bf16[4,64,256]{2,1,0:T(8,128)(2,1)} %get-tuple-element.137.args_4_), channel_id=1, source_target_pairs={{0,16},{2,18},{4,20},{6,22},{8,24},{10,26},{12,28},{14,30},{1,17},... | collective-permute-start | bytes 393224 | tf_op jit(solution)/shard_map/ppermute | solution.py:1177
  24.9 1.3 %collective-permute-start.3 = (bf16[4,64,256]{2,1,0:T(8,128)(2,1)}, bf16[4,64,256]{2,1,0:T(8,128)(2,1)S(1)}, u32[]{:S(2)}, u32[]{:S(2)}) collective-permute-start(bf16[4,64,256]{2,1,0:T(8,128)(2,1)} %get-tuple-element.138), channel_id=1, source_target_pairs={{0,18},{2,20},{4,22},{6,24},{8,26},{10,28},{12,30},{14,16},{1,19},... | collective-permute-start | bytes 393224 | tf_op jit(solution)/shard_map/ppermute | solution.py:1178
  26.2 1.3 %collective-permute-start.4 = (bf16[4,64,256]{2,1,0:T(8,128)(2,1)}, bf16[4,64,256]{2,1,0:T(8,128)(2,1)S(1)}, u32[]{:S(2)}, u32[]{:S(2)}) collective-permute-start(bf16[4,64,256]{2,1,0:T(8,128)(2,1)} %get-tuple-element.139), channel_id=1, source_target_pairs={{2,16},{4,18},{6,20},{8,22},{10,24},{12,26},{14,28},{0,30},{3,17},... | collective-permute-start | bytes 393224 | tf_op jit(solution)/shard_map/ppermute | solution.py:1179
  27.5 10.1 %shard_map.188 = (bf16[4,64,256]{2,1,0:T(8,128)(2,1)}, bf16[4,64,256]{2,1,0:T(8,128)(2,1)}, bf16[4,64,256]{2,1,0:T(8,128)(2,1)}, bf16[64,256]{1,0:T(8,128)(2,1)}, bf16[8,2,256,128]{3,2,1,0:T(8,128)(2,1)}) custom-call(s32[4]{0:T(128)} %pad_add_fusion.args_0_, bf16[2,5,16,256]{3,2,1,0:T(8,128)(2,1)} %copy-done.6, bf16[2,5,16,256]{3,2,1,0:T(8,128)(2,1)} %copy-done.9, ...), custom_call_target="tpu_custom_call" | custom-call | tf_op jit(solution)/shard_map/pallas_call | solution.py:666
  37.6 0.8 copy-done.4
  38.5 0.9 copy-done.7
  39.4 0.9 copy-done.10
  40.2 0.7 copy-done.19
  40.9 0.5 shard_map.189
  41.5 1.3 %collective-permute-start.10 = (bf16[4,64,256]{2,1,0:T(8,128)(2,1)}, bf16[4,64,256]{2,1,0:T(8,128)(2,1)S(1)}, u32[]{:S(2)}, u32[]{:S(2)}) collective-permute-start(bf16[4,64,256]{2,1,0:T(8,128)(2,1)} %get-tuple-element.163), channel_id=1, source_target_pairs={{2,16},{4,18},{6,20},{8,22},{10,24},{12,26},{14,28},{0,30},{3,17},... | collective-permute-start | bytes 393224 | tf_op jit(solution)/shard_map/ppermute | solution.py:1179
  42.8 1.3 %collective-permute-start.8 = (bf16[4,64,256]{2,1,0:T(8,128)(2,1)}, bf16[4,64,256]{2,1,0:T(8,128)(2,1)S(1)}, u32[]{:S(2)}, u32[]{:S(2)}) collective-permute-start(bf16[4,64,256]{2,1,0:T(8,128)(2,1)} %get-tuple-element.161.args_6_), channel_id=1, source_target_pairs={{0,16},{2,18},{4,20},{6,22},{8,24},{10,26},{12,28},{14,30},{1,17},... | collective-permute-start | bytes 393224 | tf_op jit(solution)/shard_map/ppermute | solution.py:1177
  44.1 1.3 %collective-permute-start.9 = (bf16[4,64,256]{2,1,0:T(8,128)(2,1)}, bf16[4,64,256]{2,1,0:T(8,128)(2,1)S(1)}, u32[]{:S(2)}, u32[]{:S(2)}) collective-permute-start(bf16[4,64,256]{2,1,0:T(8,128)(2,1)} %get-tuple-element.162), channel_id=1, source_target_pairs={{0,18},{2,20},{4,22},{6,24},{8,26},{10,28},{12,30},{14,16},{1,19},... | collective-permute-start | bytes 393224 | tf_op jit(solution)/shard_map/ppermute | solution.py:1178
  45.4 0.0 collective-permute-done.3.args_13_
  45.4 0.0 collective-permute-done.4.args_14_
  45.5 0.0 copy-start.8
  45.5 0.0 copy-start.11
  45.5 0.6 shard_map.191
  46.1 1.3 %collective-permute-start.5 = (bf16[4,64,256]{2,1,0:T(8,128)(2,1)S(1)}, bf16[4,64,256]{2,1,0:T(8,128)(2,1)S(1)}, u32[]{:S(2)}, u32[]{:S(2)}) collective-permute-start(bf16[4,64,256]{2,1,0:T(8,128)(2,1)S(1)} %get-tuple-element.152), channel_id=1, source_target_pairs={{16,0},{18,2},{20,4},{22,6},{24,8},{26,10},{28,12},{30,14},{17,1},... | collective-permute-start | bytes 393224 | tf_op jit(solution)/shard_map/ppermute | solution.py:1222
  47.4 1.3 %collective-permute-start.6 = (bf16[4,16,256]{2,1,0:T(8,128)(2,1)S(1)}, bf16[4,16,256]{2,1,0:T(8,128)(2,1)S(1)}, u32[]{:S(2)}, u32[]{:S(2)}) collective-permute-start(bf16[4,16,256]{2,1,0:T(8,128)(2,1)S(1)} %get-tuple-element.153.args_24_), channel_id=1, source_target_pairs={{16,2},{18,4},{20,6},{22,8},{24,10},{26,12},{28,14},{30,0},{17,3},... | collective-permute-start | bytes 98312 | tf_op jit(solution)/shard_map/ppermute | solution.py:1223
  48.7 0.0 collective-permute-done.10.args_14_
  48.7 1.3 %collective-permute-start.7 = (bf16[4,16,256]{2,1,0:T(8,128)(2,1)S(1)}, bf16[4,16,256]{2,1,0:T(8,128)(2,1)S(1)}, u32[]{:S(2)}, u32[]{:S(2)}) collective-permute-start(bf16[4,16,256]{2,1,0:T(8,128)(2,1)S(1)} %get-tuple-element.154.args_23_), channel_id=1, source_target_pairs={{18,0},{20,2},{22,4},{24,6},{26,8},{28,10},{30,12},{16,14},{19,1},... | collective-permute-start | bytes 98312 | tf_op jit(solution)/shard_map/ppermute | solution.py:1224
  50.0 8.0 %shard_map.192 = (f32[10,8,256]{2,1,0:T(8,128)S(1)}, bf16[8,32,256]{2,1,0:T(8,128)(2,1)S(1)}, bf16[8,256,128]{2,1,0:T(8,128)(2,1)S(1)}, bf16[8,192,256]{2,1,0:T(...) custom-call(s32[4]{0:T(128)S(1)} %copy-done.20, ...), custom_call_target="tpu_custom_call" | custom-call | tf_op jit(solution)/shard_map/pallas_call | solution.py:666
  58.0 0.0 collective-permute-done.8.args_12_
  58.1 0.0 collective-permute-done.9.args_13_
  58.1 0.0 copy-start.3
  58.1 0.7 shard_map.193
  58.9 1.3 %collective-permute-start.11 = (bf16[4,64,256]{2,1,0:T(8,128)(2,1)S(1)}, bf16[4,64,256]{2,1,0:T(8,128)(2,1)S(1)}, u32[]{:S(2)}, u32[]{:S(2)}) collective-permute-start(bf16[4,64,256]{2,1,0:T(8,128)(2,1)S(1)} %get-tuple-element.184), channel_id=1, source_target_pairs={{16,0},{18,2},{20,4},{22,6},{24,8},{26,10},{28,12},{30,14},{17,1},... | collective-permute-start | bytes 393224 | tf_op jit(solution)/shard_map/ppermute | solution.py:1222
  60.2 1.3 %collective-permute-start.12 = (bf16[4,16,256]{2,1,0:T(8,128)(2,1)S(1)}, bf16[4,16,256]{2,1,0:T(8,128)(2,1)S(1)}, u32[]{:S(2)}, u32[]{:S(2)}) collective-permute-start(bf16[4,16,256]{2,1,0:T(8,128)(2,1)S(1)} %get-tuple-element.185.args_27_), channel_id=1, source_target_pairs={{16,2},{18,4},{20,6},{22,8},{24,10},{26,12},{28,14},{30,0},{17,3},... | collective-permute-start | bytes 98312 | tf_op jit(solution)/shard_map/ppermute | solution.py:1223
  61.5 1.3 %collective-permute-start.13 = (bf16[4,16,256]{2,1,0:T(8,128)(2,1)S(1)}, bf16[4,16,256]{2,1,0:T(8,128)(2,1)S(1)}, u32[]{:S(2)}, u32[]{:S(2)}) collective-permute-start(bf16[4,16,256]{2,1,0:T(8,128)(2,1)S(1)} %get-tuple-element.186.args_26_), channel_id=1, source_target_pairs={{18,0},{20,2},{22,4},{24,6},{26,8},{28,10},{30,12},{16,14},{19,1},... | collective-permute-start | bytes 98312 | tf_op jit(solution)/shard_map/ppermute | solution.py:1224
  62.8 10.5 %shard_map.194 = (f32[4,64,256]{2,1,0:T(8,128)S(1)}, bf16[4,64,256]{2,1,0:T(8,128)(2,1)}, bf16[4,16,256]{2,1,0:T(8,128)(2,1)S(1)}, bf16[4,16,256]{2,1,0:T(8,128)...) custom-call(s32[4]{0:T(128)S(1)} %copy-done.20, ...), custom_call_target="tpu_custom_call" | custom-call | tf_op jit(solution)/shard_map/pallas_call | solution.py:666
  73.3 2.4 %collective-permute-done.12.args_18_ = bf16[4,16,256]{2,1,0:T(8,128)(2,1)S(1)} collective-permute-done((bf16[4,16,256]{2,1,0:T(8,128)(2,1)S(1)}, bf16[4,16,256]{2,1,0:T(8,128)(2,1)S(1)}, u32[]{:S(2)}, u32[]{:S(2)}) %collective-permute-start.12) | collective-permute-done | bytes 32800 | tf_op jit(solution)/shard_map/ppermute | solution.py:1223
  75.7 10.5 %shard_map.195 = (f32[4,64,256]{2,1,0:T(8,128)S(1)}, bf16[4,64,256]{2,1,0:T(8,128)(2,1)}, bf16[4,16,256]{2,1,0:T(8,128)(2,1)}, bf16[4,16,256]{2,1,0:T(8,128)(2,1...) custom-call(s32[4]{0:T(128)S(1)} %copy-done.20, ...), custom_call_target="tpu_custom_call" | custom-call | tf_op jit(solution)/shard_map/pallas_call | solution.py:666
  86.2 1.5 %shard_map.196 = (bf16[8,384,128]{2,1,0:T(8,128)(2,1)S(1)}, f32[8,384,128]{2,1,0:T(8,128)S(1)}) custom-call(s32[4]{0:T(128)S(1)} %copy-done.20, bf16[384,256]{1,0:T(8,128)(2,1)S(1)} %get-tuple-element.170.args_1_, bf16[96,1280]{1,0:T(8,128)(2,1)S(1)} %get-tuple-element.171.args_2_, bf16[192,768]{1,0:T(8,128)(2,1)S(1)} %get-tuple-element.172.args_3_, ...), custom_call_target="tpu_custom_call" | custom-call | tf_op jit(solution)/shard_map/pallas_call | solution.py:666
  87.7 0.1 collective-permute-start.14
  87.8 0.1 collective-permute-start.15
  87.9 3.6 %collective-permute-done.15.args_6_ = f32[2,8,128]{2,1,0:T(8,128)S(1)} collective-permute-done((f32[2,8,128]{2,1,0:T(8,128)S(1)}, f32[2,8,128]{2,1,0:T(8,128)S(1)}, u32[]{:S(2)}, u32[]{:S(2)}) %collective-permute-start.15) | collective-permute-done | bytes 8224 | tf_op jit(solution)/shard_map/ppermute | solution.py:1239
  91.5 0.7 shard_map.197
  92.3 0.9 collective-permute-start.18
  93.2 1.7 %collective-permute-start.19 = (bf16[384,128]{1,0:T(8,128)(2,1)S(1)}, bf16[384,128]{1,0:T(8,128)(2,1)S(1)}, u32[]{:S(2)}, u32[]{:S(2)}) collective-permute-start(bf16[384,128]{1,0:T(8,128)(2,1)S(1)} %get-tuple-element.228), channel_id=1, source_target_pairs={{0,6},{2,8},{4,10},{6,12},{8,14},{10,0},{12,2},{14,4},{1,7},{3,9},... | collective-permute-start | bytes 294920 | tf_op jit(solution)/shard_map/ppermute | solution.py:1246
  94.9 1.3 %collective-permute-start.16 = (bf16[704,128]{1,0:T(8,128)(2,1)S(1)}, bf16[704,128]{1,0:T(8,128)(2,1)S(1)}, u32[]{:S(2)}, u32[]{:S(2)}) collective-permute-start(bf16[704,128]{1,0:T(8,128)(2,1)S(1)} %get-tuple-element.215), channel_id=1, source_target_pairs={{0,2},{2,4},{4,6},{6,8},{8,10},{10,12},{12,14},{14,0},{1,3},{3,5},... | collective-permute-start | bytes 540680 | tf_op jit(solution)/shard_map/ppermute | solution.py:1246
  96.2 3.4 %collective-permute-start.17 = (bf16[704,128]{1,0:T(8,128)(2,1)S(1)}, bf16[704,128]{1,0:T(8,128)(2,1)S(1)}, u32[]{:S(2)}, u32[]{:S(2)}) collective-permute-start(bf16[704,128]{1,0:T(8,128)(2,1)S(1)} %get-tuple-element.216), channel_id=1, source_target_pairs={{0,14},{2,0},{4,2},{6,4},{8,6},{10,8},{12,10},{14,12},{1,15},{3,1}... | collective-permute-start | bytes 540680 | tf_op jit(solution)/shard_map/ppermute | solution.py:1246
  99.6 1.2 %collective-permute-start.20 = (bf16[384,128]{1,0:T(8,128)(2,1)S(1)}, bf16[384,128]{1,0:T(8,128)(2,1)S(1)}, u32[]{:S(2)}, u32[]{:S(2)}) collective-permute-start(bf16[384,128]{1,0:T(8,128)(2,1)S(1)} %get-tuple-element.229), channel_id=1, source_target_pairs={{0,8},{2,10},{4,12},{6,14},{8,0},{10,2},{12,4},{14,6},{1,9},{3,11}... | collective-permute-start | bytes 294920 | tf_op jit(solution)/shard_map/ppermute | solution.py:1246
  100.8 1.8 %collective-permute-start.21 = (bf16[384,128]{1,0:T(8,128)(2,1)S(1)}, bf16[384,128]{1,0:T(8,128)(2,1)S(1)}, u32[]{:S(2)}, u32[]{:S(2)}) collective-permute-start(bf16[384,128]{1,0:T(8,128)(2,1)S(1)} %get-tuple-element.230), channel_id=1, source_target_pairs={{0,10},{2,12},{4,14},{6,0},{8,2},{10,4},{12,6},{14,8},{1,11},{3,13... | collective-permute-start | bytes 294920 | tf_op jit(solution)/shard_map/ppermute | solution.py:1246
  102.6 7.2 %collective-permute-done.19 = bf16[384,128]{1,0:T(8,128)(2,1)S(1)} collective-permute-done((bf16[384,128]{1,0:T(8,128)(2,1)S(1)}, bf16[384,128]{1,0:T(8,128)(2,1)S(1)}, u32[]{:S(2)}, u32[]{:S(2)}) %collective-permute-start.19) | collective-permute-done | bytes 98336 | tf_op jit(solution)/shard_map/ppermute | solution.py:1246
  109.9 2.8 %collective-permute-done.20 = bf16[384,128]{1,0:T(8,128)(2,1)S(1)} collective-permute-done((bf16[384,128]{1,0:T(8,128)(2,1)S(1)}, bf16[384,128]{1,0:T(8,128)(2,1)S(1)}, u32[]{:S(2)}, u32[]{:S(2)}) %collective-permute-start.20) | collective-permute-done | bytes 98336 | tf_op jit(solution)/shard_map/ppermute | solution.py:1246
  112.6 3.0 %collective-permute-done.22 = bf16[384,128]{1,0:T(8,128)(2,1)S(1)} collective-permute-done((bf16[384,128]{1,0:T(8,128)(2,1)S(1)}, bf16[384,128]{1,0:T(8,128)(2,1)S(1)}, u32[]{:S(2)}, u32[]{:S(2)}) %collective-permute-start.22) | collective-permute-done | bytes 98336 | tf_op jit(solution)/shard_map/ppermute | solution.py:1246
  115.7 0.1 convert_add_fusion.args_1_
  115.8 0.1 collective-permute-start.23
  115.9 1.5 %shard_map.198 = (bf16[1,2,1,4,64,256]{5,4,3,2,1,0:T(8,128)(2,1)}, f32[1,2,1,4,64,256]{5,4,3,2,1,0:T(8,128)}, f32[2,3,1,64]{3,2,1,0:T(1,128)}) custom-call(s32[4]{0:T(128)S(1)} %copy-done.20, bf16[704,128]{1,0:T(8,128)(2,1)S(1)} %collective-permute-done.16.args_1_, bf16[704,128]{1,0:T(8,128)(2,1)S(1)} %collective-permute-done.17.args_2_, ...), custom_call_target="tpu_custom_call" | custom-call | tf_op jit(solution)/shard_map/pallas_call | solution.py:666
  117.4 1.3 %shard_map.199 = (f32[1,32]{1,0:T(1,128)}, f32[1,32]{1,0:T(1,128)}, f32[1,160,256]{2,1,0:T(8,128)}, f32[1,96,256]{2,1,0:T(8,128)}, f32[1,32,128]{2,1,0:T(8,128)}, /*index=5*/f32[1,96,256]{2,1,0:T(8,128)}) custom-call(s32[4]{0:T(128)S(1)} %copy-done.20, f32[384,128]{1,0:T(8,128)S(1)} %convert_add_fusion.args_1_, f32[384,128]{1,0:T(8,128)S(1)} %collective-permute-done.23.args_2_), custom_call_target="tpu_custom_call" | custom-call | tf_op jit(solution)/shard_map/pallas_call | solution.py:666
  (47 shorter events, 0.1 us)
Async XLA Ops:
  0.6 37.0 %copy-start.21 = (f32[2,1,3,64]{3,1,2,0:T(1,128)S(1)}, f32[2,1,3,64]{3,1,2,0:T(1,128)}, u32[]{:S(2)}) copy-start(f32[2,1,3,64]{3,1,2,0:T(1,128)} %param.13) | copy-start | bytes 4612
  0.7 44.8 %copy-start = (bf16[1,256,1280]{2,1,0:T(8,128)(2,1)S(1)}, bf16[1,256,1280]{2,1,0:T(8,128)(2,1)}, u32[]{:S(2)}) copy-start(bf16[1,256,1280]{2,1,0:T(8,128)(2,1)} %args_2_.12) | copy-start | bytes 1966084
  0.7 44.8 %copy-start.1 = (bf16[1,256,768]{2,1,0:T(8,128)(2,1)S(1)}, bf16[1,256,768]{2,1,0:T(8,128)(2,1)}, u32[]{:S(2)}) copy-start(bf16[1,256,768]{2,1,0:T(8,128)(2,1)} %args_3_.12) | copy-start | bytes 1179652
  0.7 44.8 %copy-start.2 = (bf16[1,256,768]{2,1,0:T(8,128)(2,1)S(1)}, bf16[1,256,768]{2,1,0:T(8,128)(2,1)}, u32[]{:S(2)}) copy-start(bf16[1,256,768]{2,1,0:T(8,128)(2,1)} %args_5_.12) | copy-start | bytes 1179652
  0.7 44.8 %copy-start.15 = (bf16[2,1,4,64,256]{4,3,2,1,0:T(8,128)(2,1)S(1)}, bf16[2,1,4,64,256]{4,3,2,1,0:T(8,128)(2,1)}, u32[]{:S(2)}) copy-start(bf16[2,1,4,64,256]{4,3,2,1,0:T(8,128)(2,1)} %args_15_.3) | copy-start | bytes 786436
  3.4 34.2 %copy-start.12 = (s32[2,104,64]{2,1,0:T(8,128)S(1)}, s32[2,104,64]{2,1,0:T(8,128)}, u32[]{:S(2)}) copy-start(s32[2,104,64]{2,1,0:T(8,128)} %get-tuple-element.141.args_4_) | copy-start | bytes 159748
  3.4 42.0 %copy-start.5 = (bf16[32,1024]{1,0:T(8,128)(2,1)S(1)}, bf16[32,1024]{1,0:T(8,128)(2,1)}, u32[]{:S(2)}) copy-start(bf16[32,1024]{1,0:T(8,128)(2,1)} %get-tuple-element.125.args_5_.args_4_) | copy-start | bytes 196612
  3.4 42.0 %copy-start.16 = (f32[8,256]{1,0:T(8,128)S(1)}, f32[8,256]{1,0:T(8,128)}, u32[]{:S(2)}) copy-start(f32[8,256]{1,0:T(8,128)} %get-tuple-element.124.args_7_.args_1_) | copy-start | bytes 24580
  3.4 8.8 %collective-permute-start = (bf16[2,5,16,256]{3,2,1,0:T(8,128)(2,1)}, bf16[2,5,16,256]{3,2,1,0:T(8,128)(2,1)S(1)}, u32[]{:S(2)}, u32[]{:S(2)}) collective-permute-start(bf16[2,5,16,256]{3,2,1,0:T(8,128)(2,1)} %get-tuple-element.126), channel_id=1, source_target_pairs={{0,2},{2,4},{4,6},{6,8},{8,10},{10,12},{12,14},{14,0},{1,3},{3,5},... | collective-permute-start | bytes 245768 | tf_op jit(solution)/shard_map/ppermute | solution.py:1141
  6.5 6.4 %collective-permute-start.1 = (bf16[2,5,16,256]{3,2,1,0:T(8,128)(2,1)}, bf16[2,5,16,256]{3,2,1,0:T(8,128)(2,1)S(1)}, u32[]{:S(2)}, u32[]{:S(2)}) collective-permute-start(bf16[2,5,16,256]{3,2,1,0:T(8,128)(2,1)} %get-tuple-element.127), channel_id=1, source_target_pairs={{2,0},{4,2},{6,4},{8,6},{10,8},{12,10},{14,12},{0,14},{3,1},{5,3},... | collective-permute-start | bytes 245768 | tf_op jit(solution)/shard_map/ppermute | solution.py:1142
  10.2 35.3 %copy-start.20 = (s32[4]{0:T(128)S(1)}, s32[4]{0:T(128)}, u32[]{:S(2)}) copy-start(s32[4]{0:T(128)} %pad_add_fusion.args_0_) | copy-start | bytes 52
  12.3 0.6 copy-start.6
  12.9 0.6 copy-start.9
  23.6 20.5 %collective-permute-start.2 = (bf16[4,64,256]{2,1,0:T(8,128)(2,1)}, bf16[4,64,256]{2,1,0:T(8,128)(2,1)S(1)}, u32[]{:S(2)}, u32[]{:S(2)}) collective-permute-start(bf16[4,64,256]{2,1,0:T(8,128)(2,1)} %get-tuple-element.137.args_4_), channel_id=1, source_target_pairs={{0,16},{2,18},{4,20},{6,22},{8,24},{10,26},{12,28},{14,30},{1,17},... | collective-permute-start | bytes 393224 | tf_op jit(solution)/shard_map/ppermute | solution.py:1177
  24.9 20.5 %collective-permute-start.3 = (bf16[4,64,256]{2,1,0:T(8,128)(2,1)}, bf16[4,64,256]{2,1,0:T(8,128)(2,1)S(1)}, u32[]{:S(2)}, u32[]{:S(2)}) collective-permute-start(bf16[4,64,256]{2,1,0:T(8,128)(2,1)} %get-tuple-element.138), channel_id=1, source_target_pairs={{0,18},{2,20},{4,22},{6,24},{8,26},{10,28},{12,30},{14,16},{1,19},... | collective-permute-start | bytes 393224 | tf_op jit(solution)/shard_map/ppermute | solution.py:1178
  26.2 19.2 %collective-permute-start.4 = (bf16[4,64,256]{2,1,0:T(8,128)(2,1)}, bf16[4,64,256]{2,1,0:T(8,128)(2,1)S(1)}, u32[]{:S(2)}, u32[]{:S(2)}) collective-permute-start(bf16[4,64,256]{2,1,0:T(8,128)(2,1)} %get-tuple-element.139), channel_id=1, source_target_pairs={{2,16},{4,18},{6,20},{8,22},{10,24},{12,26},{14,28},{0,30},{3,17},... | collective-permute-start | bytes 393224 | tf_op jit(solution)/shard_map/ppermute | solution.py:1179
  37.6 0.8 copy-start.4
  38.5 0.9 copy-start.7
  39.4 0.9 copy-start.10
  40.2 0.7 copy-start.19
  41.5 7.2 %collective-permute-start.10 = (bf16[4,64,256]{2,1,0:T(8,128)(2,1)}, bf16[4,64,256]{2,1,0:T(8,128)(2,1)S(1)}, u32[]{:S(2)}, u32[]{:S(2)}) collective-permute-start(bf16[4,64,256]{2,1,0:T(8,128)(2,1)} %get-tuple-element.163), channel_id=1, source_target_pairs={{2,16},{4,18},{6,20},{8,22},{10,24},{12,26},{14,28},{0,30},{3,17},... | collective-permute-start | bytes 393224 | tf_op jit(solution)/shard_map/ppermute | solution.py:1179
  42.8 15.3 %collective-permute-start.8 = (bf16[4,64,256]{2,1,0:T(8,128)(2,1)}, bf16[4,64,256]{2,1,0:T(8,128)(2,1)S(1)}, u32[]{:S(2)}, u32[]{:S(2)}) collective-permute-start(bf16[4,64,256]{2,1,0:T(8,128)(2,1)} %get-tuple-element.161.args_6_), channel_id=1, source_target_pairs={{0,16},{2,18},{4,20},{6,22},{8,24},{10,26},{12,28},{14,30},{1,17},... | collective-permute-start | bytes 393224 | tf_op jit(solution)/shard_map/ppermute | solution.py:1177
  44.1 14.0 %collective-permute-start.9 = (bf16[4,64,256]{2,1,0:T(8,128)(2,1)}, bf16[4,64,256]{2,1,0:T(8,128)(2,1)S(1)}, u32[]{:S(2)}, u32[]{:S(2)}) collective-permute-start(bf16[4,64,256]{2,1,0:T(8,128)(2,1)} %get-tuple-element.162), channel_id=1, source_target_pairs={{0,18},{2,20},{4,22},{6,24},{8,26},{10,28},{12,30},{14,16},{1,19},... | collective-permute-start | bytes 393224 | tf_op jit(solution)/shard_map/ppermute | solution.py:1178
  45.5 4.5 %copy-start.8 = (bf16[2,5,16,256]{3,2,1,0:T(8,128)(2,1)S(1)}, bf16[2,5,16,256]{3,2,1,0:T(8,128)(2,1)}, u32[]{:S(2)}) copy-start(bf16[2,5,16,256]{3,2,1,0:T(8,128)(2,1)} %copy-done.6) | copy-start | bytes 245764
  45.5 4.5 %copy-start.11 = (bf16[2,5,16,256]{3,2,1,0:T(8,128)(2,1)S(1)}, bf16[2,5,16,256]{3,2,1,0:T(8,128)(2,1)}, u32[]{:S(2)}) copy-start(bf16[2,5,16,256]{3,2,1,0:T(8,128)(2,1)} %copy-done.9) | copy-start | bytes 245764
  46.1 12.8 %collective-permute-start.5 = (bf16[4,64,256]{2,1,0:T(8,128)(2,1)S(1)}, bf16[4,64,256]{2,1,0:T(8,128)(2,1)S(1)}, u32[]{:S(2)}, u32[]{:S(2)}) collective-permute-start(bf16[4,64,256]{2,1,0:T(8,128)(2,1)S(1)} %get-tuple-element.152), channel_id=1, source_target_pairs={{16,0},{18,2},{20,4},{22,6},{24,8},{26,10},{28,12},{30,14},{17,1},... | collective-permute-start | bytes 393224 | tf_op jit(solution)/shard_map/ppermute | solution.py:1222
  47.4 11.5 %collective-permute-start.6 = (bf16[4,16,256]{2,1,0:T(8,128)(2,1)S(1)}, bf16[4,16,256]{2,1,0:T(8,128)(2,1)S(1)}, u32[]{:S(2)}, u32[]{:S(2)}) collective-permute-start(bf16[4,16,256]{2,1,0:T(8,128)(2,1)S(1)} %get-tuple-element.153.args_24_), channel_id=1, source_target_pairs={{16,2},{18,4},{20,6},{22,8},{24,10},{26,12},{28,14},{30,0},{17,3},... | collective-permute-start | bytes 98312 | tf_op jit(solution)/shard_map/ppermute | solution.py:1223
  48.7 10.2 %collective-permute-start.7 = (bf16[4,16,256]{2,1,0:T(8,128)(2,1)S(1)}, bf16[4,16,256]{2,1,0:T(8,128)(2,1)S(1)}, u32[]{:S(2)}, u32[]{:S(2)}) collective-permute-start(bf16[4,16,256]{2,1,0:T(8,128)(2,1)S(1)} %get-tuple-element.154.args_23_), channel_id=1, source_target_pairs={{18,0},{20,2},{22,4},{24,6},{26,8},{28,10},{30,12},{16,14},{19,1},... | collective-permute-start | bytes 98312 | tf_op jit(solution)/shard_map/ppermute | solution.py:1224
  58.1 4.7 %copy-start.3 = (bf16[2,1,4,64,256]{4,3,2,1,0:T(8,128)(2,1)S(1)}, bf16[2,1,4,64,256]{4,3,2,1,0:T(8,128)(2,1)}, u32[]{:S(2)}) copy-start(bf16[2,1,4,64,256]{4,3,2,1,0:T(8,128)(2,1)} %args_14_.3) | copy-start | bytes 786436
  58.1 4.7 %copy-start.14 = (bf16[8,2,256,128]{3,2,1,0:T(8,128)(2,1)S(1)}, bf16[8,2,256,128]{3,2,1,0:T(8,128)(2,1)}, u32[]{:S(2)}) copy-start(bf16[8,2,256,128]{3,2,1,0:T(8,128)(2,1)} %get-tuple-element.151.args_16_) | copy-start | bytes 3145732
  58.1 4.7 %copy-start.23 = (bf16[64,256]{1,0:T(8,128)(2,1)S(1)}, bf16[64,256]{1,0:T(8,128)(2,1)}, u32[]{:S(2)}) copy-start(bf16[64,256]{1,0:T(8,128)(2,1)} %get-tuple-element.150.args_15_) | copy-start | bytes 98308
  58.9 16.8 %collective-permute-start.11 = (bf16[4,64,256]{2,1,0:T(8,128)(2,1)S(1)}, bf16[4,64,256]{2,1,0:T(8,128)(2,1)S(1)}, u32[]{:S(2)}, u32[]{:S(2)}) collective-permute-start(bf16[4,64,256]{2,1,0:T(8,128)(2,1)S(1)} %get-tuple-element.184), channel_id=1, source_target_pairs={{16,0},{18,2},{20,4},{22,6},{24,8},{26,10},{28,12},{30,14},{17,1},... | collective-permute-start | bytes 393224 | tf_op jit(solution)/shard_map/ppermute | solution.py:1222
  60.2 15.5 %collective-permute-start.12 = (bf16[4,16,256]{2,1,0:T(8,128)(2,1)S(1)}, bf16[4,16,256]{2,1,0:T(8,128)(2,1)S(1)}, u32[]{:S(2)}, u32[]{:S(2)}) collective-permute-start(bf16[4,16,256]{2,1,0:T(8,128)(2,1)S(1)} %get-tuple-element.185.args_27_), channel_id=1, source_target_pairs={{16,2},{18,4},{20,6},{22,8},{24,10},{26,12},{28,14},{30,0},{17,3},... | collective-permute-start | bytes 98312 | tf_op jit(solution)/shard_map/ppermute | solution.py:1223
  61.5 14.2 %collective-permute-start.13 = (bf16[4,16,256]{2,1,0:T(8,128)(2,1)S(1)}, bf16[4,16,256]{2,1,0:T(8,128)(2,1)S(1)}, u32[]{:S(2)}, u32[]{:S(2)}) collective-permute-start(bf16[4,16,256]{2,1,0:T(8,128)(2,1)S(1)} %get-tuple-element.186.args_26_), channel_id=1, source_target_pairs={{18,0},{20,2},{22,4},{24,6},{26,8},{28,10},{30,12},{16,14},{19,1},... | collective-permute-start | bytes 98312 | tf_op jit(solution)/shard_map/ppermute | solution.py:1224
  62.8 12.9 %copy-start.13 = (bf16[8,2,256,128]{3,2,1,0:T(8,128)(2,1)S(1)}, bf16[8,2,256,128]{3,2,1,0:T(8,128)(2,1)}, u32[]{:S(2)}) copy-start(bf16[8,2,256,128]{3,2,1,0:T(8,128)(2,1)} %get-tuple-element.183.args_16_) | copy-start | bytes 3145732
  62.8 12.9 %copy-start.22 = (bf16[64,256]{1,0:T(8,128)(2,1)S(1)}, bf16[64,256]{1,0:T(8,128)(2,1)}, u32[]{:S(2)}) copy-start(bf16[64,256]{1,0:T(8,128)(2,1)} %get-tuple-element.182.args_15_) | copy-start | bytes 98308
  86.2 29.6 %copy-start.17 = (bf16[4,64,256]{2,1,0:T(8,128)(2,1)S(1)}, bf16[4,64,256]{2,1,0:T(8,128)(2,1)}, u32[]{:S(2)}) copy-start(bf16[4,64,256]{2,1,0:T(8,128)(2,1)} %get-tuple-element.137.args_4_) | copy-start | bytes 393220
  86.2 29.7 %copy-start.18 = (bf16[4,64,256]{2,1,0:T(8,128)(2,1)S(1)}, bf16[4,64,256]{2,1,0:T(8,128)(2,1)}, u32[]{:S(2)}) copy-start(bf16[4,64,256]{2,1,0:T(8,128)(2,1)} %get-tuple-element.161.args_6_) | copy-start | bytes 393220
  87.7 3.8 %collective-permute-start.14 = (bf16[8,384,128]{2,1,0:T(8,128)(2,1)S(1)}, bf16[8,384,128]{2,1,0:T(8,128)(2,1)S(1)}, u32[]{:S(2)}, u32[]{:S(2)}) collective-permute-start(bf16[8,384,128]{2,1,0:T(8,128)(2,1)S(1)} %get-tuple-element.211), channel_id=1, source_target_pairs={{0,1},{1,0},{2,3},{3,2},{4,5},{5,4},{6,7},{7,6},{8,9},{9,8},{10,11... | collective-permute-start | bytes 2359304 | tf_op jit(solution)/shard_map/ppermute | solution.py:1241
  87.8 3.7 %collective-permute-start.15 = (f32[2,8,128]{2,1,0:T(8,128)S(1)}, f32[2,8,128]{2,1,0:T(8,128)S(1)}, u32[]{:S(2)}, u32[]{:S(2)}) collective-permute-start(f32[2,8,128]{2,1,0:T(8,128)S(1)} %get-tuple-element.214.args_5_), channel_id=1, source_target_pairs={{0,16},{16,0},{1,17},{17,1},{2,18},{18,2},{3,19},{19,3},{4,20},{20... | collective-permute-start | bytes 24584 | tf_op jit(solution)/shard_map/ppermute | solution.py:1239
  92.3 8.6 %collective-permute-start.18 = (bf16[384,128]{1,0:T(8,128)(2,1)S(1)}, bf16[384,128]{1,0:T(8,128)(2,1)S(1)}, u32[]{:S(2)}, u32[]{:S(2)}) collective-permute-start(bf16[384,128]{1,0:T(8,128)(2,1)S(1)} %get-tuple-element.227), channel_id=1, source_target_pairs={{0,4},{2,6},{4,8},{6,10},{8,12},{10,14},{12,0},{14,2},{1,5},{3,7},... | collective-permute-start | bytes 294920 | tf_op jit(solution)/shard_map/ppermute | solution.py:1246
  93.2 16.7 %collective-permute-start.19 = (bf16[384,128]{1,0:T(8,128)(2,1)S(1)}, bf16[384,128]{1,0:T(8,128)(2,1)S(1)}, u32[]{:S(2)}, u32[]{:S(2)}) collective-permute-start(bf16[384,128]{1,0:T(8,128)(2,1)S(1)} %get-tuple-element.228), channel_id=1, source_target_pairs={{0,6},{2,8},{4,10},{6,12},{8,14},{10,0},{12,2},{14,4},{1,7},{3,9},... | collective-permute-start | bytes 294920 | tf_op jit(solution)/shard_map/ppermute | solution.py:1246
  94.9 20.8 %collective-permute-start.16 = (bf16[704,128]{1,0:T(8,128)(2,1)S(1)}, bf16[704,128]{1,0:T(8,128)(2,1)S(1)}, u32[]{:S(2)}, u32[]{:S(2)}) collective-permute-start(bf16[704,128]{1,0:T(8,128)(2,1)S(1)} %get-tuple-element.215), channel_id=1, source_target_pairs={{0,2},{2,4},{4,6},{6,8},{8,10},{10,12},{12,14},{14,0},{1,3},{3,5},... | collective-permute-start | bytes 540680 | tf_op jit(solution)/shard_map/ppermute | solution.py:1246
  96.2 19.4 %collective-permute-start.17 = (bf16[704,128]{1,0:T(8,128)(2,1)S(1)}, bf16[704,128]{1,0:T(8,128)(2,1)S(1)}, u32[]{:S(2)}, u32[]{:S(2)}) collective-permute-start(bf16[704,128]{1,0:T(8,128)(2,1)S(1)} %get-tuple-element.216), channel_id=1, source_target_pairs={{0,14},{2,0},{4,2},{6,4},{8,6},{10,8},{12,10},{14,12},{1,15},{3,1}... | collective-permute-start | bytes 540680 | tf_op jit(solution)/shard_map/ppermute | solution.py:1246
  99.6 13.0 %collective-permute-start.20 = (bf16[384,128]{1,0:T(8,128)(2,1)S(1)}, bf16[384,128]{1,0:T(8,128)(2,1)S(1)}, u32[]{:S(2)}, u32[]{:S(2)}) collective-permute-start(bf16[384,128]{1,0:T(8,128)(2,1)S(1)} %get-tuple-element.229), channel_id=1, source_target_pairs={{0,8},{2,10},{4,12},{6,14},{8,0},{10,2},{12,4},{14,6},{1,9},{3,11}... | collective-permute-start | bytes 294920 | tf_op jit(solution)/shard_map/ppermute | solution.py:1246
  100.8 11.8 %collective-permute-start.21 = (bf16[384,128]{1,0:T(8,128)(2,1)S(1)}, bf16[384,128]{1,0:T(8,128)(2,1)S(1)}, u32[]{:S(2)}, u32[]{:S(2)}) collective-permute-start(bf16[384,128]{1,0:T(8,128)(2,1)S(1)} %get-tuple-element.230), channel_id=1, source_target_pairs={{0,10},{2,12},{4,14},{6,0},{8,2},{10,4},{12,6},{14,8},{1,11},{3,13... | collective-permute-start | bytes 294920 | tf_op jit(solution)/shard_map/ppermute | solution.py:1246
  109.9 5.8 %collective-permute-start.22 = (bf16[384,128]{1,0:T(8,128)(2,1)S(1)}, bf16[384,128]{1,0:T(8,128)(2,1)S(1)}, u32[]{:S(2)}, u32[]{:S(2)}) collective-permute-start(bf16[384,128]{1,0:T(8,128)(2,1)S(1)} %get-tuple-element.231), channel_id=1, source_target_pairs={{0,12},{2,14},{4,0},{6,2},{8,4},{10,6},{12,8},{14,10},{1,13},{3,15... | collective-permute-start | bytes 294920 | tf_op jit(solution)/shard_map/ppermute | solution.py:1246
  115.8 1.6 %collective-permute-start.23 = (f32[384,128]{1,0:T(8,128)S(1)}, f32[384,128]{1,0:T(8,128)S(1)}, u32[]{:S(2)}, u32[]{:S(2)}) collective-permute-start(f32[384,128]{1,0:T(8,128)S(1)} %convert_add_fusion.args_1_), channel_id=1, source_target_pairs={{0,1},{1,0},{2,3},{3,2},{4,5},{5,4},{6,7},{7,6},{8,9},{9,8},{10,11... | collective-permute-start | bytes 589832 | tf_op jit(solution)/shard_map/ppermute | solution.py:1260

commit v3 on v2

--- a/solution.py
+++ b/solution.py
@@ -21,7 +21,6 @@
 F32 = jnp.float32
 BF16 = jnp.bfloat16
 VMEM = pl.BlockSpec(memory_space=pltpu.VMEM)
-SMEM = pl.BlockSpec(memory_space=pltpu.SMEM)
 HBM = pl.BlockSpec(memory_space=pltpu.HBM)
 
 
@@ -58,7 +57,7 @@
         self.edges = GROUP * atoms
         self.halves = width // LANES
         self.window = atoms + SUBLANES
-        self.sent = atoms
+        self.sent = (self.halo, atoms)
         self.widths = (5 * width // space, 3 * width // space, 3 * width // space)
         self.spare = sum(self.widths)
         self.packed = -(-(self.spare + basis) // 16) * 16
@@ -83,21 +82,21 @@
     ref[...] = low_end * (1.0 - step) + step
 
 
-def edge_geometry(r, sz, m, coords, slots):
+def edge_geometry(r, sz, coords, slots, low, high):
     A, H, E, EB, K = sz.atoms, sz.halo, sz.rows, sz.edges, sz.slots
     lane = iota((8, LANES), 1)
     row = iota((8, LANES), 0)
-    slab, last = r.scal[1], r.scal[3]
+    slab, last = lax.axis_index("space"), sz.space - 1
     spot = iota((1, LANES), 1)
-    length_x = (last + 1).astype(F32) * (A * 4.0 / H)
+    length_x = sz.space * A * 4.0 / H
     places = []
     for c in range(3):
         places.append(
             jnp.concatenate(
                 [
-                    unpacked_places(r.pack_low[m, 4], c, H),
+                    unpacked_places(low[4], c, H),
                     coords[c],
-                    unpacked_places(r.pack_high[m, 4], c, H),
+                    unpacked_places(high[4], c, H),
                     jnp.zeros((1, LANES - E), F32),
                 ],
                 axis=1,
@@ -119,10 +118,11 @@
     wide_lane = iota((8, EB), 1)
     wide_row = iota((8, EB), 0)
     wanted = GROUP * wide_row + wide_lane // A + jnp.where(wide_row >= 4, 1, 0) + wide_lane % A
-    alive = iota((K, A), 0) < slots[3 * K : 3 * K + 1, :]
-    code = jnp.where(alive, 16, 0) + (slots[K : 2 * K, :] + 1) * 4 + (slots[2 * K : 3 * K, :] + 1)
+    table = slots[:, 0:A].astype(jnp.int32)
+    alive = iota((K, A), 0) < table[3 * K : 3 * K + 1]
+    code = jnp.where(alive, 16, 0) + (table[K : 2 * K] + 1) * 4 + (table[2 * K : 3 * K] + 1)
     code = jnp.concatenate([code] * GROUP, axis=1)
-    named = jnp.concatenate([slots[0:K, :]] * GROUP, axis=1)
+    named = jnp.concatenate([table[0:K]] * GROUP, axis=1)
     found = jnp.zeros((8, EB), jnp.int32)
     for n in range(K):
         found = found + jnp.where(named[n : n + 1, :] == wanted, code[n : n + 1, :], 0)
@@ -185,14 +185,14 @@
         ).astype(BF16)
 
 
-def node_part(r, sz, own, low, high, wqkv):
+def node_part(r, sz, own, low, high, norms, wqkv):
     A, H, E, F, CG = sz.atoms, sz.halo, sz.rows, sz.width, sz.halves
     halves = halves_of(sz)
     scalars = jnp.concatenate([low[0, 0:H], own[0], high[0, 0:H]], axis=0).astype(F32)
     centred = scalars - jnp.mean(scalars, axis=-1, keepdims=True)
     spread = jnp.mean(centred * centred, axis=-1, keepdims=True)
     scale = lax.rsqrt(spread + LN_EPS)
-    normed = (centred * scale * r.norms[0:1, :] + r.norms[1:2, :]).astype(BF16)
+    normed = (centred * scale * norms[0:1, :] + norms[1:2, :]).astype(BF16)
     left = r.left
     left[0:E, :] = normed
     left[E : E + 3 * A, :] = own[1:4].reshape(3 * A, F)
@@ -267,29 +267,40 @@
 def first_forward(r, sz, m, fetch):
     A, H, E, F, EB = sz.atoms, sz.halo, sz.rows, sz.width, sz.edges
     CG = sz.halves
-    moves = [
-        (r.coords.at[m], "s_coords"),
-        (r.slots.at[m], "s_slots"),
-        (r.features.at[m, 0], "s_own"),
-        (r.wqkv.at[0], "s_wqkv"),
-        (r.wh, "s_wh"),
-        (r.wvec.at[0], "s_wvec"),
-        (r.wout.at[0], "s_wout"),
-    ]
-    early = moves[:4]
-    copies = []
-    for i, (source, name) in enumerate(moves):
-        if fetch:
-            copies.append(pltpu.make_async_copy(source, getattr(r, name), r.sems.at[i]))
-            copies[-1].start()
-        else:
-            setattr(r, name, source)
+    r.s_low, r.s_high = r.pack_low.at[m], r.pack_high.at[m]
+    copies = early = []
+    if fetch:
+        rooms = Rooms(sz)
+        early = [
+            (r.wide.at[rooms.slots, 0:LANES], r.s_slots),
+            (r.wide.at[rooms.norms.start : rooms.coords.stop], r.s_norms),
+            (r.room.at[rooms.wqkv], r.s_wqkv),
+        ]
+        for index in range(4):
+            start = rooms.own.start + index * A
+            early.append((r.room.at[start : start + A, 0:F], r.s_own.at[index]))
+        late = [
+            (r.room.at[rooms.wh, 0 : 4 * F], r.s_wh),
+            (r.room.at[rooms.wvec, 0 : 3 * F], r.s_wvec),
+            (r.room.at[rooms.wout, 0 : 3 * F], r.s_wout),
+        ]
+        copies = [
+            pltpu.make_async_copy(source, target, r.sems.at[i])
+            for i, (source, target) in enumerate(early + late)
+        ]
+        for copy in copies:
+            copy.start()
+    else:
+        r.s_slots, r.s_norms, r.s_wh = r.slots.at[m], r.norms, r.wh
+        r.s_own, r.s_wqkv = r.features.at[m, 0], r.wqkv.at[0]
+        r.s_wvec, r.s_wout = r.wvec.at[0], r.wout.at[0]
     write_constants(r, sz)
     r.sagg[...] = jnp.zeros_like(r.sagg)
     r.vagg[...] = jnp.zeros_like(r.vagg)
     for copy in copies[: len(early)]:
         copy.wait()
-    edge_geometry(r, sz, m, r.s_coords, r.s_slots)
+    coords = [r.s_norms[8 + c : 9 + c, 0:A] if fetch else r.coords[m, c] for c in range(3)]
+    edge_geometry(r, sz, coords, r.s_slots, r.s_low, r.s_high)
 
     def tables(b, carry):
         write_edge_tables(r, sz, b, F32)
@@ -297,7 +308,7 @@
 
     lax.fori_loop(0, sz.blocks, tables, 0, unroll=2)
     own = r.s_own
-    node_part(r, sz, own, r.pack_low.at[m], r.pack_high.at[m], r.s_wqkv)
+    node_part(r, sz, own, r.s_low, r.s_high, r.s_norms, r.s_wqkv)
     for copy in copies[len(early) :]:
         copy.wait()
     r.vproj[...] = dot(r.left[E : E + 3 * A, :], r.s_wvec[...])
@@ -351,22 +362,6 @@
         for c in range(3)
     ]
     write_layer_output(r, sz, own, out_proj, vector_dot(r, sz), vector_agg)
-    if not fetch:
-        return
-    copies = [
-        pltpu.make_async_copy(source, target, r.sems.at[i])
-        for i, (source, target) in enumerate([
-            (r.fresh, r.out_fresh),
-            (r.head, r.out_head),
-            (r.tail, r.out_tail),
-            (r.o_scalar, r.out_scalar),
-            (r.score, r.out_score),
-        ])
-    ]
-    for copy in copies:
-        copy.start()
-    for copy in copies:
-        copy.wait()
 
 
 def edge_filters(r, sz, which):
@@ -375,7 +370,9 @@
     for m in which:
         w = SimpleNamespace(**vars(r))
         vars(w).update(vars(buffers(r, sz, m)))
-        edge_geometry(w, sz, m, r.coords.at[m], r.slots.at[m])
+        edge_geometry(
+            w, sz, r.coords.at[m], r.slots.at[m], r.pack_low.at[m], r.pack_high.at[m]
+        )
 
         def block(b, carry, w=w):
             write_edge_tables(w, sz, b, BF16)
@@ -407,7 +404,7 @@
         own, low, high = r.features.at[m, 0], r.pack_low.at[m], r.pack_high.at[m]
     wqkv, wvec, wout = r.wqkv.at[0], r.wvec.at[0], r.wout.at[0]
     write_constants(r, sz)
-    xhat, scale = node_part(r, sz, own, low, high, wqkv)
+    xhat, scale = node_part(r, sz, own, low, high, r.norms, wqkv)
     gain = r.norms[0:1, :]
     left = r.left
     vp = r.vproj
@@ -661,7 +658,7 @@
         if role is None:
             body(refs)
         else:
-            pl.when(refs.scal[0] == role)(lambda: body(refs))
+            pl.when(lax.axis_index("section") == role)(lambda: body(refs))
 
     results = pl.pallas_call(
         kernel,
@@ -676,29 +673,28 @@
     return SimpleNamespace(**dict(zip(outs, results, strict=True)))
 
 
-def first_call(sz, m, fetch, arrays):
+def first_call(sz, m, fetch, sent, arrays):
     A, H, E, F = sz.atoms, sz.halo, sz.rows, sz.width
     EB, CG, NB = sz.edges, sz.halves, sz.blocks
     shape = jax.ShapeDtypeStruct
     results = dict(
         fresh=((4, A, F), BF16),
-        head=((4, sz.sent, F), BF16),
-        tail=((4, sz.sent, F), BF16),
+        head=((4, sent, F), BF16),
+        tail=((4, sent, F), BF16),
         o_scalar=((A, F), BF16),
         score=((NB, CG, EB, LANES), BF16),
     )
     fetched = dict(
         s_own=((4, A, F), BF16),
-        s_coords=((3, 1, A), F32),
-        s_slots=((3 * sz.slots + 8, A), jnp.int32),
+        s_slots=((3 * sz.slots + 8, LANES), F32),
+        s_norms=((16, F), F32),
         s_wqkv=((F, 5 * F), BF16),
         s_wvec=((F, 3 * F), BF16),
         s_wh=((sz.basis, 4 * F), BF16),
         s_wout=((F, 3 * F), BF16),
-        sems=pltpu.SemaphoreType.DMA((9,)),
-    )
-    named = dict(fresh="out_fresh", head="out_head", tail="out_tail", o_scalar="out_scalar", score="out_score")
-    outs = SimpleNamespace(**{(named[k] if fetch else k): shape(*v) for k, v in results.items()})
+        sems=pltpu.SemaphoreType.DMA((10,)),
+    )
+    outs = SimpleNamespace(**{k: shape(*v) for k, v in results.items()})
     scratch = dict(
         left=((sz.factors, F), BF16),
         query=((CG, A, LANES), F32),
@@ -721,18 +717,10 @@
         third=((NB, EB, F), BF16),
     )
     if fetch:
-        scratch.update(results)
         scratch.update(fetched)
-    made = call(
-        lambda r: first_forward(r, sz, m, fetch),
-        arrays,
-        outs,
-        scratch,
-        FIRST,
-        grant_mb=54 if fetch else 20,
-        place=HBM if fetch else VMEM,
-    )
-    return SimpleNamespace(**{k: getattr(made, named[k] if fetch else k) for k in results})
+    return call(
+        lambda r: first_forward(r, sz, m, fetch), arrays, outs, scratch, FIRST, grant_mb=20
+    )
 
 
 def filter_call(sz, role, which, arrays):
@@ -826,18 +814,18 @@
             r.moved[i] = places[...]
 
     def body(r):
-        @pl.when(r.scal[0] == FIRST)
+        @pl.when(lax.axis_index("section") == FIRST)
         def _():
             both_ways(r, sz, m, fwd)
             hand_on(r, FIRST)
 
-        pl.when(r.scal[0] == SECOND)(lambda: hand_on(r, SECOND))
+        pl.when(lax.axis_index("section") == SECOND)(lambda: hand_on(r, SECOND))
 
     return call(body, arrays, outs, scratch)
 
 
-def border_call(sz, features, coords, neighbours, shifts, counts, gain, bias, filter_weight):
-    A, H, F, K = sz.atoms, sz.halo, sz.width, sz.slots
+def border_call(sz, features, coords):
+    A, H, F = sz.atoms, sz.halo, sz.width
     count = features.shape[0]
 
     def body(r):
@@ -846,9 +834,6 @@
             moves += [
                 (r.features.at[m, 0, :, A - H : A, :], r.up.at[m, 0:4]),
                 (r.features.at[m, 0, :, 0:H, :], r.down.at[m, 0:4]),
-                (r.nbr.at[m, 0], r.slots.at[m, 0:K]),
-                (r.shifts.at[m, 0, 0], r.slots.at[m, K : 2 * K]),
-                (r.shifts.at[m, 0, 1], r.slots.at[m, 2 * K : 3 * K]),
             ]
         copies = [
             pltpu.make_async_copy(source, target, r.sems.at[i])
@@ -856,12 +841,6 @@
         ]
         for copy in copies:
             copy.start()
-        r.wh[...] = (r.wfilt[0].astype(F32) * 0.5).astype(BF16)
-        r.norms[0:1, :] = r.gain[...].astype(F32)
-        r.norms[1:2, :] = r.bias[...].astype(F32)
-        r.norms[2:, :] = jnp.zeros((6, F), F32)
-        for m in range(count):
-            r.slots[m, 3 * K :, :] = jnp.broadcast_to(r.counts[m], (8, A))
         copies[0].wait()
         for m in range(count):
             r.up[m, 4] = packed_places([r.s_coords[m, c][:, A - H :] for c in range(3)], F)
@@ -869,7 +848,92 @@
         for copy in copies[1:]:
             copy.wait()
 
+    shape = jax.ShapeDtypeStruct((count, 5, H, F), BF16)
+    return call(
+        body,
+        SimpleNamespace(features=(features, HBM), coords=(coords, HBM)),
+        SimpleNamespace(up=shape, down=shape),
+        dict(s_coords=(coords.shape, F32), sems=pltpu.SemaphoreType.DMA((2 * count + 1,))),
+        grant_mb=54,
+    )
+
+
+class Rooms:
+    def __init__(self, sz):
+        F = sz.width
+        ends = [0]
+        for rows in (F, F, F, 4 * sz.atoms, sz.basis):
+            ends.append(ends[-1] + rows)
+        self.wqkv, self.wvec, self.wout, self.own, self.wh = [
+            slice(*pair) for pair in zip(ends, ends[1:])
+        ]
+        table = 3 * sz.slots + 8
+        self.slots, self.norms = slice(0, table), slice(table, table + 8)
+        self.coords = slice(table + 8, table + 16)
+        self.low_shape, self.wide_shape = (20480, 5 * F), (51200, F)
+
+
+def stage_call(sz, features, coords, neighbours, shifts, counts, gain, bias, filter_weight, weights):
+    A, F, K = sz.atoms, sz.width, sz.slots
+    count = features.shape[0]
+    rooms = Rooms(sz)
+
+    def body(r):
+        moves = [(r.coords, r.s_coords), (r.counts, r.s_counts)]
+        moves += [(r.gain, r.s_gain), (r.bias, r.s_bias), (r.wfilt.at[0], r.s_wfilt)]
+        for m in range(count):
+            moves += [
+                (r.nbr.at[m, 0], r.s_slots.at[m, 0:K]),
+                (r.shifts.at[m, 0, 0], r.s_slots.at[m, K : 2 * K]),
+                (r.shifts.at[m, 0, 1], r.s_slots.at[m, 2 * K : 3 * K]),
+            ]
+        near = len(moves)
+        moves += [(r.features.at[0, 0], r.s_own), (r.wqkv.at[0], r.s_wqkv)]
+        moves += [(r.wvec.at[0], r.s_wvec), (r.wout.at[0], r.s_wout)]
+        copies = [
+            pltpu.make_async_copy(source, target, r.sems.at[i])
+            for i, (source, target) in enumerate(moves)
+        ]
+        for copy in copies:
+            copy.start()
+        for copy in copies[:near]:
+            copy.wait()
+        r.s_wh[...] = (r.s_wfilt[...].astype(F32) * 0.5).astype(BF16)
+        for m in range(count):
+            r.s_table[m, 0 : 3 * K, 0:A] = r.s_slots[m].astype(F32)
+            r.s_table[m, 3 * K :, 0:A] = jnp.broadcast_to(r.s_counts[m].astype(F32), (8, A))
+        r.s_norms[...] = jnp.zeros_like(r.s_norms)
+        r.s_norms[0:1, :] = r.s_gain[...].astype(F32)
+        r.s_norms[1:2, :] = r.s_bias[...].astype(F32)
+        for c in range(3):
+            r.s_norms[8 + c : 9 + c, 0:A] = r.s_coords[0, c]
+        for copy in copies[near:]:
+            copy.wait()
+        moves = [
+            (r.s_table, r.slots),
+            (r.s_norms.at[0:8], r.norms),
+            (r.s_wh, r.wh),
+            (r.s_table.at[0], r.wide.at[rooms.slots, 0:LANES]),
+            (r.s_norms, r.wide.at[rooms.norms.start : rooms.coords.stop]),
+            (r.s_wqkv, r.low.at[rooms.wqkv]),
+            (r.s_wvec, r.low.at[rooms.wvec, 0 : 3 * F]),
+            (r.s_wout, r.low.at[rooms.wout, 0 : 3 * F]),
+            (r.s_wh, r.low.at[rooms.wh, 0 : 4 * F]),
+        ]
+        for index in range(4):
+            start = rooms.own.start + index * A
+            moves.append((r.s_own.at[index], r.low.at[start : start + A, 0:F]))
+        later = [
+            pltpu.make_async_copy(source, target, r.sems.at[len(copies) + i])
+            for i, (source, target) in enumerate(moves)
+        ]
+        for copy in later:
+            copy.start()
+        for copy in later:
+            copy.wait()
+
     shape = jax.ShapeDtypeStruct
+    wqkv, wvec, wout = weights
     return call(
         body,
         SimpleNamespace(
@@ -877,30 +941,49 @@
             coords=(coords, HBM),
             nbr=(neighbours, HBM),
             shifts=(shifts, HBM),
-            counts=(counts, VMEM),
-            gain=(gain, VMEM),
-            bias=(bias, VMEM),
-            wfilt=(filter_weight, VMEM),
+            counts=(counts, HBM),
+            gain=(gain, HBM),
+            bias=(bias, HBM),
+            wfilt=(filter_weight, HBM),
+            wqkv=(wqkv, HBM),
+            wvec=(wvec, HBM),
+            wout=(wout, HBM),
         ),
         SimpleNamespace(
-            up=shape((count, 5, H, F), BF16),
-            down=shape((count, 5, H, F), BF16),
-            slots=shape((count, 3 * K + 8, A), jnp.int32),
+            slots=shape((count, 3 * K + 8, LANES), F32),
             norms=shape((8, F), F32),
             wh=shape((sz.basis, 4 * F), BF16),
+            low=shape(rooms.low_shape, BF16),
+            wide=shape(rooms.wide_shape, F32),
         ),
-        dict(s_coords=(coords.shape, F32), sems=pltpu.SemaphoreType.DMA((5 * count + 1,))),
+        dict(
+            s_coords=(coords.shape, F32),
+            s_counts=(counts.shape, jnp.int32),
+            s_gain=(gain.shape, BF16),
+            s_bias=(bias.shape, BF16),
+            s_wfilt=(filter_weight.shape[1:], BF16),
+            s_slots=((count, 3 * K, A), jnp.int32),
+            s_own=((4, A, F), BF16),
+            s_wqkv=(wqkv.shape[1:], BF16),
+            s_wvec=(wvec.shape[1:], BF16),
+            s_wout=(wout.shape[1:], BF16),
+            s_wh=(filter_weight.shape[1:], BF16),
+            s_table=((count, 3 * K + 8, LANES), F32),
+            s_norms=((16, F), F32),
+            sems=pltpu.SemaphoreType.DMA((3 * count + 22,)),
+        ),
         grant_mb=54,
-    )
-
-
-def gradient_call(sz, scal, sets):
+        place=HBM,
+    )
+
+
+def gradient_call(sz, sets):
     A, E, F = sz.atoms, sz.rows, sz.width
     count = len(sets[0])
     w1, w2, w3 = sz.widths
     w4, w5 = 4 * F // sz.space, F // sz.space
     half = F // 2
-    arrays = SimpleNamespace(scal=(scal, SMEM))
+    arrays = SimpleNamespace()
     for role in (FIRST, SECOND):
         for m in range(count):
             for name in FACTORS:
@@ -921,7 +1004,7 @@
         )
         filt = sum(get("gfilt", m)[...] for m in every) * 0.5
         norm = sum(get("gnorm", m)[...] for m in every)
-        core = r.scal[2]
+        core = lax.axis_index("dp")
         for k in range(sz.space):
             spare = [filt[:, k * w4 : (k + 1) * w4]]
             if half > w4:
@@ -947,7 +1030,7 @@
 
     def both(r):
         for role in (FIRST, SECOND):
-            pl.when(r.scal[0] == role)(lambda role=role: body(r, role))
+            pl.when(lax.axis_index("section") == role)(lambda role=role: body(r, role))
 
     shape = jax.ShapeDtypeStruct
     return call(
@@ -974,13 +1057,13 @@
     return jnp.concatenate([ref[rows, :] for rows in border_rows(sz, m, index)], axis=1)
 
 
-def piece_call(sz, scal, stay, recv, up, down, moved, other):
+def piece_call(sz, stay, recv, up, down, moved, other):
     A, H, E, F = sz.atoms, sz.halo, sz.rows, sz.width
     count = up.shape[0]
     half = F // 2
 
     def body(r):
-        slab, space = r.scal[1], sz.space
+        slab, space = lax.axis_index("space"), sz.space
         for hop in range(space):
             k = lax.rem(slab + hop, space)
             total = r.stay[k] + r.recv[k].astype(F32)
@@ -1014,7 +1097,6 @@
     made = call(
         body,
         SimpleNamespace(
-            scal=(scal, SMEM),
             stay=(stay, VMEM),
             recv=(recv, VMEM),
             up=(up, VMEM),
@@ -1028,11 +1110,11 @@
     return [getattr(made, f"hop{hop}") for hop in range(sz.space)], made.mine
 
 
-def result_call(sz, scal, fresh, back, from_low, from_high, mine):
+def result_call(sz, fresh, back, from_low, from_high, mine):
     A, H, F = sz.atoms, sz.halo, sz.width
     count = len(back[0])
     arrays = SimpleNamespace(
-        scal=(scal, SMEM), low=(from_low, VMEM), high=(from_high, VMEM), mine=(mine, VMEM)
+        low=(from_low, VMEM), high=(from_high, VMEM), mine=(mine, VMEM)
     )
     for role in (FIRST, SECOND):
         for m in range(count):
@@ -1059,7 +1141,7 @@
 
     def both(r):
         for role in (FIRST, SECOND):
-            pl.when(r.scal[0] == role)(lambda role=role: body(r, role))
+            pl.when(lax.axis_index("section") == role)(lambda role=role: body(r, role))
 
     shape = jax.ShapeDtypeStruct
     return call(
@@ -1074,7 +1156,7 @@
     )
 
 
-def share_call(sz, scal, total, other):
+def share_call(sz, total, other):
     F = sz.width
     w1, w2, w3 = sz.widths
     w4, w5 = 4 * F // sz.space, F // sz.space
@@ -1090,13 +1172,13 @@
         r.bias[...] = second[sz.spare + 1 : sz.spare + 2, 0:w5]
 
     def both(r):
-        pl.when(r.scal[2] == 0)(lambda: body(r, r.total, r.other))
-        pl.when(r.scal[2] == 1)(lambda: body(r, r.other, r.total))
+        pl.when(lax.axis_index("dp") == 0)(lambda: body(r, r.total, r.other))
+        pl.when(lax.axis_index("dp") == 1)(lambda: body(r, r.other, r.total))
 
     shape = jax.ShapeDtypeStruct
     return call(
         both,
-        SimpleNamespace(scal=(scal, SMEM), total=(total, VMEM), other=(other, VMEM)),
+        SimpleNamespace(total=(total, VMEM), other=(other, VMEM)),
         SimpleNamespace(
             gain=shape((1, w5), F32),
             bias=shape((1, w5), F32),
@@ -1125,19 +1207,25 @@
 ):
     micro_count = features.shape[0]
     space = lax.axis_size("space")
-    section = lax.axis_index("section")
-    slab = lax.axis_index("space")
-    core = lax.axis_index("dp")
     sz = Sizes(features.shape[3], features.shape[4], filter_weight.shape[1], neighbours.shape[2], space)
     up = [(i, (i + 1) % space) for i in range(space)]
     down = [((i + 1) % space, i) for i in range(space)]
 
-    scal = jnp.stack([section, slab, core, space - 1]).astype(jnp.int32)
     places = jnp.transpose(coords, (0, 2, 1, 3))
-    borders = border_call(
-        sz, features, places, neighbours, shifts, counts, norm_gain, norm_bias, filter_weight
-    )
-    slots, norms, half_filter = borders.slots, borders.norms, borders.wh
+    borders = border_call(sz, features, places)
+    staged = stage_call(
+        sz,
+        features,
+        places,
+        neighbours,
+        shifts,
+        counts,
+        norm_gain,
+        norm_bias,
+        filter_weight,
+        (qkv_weight, vector_weight, out_weight),
+    )
+    slots, norms, half_filter = staged.slots, staged.norms, staged.wh
     pack_low = lax.ppermute(borders.up, "space", up)
     pack_high = lax.ppermute(borders.down, "space", down)
     both = ("section", "space")
@@ -1148,29 +1236,36 @@
     back_up = [(space + k, (k + 1) % space) for k in range(space)]
     back_down = [(space + (k + 1) % space, k) for k in range(space)]
 
-    def geometry_inputs(place):
+    def geometry_inputs():
         return SimpleNamespace(
-            scal=(scal, SMEM),
             pack_low=(pack_low, VMEM),
             pack_high=(pack_high, VMEM),
-            coords=(places, place),
-            slots=(slots, place),
-            wh=(half_filter, place),
+            coords=(places, VMEM),
+            slots=(slots, VMEM),
+            wh=(half_filter, VMEM),
         )
 
     firsts, sent, filters = [], [], {}
     for m in range(micro_count):
-        arrays = geometry_inputs(HBM)
-        arrays.features = (features, HBM)
-        arrays.norms = (norms, VMEM)
-        arrays.wqkv, arrays.wvec, arrays.wout = (
-            (qkv_weight, HBM), (vector_weight, HBM), (out_weight, HBM)
-        )
-        first = first_call(sz, m, True, arrays)
+        if m == 0:
+            arrays = SimpleNamespace(
+                pack_low=(pack_low, VMEM),
+                pack_high=(pack_high, VMEM),
+                room=(staged.low, HBM),
+                wide=(staged.wide, HBM),
+            )
+        else:
+            arrays = geometry_inputs()
+            arrays.features = (features, VMEM)
+            arrays.norms = (norms, VMEM)
+            arrays.wqkv, arrays.wvec, arrays.wout = (
+                (qkv_weight, VMEM), (vector_weight, VMEM), (out_weight, VMEM)
+            )
+        first = first_call(sz, m, m == 0, sz.sent[m], arrays)
         firsts.append(first)
         if m == micro_count - 1:
             made = filters[SECOND] = filter_call(
-                sz, SECOND, range(micro_count), geometry_inputs(VMEM)
+                sz, SECOND, range(micro_count), geometry_inputs()
             )
             first.head, made[0].geo = lax.optimization_barrier((first.head, made[0].geo))
         sent.append((
@@ -1181,7 +1276,6 @@
     def both_inputs(m, role):
         made = filters[role][m]
         return SimpleNamespace(
-            scal=(scal, SMEM),
             norms=(norms, VMEM),
             wqkv=(qkv_weight, VMEM),
             wvec=(vector_weight, VMEM),
@@ -1209,7 +1303,7 @@
         second = both_call(sz, m, True, arrays)
         seconds.append(second)
         if m == 0:
-            later = geometry_inputs(VMEM)
+            later = geometry_inputs()
             held, second.gplaces = lax.optimization_barrier((slots, second.gplaces))
             later.slots = (held, VMEM)
             filters[FIRST] = filter_call(sz, FIRST, range(micro_count), later)
@@ -1237,10 +1331,9 @@
 
     last = thirds[-1]
     other = lax.ppermute(last.moved, "section", [(0, 1), (1, 0)])
-    shares = gradient_call(sz, scal, (thirds, seconds))
+    shares = gradient_call(sz, (thirds, seconds))
     recv = lax.ppermute(shares.send, "dp", [(0, 1), (1, 0)])
-    (total, *pieces), mine = piece_call(
-        sz, scal, shares.stay, recv, last.up, last.down, last.moved, other
+    (total, *pieces), mine = piece_call(sz, shares.stay, recv, last.up, last.down, last.moved, other
     )
     received = [
         lax.ppermute(piece, "space", [(i, (i + hop) % space) for i in range(space)])
@@ -1250,7 +1343,6 @@
         total = total + piece[: sz.packed].astype(F32)
     results = result_call(
         sz,
-        scal,
         ([v.fresh for v in firsts], [v.fresh for v in seconds]),
         ([v.back for v in thirds], [v.back for v in seconds]),
         received[0],
@@ -1258,7 +1350,7 @@
         mine,
     )
     other = lax.ppermute(total, "dp", [(0, 1), (1, 0)])
-    share = share_call(sz, scal, total, other)
+    share = share_call(sz, total, other)
     return (
         results.outputs,
         results.grads,

time: 119 us -> 107 us (0.90)
  Pallas kernels: 58.8 us -> 49.7 us
  local copies, waits for them, and re-layouts: 4 us -> 0.05 us
  waiting for transfers between devices: 21.7 us -> 24.4 us
    pallas_call x13 -> x14, Pallas kernels: 58.8 us -> 49.7 us  [call(): pl.pallas_call(kernel, out_shape=list(outs.values()), in_specs=[spec for...]
    unnamed x48 -> x18, local copies, waits for them, and re-layouts: 4 us -> 0.05 us
    ppermute x2, waiting for transfers between devices: 2.36 us -> 5.34 us  [on_device(): lax.ppermute(rim_high, both, back_up)]
    ppermute x1, waiting for transfers between devices: 2.04 us -> 0.01 us  [on_device(): pack_low = lax.ppermute(borders.up, 'space', up)]
    ppermute x2, waiting for transfers between devices: 0.01 us -> 1.41 us  [on_device(): lax.ppermute(first.tail, both, forth_up)]
  transfers between devices with their start and end apart: 24 -> 24, of which waited for: 7 -> 9; matrix products, arithmetic and copies ran while one was open for 1% -> 0% of each run, Pallas kernels for 27% -> 26%
where the time goes in v3:
time: 107 us
  Pallas kernels  49.7 us (46%)
  starting transfers between devices  31.3 us (29%)
  waiting for transfers between devices  24.4 us (23%)
    pallas_call x14, Pallas kernels, call(): pl.pallas_call(kernel, out_shape=list(outs.values()), in_specs=[spec for...  49.7 us
    ppermute x7, waiting for transfers between devices, on_device(): lax.ppermute(piece, 'space', [(i, (i + hop) % space) for i in range(space)])  13.3 us
    ppermute x7, starting transfers between devices, on_device(): lax.ppermute(piece, 'space', [(i, (i + hop) % space) for i in range(space)])  9.45 us
    ppermute x2, waiting for transfers between devices, on_device(): lax.ppermute(rim_high, both, back_up)  5.34 us
    ppermute x1, waiting for transfers between devices, on_device(): other = lax.ppermute(last.moved, 'section', [(0, 1), (1, 0)])  3.64 us
    ppermute x1, starting transfers between devices, on_device(): pack_high = lax.ppermute(borders.down, 'space', down)  3.1 us
    ppermute x1, starting transfers between devices, on_device(): pack_low = lax.ppermute(borders.up, 'space', up)  3.02 us
    ppermute x2, starting transfers between devices, on_device(): lax.ppermute(first.fresh, both, forth)  2.59 us
  transfers between devices with their start and end apart: 24, of which 9 were waited for; matrix products, arithmetic and copies ran while one was open for 0% of the time, Pallas kernels for 26%

profile of v3, /device:TPU:0, one launch (start us, length us, event | category | flops | bytes accessed | tf_op | source)
XLA Modules:
  0.0 106.6 jit_solution(16504966568290491915)
XLA Ops:
  0.6 1.5 %shard_map.188 = (bf16[2,5,16,256]{3,2,1,0:T(8,128)(2,1)}, bf16[2,5,16,256]{3,2,1,0:T(8,128)(2,1)}) custom-call(bf16[2,1,4,64,256]{4,3,2,1,0:T(8,128)(2,1)} %args_13_.3, f32[2,3,1,64]{3,2,1,0:T(1,128)} %bitcast.5), custom_call_target="tpu_custom_call" | custom-call | tf_op jit(solution)/shard_map/pallas_call | solution.py:663
  2.2 3.0 %collective-permute-start = (bf16[2,5,16,256]{3,2,1,0:T(8,128)(2,1)}, bf16[2,5,16,256]{3,2,1,0:T(8,128)(2,1)S(1)}, u32[]{:S(2)}, u32[]{:S(2)}) collective-permute-start(bf16[2,5,16,256]{3,2,1,0:T(8,128)(2,1)} %get-tuple-element.128), channel_id=1, source_target_pairs={{0,2},{2,4},{4,6},{6,8},{8,10},{10,12},{12,14},{14,0},{1,3},{3,5},... | collective-permute-start | bytes 245768 | tf_op jit(solution)/shard_map/ppermute | solution.py:1229
  5.2 3.1 %collective-permute-start.1 = (bf16[2,5,16,256]{3,2,1,0:T(8,128)(2,1)}, bf16[2,5,16,256]{3,2,1,0:T(8,128)(2,1)S(1)}, u32[]{:S(2)}, u32[]{:S(2)}) collective-permute-start(bf16[2,5,16,256]{3,2,1,0:T(8,128)(2,1)} %get-tuple-element.129), channel_id=1, source_target_pairs={{2,0},{4,2},{6,4},{8,6},{10,8},{12,10},{14,12},{0,14},{3,1},{5,3},... | collective-permute-start | bytes 245768 | tf_op jit(solution)/shard_map/ppermute | solution.py:1230
  8.3 3.0 %shard_map.187 = (f32[2,104,128]{2,1,0:T(8,128)}, f32[8,256]{1,0:T(8,128)}, bf16[32,1024]{1,0:T(8,128)(2,1)}, bf16[20480,1280]{1,0:T(8,128)(2,1)}, f32[51200,256]{1,0:T(8,128)}) custom-call(bf16[2,1,4,64,256]{4,3,2,1,0:T(8,128)(2,1)} %args_13_.3, f32[2,3,1,64]{3,2,1,0:T(1,128)} %bitcast.6, s32[2,1,32,64]{3,2,1,0:T(8,128)} %args_2_.8, ...), custom_call_target="tpu_custom_call" | custom-call | tf_op jit(solution)/shard_map/pallas_call | solution.py:663
  11.3 0.0 collective-permute-done.args_0_.args_11_
  11.3 0.3 collective-permute-done.1.args_1_.args_12_
  11.6 0.0 copy-start.4
  11.6 0.0 copy-start.6
  11.6 0.0 copy-start.7
  11.7 0.0 copy-start.8
  11.7 0.0 copy-start.5
  11.7 8.1 %shard_map.191 = (bf16[4,64,256]{2,1,0:T(8,128)(2,1)S(1)}, bf16[4,16,256]{2,1,0:T(8,128)(2,1)S(1)}, bf16[4,16,256]{2,1,0:T(8,128)(2,1)S(1)}, bf16[64,256]{1,0:T(8,128)(2,1)S(1)}, bf16[8,2,256,128]{3,2,1,0:T(8,128)(2,1)S(1)}) custom-call(bf16[2,5,16,256]{3,2,1,0:T(8,128)(2,1)S(1)} %collective-permute-done.args_0_.args_11_, ...), custom_call_target="tpu_custom_call" | custom-call | tf_op jit(solution)/shard_map/pallas_call | solution.py:663
  19.8 1.3 %collective-permute-start.2 = (bf16[4,64,256]{2,1,0:T(8,128)(2,1)S(1)}, bf16[4,64,256]{2,1,0:T(8,128)(2,1)S(1)}, u32[]{:S(2)}, u32[]{:S(2)}) collective-permute-start(bf16[4,64,256]{2,1,0:T(8,128)(2,1)S(1)} %get-tuple-element.141.args_3_), channel_id=1, source_target_pairs={{0,16},{2,18},{4,20},{6,22},{8,24},{10,26},{12,28},{14,30},{1,17},... | collective-permute-start | bytes 393224 | tf_op jit(solution)/shard_map/ppermute | solution.py:1272
  21.1 1.3 %collective-permute-start.3 = (bf16[4,16,256]{2,1,0:T(8,128)(2,1)S(1)}, bf16[4,16,256]{2,1,0:T(8,128)(2,1)S(1)}, u32[]{:S(2)}, u32[]{:S(2)}) collective-permute-start(bf16[4,16,256]{2,1,0:T(8,128)(2,1)S(1)} %get-tuple-element.142), channel_id=1, source_target_pairs={{0,18},{2,20},{4,22},{6,24},{8,26},{10,28},{12,30},{14,16},{1,19},... | collective-permute-start | bytes 98312 | tf_op jit(solution)/shard_map/ppermute | solution.py:1273
  22.4 1.3 %collective-permute-start.4 = (bf16[4,16,256]{2,1,0:T(8,128)(2,1)S(1)}, bf16[4,16,256]{2,1,0:T(8,128)(2,1)S(1)}, u32[]{:S(2)}, u32[]{:S(2)}) collective-permute-start(bf16[4,16,256]{2,1,0:T(8,128)(2,1)S(1)} %get-tuple-element.143), channel_id=1, source_target_pairs={{2,16},{4,18},{6,20},{8,22},{10,24},{12,26},{14,28},{0,30},{3,17},... | collective-permute-start | bytes 98312 | tf_op jit(solution)/shard_map/ppermute | solution.py:1274
  23.8 6.6 %shard_map.189 = (bf16[4,64,256]{2,1,0:T(8,128)(2,1)S(1)}, bf16[4,64,256]{2,1,0:T(8,128)(2,1)S(1)}, bf16[4,64,256]{2,1,0:T(8,128)(2,1)S(1)}, bf16[64,256]{1,0:T(8,128)(2,1)S(1)}, bf16[8,2,256,128]{3,2,1,0:T(8,128)(2,1)S(1)}) custom-call(bf16[2,5,16,256]{3,2,1,0:T(8,128)(2,1)S(1)} %collective-permute-done.args_0_.args_11_, ...), custom_call_target="tpu_custom_call" | custom-call | tf_op jit(solution)/shard_map/pallas_call | solution.py:663
  30.4 1.3 %collective-permute-start.9 = (bf16[4,64,256]{2,1,0:T(8,128)(2,1)S(1)}, bf16[4,64,256]{2,1,0:T(8,128)(2,1)S(1)}, u32[]{:S(2)}, u32[]{:S(2)}) collective-permute-start(bf16[4,64,256]{2,1,0:T(8,128)(2,1)S(1)} %get-tuple-element.166), channel_id=1, source_target_pairs={{0,18},{2,20},{4,22},{6,24},{8,26},{10,28},{12,30},{14,16},{1,19},... | collective-permute-start | bytes 393224 | tf_op jit(solution)/shard_map/ppermute | solution.py:1273
  31.7 1.3 %collective-permute-start.8 = (bf16[4,64,256]{2,1,0:T(8,128)(2,1)S(1)}, bf16[4,64,256]{2,1,0:T(8,128)(2,1)S(1)}, u32[]{:S(2)}, u32[]{:S(2)}) collective-permute-start(bf16[4,64,256]{2,1,0:T(8,128)(2,1)S(1)} %get-tuple-element.165.args_5_), channel_id=1, source_target_pairs={{0,16},{2,18},{4,20},{6,22},{8,24},{10,26},{12,28},{14,30},{1,17},... | collective-permute-start | bytes 393224 | tf_op jit(solution)/shard_map/ppermute | solution.py:1272
  33.0 0.0 collective-permute-done.3.args_12_
  33.0 1.3 %collective-permute-start.10 = (bf16[4,64,256]{2,1,0:T(8,128)(2,1)S(1)}, bf16[4,64,256]{2,1,0:T(8,128)(2,1)S(1)}, u32[]{:S(2)}, u32[]{:S(2)}) collective-permute-start(bf16[4,64,256]{2,1,0:T(8,128)(2,1)S(1)} %get-tuple-element.167), channel_id=1, source_target_pairs={{2,16},{4,18},{6,20},{8,22},{10,24},{12,26},{14,28},{0,30},{3,17},... | collective-permute-start | bytes 393224 | tf_op jit(solution)/shard_map/ppermute | solution.py:1274
  34.3 0.0 collective-permute-done.4.args_13_
  34.3 0.0 collective-permute-done.2.args_11_
  34.4 1.3 %collective-permute-start.5 = (bf16[4,64,256]{2,1,0:T(8,128)(2,1)S(1)}, bf16[4,64,256]{2,1,0:T(8,128)(2,1)S(1)}, u32[]{:S(2)}, u32[]{:S(2)}) collective-permute-start(bf16[4,64,256]{2,1,0:T(8,128)(2,1)S(1)} %get-tuple-element.156), channel_id=1, source_target_pairs={{16,0},{18,2},{20,4},{22,6},{24,8},{26,10},{28,12},{30,14},{17,1},... | collective-permute-start | bytes 393224 | tf_op jit(solution)/shard_map/ppermute | solution.py:1316
  35.7 1.3 %collective-permute-start.6 = (bf16[4,16,256]{2,1,0:T(8,128)(2,1)S(1)}, bf16[4,16,256]{2,1,0:T(8,128)(2,1)S(1)}, u32[]{:S(2)}, u32[]{:S(2)}) collective-permute-start(bf16[4,16,256]{2,1,0:T(8,128)(2,1)S(1)} %get-tuple-element.157.args_23_), channel_id=1, source_target_pairs={{16,2},{18,4},{20,6},{22,8},{24,10},{26,12},{28,14},{30,0},{17,3},... | collective-permute-start | bytes 98312 | tf_op jit(solution)/shard_map/ppermute | solution.py:1317
  37.0 1.4 %collective-permute-done.9.args_12_ = bf16[4,64,256]{2,1,0:T(8,128)(2,1)S(1)} collective-permute-done((bf16[4,64,256]{2,1,0:T(8,128)(2,1)S(1)}, bf16[4,64,256]{2,1,0:T(8,128)(2,1)S(1)}, u32[]{:S(2)}, u32[]{:S(2)}) %collective-permute-start.9) | collective-permute-done | bytes 131104 | tf_op jit(solution)/shard_map/ppermute | solution.py:1273
  38.4 1.3 %collective-permute-start.7 = (bf16[4,16,256]{2,1,0:T(8,128)(2,1)S(1)}, bf16[4,16,256]{2,1,0:T(8,128)(2,1)S(1)}, u32[]{:S(2)}, u32[]{:S(2)}) collective-permute-start(bf16[4,16,256]{2,1,0:T(8,128)(2,1)S(1)} %get-tuple-element.158.args_22_), channel_id=1, source_target_pairs={{18,0},{20,2},{22,4},{24,6},{26,8},{28,10},{30,12},{16,14},{19,1},... | collective-permute-start | bytes 98312 | tf_op jit(solution)/shard_map/ppermute | solution.py:1318
  39.7 7.5 %shard_map.193 = (f32[10,8,256]{2,1,0:T(8,128)S(1)}, bf16[8,32,256]{2,1,0:T(8,128)(2,1)S(1)}, bf16[8,256,128]{2,1,0:T(8,128)(2,1)S(1)}, bf16[8,192,256]{2,1,0:T(...) custom-call(bf16[2,5,16,256]{3,2,1,0:T(8,128)(2,1)S(1)} %collective-, ...), custom_call_target="tpu_custom_call" | custom-call | tf_op jit(solution)/shard_map/pallas_call | solution.py:663
  47.2 0.0 collective-permute-done.8.args_11_
  47.2 0.0 collective-permute-done.10.args_13_
  47.2 0.2 shard_map.194
  47.4 2.2 %collective-permute-done.6.args_17_ = bf16[4,16,256]{2,1,0:T(8,128)(2,1)S(1)} collective-permute-done((bf16[4,16,256]{2,1,0:T(8,128)(2,1)S(1)}, bf16[4,16,256]{2,1,0:T(8,128)(2,1)S(1)}, u32[]{:S(2)}, u32[]{:S(2)}) %collective-permute-start.6) | collective-permute-done | bytes 32800 | tf_op jit(solution)/shard_map/ppermute | solution.py:1317
  49.6 0.0 collective-permute-done.7.args_18_
  49.6 0.0 collective-permute-done.5.args_16_
  49.6 1.3 %collective-permute-start.11 = (bf16[4,64,256]{2,1,0:T(8,128)(2,1)S(1)}, bf16[4,64,256]{2,1,0:T(8,128)(2,1)S(1)}, u32[]{:S(2)}, u32[]{:S(2)}) collective-permute-start(bf16[4,64,256]{2,1,0:T(8,128)(2,1)S(1)} %get-tuple-element.188), channel_id=1, source_target_pairs={{16,0},{18,2},{20,4},{22,6},{24,8},{26,10},{28,12},{30,14},{17,1},... | collective-permute-start | bytes 393224 | tf_op jit(solution)/shard_map/ppermute | solution.py:1316
  50.9 1.3 %collective-permute-start.12 = (bf16[4,16,256]{2,1,0:T(8,128)(2,1)S(1)}, bf16[4,16,256]{2,1,0:T(8,128)(2,1)S(1)}, u32[]{:S(2)}, u32[]{:S(2)}) collective-permute-start(bf16[4,16,256]{2,1,0:T(8,128)(2,1)S(1)} %get-tuple-element.189.args_26_), channel_id=1, source_target_pairs={{16,2},{18,4},{20,6},{22,8},{24,10},{26,12},{28,14},{30,0},{17,3},... | collective-permute-start | bytes 98312 | tf_op jit(solution)/shard_map/ppermute | solution.py:1317
  52.2 1.3 %collective-permute-start.13 = (bf16[4,16,256]{2,1,0:T(8,128)(2,1)S(1)}, bf16[4,16,256]{2,1,0:T(8,128)(2,1)S(1)}, u32[]{:S(2)}, u32[]{:S(2)}) collective-permute-start(bf16[4,16,256]{2,1,0:T(8,128)(2,1)S(1)} %get-tuple-element.190.args_25_), channel_id=1, source_target_pairs={{18,0},{20,2},{22,4},{24,6},{26,8},{28,10},{30,12},{16,14},{19,1},... | collective-permute-start | bytes 98312 | tf_op jit(solution)/shard_map/ppermute | solution.py:1318
  53.5 9.9 %shard_map.195 = (f32[4,64,256]{2,1,0:T(8,128)S(1)}, bf16[4,64,256]{2,1,0:T(8,128)(2,1)}, bf16[4,16,256]{2,1,0:T(8,128)(2,1)S(1)}, bf16[4,16,256]{2,1,0:T(8,128)...) custom-call(f32[8,256]{1,0:T(8,128)S(1)} %copy-done.7, ...), custom_call_target="tpu_custom_call" | custom-call | tf_op jit(solution)/shard_map/pallas_call | solution.py:663
  63.4 3.1 %collective-permute-done.12.args_17_ = bf16[4,16,256]{2,1,0:T(8,128)(2,1)S(1)} collective-permute-done((bf16[4,16,256]{2,1,0:T(8,128)(2,1)S(1)}, bf16[4,16,256]{2,1,0:T(8,128)(2,1)S(1)}, u32[]{:S(2)}, u32[]{:S(2)}) %collective-permute-start.12) | collective-permute-done | bytes 32800 | tf_op jit(solution)/shard_map/ppermute | solution.py:1317
  66.5 0.0 collective-permute-done.13.args_18_
  66.5 0.0 collective-permute-done.11.args_16_
  66.5 9.9 %shard_map.196 = (f32[4,64,256]{2,1,0:T(8,128)S(1)}, bf16[4,64,256]{2,1,0:T(8,128)(2,1)}, bf16[4,16,256]{2,1,0:T(8,128)(2,1)}, bf16[4,16,256]{2,1,0:T(8,128)(2,1...) custom-call(f32[8,256]{1,0:T(8,128)S(1)} %copy-done.7, ...), custom_call_target="tpu_custom_call" | custom-call | tf_op jit(solution)/shard_map/pallas_call | solution.py:663
  76.5 1.0 shard_map.197
  77.4 0.1 collective-permute-start.14
  77.5 0.1 collective-permute-start.15
  77.6 3.6 %collective-permute-done.15.args_5_ = f32[2,8,128]{2,1,0:T(8,128)S(1)} collective-permute-done((f32[2,8,128]{2,1,0:T(8,128)S(1)}, f32[2,8,128]{2,1,0:T(8,128)S(1)}, u32[]{:S(2)}, u32[]{:S(2)}) %collective-permute-start.15) | collective-permute-done | bytes 8224 | tf_op jit(solution)/shard_map/ppermute | solution.py:1333
  81.2 0.0 collective-permute-done.14.args_1_
  81.2 0.2 shard_map.198
  81.4 0.1 collective-permute-start.18
  81.5 1.9 %collective-permute-start.19 = (bf16[384,128]{1,0:T(8,128)(2,1)S(1)}, bf16[384,128]{1,0:T(8,128)(2,1)S(1)}, u32[]{:S(2)}, u32[]{:S(2)}) collective-permute-start(bf16[384,128]{1,0:T(8,128)(2,1)S(1)} %get-tuple-element.232), channel_id=1, source_target_pairs={{0,6},{2,8},{4,10},{6,12},{8,14},{10,0},{12,2},{14,4},{1,7},{3,9},... | collective-permute-start | bytes 294920 | tf_op jit(solution)/shard_map/ppermute | solution.py:1339
  83.4 2.0 %collective-permute-start.16 = (bf16[704,128]{1,0:T(8,128)(2,1)S(1)}, bf16[704,128]{1,0:T(8,128)(2,1)S(1)}, u32[]{:S(2)}, u32[]{:S(2)}) collective-permute-start(bf16[704,128]{1,0:T(8,128)(2,1)S(1)} %get-tuple-element.219), channel_id=1, source_target_pairs={{0,2},{2,4},{4,6},{6,8},{8,10},{10,12},{12,14},{14,0},{1,3},{3,5},... | collective-permute-start | bytes 540680 | tf_op jit(solution)/shard_map/ppermute | solution.py:1339
  85.4 2.8 %collective-permute-start.17 = (bf16[704,128]{1,0:T(8,128)(2,1)S(1)}, bf16[704,128]{1,0:T(8,128)(2,1)S(1)}, u32[]{:S(2)}, u32[]{:S(2)}) collective-permute-start(bf16[704,128]{1,0:T(8,128)(2,1)S(1)} %get-tuple-element.220), channel_id=1, source_target_pairs={{0,14},{2,0},{4,2},{6,4},{8,6},{10,8},{12,10},{14,12},{1,15},{3,1}... | collective-permute-start | bytes 540680 | tf_op jit(solution)/shard_map/ppermute | solution.py:1339
  88.1 1.0 collective-permute-start.20
  89.1 0.0 collective-permute-done.18
  89.1 1.8 %collective-permute-start.21 = (bf16[384,128]{1,0:T(8,128)(2,1)S(1)}, bf16[384,128]{1,0:T(8,128)(2,1)S(1)}, u32[]{:S(2)}, u32[]{:S(2)}) collective-permute-start(bf16[384,128]{1,0:T(8,128)(2,1)S(1)} %get-tuple-element.234), channel_id=1, source_target_pairs={{0,10},{2,12},{4,14},{6,0},{8,2},{10,4},{12,6},{14,8},{1,11},{3,13... | collective-permute-start | bytes 294920 | tf_op jit(solution)/shard_map/ppermute | solution.py:1339
  90.9 7.2 %collective-permute-done.19 = bf16[384,128]{1,0:T(8,128)(2,1)S(1)} collective-permute-done((bf16[384,128]{1,0:T(8,128)(2,1)S(1)}, bf16[384,128]{1,0:T(8,128)(2,1)S(1)}, u32[]{:S(2)}, u32[]{:S(2)}) %collective-permute-start.19) | collective-permute-done | bytes 98336 | tf_op jit(solution)/shard_map/ppermute | solution.py:1339
  98.1 3.0 %collective-permute-done.20 = bf16[384,128]{1,0:T(8,128)(2,1)S(1)} collective-permute-done((bf16[384,128]{1,0:T(8,128)(2,1)S(1)}, bf16[384,128]{1,0:T(8,128)(2,1)S(1)}, u32[]{:S(2)}, u32[]{:S(2)}) %collective-permute-start.20) | collective-permute-done | bytes 98336 | tf_op jit(solution)/shard_map/ppermute | solution.py:1339
  101.1 3.0 %collective-permute-done.22 = bf16[384,128]{1,0:T(8,128)(2,1)S(1)} collective-permute-done((bf16[384,128]{1,0:T(8,128)(2,1)S(1)}, bf16[384,128]{1,0:T(8,128)(2,1)S(1)}, u32[]{:S(2)}, u32[]{:S(2)}) %collective-permute-start.22) | collective-permute-done | bytes 98336 | tf_op jit(solution)/shard_map/ppermute | solution.py:1339
  104.2 0.0 collective-permute-done.16.args_0_
  104.2 0.0 collective-permute-done.17.args_1_
  104.2 0.1 convert_add_fusion.args_0_
  104.3 0.1 collective-permute-start.23
  104.4 1.0 shard_map.199
  105.3 0.5 collective-permute-done.23.args_1_
  105.8 0.8 shard_map.200
  (17 shorter events, 0.1 us)
Async XLA Ops:
  2.2 9.1 %collective-permute-start = (bf16[2,5,16,256]{3,2,1,0:T(8,128)(2,1)}, bf16[2,5,16,256]{3,2,1,0:T(8,128)(2,1)S(1)}, u32[]{:S(2)}, u32[]{:S(2)}) collective-permute-start(bf16[2,5,16,256]{3,2,1,0:T(8,128)(2,1)} %get-tuple-element.128), channel_id=1, source_target_pairs={{0,2},{2,4},{4,6},{6,8},{8,10},{10,12},{12,14},{14,0},{1,3},{3,5},... | collective-permute-start | bytes 245768 | tf_op jit(solution)/shard_map/ppermute | solution.py:1229
  5.2 6.4 %collective-permute-start.1 = (bf16[2,5,16,256]{3,2,1,0:T(8,128)(2,1)}, bf16[2,5,16,256]{3,2,1,0:T(8,128)(2,1)S(1)}, u32[]{:S(2)}, u32[]{:S(2)}) collective-permute-start(bf16[2,5,16,256]{3,2,1,0:T(8,128)(2,1)} %get-tuple-element.129), channel_id=1, source_target_pairs={{2,0},{4,2},{6,4},{8,6},{10,8},{12,10},{14,12},{0,14},{3,1},{5,3},... | collective-permute-start | bytes 245768 | tf_op jit(solution)/shard_map/ppermute | solution.py:1230
  11.6 12.1 %copy-start = (bf16[1,256,1280]{2,1,0:T(8,128)(2,1)S(1)}, bf16[1,256,1280]{2,1,0:T(8,128)(2,1)}, u32[]{:S(2)}) copy-start(bf16[1,256,1280]{2,1,0:T(8,128)(2,1)} %args_1_.10) | copy-start | bytes 1966084
  11.6 12.1 %copy-start.1 = (bf16[1,256,768]{2,1,0:T(8,128)(2,1)S(1)}, bf16[1,256,768]{2,1,0:T(8,128)(2,1)}, u32[]{:S(2)}) copy-start(bf16[1,256,768]{2,1,0:T(8,128)(2,1)} %args_2_.12) | copy-start | bytes 1179652
  11.6 12.1 %copy-start.2 = (bf16[1,256,768]{2,1,0:T(8,128)(2,1)S(1)}, bf16[1,256,768]{2,1,0:T(8,128)(2,1)}, u32[]{:S(2)}) copy-start(bf16[1,256,768]{2,1,0:T(8,128)(2,1)} %args_4_.12) | copy-start | bytes 1179652
  11.6 12.1 %copy-start.3 = (bf16[2,1,4,64,256]{4,3,2,1,0:T(8,128)(2,1)S(1)}, bf16[2,1,4,64,256]{4,3,2,1,0:T(8,128)(2,1)}, u32[]{:S(2)}) copy-start(bf16[2,1,4,64,256]{4,3,2,1,0:T(8,128)(2,1)} %args_13_.3) | copy-start | bytes 786436
  11.6 12.1 %copy-start.4 = (bf16[32,1024]{1,0:T(8,128)(2,1)S(1)}, bf16[32,1024]{1,0:T(8,128)(2,1)}, u32[]{:S(2)}) copy-start(bf16[32,1024]{1,0:T(8,128)(2,1)} %get-tuple-element.127.args_4_.args_3_) | copy-start | bytes 196612
  11.6 12.1 %copy-start.6 = (f32[2,104,128]{2,1,0:T(8,128)S(1)}, f32[2,104,128]{2,1,0:T(8,128)}, u32[]{:S(2)}) copy-start(f32[2,104,128]{2,1,0:T(8,128)} %get-tuple-element.145.args_3_) | copy-start | bytes 319492
  11.6 12.1 %copy-start.7 = (f32[8,256]{1,0:T(8,128)S(1)}, f32[8,256]{1,0:T(8,128)}, u32[]{:S(2)}) copy-start(f32[8,256]{1,0:T(8,128)} %get-tuple-element.126.args_6_.args_0_) | copy-start | bytes 24580
  11.7 12.1 %copy-start.8 = (f32[2,1,3,64]{3,1,2,0:T(1,128)S(1)}, f32[2,1,3,64]{3,1,2,0:T(1,128)}, u32[]{:S(2)}) copy-start(f32[2,1,3,64]{3,1,2,0:T(1,128)} %param.13) | copy-start | bytes 4612
  11.7 22.7 %copy-start.5 = (bf16[2,1,4,64,256]{4,3,2,1,0:T(8,128)(2,1)S(1)}, bf16[2,1,4,64,256]{4,3,2,1,0:T(8,128)(2,1)}, u32[]{:S(2)}) copy-start(bf16[2,1,4,64,256]{4,3,2,1,0:T(8,128)(2,1)} %args_14_.3) | copy-start | bytes 786436
  19.8 14.6 %collective-permute-start.2 = (bf16[4,64,256]{2,1,0:T(8,128)(2,1)S(1)}, bf16[4,64,256]{2,1,0:T(8,128)(2,1)S(1)}, u32[]{:S(2)}, u32[]{:S(2)}) collective-permute-start(bf16[4,64,256]{2,1,0:T(8,128)(2,1)S(1)} %get-tuple-element.141.args_3_), channel_id=1, source_target_pairs={{0,16},{2,18},{4,20},{6,22},{8,24},{10,26},{12,28},{14,30},{1,17},... | collective-permute-start | bytes 393224 | tf_op jit(solution)/shard_map/ppermute | solution.py:1272
  21.1 11.9 %collective-permute-start.3 = (bf16[4,16,256]{2,1,0:T(8,128)(2,1)S(1)}, bf16[4,16,256]{2,1,0:T(8,128)(2,1)S(1)}, u32[]{:S(2)}, u32[]{:S(2)}) collective-permute-start(bf16[4,16,256]{2,1,0:T(8,128)(2,1)S(1)} %get-tuple-element.142), channel_id=1, source_target_pairs={{0,18},{2,20},{4,22},{6,24},{8,26},{10,28},{12,30},{14,16},{1,19},... | collective-permute-start | bytes 98312 | tf_op jit(solution)/shard_map/ppermute | solution.py:1273
  22.4 11.9 %collective-permute-start.4 = (bf16[4,16,256]{2,1,0:T(8,128)(2,1)S(1)}, bf16[4,16,256]{2,1,0:T(8,128)(2,1)S(1)}, u32[]{:S(2)}, u32[]{:S(2)}) collective-permute-start(bf16[4,16,256]{2,1,0:T(8,128)(2,1)S(1)} %get-tuple-element.143), channel_id=1, source_target_pairs={{2,16},{4,18},{6,20},{8,22},{10,24},{12,26},{14,28},{0,30},{3,17},... | collective-permute-start | bytes 98312 | tf_op jit(solution)/shard_map/ppermute | solution.py:1274
  30.4 8.0 %collective-permute-start.9 = (bf16[4,64,256]{2,1,0:T(8,128)(2,1)S(1)}, bf16[4,64,256]{2,1,0:T(8,128)(2,1)S(1)}, u32[]{:S(2)}, u32[]{:S(2)}) collective-permute-start(bf16[4,64,256]{2,1,0:T(8,128)(2,1)S(1)} %get-tuple-element.166), channel_id=1, source_target_pairs={{0,18},{2,20},{4,22},{6,24},{8,26},{10,28},{12,30},{14,16},{1,19},... | collective-permute-start | bytes 393224 | tf_op jit(solution)/shard_map/ppermute | solution.py:1273
  31.7 15.5 %collective-permute-start.8 = (bf16[4,64,256]{2,1,0:T(8,128)(2,1)S(1)}, bf16[4,64,256]{2,1,0:T(8,128)(2,1)S(1)}, u32[]{:S(2)}, u32[]{:S(2)}) collective-permute-start(bf16[4,64,256]{2,1,0:T(8,128)(2,1)S(1)} %get-tuple-element.165.args_5_), channel_id=1, source_target_pairs={{0,16},{2,18},{4,20},{6,22},{8,24},{10,26},{12,28},{14,30},{1,17},... | collective-permute-start | bytes 393224 | tf_op jit(solution)/shard_map/ppermute | solution.py:1272
  33.0 14.2 %collective-permute-start.10 = (bf16[4,64,256]{2,1,0:T(8,128)(2,1)S(1)}, bf16[4,64,256]{2,1,0:T(8,128)(2,1)S(1)}, u32[]{:S(2)}, u32[]{:S(2)}) collective-permute-start(bf16[4,64,256]{2,1,0:T(8,128)(2,1)S(1)} %get-tuple-element.167), channel_id=1, source_target_pairs={{2,16},{4,18},{6,20},{8,22},{10,24},{12,26},{14,28},{0,30},{3,17},... | collective-permute-start | bytes 393224 | tf_op jit(solution)/shard_map/ppermute | solution.py:1274
  34.4 15.2 %collective-permute-start.5 = (bf16[4,64,256]{2,1,0:T(8,128)(2,1)S(1)}, bf16[4,64,256]{2,1,0:T(8,128)(2,1)S(1)}, u32[]{:S(2)}, u32[]{:S(2)}) collective-permute-start(bf16[4,64,256]{2,1,0:T(8,128)(2,1)S(1)} %get-tuple-element.156), channel_id=1, source_target_pairs={{16,0},{18,2},{20,4},{22,6},{24,8},{26,10},{28,12},{30,14},{17,1},... | collective-permute-start | bytes 393224 | tf_op jit(solution)/shard_map/ppermute | solution.py:1316
  35.7 13.9 %collective-permute-start.6 = (bf16[4,16,256]{2,1,0:T(8,128)(2,1)S(1)}, bf16[4,16,256]{2,1,0:T(8,128)(2,1)S(1)}, u32[]{:S(2)}, u32[]{:S(2)}) collective-permute-start(bf16[4,16,256]{2,1,0:T(8,128)(2,1)S(1)} %get-tuple-element.157.args_23_), channel_id=1, source_target_pairs={{16,2},{18,4},{20,6},{22,8},{24,10},{26,12},{28,14},{30,0},{17,3},... | collective-permute-start | bytes 98312 | tf_op jit(solution)/shard_map/ppermute | solution.py:1317
  38.4 11.2 %collective-permute-start.7 = (bf16[4,16,256]{2,1,0:T(8,128)(2,1)S(1)}, bf16[4,16,256]{2,1,0:T(8,128)(2,1)S(1)}, u32[]{:S(2)}, u32[]{:S(2)}) collective-permute-start(bf16[4,16,256]{2,1,0:T(8,128)(2,1)S(1)} %get-tuple-element.158.args_22_), channel_id=1, source_target_pairs={{18,0},{20,2},{22,4},{24,6},{26,8},{28,10},{30,12},{16,14},{19,1},... | collective-permute-start | bytes 98312 | tf_op jit(solution)/shard_map/ppermute | solution.py:1318
  49.6 16.9 %collective-permute-start.11 = (bf16[4,64,256]{2,1,0:T(8,128)(2,1)S(1)}, bf16[4,64,256]{2,1,0:T(8,128)(2,1)S(1)}, u32[]{:S(2)}, u32[]{:S(2)}) collective-permute-start(bf16[4,64,256]{2,1,0:T(8,128)(2,1)S(1)} %get-tuple-element.188), channel_id=1, source_target_pairs={{16,0},{18,2},{20,4},{22,6},{24,8},{26,10},{28,12},{30,14},{17,1},... | collective-permute-start | bytes 393224 | tf_op jit(solution)/shard_map/ppermute | solution.py:1316
  50.9 15.6 %collective-permute-start.12 = (bf16[4,16,256]{2,1,0:T(8,128)(2,1)S(1)}, bf16[4,16,256]{2,1,0:T(8,128)(2,1)S(1)}, u32[]{:S(2)}, u32[]{:S(2)}) collective-permute-start(bf16[4,16,256]{2,1,0:T(8,128)(2,1)S(1)} %get-tuple-element.189.args_26_), channel_id=1, source_target_pairs={{16,2},{18,4},{20,6},{22,8},{24,10},{26,12},{28,14},{30,0},{17,3},... | collective-permute-start | bytes 98312 | tf_op jit(solution)/shard_map/ppermute | solution.py:1317
  52.2 14.3 %collective-permute-start.13 = (bf16[4,16,256]{2,1,0:T(8,128)(2,1)S(1)}, bf16[4,16,256]{2,1,0:T(8,128)(2,1)S(1)}, u32[]{:S(2)}, u32[]{:S(2)}) collective-permute-start(bf16[4,16,256]{2,1,0:T(8,128)(2,1)S(1)} %get-tuple-element.190.args_25_), channel_id=1, source_target_pairs={{18,0},{20,2},{22,4},{24,6},{26,8},{28,10},{30,12},{16,14},{19,1},... | collective-permute-start | bytes 98312 | tf_op jit(solution)/shard_map/ppermute | solution.py:1318
  77.4 3.8 %collective-permute-start.14 = (bf16[8,384,128]{2,1,0:T(8,128)(2,1)S(1)}, bf16[8,384,128]{2,1,0:T(8,128)(2,1)S(1)}, u32[]{:S(2)}, u32[]{:S(2)}) collective-permute-start(bf16[8,384,128]{2,1,0:T(8,128)(2,1)S(1)} %get-tuple-element.215), channel_id=1, source_target_pairs={{0,1},{1,0},{2,3},{3,2},{4,5},{5,4},{6,7},{7,6},{8,9},{9,8},{10,11... | collective-permute-start | bytes 2359304 | tf_op jit(solution)/shard_map/ppermute | solution.py:1335
  77.5 3.7 %collective-permute-start.15 = (f32[2,8,128]{2,1,0:T(8,128)S(1)}, f32[2,8,128]{2,1,0:T(8,128)S(1)}, u32[]{:S(2)}, u32[]{:S(2)}) collective-permute-start(f32[2,8,128]{2,1,0:T(8,128)S(1)} %get-tuple-element.218.args_4_), channel_id=1, source_target_pairs={{0,16},{16,0},{1,17},{17,1},{2,18},{18,2},{3,19},{19,3},{4,20},{20... | collective-permute-start | bytes 24584 | tf_op jit(solution)/shard_map/ppermute | solution.py:1333
  81.4 7.7 %collective-permute-start.18 = (bf16[384,128]{1,0:T(8,128)(2,1)S(1)}, bf16[384,128]{1,0:T(8,128)(2,1)S(1)}, u32[]{:S(2)}, u32[]{:S(2)}) collective-permute-start(bf16[384,128]{1,0:T(8,128)(2,1)S(1)} %get-tuple-element.231), channel_id=1, source_target_pairs={{0,4},{2,6},{4,8},{6,10},{8,12},{10,14},{12,0},{14,2},{1,5},{3,7},... | collective-permute-start | bytes 294920 | tf_op jit(solution)/shard_map/ppermute | solution.py:1339
  81.5 16.6 %collective-permute-start.19 = (bf16[384,128]{1,0:T(8,128)(2,1)S(1)}, bf16[384,128]{1,0:T(8,128)(2,1)S(1)}, u32[]{:S(2)}, u32[]{:S(2)}) collective-permute-start(bf16[384,128]{1,0:T(8,128)(2,1)S(1)} %get-tuple-element.232), channel_id=1, source_target_pairs={{0,6},{2,8},{4,10},{6,12},{8,14},{10,0},{12,2},{14,4},{1,7},{3,9},... | collective-permute-start | bytes 294920 | tf_op jit(solution)/shard_map/ppermute | solution.py:1339
  83.4 20.8 %collective-permute-start.16 = (bf16[704,128]{1,0:T(8,128)(2,1)S(1)}, bf16[704,128]{1,0:T(8,128)(2,1)S(1)}, u32[]{:S(2)}, u32[]{:S(2)}) collective-permute-start(bf16[704,128]{1,0:T(8,128)(2,1)S(1)} %get-tuple-element.219), channel_id=1, source_target_pairs={{0,2},{2,4},{4,6},{6,8},{8,10},{10,12},{12,14},{14,0},{1,3},{3,5},... | collective-permute-start | bytes 540680 | tf_op jit(solution)/shard_map/ppermute | solution.py:1339
  85.4 18.8 %collective-permute-start.17 = (bf16[704,128]{1,0:T(8,128)(2,1)S(1)}, bf16[704,128]{1,0:T(8,128)(2,1)S(1)}, u32[]{:S(2)}, u32[]{:S(2)}) collective-permute-start(bf16[704,128]{1,0:T(8,128)(2,1)S(1)} %get-tuple-element.220), channel_id=1, source_target_pairs={{0,14},{2,0},{4,2},{6,4},{8,6},{10,8},{12,10},{14,12},{1,15},{3,1}... | collective-permute-start | bytes 540680 | tf_op jit(solution)/shard_map/ppermute | solution.py:1339
  88.1 13.0 %collective-permute-start.20 = (bf16[384,128]{1,0:T(8,128)(2,1)S(1)}, bf16[384,128]{1,0:T(8,128)(2,1)S(1)}, u32[]{:S(2)}, u32[]{:S(2)}) collective-permute-start(bf16[384,128]{1,0:T(8,128)(2,1)S(1)} %get-tuple-element.233), channel_id=1, source_target_pairs={{0,8},{2,10},{4,12},{6,14},{8,0},{10,2},{12,4},{14,6},{1,9},{3,11}... | collective-permute-start | bytes 294920 | tf_op jit(solution)/shard_map/ppermute | solution.py:1339
  89.1 12.0 %collective-permute-start.21 = (bf16[384,128]{1,0:T(8,128)(2,1)S(1)}, bf16[384,128]{1,0:T(8,128)(2,1)S(1)}, u32[]{:S(2)}, u32[]{:S(2)}) collective-permute-start(bf16[384,128]{1,0:T(8,128)(2,1)S(1)} %get-tuple-element.234), channel_id=1, source_target_pairs={{0,10},{2,12},{4,14},{6,0},{8,2},{10,4},{12,6},{14,8},{1,11},{3,13... | collective-permute-start | bytes 294920 | tf_op jit(solution)/shard_map/ppermute | solution.py:1339
  98.1 6.0 %collective-permute-start.22 = (bf16[384,128]{1,0:T(8,128)(2,1)S(1)}, bf16[384,128]{1,0:T(8,128)(2,1)S(1)}, u32[]{:S(2)}, u32[]{:S(2)}) collective-permute-start(bf16[384,128]{1,0:T(8,128)(2,1)S(1)} %get-tuple-element.235), channel_id=1, source_target_pairs={{0,12},{2,14},{4,0},{6,2},{8,4},{10,6},{12,8},{14,10},{1,13},{3,15... | collective-permute-start | bytes 294920 | tf_op jit(solution)/shard_map/ppermute | solution.py:1339
  104.3 1.5 %collective-permute-start.23 = (f32[384,128]{1,0:T(8,128)S(1)}, f32[384,128]{1,0:T(8,128)S(1)}, u32[]{:S(2)}, u32[]{:S(2)}) collective-permute-start(f32[384,128]{1,0:T(8,128)S(1)} %convert_add_fusion.args_0_), channel_id=1, source_target_pairs={{0,1},{1,0},{2,3},{3,2},{4,5},{5,4},{6,7},{7,6},{8,9},{9,8},{10,11... | collective-permute-start | bytes 589832 | tf_op jit(solution)/shard_map/ppermute | solution.py:1352

commit v4 on v3

--- a/solution.py
+++ b/solution.py
@@ -34,18 +34,22 @@
     return lax.broadcasted_iota(jnp.int32, shape, dim)
 
 
-def packed_places(parts, width):
-    row = jnp.concatenate(parts, axis=1)
-    high = row.astype(BF16).astype(F32)
-    rest = row - high
-    middle = rest.astype(BF16).astype(F32)
-    rows = jnp.concatenate([high, middle, rest - middle, jnp.zeros((13, row.shape[1]), F32)], axis=0)
-    return jnp.concatenate([rows, jnp.zeros((16, width - row.shape[1]), F32)], axis=1).astype(BF16)
-
-
-def unpacked_places(block, c, count):
+def packed_places(rows, width):
+    parts = []
+    for row in rows:
+        high = row.astype(BF16).astype(F32)
+        rest = row - high
+        middle = rest.astype(BF16).astype(F32)
+        parts += [high, middle, rest - middle]
+    gap = 16 - len(parts)
+    whole = jnp.concatenate(parts + [jnp.zeros((gap, rows[0].shape[1]), F32)], axis=0)
+    wide = [whole, jnp.zeros((16, width - whole.shape[1]), F32)]
+    return jnp.concatenate(wide, axis=1).astype(BF16)
+
+
+def unpacked_places(block, m, c, count):
     rows = block[:, c * count : (c + 1) * count].astype(F32)
-    return rows[0:1] + rows[1:2] + rows[2:3]
+    return rows[3 * m : 3 * m + 1] + rows[3 * m + 1 : 3 * m + 2] + rows[3 * m + 2 : 3 * m + 3]
 
 
 class Sizes:
@@ -82,11 +86,12 @@
     ref[...] = low_end * (1.0 - step) + step
 
 
-def edge_geometry(r, sz, coords, slots, low, high):
+def edge_geometry(r, sz, m, coords, slots):
     A, H, E, EB, K = sz.atoms, sz.halo, sz.rows, sz.edges, sz.slots
     lane = iota((8, LANES), 1)
     row = iota((8, LANES), 0)
     slab, last = lax.axis_index("space"), sz.space - 1
+    last_block = r.pack_low.shape[0] - 1
     spot = iota((1, LANES), 1)
     length_x = sz.space * A * 4.0 / H
     places = []
@@ -94,9 +99,9 @@
         places.append(
             jnp.concatenate(
                 [
-                    unpacked_places(low[4], c, H),
+                    unpacked_places(r.pack_low[last_block], m, c, H),
                     coords[c],
-                    unpacked_places(high[4], c, H),
+                    unpacked_places(r.pack_high[last_block], m, c, H),
                     jnp.zeros((1, LANES - E), F32),
                 ],
                 axis=1,
@@ -267,7 +272,7 @@
 def first_forward(r, sz, m, fetch):
     A, H, E, F, EB = sz.atoms, sz.halo, sz.rows, sz.width, sz.edges
     CG = sz.halves
-    r.s_low, r.s_high = r.pack_low.at[m], r.pack_high.at[m]
+    r.s_low, r.s_high = r.pack_low.at[4 * m : 4 * m + 4], r.pack_high.at[4 * m : 4 * m + 4]
     copies = early = []
     if fetch:
         rooms = Rooms(sz)
@@ -300,7 +305,7 @@
     for copy in copies[: len(early)]:
         copy.wait()
     coords = [r.s_norms[8 + c : 9 + c, 0:A] if fetch else r.coords[m, c] for c in range(3)]
-    edge_geometry(r, sz, coords, r.s_slots, r.s_low, r.s_high)
+    edge_geometry(r, sz, m, coords, r.s_slots)
 
     def tables(b, carry):
         write_edge_tables(r, sz, b, F32)
@@ -308,7 +313,11 @@
 
     lax.fori_loop(0, sz.blocks, tables, 0, unroll=2)
     own = r.s_own
-    node_part(r, sz, own, r.s_low, r.s_high, r.s_norms, r.s_wqkv)
+    xhat, scale = node_part(r, sz, own, r.s_low, r.s_high, r.s_norms, r.s_wqkv)
+    r.xhat[...] = xhat
+    r.scale[...] = jnp.broadcast_to(scale, r.scale.shape)
+    for cg in range(CG):
+        r.query_low[:, cg * LANES : (cg + 1) * LANES] = r.query[cg].astype(BF16)
     for copy in copies[len(early) :]:
         copy.wait()
     r.vproj[...] = dot(r.left[E : E + 3 * A, :], r.s_wvec[...])
@@ -354,14 +363,17 @@
     lax.fori_loop(0, sz.blocks // 2, pair, 0)
     third = sum(dot(r.units[b], r.third[b]) for b in range(sz.blocks))
     scalar_low = jnp.concatenate([r.sagg[cg] for cg in range(CG)], axis=1).astype(BF16)
-    r.o_scalar[...] = scalar_low
+    r.left[E + 3 * A : E + 4 * A, :] = scalar_low
     out_proj = dot(scalar_low, r.s_wout[...])
+    vec_dot = vector_dot(r, sz)
+    r.out_proj[...] = out_proj
+    r.vec_dot[...] = vec_dot
     vector_agg = [
         jnp.concatenate([r.vagg[c * CG + cg] for cg in range(CG)], axis=1)
         + third[c * A : (c + 1) * A, :]
         for c in range(3)
     ]
-    write_layer_output(r, sz, own, out_proj, vector_dot(r, sz), vector_agg)
+    write_layer_output(r, sz, own, out_proj, vec_dot, vector_agg)
 
 
 def edge_filters(r, sz, which):
@@ -370,19 +382,22 @@
     for m in which:
         w = SimpleNamespace(**vars(r))
         vars(w).update(vars(buffers(r, sz, m)))
-        edge_geometry(
-            w, sz, r.coords.at[m], r.slots.at[m], r.pack_low.at[m], r.pack_high.at[m]
-        )
+        edge_geometry(w, sz, m, r.coords.at[m], r.slots.at[m])
 
         def block(b, carry, w=w):
             write_edge_tables(w, sz, b, BF16)
             for part in range(4):
                 cols = slice(part * F, (part + 1) * F)
                 h = dot(r.smear_t[b], r.wh[:, cols])
-                t = jnp.tanh(h)
-                f = h + h * t
-                f, t = f.astype(BF16), t.astype(BF16)
-                slope = (1.0 + t) + f * (1.0 - t)
+                if part:
+                    h = h.astype(BF16)
+                up = 1.0 + jnp.tanh(h)
+                f = h * up
+                for cg in range(sz.halves):
+                    if part == 0 and hasattr(w, "key"):
+                        w.key[b, cg] = f[:, cg * LANES : (cg + 1) * LANES]
+                f, up = f.astype(BF16), up.astype(BF16)
+                slope = up + f * (2.0 - up)
                 for cg in range(sz.halves):
                     half = slice(cg * LANES, (cg + 1) * LANES)
                     w.silu[b, part * sz.halves + cg] = f[:, half]
@@ -398,19 +413,18 @@
     lane = iota((8, LANES), 1)
     row = iota((8, LANES), 0)
     halves = halves_of(sz)
-    if fwd:
-        own, low, high = r.own, r.low, r.high
-    else:
-        own, low, high = r.features.at[m, 0], r.pack_low.at[m], r.pack_high.at[m]
     wqkv, wvec, wout = r.wqkv.at[0], r.wvec.at[0], r.wout.at[0]
     write_constants(r, sz)
-    xhat, scale = node_part(r, sz, own, low, high, r.norms, wqkv)
     gain = r.norms[0:1, :]
-    left = r.left
     vp = r.vproj
-    vp[...] = dot(left[E : E + 3 * A, :], wvec[...])
-    for cg in range(CG):
-        r.query_low[:, halves[cg]] = r.query[cg].astype(BF16)
+    if fwd:
+        own, left = r.own, r.left
+        xhat, scale = node_part(r, sz, own, r.low, r.high, r.norms, wqkv)
+        vp[...] = dot(left[E : E + 3 * A, :], wvec[...])
+        for cg in range(CG):
+            r.query_low[:, halves[cg]] = r.query[cg].astype(BF16)
+    else:
+        xhat, scale = r.xhat[...], r.scale[:, 0:1]
 
     if fwd:
         r.sagg[...] = jnp.zeros_like(r.sagg)
@@ -424,12 +438,10 @@
                 return r.silu[b, part * CG + cg, at, :]
 
             def keys(cg, at, cols, near_rows):
-                product = r.query[cg] * r.kv[cg, near_rows, :] * filters(0, cg, at).astype(F32)
-                coarse = product.astype(BF16)
-                return coarse, (product - coarse.astype(F32)).astype(BF16)
-
-            coarse, fine = stacked(sz, first, keys)
-            score = dot(coarse, r.heads[...]) + dot(fine, r.heads[...])
+                product = r.query[cg] * r.kv[cg, near_rows, :] * r.key[b, cg, at, :]
+                return [product.astype(BF16)]
+
+            score = dot(*stacked(sz, first, keys), r.heads[...])
             for cg in range(CG):
                 r.score[b, cg] = score[:, halves[cg]].astype(BF16)
 
@@ -454,13 +466,13 @@
             r.sagg[...] += dot(r.fold[...], *stacked(sz, first, scalars))
             return carry
 
-        lax.fori_loop(0, NB, forward_block, 0, unroll=4)
+        lax.fori_loop(0, NB, forward_block, 0, unroll=8)
         scalar_low = r.sagg[...].astype(BF16)
+        left[E + 3 * A : E + 4 * A, :] = scalar_low
+        out_proj = dot(scalar_low, wout[...])
+        vec_dot = vector_dot(r, sz)
     else:
-        scalar_low = r.scalar_in[...]
-    left[E + 3 * A : E + 4 * A, :] = scalar_low
-    out_proj = dot(scalar_low, wout[...])
-    vec_dot = vector_dot(r, sz)
+        out_proj, vec_dot = r.out_proj, r.vec_dot[...]
     if fwd:
         vector_agg = [r.vagg[c] + r.uagg[c * A : (c + 1) * A, :] for c in range(3)]
         write_layer_output(r, sz, own, out_proj, vec_dot, vector_agg)
@@ -493,6 +505,10 @@
     for total in (r.gnear, r.gq, r.gfilt):
         total[...] = jnp.zeros_like(total)
 
+    scores = r.score if fwd else r.score_here
+    if not fwd:
+        scores[...] = r.score[...]
+
     def backward_block(b, carry):
         first = first_row(b)
         base = pl.multiple_of(first // SUBLANES * SUBLANES, SUBLANES)
@@ -547,7 +563,7 @@
             )
 
         def attention(cg, at, cols, near_rows):
-            s = r.score[b, cg, at, :]
+            s = scores[b, cg, at, :]
             t = jnp.tanh(s)
             up = 1.0 + t
             act = s * up
@@ -565,9 +581,9 @@
             return made + [g_edge * f, g_edge * (value * slope)]
 
         g_act, g_query, g_key, pre[0], g_value, pre[1] = stacked(sz, first, attention)
+        collect(1, g_value)
+        collect(0, g_key)
         r.gq[...] += dot(r.fold[...], g_query)
-        collect(0, g_key)
-        collect(1, g_value)
         g_cut = dot(jnp.ones((16, F), BF16), g_act, 1, 1)[0:1, :] * (2.0 * HEADS / F)
         g_smear = jnp.zeros((sz.basis, EB), F32)
         for part in range(4):
@@ -646,6 +662,9 @@
 
 
 FACTORS = ("left", "gproj", "gvproj", "gout", "gfilt", "gnorm")
+HANDED = (
+    "query_low", "kv", "vec", "vproj", "xhat", "scale", "out_proj", "vec_dot", "score"
+)
 BORDERS = ("rim_low", "rim_high", "gplaces")
 
 
@@ -681,7 +700,15 @@
         fresh=((4, A, F), BF16),
         head=((4, sent, F), BF16),
         tail=((4, sent, F), BF16),
-        o_scalar=((A, F), BF16),
+        left=((sz.factors, F), BF16),
+        query_low=((A, F), BF16),
+        kv=((4 * CG, E, LANES), F32),
+        vec=((3 * CG, E, LANES), F32),
+        vproj=((3 * A, 3 * F), F32),
+        xhat=((E, F), F32),
+        scale=((E, LANES), F32),
+        out_proj=((A, 3 * F), F32),
+        vec_dot=((A, F), F32),
         score=((NB, CG, EB, LANES), BF16),
     )
     fetched = dict(
@@ -696,11 +723,7 @@
     )
     outs = SimpleNamespace(**{k: shape(*v) for k, v in results.items()})
     scratch = dict(
-        left=((sz.factors, F), BF16),
         query=((CG, A, LANES), F32),
-        kv=((4 * CG, E, LANES), F32),
-        vec=((3 * CG, E, LANES), F32),
-        vproj=((3 * A, 3 * F), F32),
         heads=((F, F), BF16),
         diag=((A, EB), F32),
         geo=((10, 8, EB), F32),
@@ -735,6 +758,8 @@
         silu=shape((NB, 4 * CG, EB, LANES), BF16),
         slope=shape((NB, 4 * CG, EB, LANES), BF16),
     )
+    if role == SECOND:
+        outs.update(key=shape((NB, CG, EB, LANES), F32))
     scratch = dict(
         diag=((A, EB), F32),
         centres=((sz.basis, EB), F32),
@@ -761,7 +786,6 @@
         rim_low=shape((4, H, F), BF16),
         rim_high=shape((4, H, F), BF16),
         gplaces=shape((8, LANES), F32),
-        left=shape((sz.factors, F), BF16),
         gproj=shape((E, 5 * F), BF16),
         gvproj=shape((3 * A, 3 * F), BF16),
         gout=shape((A, 3 * F), BF16),
@@ -769,11 +793,6 @@
         gnorm=shape((8, F), F32),
     )
     scratch = dict(
-        query=((CG, A, LANES), F32),
-        query_low=((A, F), BF16),
-        kv=((4 * CG, E, LANES), F32),
-        vec=((3 * CG, E, LANES), F32),
-        vproj=((3 * A, 3 * F), F32),
         heads=((F, F), BF16),
         diag=((A, EB), F32),
         fold=((A, EB), BF16),
@@ -787,17 +806,38 @@
         gcut=((8, EB), F32),
         gshrink=((8, EB), F32),
     )
+    if not fwd:
+        scratch.update(score_here=((NB, CG, EB, LANES), BF16))
     if fwd:
         outs.fresh = shape((4, A, F), BF16)
+        outs.left = shape((sz.factors, F), BF16)
         scratch.update(
+            query=((CG, A, LANES), F32),
+            query_low=((A, F), BF16),
+            kv=((4 * CG, E, LANES), F32),
+            vec=((3 * CG, E, LANES), F32),
+            vproj=((3 * A, 3 * F), F32),
             score=((NB, CG, EB, LANES), BF16), sagg=((A, F), F32), vagg=((3, A, F), F32), uagg=((3 * A, F), F32)
         )
+    if fwd and m:
+        outs.all_places = shape((m + 1, 8, LANES), F32)
+        for i, made in enumerate(border_sets):
+            setattr(arrays, f"gplaces_{i}", (made.gplaces, VMEM))
+
+        def layer(r):
+            both_ways(r, sz, m, fwd)
+            for i in range(m):
+                r.all_places[i] = getattr(r, f"gplaces_{i}")[...]
+            r.all_places[m] = r.gplaces[...]
+
+        return call(layer, arrays, outs, scratch, SECOND)
     if not border_sets:
         role = SECOND if fwd else FIRST
         return call(lambda r: both_ways(r, sz, m, fwd), arrays, outs, scratch, role)
     count = m + 1
     outs.up, outs.down = shape((count, 4, H, F), BF16), shape((count, 4, H, F), BF16)
     outs.moved = shape((count, 8, LANES), F32)
+    outs.total = shape((count, 8, LANES), F32)
     for role, sets in enumerate(border_sets):
         for i, made in enumerate(sets):
             for name in BORDERS:
@@ -812,6 +852,7 @@
             r.up[i] = high[...]
             r.down[i] = low[...]
             r.moved[i] = places[...]
+            r.total[i] = places[...] + r.early[i] if role == FIRST else places[...]
 
     def body(r):
         @pl.when(lax.axis_index("section") == FIRST)
@@ -832,8 +873,8 @@
         moves = [(r.coords, r.s_coords)]
         for m in range(count):
             moves += [
-                (r.features.at[m, 0, :, A - H : A, :], r.up.at[m, 0:4]),
-                (r.features.at[m, 0, :, 0:H, :], r.down.at[m, 0:4]),
+                (r.features.at[m, 0, :, A - H : A, :], r.up.at[4 * m : 4 * m + 4]),
+                (r.features.at[m, 0, :, 0:H, :], r.down.at[4 * m : 4 * m + 4]),
             ]
         copies = [
             pltpu.make_async_copy(source, target, r.sems.at[i])
@@ -842,13 +883,16 @@
         for copy in copies:
             copy.start()
         copies[0].wait()
-        for m in range(count):
-            r.up[m, 4] = packed_places([r.s_coords[m, c][:, A - H :] for c in range(3)], F)
-            r.down[m, 4] = packed_places([r.s_coords[m, c][:, :H] for c in range(3)], F)
+        for target, ends in ((r.up, slice(A - H, A)), (r.down, slice(0, H))):
+            rows = []
+            for m in range(count):
+                parts = [r.s_coords[m, c][:, ends] for c in range(3)]
+                rows.append(jnp.concatenate(parts, axis=1))
+            target[4 * count] = packed_places(rows, F)
         for copy in copies[1:]:
             copy.wait()
 
-    shape = jax.ShapeDtypeStruct((count, 5, H, F), BF16)
+    shape = jax.ShapeDtypeStruct((4 * count + 1, H, F), BF16)
     return call(
         body,
         SimpleNamespace(features=(features, HBM), coords=(coords, HBM)),
@@ -1048,16 +1092,16 @@
     )
 
 
-def border_rows(sz, m, index):
-    start = sz.packed + (m * 5 + index) * 2 * sz.halo
+def border_rows(sz, index):
+    start = sz.packed + index * 2 * sz.halo
     return [slice(start + i * sz.halo, start + (i + 1) * sz.halo) for i in range(2)]
 
 
-def border_block(sz, ref, m, index):
-    return jnp.concatenate([ref[rows, :] for rows in border_rows(sz, m, index)], axis=1)
-
-
-def piece_call(sz, stay, recv, up, down, moved, other):
+def border_block(sz, ref, index):
+    return jnp.concatenate([ref[rows, :] for rows in border_rows(sz, index)], axis=1)
+
+
+def piece_call(sz, stay, recv, up, down, total, late):
     A, H, E, F = sz.atoms, sz.halo, sz.rows, sz.width
     count = up.shape[0]
     half = F // 2
@@ -1066,29 +1110,32 @@
         slab, space = lax.axis_index("space"), sz.space
         for hop in range(space):
             k = lax.rem(slab + hop, space)
-            total = r.stay[k] + r.recv[k].astype(F32)
+            share = r.stay[k] + r.recv[k].astype(F32)
             target = getattr(r, f"hop{hop}")
-            target[0 : sz.packed, :] = total.astype(target.dtype)
+            target[0 : sz.packed, :] = share.astype(target.dtype)
+        places = [r.total[m] + r.late[m] for m in range(count)]
+        ends = (
+            (r.hop1, r.up, slice(H + A, E)),
+            (getattr(r, f"hop{space - 1}"), r.down, slice(0, H)),
+        )
+        for target, border, lanes in ends:
+            rows = []
+            for m in range(count):
+                parts = [places[m][c : c + 1, lanes] for c in range(3)]
+                rows.append(jnp.concatenate(parts, axis=1))
+            blocks = [border[m, index] for m in range(count) for index in range(4)]
+            for index, block in enumerate(blocks + [packed_places(rows, F)]):
+                first, second = border_rows(sz, index)
+                target[first, :] = block[:, :half]
+                target[second, :] = block[:, half:]
         for m in range(count):
-            places = r.moved[m] + r.other[m]
-            rows = [places[c : c + 1, :] for c in range(3)]
-            ends = (
-                (r.hop1, r.up, [row[:, H + A : E] for row in rows]),
-                (getattr(r, f"hop{space - 1}"), r.down, [row[:, 0:H] for row in rows]),
-            )
-            for target, border, part in ends:
-                blocks = [border[m, index] for index in range(4)] + [packed_places(part, F)]
-                for index, block in enumerate(blocks):
-                    first, second = border_rows(sz, m, index)
-                    target[first, :] = block[:, :half]
-                    target[second, :] = block[:, half:]
             for c in range(3):
-                r.mine[m, c] = rows[c][:, H : H + A]
+                r.mine[m, c] = places[m][c : c + 1, H : H + A]
 
     shape = jax.ShapeDtypeStruct
     outs = {
         f"hop{hop}": shape(
-            (sz.packed + (10 * H * count if hop in (1, sz.space - 1) else 0), half),
+            (sz.packed + ((8 * count + 2) * H if hop in (1, sz.space - 1) else 0), half),
             BF16 if hop else F32,
         )
         for hop in range(sz.space)
@@ -1101,8 +1148,8 @@
             recv=(recv, VMEM),
             up=(up, VMEM),
             down=(down, VMEM),
-            moved=(moved, VMEM),
-            other=(other, VMEM),
+            total=(total, VMEM),
+            late=(late, VMEM),
         ),
         SimpleNamespace(**outs),
         {},
@@ -1126,16 +1173,16 @@
             r.outputs[0, m, 0] = getattr(r, f"fresh_{role}_{m}")[...]
             whole = getattr(r, f"back_{role}_{m}")
             for index in range(4):
-                low = border_block(sz, r.low, m, index).astype(F32)
-                high = border_block(sz, r.high, m, index).astype(F32)
+                low = border_block(sz, r.low, 4 * m + index).astype(F32)
+                high = border_block(sz, r.high, 4 * m + index).astype(F32)
                 r.grads[0, m, 0, index, 0:H, :] = whole[index, 0:H, :] + low
                 r.grads[0, m, 0, index, H : A - H, :] = whole[index, H : A - H, :]
                 r.grads[0, m, 0, index, A - H :, :] = whole[index, A - H :, :] + high
             for c in range(3):
                 edge = [
-                    unpacked_places(border_block(sz, r.low, m, 4), c, H),
+                    unpacked_places(border_block(sz, r.low, 4 * count), m, c, H),
                     jnp.zeros((1, A - 2 * H), F32),
-                    unpacked_places(border_block(sz, r.high, m, 4), c, H),
+                    unpacked_places(border_block(sz, r.high, 4 * count), m, c, H),
                 ]
                 r.places[m, c] = r.mine[m, c] + jnp.concatenate(edge, axis=1)
 
@@ -1297,10 +1344,11 @@
                 (other.geo, filters[SECOND][m].geo)
             )
         arrays = both_inputs(m, SECOND)
+        arrays.key = (filters[SECOND][m].key, VMEM)
         own, low, high = sent[m]
         arrays.own, arrays.low, arrays.high = (own, VMEM), (low, VMEM), (high, VMEM)
         arrays.cotangent = (cotangent, VMEM)
-        second = both_call(sz, m, True, arrays)
+        second = both_call(sz, m, True, arrays, seconds)
         seconds.append(second)
         if m == 0:
             later = geometry_inputs()
@@ -1320,20 +1368,22 @@
     thirds = []
     for m in range(micro_count):
         arrays = both_inputs(m, FIRST)
-        arrays.pack_low, arrays.pack_high = (pack_low, VMEM), (pack_high, VMEM)
-        arrays.features = (features, VMEM)
-        arrays.scalar_in = (firsts[m].o_scalar, VMEM)
-        arrays.score = (firsts[m].score, VMEM)
+        for name in HANDED:
+            setattr(arrays, name, (getattr(firsts[m], name), VMEM))
         inc, inc_low, inc_high = returned[m]
         arrays.inc, arrays.inc_low, arrays.inc_high = (inc, VMEM), (inc_low, VMEM), (inc_high, VMEM)
         sets = (thirds, seconds) if m == micro_count - 1 else ()
-        thirds.append(both_call(sz, m, False, arrays, sets))
+        if sets:
+            arrays.early = (lax.ppermute(seconds[-1].all_places, both, back), VMEM)
+        third = both_call(sz, m, False, arrays, sets)
+        third.left = firsts[m].left
+        thirds.append(third)
 
     last = thirds[-1]
-    other = lax.ppermute(last.moved, "section", [(0, 1), (1, 0)])
+    late = lax.ppermute(last.moved, both, forth)
     shares = gradient_call(sz, (thirds, seconds))
     recv = lax.ppermute(shares.send, "dp", [(0, 1), (1, 0)])
-    (total, *pieces), mine = piece_call(sz, shares.stay, recv, last.up, last.down, last.moved, other
+    (total, *pieces), mine = piece_call(sz, shares.stay, recv, last.up, last.down, last.total, late
     )
     received = [
         lax.ppermute(piece, "space", [(i, (i + hop) % space) for i in range(space)])

time: 107 us -> 106 us (level)
  Pallas kernels: 49.7 us -> 48.4 us
    ppermute x2, waiting for transfers between devices: 5.34 us -> 1.89 us  [on_device(): lax.ppermute(rim_high, both, back_up)]
    ppermute x1 -> x2, starting transfers between devices: 0.07 us -> 2.58 us  [the longest x1 1.29 us: on_device(): arrays.early = (lax.ppermute(seconds[-1].all_places, both, back), VMEM)]
    ppermute x7, waiting for transfers between devices: 13.3 us -> 15.6 us  [on_device(): lax.ppermute(piece, 'space', [(i, (i + hop) % space) for i in range(space)])]
    ppermute x7, starting transfers between devices: 9.45 us -> 7.23 us  [on_device(): lax.ppermute(piece, 'space', [(i, (i + hop) % space) for i in range(space)])]
    pallas_call x14, Pallas kernels: 49.7 us -> 48.4 us  [call(): pl.pallas_call(kernel, out_shape=list(outs.values()), in_specs=[spec for...]
    ppermute x1 -> x2, waiting for transfers between devices: 3.64 us -> 4.76 us  [the longest x1 3.41 us: on_device(): arrays.early = (lax.ppermute(seconds[-1].all_places, both, back), VMEM)]
  transfers between devices with their start and end apart: 24 -> 25, of which waited for: 9 -> 9; matrix products, arithmetic and copies ran while one was open for 0% -> 0% of each run, Pallas kernels for 26% -> 26%
where the time goes in v4:
time: 106 us; the launch traced here: 105 us
  Pallas kernels  48.4 us (46%)
  starting transfers between devices  31.6 us (30%)
  waiting for transfers between devices  24.1 us (23%)
  between operations  1.06 us (1%)
    pallas_call x14, Pallas kernels, call(): pl.pallas_call(kernel, out_shape=list(outs.values()), in_specs=[spec for...  48.4 us
    ppermute x7, waiting for transfers between devices, on_device(): lax.ppermute(piece, 'space', [(i, (i + hop) % space) for i in range(space)])  15.6 us
    ppermute x7, starting transfers between devices, on_device(): lax.ppermute(piece, 'space', [(i, (i + hop) % space) for i in range(space)])  7.23 us
    ppermute x1, waiting for transfers between devices, on_device(): arrays.early = (lax.ppermute(seconds[-1].all_places, both, back), VMEM)  3.41 us
    ppermute x1, starting transfers between devices, on_device(): pack_high = lax.ppermute(borders.down, 'space', down)  3.1 us
    ppermute x1, starting transfers between devices, on_device(): pack_low = lax.ppermute(borders.up, 'space', up)  3.02 us
    ppermute x2, starting transfers between devices, on_device(): lax.ppermute(first.fresh, both, forth)  2.59 us
    ppermute x2, starting transfers between devices, on_device(): lax.ppermute(first.tail, both, forth_up)  2.59 us
  transfers between devices with their start and end apart: 25, of which 9 were waited for; matrix products, arithmetic and copies ran while one was open for 0% of the time, Pallas kernels for 26%

profile of v4, /device:TPU:0, one launch (start us, length us, event | category | flops | bytes accessed | tf_op | source)
XLA Modules:
  0.0 105.3 jit_solution(16959340413511512115)
XLA Ops:
  0.6 1.5 %shard_map.187 = (bf16[9,16,256]{2,1,0:T(8,128)(2,1)}, bf16[9,16,256]{2,1,0:T(8,128)(2,1)}) custom-call(bf16[2,1,4,64,256]{4,3,2,1,0:T(8,128)(2,1)} %args_5_.6, f32[2,3,1,64]{3,2,1,0:T(1,128)} %bitcast.5), custom_call_target="tpu_custom_call" | custom-call | tf_op jit(solution)/shard_map/pallas_call | solution.py:682
  2.2 3.0 %collective-permute-start = (bf16[9,16,256]{2,1,0:T(8,128)(2,1)}, bf16[9,16,256]{2,1,0:T(8,128)(2,1)S(1)}, u32[]{:S(2)}, u32[]{:S(2)}) collective-permute-start(bf16[9,16,256]{2,1,0:T(8,128)(2,1)} %get-tuple-element.144), channel_id=1, source_target_pairs={{0,2},{2,4},{4,6},{6,8},{8,10},{10,12},{12,14},{14,0},{1,3},{3,5},... | collective-permute-start | bytes 221192 | tf_op jit(solution)/shard_map/ppermute | solution.py:1276
  5.2 3.1 %collective-permute-start.1 = (bf16[9,16,256]{2,1,0:T(8,128)(2,1)}, bf16[9,16,256]{2,1,0:T(8,128)(2,1)S(1)}, u32[]{:S(2)}, u32[]{:S(2)}) collective-permute-start(bf16[9,16,256]{2,1,0:T(8,128)(2,1)} %get-tuple-element.145), channel_id=1, source_target_pairs={{2,0},{4,2},{6,4},{8,6},{10,8},{12,10},{14,12},{0,14},{3,1},{5,3},... | collective-permute-start | bytes 221192 | tf_op jit(solution)/shard_map/ppermute | solution.py:1277
  8.3 3.0 %shard_map.188 = (f32[2,104,128]{2,1,0:T(8,128)}, f32[8,256]{1,0:T(8,128)}, bf16[32,1024]{1,0:T(8,128)(2,1)}, bf16[20480,1280]{1,0:T(8,128)(2,1)}, f32[51200,256]{1,0:T(8,128)}) custom-call(bf16[2,1,4,64,256]{4,3,2,1,0:T(8,128)(2,1)} %args_5_.6, f32[2,3,1,64]{3,2,1,0:T(1,128)} %bitcast.6, s32[2,1,32,64]{3,2,1,0:T(8,128)} %args_2_.8, ...), custom_call_target="tpu_custom_call" | custom-call | tf_op jit(solution)/shard_map/pallas_call | solution.py:682
  11.3 0.0 collective-permute-done.args_0_
  11.3 0.0 collective-permute-done.1.args_1_
  11.3 0.0 copy-start.1
  11.4 0.0 copy-start.2
  11.4 0.0 copy-start.3
  11.4 0.0 copy-start.4
  11.4 0.0 copy-start.6
  11.4 0.0 copy-start.7
  11.4 0.0 copy-start.8
  11.4 0.0 copy-start.5
  11.4 8.1 %shard_map.189 = (bf16[4,64,256]{2,1,0:T(8,128)(2,1)S(1)}, bf16[4,16,256]{2,1,0:T(8,128)(2,1)S(1)}, bf16[4,16,256]{2,1,0:T(8,128)(2,1)S(1)}, bf16[384,256]{1,0:T...) custom-call(bf16[9,16,256]{2,1,0:T(8,128)(2,1)S(1)} %collective-perm, ...), custom_call_target="tpu_custom_call" | custom-call | tf_op jit(solution)/shard_map/pallas_call | solution.py:682
  19.5 1.3 %collective-permute-start.2 = (bf16[4,64,256]{2,1,0:T(8,128)(2,1)S(1)}, bf16[4,64,256]{2,1,0:T(8,128)(2,1)S(1)}, u32[]{:S(2)}, u32[]{:S(2)}) collective-permute-start(bf16[4,64,256]{2,1,0:T(8,128)(2,1)S(1)} %get-tuple-element.161.args_3_), channel_id=1, source_target_pairs={{0,16},{2,18},{4,20},{6,22},{8,24},{10,26},{12,28},{14,30},{1,17},... | collective-permute-start | bytes 393224 | tf_op jit(solution)/shard_map/ppermute | solution.py:1319
  20.8 1.3 %collective-permute-start.3 = (bf16[4,16,256]{2,1,0:T(8,128)(2,1)S(1)}, bf16[4,16,256]{2,1,0:T(8,128)(2,1)S(1)}, u32[]{:S(2)}, u32[]{:S(2)}) collective-permute-start(bf16[4,16,256]{2,1,0:T(8,128)(2,1)S(1)} %get-tuple-element.162), channel_id=1, source_target_pairs={{0,18},{2,20},{4,22},{6,24},{8,26},{10,28},{12,30},{14,16},{1,19},... | collective-permute-start | bytes 98312 | tf_op jit(solution)/shard_map/ppermute | solution.py:1320
  22.1 1.3 %collective-permute-start.4 = (bf16[4,16,256]{2,1,0:T(8,128)(2,1)S(1)}, bf16[4,16,256]{2,1,0:T(8,128)(2,1)S(1)}, u32[]{:S(2)}, u32[]{:S(2)}) collective-permute-start(bf16[4,16,256]{2,1,0:T(8,128)(2,1)S(1)} %get-tuple-element.163), channel_id=1, source_target_pairs={{2,16},{4,18},{6,20},{8,22},{10,24},{12,26},{14,28},{0,30},{3,17},... | collective-permute-start | bytes 98312 | tf_op jit(solution)/shard_map/ppermute | solution.py:1321
  23.5 6.7 %shard_map.190 = (bf16[4,64,256]{2,1,0:T(8,128)(2,1)S(1)}, bf16[4,64,256]{2,1,0:T(8,128)(2,1)S(1)}, bf16[4,64,256]{2,1,0:T(8,128)(2,1)S(1)}, bf16[384,256]{1,0:T...) custom-call(bf16[9,16,256]{2,1,0:T(8,128)(2,1)S(1)} %collective-perm, ...), custom_call_target="tpu_custom_call" | custom-call | tf_op jit(solution)/shard_map/pallas_call | solution.py:682
  30.2 1.3 %collective-permute-start.9 = (bf16[4,64,256]{2,1,0:T(8,128)(2,1)S(1)}, bf16[4,64,256]{2,1,0:T(8,128)(2,1)S(1)}, u32[]{:S(2)}, u32[]{:S(2)}) collective-permute-start(bf16[4,64,256]{2,1,0:T(8,128)(2,1)S(1)} %get-tuple-element.194), channel_id=1, source_target_pairs={{0,18},{2,20},{4,22},{6,24},{8,26},{10,28},{12,30},{14,16},{1,19},... | collective-permute-start | bytes 393224 | tf_op jit(solution)/shard_map/ppermute | solution.py:1320
  31.5 1.3 %collective-permute-start.8 = (bf16[4,64,256]{2,1,0:T(8,128)(2,1)S(1)}, bf16[4,64,256]{2,1,0:T(8,128)(2,1)S(1)}, u32[]{:S(2)}, u32[]{:S(2)}) collective-permute-start(bf16[4,64,256]{2,1,0:T(8,128)(2,1)S(1)} %get-tuple-element.193.args_5_), channel_id=1, source_target_pairs={{0,16},{2,18},{4,20},{6,22},{8,24},{10,26},{12,28},{14,30},{1,17},... | collective-permute-start | bytes 393224 | tf_op jit(solution)/shard_map/ppermute | solution.py:1319
  32.8 1.3 %collective-permute-start.10 = (bf16[4,64,256]{2,1,0:T(8,128)(2,1)S(1)}, bf16[4,64,256]{2,1,0:T(8,128)(2,1)S(1)}, u32[]{:S(2)}, u32[]{:S(2)}) collective-permute-start(bf16[4,64,256]{2,1,0:T(8,128)(2,1)S(1)} %get-tuple-element.195), channel_id=1, source_target_pairs={{2,16},{4,18},{6,20},{8,22},{10,24},{12,26},{14,28},{0,30},{3,17},... | collective-permute-start | bytes 393224 | tf_op jit(solution)/shard_map/ppermute | solution.py:1321
  34.1 0.0 collective-permute-done.4.args_14_
  34.1 0.0 collective-permute-done.2.args_12_
  34.2 1.3 %collective-permute-start.5 = (bf16[4,64,256]{2,1,0:T(8,128)(2,1)S(1)}, bf16[4,64,256]{2,1,0:T(8,128)(2,1)S(1)}, u32[]{:S(2)}, u32[]{:S(2)}) collective-permute-start(bf16[4,64,256]{2,1,0:T(8,128)(2,1)S(1)} %get-tuple-element.183), channel_id=1, source_target_pairs={{16,0},{18,2},{20,4},{22,6},{24,8},{26,10},{28,12},{30,14},{17,1},... | collective-permute-start | bytes 393224 | tf_op jit(solution)/shard_map/ppermute | solution.py:1364
  35.5 1.3 %collective-permute-start.6 = (bf16[4,16,256]{2,1,0:T(8,128)(2,1)S(1)}, bf16[4,16,256]{2,1,0:T(8,128)(2,1)S(1)}, u32[]{:S(2)}, u32[]{:S(2)}) collective-permute-start(bf16[4,16,256]{2,1,0:T(8,128)(2,1)S(1)} %get-tuple-element.184.args_28_), channel_id=1, source_target_pairs={{16,2},{18,4},{20,6},{22,8},{24,10},{26,12},{28,14},{30,0},{17,3},... | collective-permute-start | bytes 98312 | tf_op jit(solution)/shard_map/ppermute | solution.py:1365
  36.8 1.4 %collective-permute-done.9.args_13_ = bf16[4,64,256]{2,1,0:T(8,128)(2,1)S(1)} collective-permute-done((bf16[4,64,256]{2,1,0:T(8,128)(2,1)S(1)}, bf16[4,64,256]{2,1,0:T(8,128)(2,1)S(1)}, u32[]{:S(2)}, u32[]{:S(2)}) %collective-permute-start.9) | collective-permute-done | bytes 131104 | tf_op jit(solution)/shard_map/ppermute | solution.py:1320
  38.2 1.3 %collective-permute-start.7 = (bf16[4,16,256]{2,1,0:T(8,128)(2,1)S(1)}, bf16[4,16,256]{2,1,0:T(8,128)(2,1)S(1)}, u32[]{:S(2)}, u32[]{:S(2)}) collective-permute-start(bf16[4,16,256]{2,1,0:T(8,128)(2,1)S(1)} %get-tuple-element.185.args_27_), channel_id=1, source_target_pairs={{18,0},{20,2},{22,4},{24,6},{26,8},{28,10},{30,12},{16,14},{19,1},... | collective-permute-start | bytes 98312 | tf_op jit(solution)/shard_map/ppermute | solution.py:1366
  39.5 6.8 %shard_map.193 = (f32[10,8,256]{2,1,0:T(8,128)S(1)}, bf16[8,32,256]{2,1,0:T(8,128)(2,1)S(1)}, bf16[8,256,128]{2,1,0:T(8,128)(2,1)S(1)}, bf16[8,192,256]{2,1,0:T(...) custom-call(bf16[9,16,256]{2,1,0:T(8,128)(2,1)S(1)} %collective-perm, ...), custom_call_target="tpu_custom_call" | custom-call | tf_op jit(solution)/shard_map/pallas_call | solution.py:682
  46.3 0.0 collective-permute-done.8.args_12_
  46.3 0.0 collective-permute-done.10.args_14_
  46.3 0.1 shard_map.194
  46.4 1.9 %collective-permute-done.6.args_21_ = bf16[4,16,256]{2,1,0:T(8,128)(2,1)S(1)} collective-permute-done((bf16[4,16,256]{2,1,0:T(8,128)(2,1)S(1)}, bf16[4,16,256]{2,1,0:T(8,128)(2,1)S(1)}, u32[]{:S(2)}, u32[]{:S(2)}) %collective-permute-start.6) | collective-permute-done | bytes 32800 | tf_op jit(solution)/shard_map/ppermute | solution.py:1365
  48.3 1.3 %collective-permute-start.11 = (bf16[4,64,256]{2,1,0:T(8,128)(2,1)S(1)}, bf16[4,64,256]{2,1,0:T(8,128)(2,1)S(1)}, u32[]{:S(2)}, u32[]{:S(2)}) collective-permute-start(bf16[4,64,256]{2,1,0:T(8,128)(2,1)S(1)} %get-tuple-element.224), channel_id=1, source_target_pairs={{16,0},{18,2},{20,4},{22,6},{24,8},{26,10},{28,12},{30,14},{17,1},... | collective-permute-start | bytes 393224 | tf_op jit(solution)/shard_map/ppermute | solution.py:1364
  49.5 1.3 %collective-permute-start.12 = (bf16[4,16,256]{2,1,0:T(8,128)(2,1)S(1)}, bf16[4,16,256]{2,1,0:T(8,128)(2,1)S(1)}, u32[]{:S(2)}, u32[]{:S(2)}) collective-permute-start(bf16[4,16,256]{2,1,0:T(8,128)(2,1)S(1)} %get-tuple-element.225.args_31_), channel_id=1, source_target_pairs={{16,2},{18,4},{20,6},{22,8},{24,10},{26,12},{28,14},{30,0},{17,3},... | collective-permute-start | bytes 98312 | tf_op jit(solution)/shard_map/ppermute | solution.py:1365
  50.8 1.3 %collective-permute-start.13 = (bf16[4,16,256]{2,1,0:T(8,128)(2,1)S(1)}, bf16[4,16,256]{2,1,0:T(8,128)(2,1)S(1)}, u32[]{:S(2)}, u32[]{:S(2)}) collective-permute-start(bf16[4,16,256]{2,1,0:T(8,128)(2,1)S(1)} %get-tuple-element.226.args_30_), channel_id=1, source_target_pairs={{18,0},{20,2},{22,4},{24,6},{26,8},{28,10},{30,12},{16,14},{19,1},... | collective-permute-start | bytes 98312 | tf_op jit(solution)/shard_map/ppermute | solution.py:1366
  52.1 1.3 %collective-permute-start.14 = (f32[2,8,128]{2,1,0:T(8,128)S(1)}, f32[2,8,128]{2,1,0:T(8,128)S(1)}, u32[]{:S(2)}, u32[]{:S(2)}) collective-permute-start(f32[2,8,128]{2,1,0:T(8,128)S(1)} %get-tuple-element.227), channel_id=1, source_target_pairs={{16,0},{18,2},{20,4},{22,6},{24,8},{26,10},{28,12},{30,14},{17,1},... | collective-permute-start | bytes 24584 | tf_op jit(solution)/shard_map/ppermute | solution.py:1377
  53.4 9.7 %shard_map.195 = (f32[4,64,256]{2,1,0:T(8,128)S(1)}, bf16[4,64,256]{2,1,0:T(8,128)(2,1)}, bf16[4,16,256]{2,1,0:T(8,128)(2,1)S(1)}, bf16[4,16,256]{2,1,0:T(8,128)...) custom-call(f32[8,256]{1,0:T(8,128)S(1)} %copy-done.7, ...), custom_call_target="tpu_custom_call" | custom-call | tf_op jit(solution)/shard_map/pallas_call | solution.py:682
  63.1 3.4 %collective-permute-done.14.args_23_ = f32[2,8,128]{2,1,0:T(8,128)S(1)} collective-permute-done((f32[2,8,128]{2,1,0:T(8,128)S(1)}, f32[2,8,128]{2,1,0:T(8,128)S(1)}, u32[]{:S(2)}, u32[]{:S(2)}) %collective-permute-start.14) | collective-permute-done | bytes 8224 | tf_op jit(solution)/shard_map/ppermute | solution.py:1377
  66.5 0.0 collective-permute-done.12.args_21_
  66.5 0.0 collective-permute-done.13.args_22_
  66.6 0.0 collective-permute-done.11.args_20_
  66.6 9.7 %shard_map.196 = (f32[4,64,256]{2,1,0:T(8,128)S(1)}, bf16[4,64,256]{2,1,0:T(8,128)(2,1)}, bf16[4,16,256]{2,1,0:T(8,128)(2,1)}, bf16[4,16,256]{2,1,0:T(8,128)(2,1...) custom-call(f32[8,256]{1,0:T(8,128)S(1)} %copy-done.7, ...), custom_call_target="tpu_custom_call" | custom-call | tf_op jit(solution)/shard_map/pallas_call | solution.py:682
  76.2 1.0 shard_map.197
  77.2 0.1 collective-permute-start.15
  77.3 1.3 %collective-permute-start.16 = (f32[2,8,128]{2,1,0:T(8,128)S(1)}, f32[2,8,128]{2,1,0:T(8,128)S(1)}, u32[]{:S(2)}, u32[]{:S(2)}) collective-permute-start(f32[2,8,128]{2,1,0:T(8,128)S(1)} %get-tuple-element.254), channel_id=1, source_target_pairs={{0,16},{2,18},{4,20},{6,22},{8,24},{10,26},{12,28},{14,30},{1,17},... | collective-permute-start | bytes 24584 | tf_op jit(solution)/shard_map/ppermute | solution.py:1383
  78.6 1.3 %collective-permute-done.16.args_5_ = f32[2,8,128]{2,1,0:T(8,128)S(1)} collective-permute-done((f32[2,8,128]{2,1,0:T(8,128)S(1)}, f32[2,8,128]{2,1,0:T(8,128)S(1)}, u32[]{:S(2)}, u32[]{:S(2)}) %collective-permute-start.16) | collective-permute-done | bytes 8224 | tf_op jit(solution)/shard_map/ppermute | solution.py:1383
  79.9 0.0 collective-permute-done.15.args_1_
  79.9 0.2 shard_map.198
  80.1 0.1 collective-permute-start.19
  80.2 0.9 collective-permute-start.20
  81.1 1.6 %collective-permute-start.17 = (bf16[672,128]{1,0:T(8,128)(2,1)S(1)}, bf16[672,128]{1,0:T(8,128)(2,1)S(1)}, u32[]{:S(2)}, u32[]{:S(2)}) collective-permute-start(bf16[672,128]{1,0:T(8,128)(2,1)S(1)} %get-tuple-element.255), channel_id=1, source_target_pairs={{0,2},{2,4},{4,6},{6,8},{8,10},{10,12},{12,14},{14,0},{1,3},{3,5},... | collective-permute-start | bytes 516104 | tf_op jit(solution)/shard_map/ppermute | solution.py:1389
  82.8 3.1 %collective-permute-start.18 = (bf16[672,128]{1,0:T(8,128)(2,1)S(1)}, bf16[672,128]{1,0:T(8,128)(2,1)S(1)}, u32[]{:S(2)}, u32[]{:S(2)}) collective-permute-start(bf16[672,128]{1,0:T(8,128)(2,1)S(1)} %get-tuple-element.256), channel_id=1, source_target_pairs={{0,14},{2,0},{4,2},{6,4},{8,6},{10,8},{12,10},{14,12},{1,15},{3,1}... | collective-permute-start | bytes 516104 | tf_op jit(solution)/shard_map/ppermute | solution.py:1389
  85.8 1.1 %collective-permute-start.21 = (bf16[384,128]{1,0:T(8,128)(2,1)S(1)}, bf16[384,128]{1,0:T(8,128)(2,1)S(1)}, u32[]{:S(2)}, u32[]{:S(2)}) collective-permute-start(bf16[384,128]{1,0:T(8,128)(2,1)S(1)} %get-tuple-element.269), channel_id=1, source_target_pairs={{0,8},{2,10},{4,12},{6,14},{8,0},{10,2},{12,4},{14,6},{1,9},{3,11}... | collective-permute-start | bytes 294920 | tf_op jit(solution)/shard_map/ppermute | solution.py:1389
  87.0 0.8 collective-permute-done.19
  87.8 0.4 collective-permute-start.22
  88.2 8.2 %collective-permute-done.20 = bf16[384,128]{1,0:T(8,128)(2,1)S(1)} collective-permute-done((bf16[384,128]{1,0:T(8,128)(2,1)S(1)}, bf16[384,128]{1,0:T(8,128)(2,1)S(1)}, u32[]{:S(2)}, u32[]{:S(2)}) %collective-permute-start.20) | collective-permute-done | bytes 98336 | tf_op jit(solution)/shard_map/ppermute | solution.py:1389
  96.4 2.8 %collective-permute-done.21 = bf16[384,128]{1,0:T(8,128)(2,1)S(1)} collective-permute-done((bf16[384,128]{1,0:T(8,128)(2,1)S(1)}, bf16[384,128]{1,0:T(8,128)(2,1)S(1)}, u32[]{:S(2)}, u32[]{:S(2)}) %collective-permute-start.21) | collective-permute-done | bytes 98336 | tf_op jit(solution)/shard_map/ppermute | solution.py:1389
  99.2 3.7 %collective-permute-done.23 = bf16[384,128]{1,0:T(8,128)(2,1)S(1)} collective-permute-done((bf16[384,128]{1,0:T(8,128)(2,1)S(1)}, bf16[384,128]{1,0:T(8,128)(2,1)S(1)}, u32[]{:S(2)}, u32[]{:S(2)}) %collective-permute-start.23) | collective-permute-done | bytes 98336 | tf_op jit(solution)/shard_map/ppermute | solution.py:1389
  102.9 0.1 convert_add_fusion.args_0_
  103.0 0.1 collective-permute-start.24
  103.1 1.0 shard_map.199
  104.1 0.5 collective-permute-done.24.args_1_
  104.6 0.8 shard_map.200
  (19 shorter events, 0.1 us)
Async XLA Ops:
  2.2 9.1 %collective-permute-start = (bf16[9,16,256]{2,1,0:T(8,128)(2,1)}, bf16[9,16,256]{2,1,0:T(8,128)(2,1)S(1)}, u32[]{:S(2)}, u32[]{:S(2)}) collective-permute-start(bf16[9,16,256]{2,1,0:T(8,128)(2,1)} %get-tuple-element.144), channel_id=1, source_target_pairs={{0,2},{2,4},{4,6},{6,8},{8,10},{10,12},{12,14},{14,0},{1,3},{3,5},... | collective-permute-start | bytes 221192 | tf_op jit(solution)/shard_map/ppermute | solution.py:1276
  5.2 6.1 %collective-permute-start.1 = (bf16[9,16,256]{2,1,0:T(8,128)(2,1)}, bf16[9,16,256]{2,1,0:T(8,128)(2,1)S(1)}, u32[]{:S(2)}, u32[]{:S(2)}) collective-permute-start(bf16[9,16,256]{2,1,0:T(8,128)(2,1)} %get-tuple-element.145), channel_id=1, source_target_pairs={{2,0},{4,2},{6,4},{8,6},{10,8},{12,10},{14,12},{0,14},{3,1},{5,3},... | collective-permute-start | bytes 221192 | tf_op jit(solution)/shard_map/ppermute | solution.py:1277
  11.3 12.1 %copy-start = (bf16[1,256,1280]{2,1,0:T(8,128)(2,1)S(1)}, bf16[1,256,1280]{2,1,0:T(8,128)(2,1)}, u32[]{:S(2)}) copy-start(bf16[1,256,1280]{2,1,0:T(8,128)(2,1)} %args_1_.10) | copy-start | bytes 1966084
  11.3 12.1 %copy-start.1 = (bf16[1,256,768]{2,1,0:T(8,128)(2,1)S(1)}, bf16[1,256,768]{2,1,0:T(8,128)(2,1)}, u32[]{:S(2)}) copy-start(bf16[1,256,768]{2,1,0:T(8,128)(2,1)} %args_2_.12) | copy-start | bytes 1179652
  11.4 12.1 %copy-start.2 = (bf16[1,256,768]{2,1,0:T(8,128)(2,1)S(1)}, bf16[1,256,768]{2,1,0:T(8,128)(2,1)}, u32[]{:S(2)}) copy-start(bf16[1,256,768]{2,1,0:T(8,128)(2,1)} %args_4_.12) | copy-start | bytes 1179652
  11.4 12.1 %copy-start.3 = (bf16[32,1024]{1,0:T(8,128)(2,1)S(1)}, bf16[32,1024]{1,0:T(8,128)(2,1)}, u32[]{:S(2)}) copy-start(bf16[32,1024]{1,0:T(8,128)(2,1)} %get-tuple-element.150.args_4_.args_3_) | copy-start | bytes 196612
  11.4 12.1 %copy-start.4 = (bf16[2,1,4,64,256]{4,3,2,1,0:T(8,128)(2,1)S(1)}, bf16[2,1,4,64,256]{4,3,2,1,0:T(8,128)(2,1)}, u32[]{:S(2)}) copy-start(bf16[2,1,4,64,256]{4,3,2,1,0:T(8,128)(2,1)} %args_5_.6) | copy-start | bytes 786436
  11.4 12.1 %copy-start.6 = (f32[2,104,128]{2,1,0:T(8,128)S(1)}, f32[2,104,128]{2,1,0:T(8,128)}, u32[]{:S(2)}) copy-start(f32[2,104,128]{2,1,0:T(8,128)} %get-tuple-element.165.args_3_) | copy-start | bytes 319492
  11.4 12.1 %copy-start.7 = (f32[8,256]{1,0:T(8,128)S(1)}, f32[8,256]{1,0:T(8,128)}, u32[]{:S(2)}) copy-start(f32[8,256]{1,0:T(8,128)} %get-tuple-element.149.args_6_.args_0_) | copy-start | bytes 24580
  11.4 12.1 %copy-start.8 = (f32[2,1,3,64]{3,1,2,0:T(1,128)S(1)}, f32[2,1,3,64]{3,1,2,0:T(1,128)}, u32[]{:S(2)}) copy-start(f32[2,1,3,64]{3,1,2,0:T(1,128)} %param.13) | copy-start | bytes 4612
  11.4 22.7 %copy-start.5 = (bf16[2,1,4,64,256]{4,3,2,1,0:T(8,128)(2,1)S(1)}, bf16[2,1,4,64,256]{4,3,2,1,0:T(8,128)(2,1)}, u32[]{:S(2)}) copy-start(bf16[2,1,4,64,256]{4,3,2,1,0:T(8,128)(2,1)} %args_15_.3) | copy-start | bytes 786436
  19.5 14.6 %collective-permute-start.2 = (bf16[4,64,256]{2,1,0:T(8,128)(2,1)S(1)}, bf16[4,64,256]{2,1,0:T(8,128)(2,1)S(1)}, u32[]{:S(2)}, u32[]{:S(2)}) collective-permute-start(bf16[4,64,256]{2,1,0:T(8,128)(2,1)S(1)} %get-tuple-element.161.args_3_), channel_id=1, source_target_pairs={{0,16},{2,18},{4,20},{6,22},{8,24},{10,26},{12,28},{14,30},{1,17},... | collective-permute-start | bytes 393224 | tf_op jit(solution)/shard_map/ppermute | solution.py:1319
  20.8 12.0 %collective-permute-start.3 = (bf16[4,16,256]{2,1,0:T(8,128)(2,1)S(1)}, bf16[4,16,256]{2,1,0:T(8,128)(2,1)S(1)}, u32[]{:S(2)}, u32[]{:S(2)}) collective-permute-start(bf16[4,16,256]{2,1,0:T(8,128)(2,1)S(1)} %get-tuple-element.162), channel_id=1, source_target_pairs={{0,18},{2,20},{4,22},{6,24},{8,26},{10,28},{12,30},{14,16},{1,19},... | collective-permute-start | bytes 98312 | tf_op jit(solution)/shard_map/ppermute | solution.py:1320
  22.1 12.0 %collective-permute-start.4 = (bf16[4,16,256]{2,1,0:T(8,128)(2,1)S(1)}, bf16[4,16,256]{2,1,0:T(8,128)(2,1)S(1)}, u32[]{:S(2)}, u32[]{:S(2)}) collective-permute-start(bf16[4,16,256]{2,1,0:T(8,128)(2,1)S(1)} %get-tuple-element.163), channel_id=1, source_target_pairs={{2,16},{4,18},{6,20},{8,22},{10,24},{12,26},{14,28},{0,30},{3,17},... | collective-permute-start | bytes 98312 | tf_op jit(solution)/shard_map/ppermute | solution.py:1321
  30.2 8.0 %collective-permute-start.9 = (bf16[4,64,256]{2,1,0:T(8,128)(2,1)S(1)}, bf16[4,64,256]{2,1,0:T(8,128)(2,1)S(1)}, u32[]{:S(2)}, u32[]{:S(2)}) collective-permute-start(bf16[4,64,256]{2,1,0:T(8,128)(2,1)S(1)} %get-tuple-element.194), channel_id=1, source_target_pairs={{0,18},{2,20},{4,22},{6,24},{8,26},{10,28},{12,30},{14,16},{1,19},... | collective-permute-start | bytes 393224 | tf_op jit(solution)/shard_map/ppermute | solution.py:1320
  31.5 14.8 %collective-permute-start.8 = (bf16[4,64,256]{2,1,0:T(8,128)(2,1)S(1)}, bf16[4,64,256]{2,1,0:T(8,128)(2,1)S(1)}, u32[]{:S(2)}, u32[]{:S(2)}) collective-permute-start(bf16[4,64,256]{2,1,0:T(8,128)(2,1)S(1)} %get-tuple-element.193.args_5_), channel_id=1, source_target_pairs={{0,16},{2,18},{4,20},{6,22},{8,24},{10,26},{12,28},{14,30},{1,17},... | collective-permute-start | bytes 393224 | tf_op jit(solution)/shard_map/ppermute | solution.py:1319
  32.8 13.5 %collective-permute-start.10 = (bf16[4,64,256]{2,1,0:T(8,128)(2,1)S(1)}, bf16[4,64,256]{2,1,0:T(8,128)(2,1)S(1)}, u32[]{:S(2)}, u32[]{:S(2)}) collective-permute-start(bf16[4,64,256]{2,1,0:T(8,128)(2,1)S(1)} %get-tuple-element.195), channel_id=1, source_target_pairs={{2,16},{4,18},{6,20},{8,22},{10,24},{12,26},{14,28},{0,30},{3,17},... | collective-permute-start | bytes 393224 | tf_op jit(solution)/shard_map/ppermute | solution.py:1321
  34.2 14.1 %collective-permute-start.5 = (bf16[4,64,256]{2,1,0:T(8,128)(2,1)S(1)}, bf16[4,64,256]{2,1,0:T(8,128)(2,1)S(1)}, u32[]{:S(2)}, u32[]{:S(2)}) collective-permute-start(bf16[4,64,256]{2,1,0:T(8,128)(2,1)S(1)} %get-tuple-element.183), channel_id=1, source_target_pairs={{16,0},{18,2},{20,4},{22,6},{24,8},{26,10},{28,12},{30,14},{17,1},... | collective-permute-start | bytes 393224 | tf_op jit(solution)/shard_map/ppermute | solution.py:1364
  35.5 12.8 %collective-permute-start.6 = (bf16[4,16,256]{2,1,0:T(8,128)(2,1)S(1)}, bf16[4,16,256]{2,1,0:T(8,128)(2,1)S(1)}, u32[]{:S(2)}, u32[]{:S(2)}) collective-permute-start(bf16[4,16,256]{2,1,0:T(8,128)(2,1)S(1)} %get-tuple-element.184.args_28_), channel_id=1, source_target_pairs={{16,2},{18,4},{20,6},{22,8},{24,10},{26,12},{28,14},{30,0},{17,3},... | collective-permute-start | bytes 98312 | tf_op jit(solution)/shard_map/ppermute | solution.py:1365
  38.2 10.1 %collective-permute-start.7 = (bf16[4,16,256]{2,1,0:T(8,128)(2,1)S(1)}, bf16[4,16,256]{2,1,0:T(8,128)(2,1)S(1)}, u32[]{:S(2)}, u32[]{:S(2)}) collective-permute-start(bf16[4,16,256]{2,1,0:T(8,128)(2,1)S(1)} %get-tuple-element.185.args_27_), channel_id=1, source_target_pairs={{18,0},{20,2},{22,4},{24,6},{26,8},{28,10},{30,12},{16,14},{19,1},... | collective-permute-start | bytes 98312 | tf_op jit(solution)/shard_map/ppermute | solution.py:1366
  48.3 18.3 %collective-permute-start.11 = (bf16[4,64,256]{2,1,0:T(8,128)(2,1)S(1)}, bf16[4,64,256]{2,1,0:T(8,128)(2,1)S(1)}, u32[]{:S(2)}, u32[]{:S(2)}) collective-permute-start(bf16[4,64,256]{2,1,0:T(8,128)(2,1)S(1)} %get-tuple-element.224), channel_id=1, source_target_pairs={{16,0},{18,2},{20,4},{22,6},{24,8},{26,10},{28,12},{30,14},{17,1},... | collective-permute-start | bytes 393224 | tf_op jit(solution)/shard_map/ppermute | solution.py:1364
  49.5 17.0 %collective-permute-start.12 = (bf16[4,16,256]{2,1,0:T(8,128)(2,1)S(1)}, bf16[4,16,256]{2,1,0:T(8,128)(2,1)S(1)}, u32[]{:S(2)}, u32[]{:S(2)}) collective-permute-start(bf16[4,16,256]{2,1,0:T(8,128)(2,1)S(1)} %get-tuple-element.225.args_31_), channel_id=1, source_target_pairs={{16,2},{18,4},{20,6},{22,8},{24,10},{26,12},{28,14},{30,0},{17,3},... | collective-permute-start | bytes 98312 | tf_op jit(solution)/shard_map/ppermute | solution.py:1365
  50.8 15.7 %collective-permute-start.13 = (bf16[4,16,256]{2,1,0:T(8,128)(2,1)S(1)}, bf16[4,16,256]{2,1,0:T(8,128)(2,1)S(1)}, u32[]{:S(2)}, u32[]{:S(2)}) collective-permute-start(bf16[4,16,256]{2,1,0:T(8,128)(2,1)S(1)} %get-tuple-element.226.args_30_), channel_id=1, source_target_pairs={{18,0},{20,2},{22,4},{24,6},{26,8},{28,10},{30,12},{16,14},{19,1},... | collective-permute-start | bytes 98312 | tf_op jit(solution)/shard_map/ppermute | solution.py:1366
  52.1 14.4 %collective-permute-start.14 = (f32[2,8,128]{2,1,0:T(8,128)S(1)}, f32[2,8,128]{2,1,0:T(8,128)S(1)}, u32[]{:S(2)}, u32[]{:S(2)}) collective-permute-start(f32[2,8,128]{2,1,0:T(8,128)S(1)} %get-tuple-element.227), channel_id=1, source_target_pairs={{16,0},{18,2},{20,4},{22,6},{24,8},{26,10},{28,12},{30,14},{17,1},... | collective-permute-start | bytes 24584 | tf_op jit(solution)/shard_map/ppermute | solution.py:1377
  77.2 2.7 %collective-permute-start.15 = (bf16[8,384,128]{2,1,0:T(8,128)(2,1)S(1)}, bf16[8,384,128]{2,1,0:T(8,128)(2,1)S(1)}, u32[]{:S(2)}, u32[]{:S(2)}) collective-permute-start(bf16[8,384,128]{2,1,0:T(8,128)(2,1)S(1)} %get-tuple-element.250), channel_id=1, source_target_pairs={{0,1},{1,0},{2,3},{3,2},{4,5},{5,4},{6,7},{7,6},{8,9},{9,8},{10,11... | collective-permute-start | bytes 2359304 | tf_op jit(solution)/shard_map/ppermute | solution.py:1385
  77.3 2.6 %collective-permute-start.16 = (f32[2,8,128]{2,1,0:T(8,128)S(1)}, f32[2,8,128]{2,1,0:T(8,128)S(1)}, u32[]{:S(2)}, u32[]{:S(2)}) collective-permute-start(f32[2,8,128]{2,1,0:T(8,128)S(1)} %get-tuple-element.254), channel_id=1, source_target_pairs={{0,16},{2,18},{4,20},{6,22},{8,24},{10,26},{12,28},{14,30},{1,17},... | collective-permute-start | bytes 24584 | tf_op jit(solution)/shard_map/ppermute | solution.py:1383
  80.1 7.6 %collective-permute-start.19 = (bf16[384,128]{1,0:T(8,128)(2,1)S(1)}, bf16[384,128]{1,0:T(8,128)(2,1)S(1)}, u32[]{:S(2)}, u32[]{:S(2)}) collective-permute-start(bf16[384,128]{1,0:T(8,128)(2,1)S(1)} %get-tuple-element.267), channel_id=1, source_target_pairs={{0,4},{2,6},{4,8},{6,10},{8,12},{10,14},{12,0},{14,2},{1,5},{3,7},... | collective-permute-start | bytes 294920 | tf_op jit(solution)/shard_map/ppermute | solution.py:1389
  80.2 16.2 %collective-permute-start.20 = (bf16[384,128]{1,0:T(8,128)(2,1)S(1)}, bf16[384,128]{1,0:T(8,128)(2,1)S(1)}, u32[]{:S(2)}, u32[]{:S(2)}) collective-permute-start(bf16[384,128]{1,0:T(8,128)(2,1)S(1)} %get-tuple-element.268), channel_id=1, source_target_pairs={{0,6},{2,8},{4,10},{6,12},{8,14},{10,0},{12,2},{14,4},{1,7},{3,9},... | collective-permute-start | bytes 294920 | tf_op jit(solution)/shard_map/ppermute | solution.py:1389
  81.1 21.8 %collective-permute-start.17 = (bf16[672,128]{1,0:T(8,128)(2,1)S(1)}, bf16[672,128]{1,0:T(8,128)(2,1)S(1)}, u32[]{:S(2)}, u32[]{:S(2)}) collective-permute-start(bf16[672,128]{1,0:T(8,128)(2,1)S(1)} %get-tuple-element.255), channel_id=1, source_target_pairs={{0,2},{2,4},{4,6},{6,8},{8,10},{10,12},{12,14},{14,0},{1,3},{3,5},... | collective-permute-start | bytes 516104 | tf_op jit(solution)/shard_map/ppermute | solution.py:1389
  82.8 20.2 %collective-permute-start.18 = (bf16[672,128]{1,0:T(8,128)(2,1)S(1)}, bf16[672,128]{1,0:T(8,128)(2,1)S(1)}, u32[]{:S(2)}, u32[]{:S(2)}) collective-permute-start(bf16[672,128]{1,0:T(8,128)(2,1)S(1)} %get-tuple-element.256), channel_id=1, source_target_pairs={{0,14},{2,0},{4,2},{6,4},{8,6},{10,8},{12,10},{14,12},{1,15},{3,1}... | collective-permute-start | bytes 516104 | tf_op jit(solution)/shard_map/ppermute | solution.py:1389
  85.8 13.4 %collective-permute-start.21 = (bf16[384,128]{1,0:T(8,128)(2,1)S(1)}, bf16[384,128]{1,0:T(8,128)(2,1)S(1)}, u32[]{:S(2)}, u32[]{:S(2)}) collective-permute-start(bf16[384,128]{1,0:T(8,128)(2,1)S(1)} %get-tuple-element.269), channel_id=1, source_target_pairs={{0,8},{2,10},{4,12},{6,14},{8,0},{10,2},{12,4},{14,6},{1,9},{3,11}... | collective-permute-start | bytes 294920 | tf_op jit(solution)/shard_map/ppermute | solution.py:1389
  87.8 11.5 %collective-permute-start.22 = (bf16[384,128]{1,0:T(8,128)(2,1)S(1)}, bf16[384,128]{1,0:T(8,128)(2,1)S(1)}, u32[]{:S(2)}, u32[]{:S(2)}) collective-permute-start(bf16[384,128]{1,0:T(8,128)(2,1)S(1)} %get-tuple-element.270), channel_id=1, source_target_pairs={{0,10},{2,12},{4,14},{6,0},{8,2},{10,4},{12,6},{14,8},{1,11},{3,13... | collective-permute-start | bytes 294920 | tf_op jit(solution)/shard_map/ppermute | solution.py:1389
  96.4 6.5 %collective-permute-start.23 = (bf16[384,128]{1,0:T(8,128)(2,1)S(1)}, bf16[384,128]{1,0:T(8,128)(2,1)S(1)}, u32[]{:S(2)}, u32[]{:S(2)}) collective-permute-start(bf16[384,128]{1,0:T(8,128)(2,1)S(1)} %get-tuple-element.271), channel_id=1, source_target_pairs={{0,12},{2,14},{4,0},{6,2},{8,4},{10,6},{12,8},{14,10},{1,13},{3,15... | collective-permute-start | bytes 294920 | tf_op jit(solution)/shard_map/ppermute | solution.py:1389
  103.0 1.5 %collective-permute-start.24 = (f32[384,128]{1,0:T(8,128)S(1)}, f32[384,128]{1,0:T(8,128)S(1)}, u32[]{:S(2)}, u32[]{:S(2)}) collective-permute-start(f32[384,128]{1,0:T(8,128)S(1)} %convert_add_fusion.args_0_), channel_id=1, source_target_pairs={{0,1},{1,0},{2,3},{3,2},{4,5},{5,4},{6,7},{7,6},{8,9},{9,8},{10,11... | collective-permute-start | bytes 589832 | tf_op jit(solution)/shard_map/ppermute | solution.py:1402

commit v5 on v4

--- a/solution.py
+++ b/solution.py
@@ -311,7 +311,7 @@
         write_edge_tables(r, sz, b, F32)
         return carry
 
-    lax.fori_loop(0, sz.blocks, tables, 0, unroll=2)
+    lax.fori_loop(0, sz.blocks, tables, 0, unroll=4)
     own = r.s_own
     xhat, scale = node_part(r, sz, own, r.s_low, r.s_high, r.s_norms, r.s_wqkv)
     r.xhat[...] = xhat
@@ -360,7 +360,7 @@
             block(2 * i + which, buffers(r, sz, which))
         return carry
 
-    lax.fori_loop(0, sz.blocks // 2, pair, 0)
+    lax.fori_loop(0, sz.blocks // 2, pair, 0, unroll=2)
     third = sum(dot(r.units[b], r.third[b]) for b in range(sz.blocks))
     scalar_low = jnp.concatenate([r.sagg[cg] for cg in range(CG)], axis=1).astype(BF16)
     r.left[E + 3 * A : E + 4 * A, :] = scalar_low
@@ -1314,7 +1314,11 @@
             made = filters[SECOND] = filter_call(
                 sz, SECOND, range(micro_count), geometry_inputs()
             )
-            first.head, made[0].geo = lax.optimization_barrier((first.head, made[0].geo))
+            own, *rest = sent[0]
+            first.head, made[0].geo, own = lax.optimization_barrier(
+                (first.head, made[0].geo, own)
+            )
+            sent[0] = (own, *rest)
         sent.append((
             lax.ppermute(first.fresh, both, forth),
             lax.ppermute(first.tail, both, forth_up),

time: 106 us -> 104 us (0.981)
  Pallas kernels: 48.4 us -> 47.1 us
  waiting for transfers between devices: 24.1 us -> 23 us
    ppermute x1, waiting for transfers between devices: 3.41 us -> 1.45 us  [on_device(): arrays.early = (lax.ppermute(seconds[-1].all_places, both, back), VMEM)]
    ppermute x2, waiting for transfers between devices: 1.89 us -> 3.39 us  [on_device(): lax.ppermute(rim_high, both, back_up)]
    pallas_call x14, Pallas kernels: 48.4 us -> 47.1 us  [call(): pl.pallas_call(kernel, out_shape=list(outs.values()), in_specs=[spec for...]
  transfers between devices with their start and end apart: 25 -> 25, of which waited for: 9 -> 10; matrix products, arithmetic and copies ran while one was open for 0% -> 0% of each run, Pallas kernels for 26% -> 26%
where the time goes in v5:
time: 104 us; the launch traced here: 103 us
  Pallas kernels  47.1 us (45%)
  starting transfers between devices  32.2 us (31%)
  waiting for transfers between devices  23 us (22%)
  between operations  1.06 us (1%)
    pallas_call x14, Pallas kernels, call(): pl.pallas_call(kernel, out_shape=list(outs.values()), in_specs=[spec for...  47.1 us
    ppermute x7, waiting for transfers between devices, on_device(): lax.ppermute(piece, 'space', [(i, (i + hop) % space) for i in range(space)])  15.1 us
    ppermute x7, starting transfers between devices, on_device(): lax.ppermute(piece, 'space', [(i, (i + hop) % space) for i in range(space)])  7.63 us
    ppermute x2, waiting for transfers between devices, on_device(): lax.ppermute(rim_high, both, back_up)  3.39 us
    ppermute x1, starting transfers between devices, on_device(): pack_high = lax.ppermute(borders.down, 'space', down)  3.1 us
    ppermute x1, starting transfers between devices, on_device(): pack_low = lax.ppermute(borders.up, 'space', up)  3.02 us
    ppermute x2, starting transfers between devices, on_device(): lax.ppermute(rim_high, both, back_up)  2.76 us
    ppermute x2, starting transfers between devices, on_device(): lax.ppermute(first.fresh, both, forth)  2.59 us
  transfers between devices with their start and end apart: 25, of which 10 were waited for; matrix products, arithmetic and copies ran while one was open for 0% of the time, Pallas kernels for 26%

profile of v5, /device:TPU:0, one launch (start us, length us, event | category | flops | bytes accessed | tf_op | source)
XLA Modules:
  0.0 103.5 jit_solution(10356309982218551462)
XLA Ops:
  0.6 1.5 %shard_map.187 = (bf16[9,16,256]{2,1,0:T(8,128)(2,1)}, bf16[9,16,256]{2,1,0:T(8,128)(2,1)}) custom-call(bf16[2,1,4,64,256]{4,3,2,1,0:T(8,128)(2,1)} %args_5_.6, f32[2,3,1,64]{3,2,1,0:T(1,128)} %bitcast.5), custom_call_target="tpu_custom_call" | custom-call | tf_op jit(solution)/shard_map/pallas_call | solution.py:682
  2.2 3.0 %collective-permute-start = (bf16[9,16,256]{2,1,0:T(8,128)(2,1)}, bf16[9,16,256]{2,1,0:T(8,128)(2,1)S(1)}, u32[]{:S(2)}, u32[]{:S(2)}) collective-permute-start(bf16[9,16,256]{2,1,0:T(8,128)(2,1)} %get-tuple-element.145), channel_id=1, source_target_pairs={{0,2},{2,4},{4,6},{6,8},{8,10},{10,12},{12,14},{14,0},{1,3},{3,5},... | collective-permute-start | bytes 221192 | tf_op jit(solution)/shard_map/ppermute | solution.py:1276
  5.2 3.1 %collective-permute-start.1 = (bf16[9,16,256]{2,1,0:T(8,128)(2,1)}, bf16[9,16,256]{2,1,0:T(8,128)(2,1)S(1)}, u32[]{:S(2)}, u32[]{:S(2)}) collective-permute-start(bf16[9,16,256]{2,1,0:T(8,128)(2,1)} %get-tuple-element.146), channel_id=1, source_target_pairs={{2,0},{4,2},{6,4},{8,6},{10,8},{12,10},{14,12},{0,14},{3,1},{5,3},... | collective-permute-start | bytes 221192 | tf_op jit(solution)/shard_map/ppermute | solution.py:1277
  8.3 3.0 %shard_map.188 = (f32[2,104,128]{2,1,0:T(8,128)}, f32[8,256]{1,0:T(8,128)}, bf16[32,1024]{1,0:T(8,128)(2,1)}, bf16[20480,1280]{1,0:T(8,128)(2,1)}, f32[51200,256]{1,0:T(8,128)}) custom-call(bf16[2,1,4,64,256]{4,3,2,1,0:T(8,128)(2,1)} %args_5_.6, f32[2,3,1,64]{3,2,1,0:T(1,128)} %bitcast.6, s32[2,1,32,64]{3,2,1,0:T(8,128)} %args_2_.8, ...), custom_call_target="tpu_custom_call" | custom-call | tf_op jit(solution)/shard_map/pallas_call | solution.py:682
  11.3 0.0 collective-permute-done.args_0_
  11.3 0.0 collective-permute-done.1.args_1_
  11.3 0.0 copy-start.1
  11.4 0.0 copy-start.2
  11.4 0.0 copy-start.3
  11.4 0.0 copy-start.4
  11.4 0.0 copy-start.6
  11.4 0.0 copy-start.7
  11.4 0.0 copy-start.8
  11.4 0.0 copy-start.5
  11.4 7.4 %shard_map.189 = (bf16[4,64,256]{2,1,0:T(8,128)(2,1)S(1)}, bf16[4,16,256]{2,1,0:T(8,128)(2,1)S(1)}, bf16[4,16,256]{2,1,0:T(8,128)(2,1)S(1)}, bf16[384,256]{1,0:T...) custom-call(bf16[9,16,256]{2,1,0:T(8,128)(2,1)S(1)} %collective-perm, ...), custom_call_target="tpu_custom_call" | custom-call | tf_op jit(solution)/shard_map/pallas_call | solution.py:682
  18.9 1.3 %collective-permute-start.2 = (bf16[4,64,256]{2,1,0:T(8,128)(2,1)S(1)}, bf16[4,64,256]{2,1,0:T(8,128)(2,1)S(1)}, u32[]{:S(2)}, u32[]{:S(2)}) collective-permute-start(bf16[4,64,256]{2,1,0:T(8,128)(2,1)S(1)} %get-tuple-element.155.args_3_), channel_id=1, source_target_pairs={{0,16},{2,18},{4,20},{6,22},{8,24},{10,26},{12,28},{14,30},{1,17},... | collective-permute-start | bytes 393224 | tf_op jit(solution)/shard_map/ppermute | solution.py:1323
  20.2 1.3 %collective-permute-start.3 = (bf16[4,16,256]{2,1,0:T(8,128)(2,1)S(1)}, bf16[4,16,256]{2,1,0:T(8,128)(2,1)S(1)}, u32[]{:S(2)}, u32[]{:S(2)}) collective-permute-start(bf16[4,16,256]{2,1,0:T(8,128)(2,1)S(1)} %get-tuple-element.164), channel_id=1, source_target_pairs={{0,18},{2,20},{4,22},{6,24},{8,26},{10,28},{12,30},{14,16},{1,19},... | collective-permute-start | bytes 98312 | tf_op jit(solution)/shard_map/ppermute | solution.py:1324
  21.5 1.3 %collective-permute-start.4 = (bf16[4,16,256]{2,1,0:T(8,128)(2,1)S(1)}, bf16[4,16,256]{2,1,0:T(8,128)(2,1)S(1)}, u32[]{:S(2)}, u32[]{:S(2)}) collective-permute-start(bf16[4,16,256]{2,1,0:T(8,128)(2,1)S(1)} %get-tuple-element.165), channel_id=1, source_target_pairs={{2,16},{4,18},{6,20},{8,22},{10,24},{12,26},{14,28},{0,30},{3,17},... | collective-permute-start | bytes 98312 | tf_op jit(solution)/shard_map/ppermute | solution.py:1325
  22.9 6.1 %shard_map.190 = (bf16[4,64,256]{2,1,0:T(8,128)(2,1)S(1)}, bf16[4,64,256]{2,1,0:T(8,128)(2,1)S(1)}, bf16[4,64,256]{2,1,0:T(8,128)(2,1)S(1)}, bf16[384,256]{1,0:T...) custom-call(bf16[9,16,256]{2,1,0:T(8,128)(2,1)S(1)} %collective-perm, ...), custom_call_target="tpu_custom_call" | custom-call | tf_op jit(solution)/shard_map/pallas_call | solution.py:682
  29.0 1.3 %collective-permute-start.9 = (bf16[4,64,256]{2,1,0:T(8,128)(2,1)S(1)}, bf16[4,64,256]{2,1,0:T(8,128)(2,1)S(1)}, u32[]{:S(2)}, u32[]{:S(2)}) collective-permute-start(bf16[4,64,256]{2,1,0:T(8,128)(2,1)S(1)} %get-tuple-element.196), channel_id=1, source_target_pairs={{0,18},{2,20},{4,22},{6,24},{8,26},{10,28},{12,30},{14,16},{1,19},... | collective-permute-start | bytes 393224 | tf_op jit(solution)/shard_map/ppermute | solution.py:1324
  30.3 1.3 %collective-permute-start.8 = (bf16[4,64,256]{2,1,0:T(8,128)(2,1)S(1)}, bf16[4,64,256]{2,1,0:T(8,128)(2,1)S(1)}, u32[]{:S(2)}, u32[]{:S(2)}) collective-permute-start(bf16[4,64,256]{2,1,0:T(8,128)(2,1)S(1)} %get-tuple-element.195.args_5_), channel_id=1, source_target_pairs={{0,16},{2,18},{4,20},{6,22},{8,24},{10,26},{12,28},{14,30},{1,17},... | collective-permute-start | bytes 393224 | tf_op jit(solution)/shard_map/ppermute | solution.py:1323
  31.7 1.3 %collective-permute-start.10 = (bf16[4,64,256]{2,1,0:T(8,128)(2,1)S(1)}, bf16[4,64,256]{2,1,0:T(8,128)(2,1)S(1)}, u32[]{:S(2)}, u32[]{:S(2)}) collective-permute-start(bf16[4,64,256]{2,1,0:T(8,128)(2,1)S(1)} %get-tuple-element.197), channel_id=1, source_target_pairs={{2,16},{4,18},{6,20},{8,22},{10,24},{12,26},{14,28},{0,30},{3,17},... | collective-permute-start | bytes 393224 | tf_op jit(solution)/shard_map/ppermute | solution.py:1325
  33.0 0.0 collective-permute-done.3.args_13_
  33.0 0.0 collective-permute-done.4.args_14_
  33.1 1.3 %collective-permute-start.5 = (bf16[4,64,256]{2,1,0:T(8,128)(2,1)S(1)}, bf16[4,64,256]{2,1,0:T(8,128)(2,1)S(1)}, u32[]{:S(2)}, u32[]{:S(2)}) collective-permute-start(bf16[4,64,256]{2,1,0:T(8,128)(2,1)S(1)} %get-tuple-element.185), channel_id=1, source_target_pairs={{16,0},{18,2},{20,4},{22,6},{24,8},{26,10},{28,12},{30,14},{17,1},... | collective-permute-start | bytes 393224 | tf_op jit(solution)/shard_map/ppermute | solution.py:1368
  34.4 1.5 %collective-permute-start.6 = (bf16[4,16,256]{2,1,0:T(8,128)(2,1)S(1)}, bf16[4,16,256]{2,1,0:T(8,128)(2,1)S(1)}, u32[]{:S(2)}, u32[]{:S(2)}) collective-permute-start(bf16[4,16,256]{2,1,0:T(8,128)(2,1)S(1)} %get-tuple-element.186.args_28_), channel_id=1, source_target_pairs={{16,2},{18,4},{20,6},{22,8},{24,10},{26,12},{28,14},{30,0},{17,3},... | collective-permute-start | bytes 98312 | tf_op jit(solution)/shard_map/ppermute | solution.py:1369
  35.8 1.2 %collective-permute-done.9.args_13_ = bf16[4,64,256]{2,1,0:T(8,128)(2,1)S(1)} collective-permute-done((bf16[4,64,256]{2,1,0:T(8,128)(2,1)S(1)}, bf16[4,64,256]{2,1,0:T(8,128)(2,1)S(1)}, u32[]{:S(2)}, u32[]{:S(2)}) %collective-permute-start.9) | collective-permute-done | bytes 131104 | tf_op jit(solution)/shard_map/ppermute | solution.py:1324
  37.0 1.3 %collective-permute-start.7 = (bf16[4,16,256]{2,1,0:T(8,128)(2,1)S(1)}, bf16[4,16,256]{2,1,0:T(8,128)(2,1)S(1)}, u32[]{:S(2)}, u32[]{:S(2)}) collective-permute-start(bf16[4,16,256]{2,1,0:T(8,128)(2,1)S(1)} %get-tuple-element.187.args_27_), channel_id=1, source_target_pairs={{18,0},{20,2},{22,4},{24,6},{26,8},{28,10},{30,12},{16,14},{19,1},... | collective-permute-start | bytes 98312 | tf_op jit(solution)/shard_map/ppermute | solution.py:1370
  38.3 6.6 %shard_map.193 = (f32[10,8,256]{2,1,0:T(8,128)S(1)}, bf16[8,32,256]{2,1,0:T(8,128)(2,1)S(1)}, bf16[8,256,128]{2,1,0:T(8,128)(2,1)S(1)}, bf16[8,192,256]{2,1,0:T(...) custom-call(bf16[9,16,256]{2,1,0:T(8,128)(2,1)S(1)} %collective-perm, ...), custom_call_target="tpu_custom_call" | custom-call | tf_op jit(solution)/shard_map/pallas_call | solution.py:682
  44.9 0.0 collective-permute-done.8.args_12_
  45.0 0.0 collective-permute-done.10.args_14_
  45.0 0.1 shard_map.194
  45.0 3.2 %collective-permute-done.6.args_21_ = bf16[4,16,256]{2,1,0:T(8,128)(2,1)S(1)} collective-permute-done((bf16[4,16,256]{2,1,0:T(8,128)(2,1)S(1)}, bf16[4,16,256]{2,1,0:T(8,128)(2,1)S(1)}, u32[]{:S(2)}, u32[]{:S(2)}) %collective-permute-start.6) | collective-permute-done | bytes 32800 | tf_op jit(solution)/shard_map/ppermute | solution.py:1369
  48.3 1.3 %collective-permute-start.11 = (bf16[4,64,256]{2,1,0:T(8,128)(2,1)S(1)}, bf16[4,64,256]{2,1,0:T(8,128)(2,1)S(1)}, u32[]{:S(2)}, u32[]{:S(2)}) collective-permute-start(bf16[4,64,256]{2,1,0:T(8,128)(2,1)S(1)} %get-tuple-element.226), channel_id=1, source_target_pairs={{16,0},{18,2},{20,4},{22,6},{24,8},{26,10},{28,12},{30,14},{17,1},... | collective-permute-start | bytes 393224 | tf_op jit(solution)/shard_map/ppermute | solution.py:1368
  49.5 1.3 %collective-permute-start.12 = (bf16[4,16,256]{2,1,0:T(8,128)(2,1)S(1)}, bf16[4,16,256]{2,1,0:T(8,128)(2,1)S(1)}, u32[]{:S(2)}, u32[]{:S(2)}) collective-permute-start(bf16[4,16,256]{2,1,0:T(8,128)(2,1)S(1)} %get-tuple-element.227.args_31_), channel_id=1, source_target_pairs={{16,2},{18,4},{20,6},{22,8},{24,10},{26,12},{28,14},{30,0},{17,3},... | collective-permute-start | bytes 98312 | tf_op jit(solution)/shard_map/ppermute | solution.py:1369
  50.8 1.3 %collective-permute-start.13 = (bf16[4,16,256]{2,1,0:T(8,128)(2,1)S(1)}, bf16[4,16,256]{2,1,0:T(8,128)(2,1)S(1)}, u32[]{:S(2)}, u32[]{:S(2)}) collective-permute-start(bf16[4,16,256]{2,1,0:T(8,128)(2,1)S(1)} %get-tuple-element.228.args_30_), channel_id=1, source_target_pairs={{18,0},{20,2},{22,4},{24,6},{26,8},{28,10},{30,12},{16,14},{19,1},... | collective-permute-start | bytes 98312 | tf_op jit(solution)/shard_map/ppermute | solution.py:1370
  52.1 1.3 %collective-permute-start.14 = (f32[2,8,128]{2,1,0:T(8,128)S(1)}, f32[2,8,128]{2,1,0:T(8,128)S(1)}, u32[]{:S(2)}, u32[]{:S(2)}) collective-permute-start(f32[2,8,128]{2,1,0:T(8,128)S(1)} %get-tuple-element.229), channel_id=1, source_target_pairs={{16,0},{18,2},{20,4},{22,6},{24,8},{26,10},{28,12},{30,14},{17,1},... | collective-permute-start | bytes 24584 | tf_op jit(solution)/shard_map/ppermute | solution.py:1381
  53.4 9.7 %shard_map.195 = (f32[4,64,256]{2,1,0:T(8,128)S(1)}, bf16[4,64,256]{2,1,0:T(8,128)(2,1)}, bf16[4,16,256]{2,1,0:T(8,128)(2,1)S(1)}, bf16[4,16,256]{2,1,0:T(8,128)...) custom-call(f32[8,256]{1,0:T(8,128)S(1)} %copy-done.7, ...), custom_call_target="tpu_custom_call" | custom-call | tf_op jit(solution)/shard_map/pallas_call | solution.py:682
  63.1 1.5 %collective-permute-done.14.args_23_ = f32[2,8,128]{2,1,0:T(8,128)S(1)} collective-permute-done((f32[2,8,128]{2,1,0:T(8,128)S(1)}, f32[2,8,128]{2,1,0:T(8,128)S(1)}, u32[]{:S(2)}, u32[]{:S(2)}) %collective-permute-start.14) | collective-permute-done | bytes 8224 | tf_op jit(solution)/shard_map/ppermute | solution.py:1381
  64.6 0.2 collective-permute-done.12.args_21_
  64.8 0.0 collective-permute-done.13.args_22_
  64.8 0.0 collective-permute-done.11.args_20_
  64.8 9.6 %shard_map.196 = (f32[4,64,256]{2,1,0:T(8,128)S(1)}, bf16[4,64,256]{2,1,0:T(8,128)(2,1)}, bf16[4,16,256]{2,1,0:T(8,128)(2,1)}, bf16[4,16,256]{2,1,0:T(8,128)(2,1...) custom-call(f32[8,256]{1,0:T(8,128)S(1)} %copy-done.7, ...), custom_call_target="tpu_custom_call" | custom-call | tf_op jit(solution)/shard_map/pallas_call | solution.py:682
  74.4 1.0 shard_map.197
  75.3 0.1 collective-permute-start.15
  75.4 1.3 %collective-permute-start.16 = (f32[2,8,128]{2,1,0:T(8,128)S(1)}, f32[2,8,128]{2,1,0:T(8,128)S(1)}, u32[]{:S(2)}, u32[]{:S(2)}) collective-permute-start(f32[2,8,128]{2,1,0:T(8,128)S(1)} %get-tuple-element.256), channel_id=1, source_target_pairs={{0,16},{2,18},{4,20},{6,22},{8,24},{10,26},{12,28},{14,30},{1,17},... | collective-permute-start | bytes 24584 | tf_op jit(solution)/shard_map/ppermute | solution.py:1387
  76.7 1.3 %collective-permute-done.16.args_5_ = f32[2,8,128]{2,1,0:T(8,128)S(1)} collective-permute-done((f32[2,8,128]{2,1,0:T(8,128)S(1)}, f32[2,8,128]{2,1,0:T(8,128)S(1)}, u32[]{:S(2)}, u32[]{:S(2)}) %collective-permute-start.16) | collective-permute-done | bytes 8224 | tf_op jit(solution)/shard_map/ppermute | solution.py:1387
  78.1 0.2 shard_map.198
  78.3 0.1 collective-permute-start.19
  78.3 2.1 %collective-permute-start.20 = (bf16[384,128]{1,0:T(8,128)(2,1)S(1)}, bf16[384,128]{1,0:T(8,128)(2,1)S(1)}, u32[]{:S(2)}, u32[]{:S(2)}) collective-permute-start(bf16[384,128]{1,0:T(8,128)(2,1)S(1)} %get-tuple-element.270), channel_id=1, source_target_pairs={{0,6},{2,8},{4,10},{6,12},{8,14},{10,0},{12,2},{14,4},{1,7},{3,9},... | collective-permute-start | bytes 294920 | tf_op jit(solution)/shard_map/ppermute | solution.py:1393
  80.5 1.7 %collective-permute-start.17 = (bf16[672,128]{1,0:T(8,128)(2,1)S(1)}, bf16[672,128]{1,0:T(8,128)(2,1)S(1)}, u32[]{:S(2)}, u32[]{:S(2)}) collective-permute-start(bf16[672,128]{1,0:T(8,128)(2,1)S(1)} %get-tuple-element.257), channel_id=1, source_target_pairs={{0,2},{2,4},{4,6},{6,8},{8,10},{10,12},{12,14},{14,0},{1,3},{3,5},... | collective-permute-start | bytes 516104 | tf_op jit(solution)/shard_map/ppermute | solution.py:1393
  82.2 3.0 %collective-permute-start.18 = (bf16[672,128]{1,0:T(8,128)(2,1)S(1)}, bf16[672,128]{1,0:T(8,128)(2,1)S(1)}, u32[]{:S(2)}, u32[]{:S(2)}) collective-permute-start(bf16[672,128]{1,0:T(8,128)(2,1)S(1)} %get-tuple-element.258), channel_id=1, source_target_pairs={{0,14},{2,0},{4,2},{6,4},{8,6},{10,8},{12,10},{14,12},{1,15},{3,1}... | collective-permute-start | bytes 516104 | tf_op jit(solution)/shard_map/ppermute | solution.py:1393
  85.2 0.7 collective-permute-done.19
  85.9 0.7 collective-permute-start.22
  86.6 7.8 %collective-permute-done.20 = bf16[384,128]{1,0:T(8,128)(2,1)S(1)} collective-permute-done((bf16[384,128]{1,0:T(8,128)(2,1)S(1)}, bf16[384,128]{1,0:T(8,128)(2,1)S(1)}, u32[]{:S(2)}, u32[]{:S(2)}) %collective-permute-start.20) | collective-permute-done | bytes 98336 | tf_op jit(solution)/shard_map/ppermute | solution.py:1393
  94.4 0.0 collective-permute-start.23
  94.4 3.0 %collective-permute-done.21 = bf16[384,128]{1,0:T(8,128)(2,1)S(1)} collective-permute-done((bf16[384,128]{1,0:T(8,128)(2,1)S(1)}, bf16[384,128]{1,0:T(8,128)(2,1)S(1)}, u32[]{:S(2)}, u32[]{:S(2)}) %collective-permute-start.21) | collective-permute-done | bytes 98336 | tf_op jit(solution)/shard_map/ppermute | solution.py:1393
  97.4 0.0 collective-permute-done.22
  97.4 3.7 %collective-permute-done.23 = bf16[384,128]{1,0:T(8,128)(2,1)S(1)} collective-permute-done((bf16[384,128]{1,0:T(8,128)(2,1)S(1)}, bf16[384,128]{1,0:T(8,128)(2,1)S(1)}, u32[]{:S(2)}, u32[]{:S(2)}) %collective-permute-start.23) | collective-permute-done | bytes 98336 | tf_op jit(solution)/shard_map/ppermute | solution.py:1393
  101.1 0.1 convert_add_fusion.args_0_
  101.2 0.1 collective-permute-start.24
  101.3 1.0 shard_map.199
  102.2 0.5 collective-permute-done.24.args_1_
  102.7 0.8 shard_map.200
  (19 shorter events, 0.1 us)
Async XLA Ops:
  2.2 9.1 %collective-permute-start = (bf16[9,16,256]{2,1,0:T(8,128)(2,1)}, bf16[9,16,256]{2,1,0:T(8,128)(2,1)S(1)}, u32[]{:S(2)}, u32[]{:S(2)}) collective-permute-start(bf16[9,16,256]{2,1,0:T(8,128)(2,1)} %get-tuple-element.145), channel_id=1, source_target_pairs={{0,2},{2,4},{4,6},{6,8},{8,10},{10,12},{12,14},{14,0},{1,3},{3,5},... | collective-permute-start | bytes 221192 | tf_op jit(solution)/shard_map/ppermute | solution.py:1276
  5.2 6.1 %collective-permute-start.1 = (bf16[9,16,256]{2,1,0:T(8,128)(2,1)}, bf16[9,16,256]{2,1,0:T(8,128)(2,1)S(1)}, u32[]{:S(2)}, u32[]{:S(2)}) collective-permute-start(bf16[9,16,256]{2,1,0:T(8,128)(2,1)} %get-tuple-element.146), channel_id=1, source_target_pairs={{2,0},{4,2},{6,4},{8,6},{10,8},{12,10},{14,12},{0,14},{3,1},{5,3},... | collective-permute-start | bytes 221192 | tf_op jit(solution)/shard_map/ppermute | solution.py:1277
  11.3 11.5 %copy-start = (bf16[1,256,1280]{2,1,0:T(8,128)(2,1)S(1)}, bf16[1,256,1280]{2,1,0:T(8,128)(2,1)}, u32[]{:S(2)}) copy-start(bf16[1,256,1280]{2,1,0:T(8,128)(2,1)} %args_1_.10) | copy-start | bytes 1966084
  11.3 11.5 %copy-start.1 = (bf16[1,256,768]{2,1,0:T(8,128)(2,1)S(1)}, bf16[1,256,768]{2,1,0:T(8,128)(2,1)}, u32[]{:S(2)}) copy-start(bf16[1,256,768]{2,1,0:T(8,128)(2,1)} %args_2_.12) | copy-start | bytes 1179652
  11.4 11.5 %copy-start.2 = (bf16[1,256,768]{2,1,0:T(8,128)(2,1)S(1)}, bf16[1,256,768]{2,1,0:T(8,128)(2,1)}, u32[]{:S(2)}) copy-start(bf16[1,256,768]{2,1,0:T(8,128)(2,1)} %args_4_.12) | copy-start | bytes 1179652
  11.4 11.5 %copy-start.3 = (bf16[32,1024]{1,0:T(8,128)(2,1)S(1)}, bf16[32,1024]{1,0:T(8,128)(2,1)}, u32[]{:S(2)}) copy-start(bf16[32,1024]{1,0:T(8,128)(2,1)} %get-tuple-element.151.args_4_.args_3_) | copy-start | bytes 196612
  11.4 11.5 %copy-start.4 = (bf16[2,1,4,64,256]{4,3,2,1,0:T(8,128)(2,1)S(1)}, bf16[2,1,4,64,256]{4,3,2,1,0:T(8,128)(2,1)}, u32[]{:S(2)}) copy-start(bf16[2,1,4,64,256]{4,3,2,1,0:T(8,128)(2,1)} %args_5_.6) | copy-start | bytes 786436
  11.4 11.5 %copy-start.6 = (f32[2,104,128]{2,1,0:T(8,128)S(1)}, f32[2,104,128]{2,1,0:T(8,128)}, u32[]{:S(2)}) copy-start(f32[2,104,128]{2,1,0:T(8,128)} %get-tuple-element.167.args_3_) | copy-start | bytes 319492
  11.4 11.5 %copy-start.7 = (f32[8,256]{1,0:T(8,128)S(1)}, f32[8,256]{1,0:T(8,128)}, u32[]{:S(2)}) copy-start(f32[8,256]{1,0:T(8,128)} %get-tuple-element.150.args_6_.args_0_) | copy-start | bytes 24580
  11.4 11.5 %copy-start.8 = (f32[2,1,3,64]{3,1,2,0:T(1,128)S(1)}, f32[2,1,3,64]{3,1,2,0:T(1,128)}, u32[]{:S(2)}) copy-start(f32[2,1,3,64]{3,1,2,0:T(1,128)} %param.13) | copy-start | bytes 4612
  11.4 21.6 %copy-start.5 = (bf16[2,1,4,64,256]{4,3,2,1,0:T(8,128)(2,1)S(1)}, bf16[2,1,4,64,256]{4,3,2,1,0:T(8,128)(2,1)}, u32[]{:S(2)}) copy-start(bf16[2,1,4,64,256]{4,3,2,1,0:T(8,128)(2,1)} %args_15_.3) | copy-start | bytes 786436
  18.9 12.8 %collective-permute-start.2 = (bf16[4,64,256]{2,1,0:T(8,128)(2,1)S(1)}, bf16[4,64,256]{2,1,0:T(8,128)(2,1)S(1)}, u32[]{:S(2)}, u32[]{:S(2)}) collective-permute-start(bf16[4,64,256]{2,1,0:T(8,128)(2,1)S(1)} %get-tuple-element.155.args_3_), channel_id=1, source_target_pairs={{0,16},{2,18},{4,20},{6,22},{8,24},{10,26},{12,28},{14,30},{1,17},... | collective-permute-start | bytes 393224 | tf_op jit(solution)/shard_map/ppermute | solution.py:1323
  20.2 12.8 %collective-permute-start.3 = (bf16[4,16,256]{2,1,0:T(8,128)(2,1)S(1)}, bf16[4,16,256]{2,1,0:T(8,128)(2,1)S(1)}, u32[]{:S(2)}, u32[]{:S(2)}) collective-permute-start(bf16[4,16,256]{2,1,0:T(8,128)(2,1)S(1)} %get-tuple-element.164), channel_id=1, source_target_pairs={{0,18},{2,20},{4,22},{6,24},{8,26},{10,28},{12,30},{14,16},{1,19},... | collective-permute-start | bytes 98312 | tf_op jit(solution)/shard_map/ppermute | solution.py:1324
  21.5 11.5 %collective-permute-start.4 = (bf16[4,16,256]{2,1,0:T(8,128)(2,1)S(1)}, bf16[4,16,256]{2,1,0:T(8,128)(2,1)S(1)}, u32[]{:S(2)}, u32[]{:S(2)}) collective-permute-start(bf16[4,16,256]{2,1,0:T(8,128)(2,1)S(1)} %get-tuple-element.165), channel_id=1, source_target_pairs={{2,16},{4,18},{6,20},{8,22},{10,24},{12,26},{14,28},{0,30},{3,17},... | collective-permute-start | bytes 98312 | tf_op jit(solution)/shard_map/ppermute | solution.py:1325
  29.0 8.0 %collective-permute-start.9 = (bf16[4,64,256]{2,1,0:T(8,128)(2,1)S(1)}, bf16[4,64,256]{2,1,0:T(8,128)(2,1)S(1)}, u32[]{:S(2)}, u32[]{:S(2)}) collective-permute-start(bf16[4,64,256]{2,1,0:T(8,128)(2,1)S(1)} %get-tuple-element.196), channel_id=1, source_target_pairs={{0,18},{2,20},{4,22},{6,24},{8,26},{10,28},{12,30},{14,16},{1,19},... | collective-permute-start | bytes 393224 | tf_op jit(solution)/shard_map/ppermute | solution.py:1324
  30.3 14.6 %collective-permute-start.8 = (bf16[4,64,256]{2,1,0:T(8,128)(2,1)S(1)}, bf16[4,64,256]{2,1,0:T(8,128)(2,1)S(1)}, u32[]{:S(2)}, u32[]{:S(2)}) collective-permute-start(bf16[4,64,256]{2,1,0:T(8,128)(2,1)S(1)} %get-tuple-element.195.args_5_), channel_id=1, source_target_pairs={{0,16},{2,18},{4,20},{6,22},{8,24},{10,26},{12,28},{14,30},{1,17},... | collective-permute-start | bytes 393224 | tf_op jit(solution)/shard_map/ppermute | solution.py:1323
  31.7 13.3 %collective-permute-start.10 = (bf16[4,64,256]{2,1,0:T(8,128)(2,1)S(1)}, bf16[4,64,256]{2,1,0:T(8,128)(2,1)S(1)}, u32[]{:S(2)}, u32[]{:S(2)}) collective-permute-start(bf16[4,64,256]{2,1,0:T(8,128)(2,1)S(1)} %get-tuple-element.197), channel_id=1, source_target_pairs={{2,16},{4,18},{6,20},{8,22},{10,24},{12,26},{14,28},{0,30},{3,17},... | collective-permute-start | bytes 393224 | tf_op jit(solution)/shard_map/ppermute | solution.py:1325
  33.1 15.2 %collective-permute-start.5 = (bf16[4,64,256]{2,1,0:T(8,128)(2,1)S(1)}, bf16[4,64,256]{2,1,0:T(8,128)(2,1)S(1)}, u32[]{:S(2)}, u32[]{:S(2)}) collective-permute-start(bf16[4,64,256]{2,1,0:T(8,128)(2,1)S(1)} %get-tuple-element.185), channel_id=1, source_target_pairs={{16,0},{18,2},{20,4},{22,6},{24,8},{26,10},{28,12},{30,14},{17,1},... | collective-permute-start | bytes 393224 | tf_op jit(solution)/shard_map/ppermute | solution.py:1368
  34.4 13.9 %collective-permute-start.6 = (bf16[4,16,256]{2,1,0:T(8,128)(2,1)S(1)}, bf16[4,16,256]{2,1,0:T(8,128)(2,1)S(1)}, u32[]{:S(2)}, u32[]{:S(2)}) collective-permute-start(bf16[4,16,256]{2,1,0:T(8,128)(2,1)S(1)} %get-tuple-element.186.args_28_), channel_id=1, source_target_pairs={{16,2},{18,4},{20,6},{22,8},{24,10},{26,12},{28,14},{30,0},{17,3},... | collective-permute-start | bytes 98312 | tf_op jit(solution)/shard_map/ppermute | solution.py:1369
  37.0 11.2 %collective-permute-start.7 = (bf16[4,16,256]{2,1,0:T(8,128)(2,1)S(1)}, bf16[4,16,256]{2,1,0:T(8,128)(2,1)S(1)}, u32[]{:S(2)}, u32[]{:S(2)}) collective-permute-start(bf16[4,16,256]{2,1,0:T(8,128)(2,1)S(1)} %get-tuple-element.187.args_27_), channel_id=1, source_target_pairs={{18,0},{20,2},{22,4},{24,6},{26,8},{28,10},{30,12},{16,14},{19,1},... | collective-permute-start | bytes 98312 | tf_op jit(solution)/shard_map/ppermute | solution.py:1370
  48.3 16.5 %collective-permute-start.11 = (bf16[4,64,256]{2,1,0:T(8,128)(2,1)S(1)}, bf16[4,64,256]{2,1,0:T(8,128)(2,1)S(1)}, u32[]{:S(2)}, u32[]{:S(2)}) collective-permute-start(bf16[4,64,256]{2,1,0:T(8,128)(2,1)S(1)} %get-tuple-element.226), channel_id=1, source_target_pairs={{16,0},{18,2},{20,4},{22,6},{24,8},{26,10},{28,12},{30,14},{17,1},... | collective-permute-start | bytes 393224 | tf_op jit(solution)/shard_map/ppermute | solution.py:1368
  49.5 15.2 %collective-permute-start.12 = (bf16[4,16,256]{2,1,0:T(8,128)(2,1)S(1)}, bf16[4,16,256]{2,1,0:T(8,128)(2,1)S(1)}, u32[]{:S(2)}, u32[]{:S(2)}) collective-permute-start(bf16[4,16,256]{2,1,0:T(8,128)(2,1)S(1)} %get-tuple-element.227.args_31_), channel_id=1, source_target_pairs={{16,2},{18,4},{20,6},{22,8},{24,10},{26,12},{28,14},{30,0},{17,3},... | collective-permute-start | bytes 98312 | tf_op jit(solution)/shard_map/ppermute | solution.py:1369
  50.8 13.9 %collective-permute-start.13 = (bf16[4,16,256]{2,1,0:T(8,128)(2,1)S(1)}, bf16[4,16,256]{2,1,0:T(8,128)(2,1)S(1)}, u32[]{:S(2)}, u32[]{:S(2)}) collective-permute-start(bf16[4,16,256]{2,1,0:T(8,128)(2,1)S(1)} %get-tuple-element.228.args_30_), channel_id=1, source_target_pairs={{18,0},{20,2},{22,4},{24,6},{26,8},{28,10},{30,12},{16,14},{19,1},... | collective-permute-start | bytes 98312 | tf_op jit(solution)/shard_map/ppermute | solution.py:1370
  52.1 12.4 %collective-permute-start.14 = (f32[2,8,128]{2,1,0:T(8,128)S(1)}, f32[2,8,128]{2,1,0:T(8,128)S(1)}, u32[]{:S(2)}, u32[]{:S(2)}) collective-permute-start(f32[2,8,128]{2,1,0:T(8,128)S(1)} %get-tuple-element.229), channel_id=1, source_target_pairs={{16,0},{18,2},{20,4},{22,6},{24,8},{26,10},{28,12},{30,14},{17,1},... | collective-permute-start | bytes 24584 | tf_op jit(solution)/shard_map/ppermute | solution.py:1381
  75.3 2.7 %collective-permute-start.15 = (bf16[8,384,128]{2,1,0:T(8,128)(2,1)S(1)}, bf16[8,384,128]{2,1,0:T(8,128)(2,1)S(1)}, u32[]{:S(2)}, u32[]{:S(2)}) collective-permute-start(bf16[8,384,128]{2,1,0:T(8,128)(2,1)S(1)} %get-tuple-element.252), channel_id=1, source_target_pairs={{0,1},{1,0},{2,3},{3,2},{4,5},{5,4},{6,7},{7,6},{8,9},{9,8},{10,11... | collective-permute-start | bytes 2359304 | tf_op jit(solution)/shard_map/ppermute | solution.py:1389
  75.4 2.6 %collective-permute-start.16 = (f32[2,8,128]{2,1,0:T(8,128)S(1)}, f32[2,8,128]{2,1,0:T(8,128)S(1)}, u32[]{:S(2)}, u32[]{:S(2)}) collective-permute-start(f32[2,8,128]{2,1,0:T(8,128)S(1)} %get-tuple-element.256), channel_id=1, source_target_pairs={{0,16},{2,18},{4,20},{6,22},{8,24},{10,26},{12,28},{14,30},{1,17},... | collective-permute-start | bytes 24584 | tf_op jit(solution)/shard_map/ppermute | solution.py:1387
  78.3 7.6 %collective-permute-start.19 = (bf16[384,128]{1,0:T(8,128)(2,1)S(1)}, bf16[384,128]{1,0:T(8,128)(2,1)S(1)}, u32[]{:S(2)}, u32[]{:S(2)}) collective-permute-start(bf16[384,128]{1,0:T(8,128)(2,1)S(1)} %get-tuple-element.269), channel_id=1, source_target_pairs={{0,4},{2,6},{4,8},{6,10},{8,12},{10,14},{12,0},{14,2},{1,5},{3,7},... | collective-permute-start | bytes 294920 | tf_op jit(solution)/shard_map/ppermute | solution.py:1393
  78.3 16.0 %collective-permute-start.20 = (bf16[384,128]{1,0:T(8,128)(2,1)S(1)}, bf16[384,128]{1,0:T(8,128)(2,1)S(1)}, u32[]{:S(2)}, u32[]{:S(2)}) collective-permute-start(bf16[384,128]{1,0:T(8,128)(2,1)S(1)} %get-tuple-element.270), channel_id=1, source_target_pairs={{0,6},{2,8},{4,10},{6,12},{8,14},{10,0},{12,2},{14,4},{1,7},{3,9},... | collective-permute-start | bytes 294920 | tf_op jit(solution)/shard_map/ppermute | solution.py:1393
  80.5 20.6 %collective-permute-start.17 = (bf16[672,128]{1,0:T(8,128)(2,1)S(1)}, bf16[672,128]{1,0:T(8,128)(2,1)S(1)}, u32[]{:S(2)}, u32[]{:S(2)}) collective-permute-start(bf16[672,128]{1,0:T(8,128)(2,1)S(1)} %get-tuple-element.257), channel_id=1, source_target_pairs={{0,2},{2,4},{4,6},{6,8},{8,10},{10,12},{12,14},{14,0},{1,3},{3,5},... | collective-permute-start | bytes 516104 | tf_op jit(solution)/shard_map/ppermute | solution.py:1393
  82.2 18.9 %collective-permute-start.18 = (bf16[672,128]{1,0:T(8,128)(2,1)S(1)}, bf16[672,128]{1,0:T(8,128)(2,1)S(1)}, u32[]{:S(2)}, u32[]{:S(2)}) collective-permute-start(bf16[672,128]{1,0:T(8,128)(2,1)S(1)} %get-tuple-element.258), channel_id=1, source_target_pairs={{0,14},{2,0},{4,2},{6,4},{8,6},{10,8},{12,10},{14,12},{1,15},{3,1}... | collective-permute-start | bytes 516104 | tf_op jit(solution)/shard_map/ppermute | solution.py:1393
  85.2 12.2 %collective-permute-start.21 = (bf16[384,128]{1,0:T(8,128)(2,1)S(1)}, bf16[384,128]{1,0:T(8,128)(2,1)S(1)}, u32[]{:S(2)}, u32[]{:S(2)}) collective-permute-start(bf16[384,128]{1,0:T(8,128)(2,1)S(1)} %get-tuple-element.271), channel_id=1, source_target_pairs={{0,8},{2,10},{4,12},{6,14},{8,0},{10,2},{12,4},{14,6},{1,9},{3,11}... | collective-permute-start | bytes 294920 | tf_op jit(solution)/shard_map/ppermute | solution.py:1393
  85.9 11.5 %collective-permute-start.22 = (bf16[384,128]{1,0:T(8,128)(2,1)S(1)}, bf16[384,128]{1,0:T(8,128)(2,1)S(1)}, u32[]{:S(2)}, u32[]{:S(2)}) collective-permute-start(bf16[384,128]{1,0:T(8,128)(2,1)S(1)} %get-tuple-element.272), channel_id=1, source_target_pairs={{0,10},{2,12},{4,14},{6,0},{8,2},{10,4},{12,6},{14,8},{1,11},{3,13... | collective-permute-start | bytes 294920 | tf_op jit(solution)/shard_map/ppermute | solution.py:1393
  94.4 6.7 %collective-permute-start.23 = (bf16[384,128]{1,0:T(8,128)(2,1)S(1)}, bf16[384,128]{1,0:T(8,128)(2,1)S(1)}, u32[]{:S(2)}, u32[]{:S(2)}) collective-permute-start(bf16[384,128]{1,0:T(8,128)(2,1)S(1)} %get-tuple-element.273), channel_id=1, source_target_pairs={{0,12},{2,14},{4,0},{6,2},{8,4},{10,6},{12,8},{14,10},{1,13},{3,15... | collective-permute-start | bytes 294920 | tf_op jit(solution)/shard_map/ppermute | solution.py:1393
  101.2 1.5 %collective-permute-start.24 = (f32[384,128]{1,0:T(8,128)S(1)}, f32[384,128]{1,0:T(8,128)S(1)}, u32[]{:S(2)}, u32[]{:S(2)}) collective-permute-start(f32[384,128]{1,0:T(8,128)S(1)} %convert_add_fusion.args_0_), channel_id=1, source_target_pairs={{0,1},{1,0},{2,3},{3,2},{4,5},{5,4},{6,7},{7,6},{8,9},{9,8},{10,11... | collective-permute-start | bytes 589832 | tf_op jit(solution)/shard_map/ppermute | solution.py:1406

commit v6 on v5

--- a/solution.py
+++ b/solution.py
@@ -404,7 +404,7 @@
                     w.slope[b, part * sz.halves + cg] = slope[:, half]
             return carry
 
-        lax.fori_loop(0, sz.blocks, block, 0, unroll=2)
+        lax.fori_loop(0, sz.blocks, block, 0, unroll=4)
 
 
 def both_ways(r, sz, m, fwd):
@@ -782,7 +782,7 @@
     shape = jax.ShapeDtypeStruct
     outs = SimpleNamespace(
         back=shape((4, A, F), F32),
-        back_low=shape((4, A, F), BF16),
+        back_low=shape((5 if fwd and m else 4, A, F), BF16),
         rim_low=shape((4, H, F), BF16),
         rim_high=shape((4, H, F), BF16),
         gplaces=shape((8, LANES), F32),
@@ -820,15 +820,15 @@
             score=((NB, CG, EB, LANES), BF16), sagg=((A, F), F32), vagg=((3, A, F), F32), uagg=((3 * A, F), F32)
         )
     if fwd and m:
-        outs.all_places = shape((m + 1, 8, LANES), F32)
         for i, made in enumerate(border_sets):
             setattr(arrays, f"gplaces_{i}", (made.gplaces, VMEM))
 
         def layer(r):
             both_ways(r, sz, m, fwd)
-            for i in range(m):
-                r.all_places[i] = getattr(r, f"gplaces_{i}")[...]
-            r.all_places[m] = r.gplaces[...]
+            for i in range(m + 1):
+                places = r.gplaces if i == m else getattr(r, f"gplaces_{i}")
+                rows = [places[c : c + 1, :] for c in range(3)]
+                r.back_low[4, 16 * i : 16 * i + 16, :] = packed_places(rows, F)
 
         return call(layer, arrays, outs, scratch, SECOND)
     if not border_sets:
@@ -852,7 +852,11 @@
             r.up[i] = high[...]
             r.down[i] = low[...]
             r.moved[i] = places[...]
-            r.total[i] = places[...] + r.early[i] if role == FIRST else places[...]
+            r.total[i] = places[...]
+            if role == FIRST:
+                block = r.inc[4, 16 * i : 16 * i + 16, :]
+                for c in range(3):
+                    r.total[i, c : c + 1, :] += unpacked_places(block, c, 0, LANES)
 
     def body(r):
         @pl.when(lax.axis_index("section") == FIRST)
@@ -1377,8 +1381,6 @@
         inc, inc_low, inc_high = returned[m]
         arrays.inc, arrays.inc_low, arrays.inc_high = (inc, VMEM), (inc_low, VMEM), (inc_high, VMEM)
         sets = (thirds, seconds) if m == micro_count - 1 else ()
-        if sets:
-            arrays.early = (lax.ppermute(seconds[-1].all_places, both, back), VMEM)
         third = both_call(sz, m, False, arrays, sets)
         third.left = firsts[m].left
         thirds.append(third)

time: 104 us -> 102 us (0.981)
  starting transfers between devices: 32.2 us -> 30.7 us
    ppermute x2, waiting for transfers between devices: 3.39 us -> 4.99 us  [on_device(): lax.ppermute(rim_high, both, back_up)]
    ppermute x1 -> x0, waiting for transfers between devices: 1.45 us -> none  [on_device(): arrays.early = (lax.ppermute(seconds[-1].all_places, both, back), VMEM)]
    ppermute x1 -> x0, starting transfers between devices: 1.29 us -> none  [on_device(): arrays.early = (lax.ppermute(seconds[-1].all_places, both, back), VMEM)]
  transfers between devices with their start and end apart: 25 -> 24, of which waited for: 10 -> 9; matrix products, arithmetic and copies ran while one was open for 0% -> 0% of each run, Pallas kernels for 26% -> 26%
where the time goes in v6:
time: 102 us
  Pallas kernels  46.5 us (46%)
  starting transfers between devices  30.7 us (30%)
  waiting for transfers between devices  23.1 us (23%)
  between operations  1.05 us (1%)
    pallas_call x14, Pallas kernels, call(): pl.pallas_call(kernel, out_shape=list(outs.values()), in_specs=[spec for...  46.5 us
    ppermute x7, waiting for transfers between devices, on_device(): lax.ppermute(piece, 'space', [(i, (i + hop) % space) for i in range(space)])  15.1 us
    ppermute x7, starting transfers between devices, on_device(): lax.ppermute(piece, 'space', [(i, (i + hop) % space) for i in range(space)])  7.68 us
    ppermute x2, waiting for transfers between devices, on_device(): lax.ppermute(rim_high, both, back_up)  4.99 us
    ppermute x1, starting transfers between devices, on_device(): pack_high = lax.ppermute(borders.down, 'space', down)  3.1 us
    ppermute x1, starting transfers between devices, on_device(): pack_low = lax.ppermute(borders.up, 'space', up)  3.02 us
    ppermute x2, starting transfers between devices, on_device(): lax.ppermute(first.fresh, both, forth)  2.59 us
    ppermute x2, starting transfers between devices, on_device(): lax.ppermute(first.head, both, forth_down)  2.59 us
  transfers between devices with their start and end apart: 24, of which 9 were waited for; matrix products, arithmetic and copies ran while one was open for 0% of the time, Pallas kernels for 26%

profile of v6, /device:TPU:0, one launch (start us, length us, event | category | flops | bytes accessed | tf_op | source)
XLA Modules:
  0.0 101.5 jit_solution(3479080381158493554)
XLA Ops:
  0.6 1.5 %shard_map.187 = (bf16[9,16,256]{2,1,0:T(8,128)(2,1)}, bf16[9,16,256]{2,1,0:T(8,128)(2,1)}) custom-call(bf16[2,1,4,64,256]{4,3,2,1,0:T(8,128)(2,1)} %args_5_.6, f32[2,3,1,64]{3,2,1,0:T(1,128)} %bitcast.5), custom_call_target="tpu_custom_call" | custom-call | tf_op jit(solution)/shard_map/pallas_call | solution.py:682
  2.2 3.0 %collective-permute-start = (bf16[9,16,256]{2,1,0:T(8,128)(2,1)}, bf16[9,16,256]{2,1,0:T(8,128)(2,1)S(1)}, u32[]{:S(2)}, u32[]{:S(2)}) collective-permute-start(bf16[9,16,256]{2,1,0:T(8,128)(2,1)} %get-tuple-element.144), channel_id=1, source_target_pairs={{0,2},{2,4},{4,6},{6,8},{8,10},{10,12},{12,14},{14,0},{1,3},{3,5},... | collective-permute-start | bytes 221192 | tf_op jit(solution)/shard_map/ppermute | solution.py:1280
  5.2 3.1 %collective-permute-start.1 = (bf16[9,16,256]{2,1,0:T(8,128)(2,1)}, bf16[9,16,256]{2,1,0:T(8,128)(2,1)S(1)}, u32[]{:S(2)}, u32[]{:S(2)}) collective-permute-start(bf16[9,16,256]{2,1,0:T(8,128)(2,1)} %get-tuple-element.145), channel_id=1, source_target_pairs={{2,0},{4,2},{6,4},{8,6},{10,8},{12,10},{14,12},{0,14},{3,1},{5,3},... | collective-permute-start | bytes 221192 | tf_op jit(solution)/shard_map/ppermute | solution.py:1281
  8.3 3.0 %shard_map.188 = (f32[2,104,128]{2,1,0:T(8,128)}, f32[8,256]{1,0:T(8,128)}, bf16[32,1024]{1,0:T(8,128)(2,1)}, bf16[20480,1280]{1,0:T(8,128)(2,1)}, f32[51200,256]{1,0:T(8,128)}) custom-call(bf16[2,1,4,64,256]{4,3,2,1,0:T(8,128)(2,1)} %args_5_.6, f32[2,3,1,64]{3,2,1,0:T(1,128)} %bitcast.6, s32[2,1,32,64]{3,2,1,0:T(8,128)} %args_2_.8, ...), custom_call_target="tpu_custom_call" | custom-call | tf_op jit(solution)/shard_map/pallas_call | solution.py:682
  11.3 0.0 collective-permute-done.args_0_
  11.3 0.0 collective-permute-done.1.args_1_
  11.3 0.0 copy-start
  11.4 0.0 copy-start.1
  11.4 0.0 copy-start.2
  11.4 0.0 copy-start.3
  11.4 0.0 copy-start.4
  11.4 0.0 copy-start.6
  11.4 0.0 copy-start.7
  11.4 0.0 copy-start.8
  11.4 0.0 copy-start.5
  11.4 7.5 %shard_map.189 = (bf16[4,64,256]{2,1,0:T(8,128)(2,1)S(1)}, bf16[4,16,256]{2,1,0:T(8,128)(2,1)S(1)}, bf16[4,16,256]{2,1,0:T(8,128)(2,1)S(1)}, bf16[384,256]{1,0:T...) custom-call(bf16[9,16,256]{2,1,0:T(8,128)(2,1)S(1)} %collective-perm, ...), custom_call_target="tpu_custom_call" | custom-call | tf_op jit(solution)/shard_map/pallas_call | solution.py:682
  18.9 1.3 %collective-permute-start.2 = (bf16[4,64,256]{2,1,0:T(8,128)(2,1)S(1)}, bf16[4,64,256]{2,1,0:T(8,128)(2,1)S(1)}, u32[]{:S(2)}, u32[]{:S(2)}) collective-permute-start(bf16[4,64,256]{2,1,0:T(8,128)(2,1)S(1)} %get-tuple-element.154.args_3_), channel_id=1, source_target_pairs={{0,16},{2,18},{4,20},{6,22},{8,24},{10,26},{12,28},{14,30},{1,17},... | collective-permute-start | bytes 393224 | tf_op jit(solution)/shard_map/ppermute | solution.py:1327
  20.2 1.3 %collective-permute-start.3 = (bf16[4,16,256]{2,1,0:T(8,128)(2,1)S(1)}, bf16[4,16,256]{2,1,0:T(8,128)(2,1)S(1)}, u32[]{:S(2)}, u32[]{:S(2)}) collective-permute-start(bf16[4,16,256]{2,1,0:T(8,128)(2,1)S(1)} %get-tuple-element.163), channel_id=1, source_target_pairs={{0,18},{2,20},{4,22},{6,24},{8,26},{10,28},{12,30},{14,16},{1,19},... | collective-permute-start | bytes 98312 | tf_op jit(solution)/shard_map/ppermute | solution.py:1328
  21.5 1.3 %collective-permute-start.4 = (bf16[4,16,256]{2,1,0:T(8,128)(2,1)S(1)}, bf16[4,16,256]{2,1,0:T(8,128)(2,1)S(1)}, u32[]{:S(2)}, u32[]{:S(2)}) collective-permute-start(bf16[4,16,256]{2,1,0:T(8,128)(2,1)S(1)} %get-tuple-element.164), channel_id=1, source_target_pairs={{2,16},{4,18},{6,20},{8,22},{10,24},{12,26},{14,28},{0,30},{3,17},... | collective-permute-start | bytes 98312 | tf_op jit(solution)/shard_map/ppermute | solution.py:1329
  22.9 6.2 %shard_map.190 = (bf16[4,64,256]{2,1,0:T(8,128)(2,1)S(1)}, bf16[4,64,256]{2,1,0:T(8,128)(2,1)S(1)}, bf16[4,64,256]{2,1,0:T(8,128)(2,1)S(1)}, bf16[384,256]{1,0:T...) custom-call(bf16[9,16,256]{2,1,0:T(8,128)(2,1)S(1)} %collective-perm, ...), custom_call_target="tpu_custom_call" | custom-call | tf_op jit(solution)/shard_map/pallas_call | solution.py:682
  29.0 1.3 %collective-permute-start.9 = (bf16[4,64,256]{2,1,0:T(8,128)(2,1)S(1)}, bf16[4,64,256]{2,1,0:T(8,128)(2,1)S(1)}, u32[]{:S(2)}, u32[]{:S(2)}) collective-permute-start(bf16[4,64,256]{2,1,0:T(8,128)(2,1)S(1)} %get-tuple-element.195), channel_id=1, source_target_pairs={{0,18},{2,20},{4,22},{6,24},{8,26},{10,28},{12,30},{14,16},{1,19},... | collective-permute-start | bytes 393224 | tf_op jit(solution)/shard_map/ppermute | solution.py:1328
  30.4 1.3 %collective-permute-start.8 = (bf16[4,64,256]{2,1,0:T(8,128)(2,1)S(1)}, bf16[4,64,256]{2,1,0:T(8,128)(2,1)S(1)}, u32[]{:S(2)}, u32[]{:S(2)}) collective-permute-start(bf16[4,64,256]{2,1,0:T(8,128)(2,1)S(1)} %get-tuple-element.194.args_5_), channel_id=1, source_target_pairs={{0,16},{2,18},{4,20},{6,22},{8,24},{10,26},{12,28},{14,30},{1,17},... | collective-permute-start | bytes 393224 | tf_op jit(solution)/shard_map/ppermute | solution.py:1327
  31.7 0.0 collective-permute-done.2.args_12_
  31.7 1.3 %collective-permute-start.10 = (bf16[4,64,256]{2,1,0:T(8,128)(2,1)S(1)}, bf16[4,64,256]{2,1,0:T(8,128)(2,1)S(1)}, u32[]{:S(2)}, u32[]{:S(2)}) collective-permute-start(bf16[4,64,256]{2,1,0:T(8,128)(2,1)S(1)} %get-tuple-element.196), channel_id=1, source_target_pairs={{2,16},{4,18},{6,20},{8,22},{10,24},{12,26},{14,28},{0,30},{3,17},... | collective-permute-start | bytes 393224 | tf_op jit(solution)/shard_map/ppermute | solution.py:1329
  33.0 0.0 collective-permute-done.3.args_13_
  33.0 0.2 shard_map.192
  33.2 1.3 %collective-permute-start.5 = (bf16[4,64,256]{2,1,0:T(8,128)(2,1)S(1)}, bf16[4,64,256]{2,1,0:T(8,128)(2,1)S(1)}, u32[]{:S(2)}, u32[]{:S(2)}) collective-permute-start(bf16[4,64,256]{2,1,0:T(8,128)(2,1)S(1)} %get-tuple-element.184), channel_id=1, source_target_pairs={{16,0},{18,2},{20,4},{22,6},{24,8},{26,10},{28,12},{30,14},{17,1},... | collective-permute-start | bytes 393224 | tf_op jit(solution)/shard_map/ppermute | solution.py:1372
  34.5 1.3 %collective-permute-start.6 = (bf16[4,16,256]{2,1,0:T(8,128)(2,1)S(1)}, bf16[4,16,256]{2,1,0:T(8,128)(2,1)S(1)}, u32[]{:S(2)}, u32[]{:S(2)}) collective-permute-start(bf16[4,16,256]{2,1,0:T(8,128)(2,1)S(1)} %get-tuple-element.185.args_27_), channel_id=1, source_target_pairs={{16,2},{18,4},{20,6},{22,8},{24,10},{26,12},{28,14},{30,0},{17,3},... | collective-permute-start | bytes 98312 | tf_op jit(solution)/shard_map/ppermute | solution.py:1373
  35.8 1.2 %collective-permute-done.9.args_13_ = bf16[4,64,256]{2,1,0:T(8,128)(2,1)S(1)} collective-permute-done((bf16[4,64,256]{2,1,0:T(8,128)(2,1)S(1)}, bf16[4,64,256]{2,1,0:T(8,128)(2,1)S(1)}, u32[]{:S(2)}, u32[]{:S(2)}) %collective-permute-start.9) | collective-permute-done | bytes 131104 | tf_op jit(solution)/shard_map/ppermute | solution.py:1328
  37.0 1.3 %collective-permute-start.7 = (bf16[4,16,256]{2,1,0:T(8,128)(2,1)S(1)}, bf16[4,16,256]{2,1,0:T(8,128)(2,1)S(1)}, u32[]{:S(2)}, u32[]{:S(2)}) collective-permute-start(bf16[4,16,256]{2,1,0:T(8,128)(2,1)S(1)} %get-tuple-element.186.args_26_), channel_id=1, source_target_pairs={{18,0},{20,2},{22,4},{24,6},{26,8},{28,10},{30,12},{16,14},{19,1},... | collective-permute-start | bytes 98312 | tf_op jit(solution)/shard_map/ppermute | solution.py:1374
  38.3 6.2 %shard_map.193 = (f32[10,8,256]{2,1,0:T(8,128)S(1)}, bf16[8,32,256]{2,1,0:T(8,128)(2,1)S(1)}, bf16[8,256,128]{2,1,0:T(8,128)(2,1)S(1)}, bf16[8,192,256]{2,1,0:T(...) custom-call(bf16[9,16,256]{2,1,0:T(8,128)(2,1)S(1)} %collective-perm, ...), custom_call_target="tpu_custom_call" | custom-call | tf_op jit(solution)/shard_map/pallas_call | solution.py:682
  44.5 0.0 collective-permute-done.10.args_14_
  44.6 2.9 %collective-permute-done.6.args_21_ = bf16[4,16,256]{2,1,0:T(8,128)(2,1)S(1)} collective-permute-done((bf16[4,16,256]{2,1,0:T(8,128)(2,1)S(1)}, bf16[4,16,256]{2,1,0:T(8,128)(2,1)S(1)}, u32[]{:S(2)}, u32[]{:S(2)}) %collective-permute-start.6) | collective-permute-done | bytes 32800 | tf_op jit(solution)/shard_map/ppermute | solution.py:1373
  47.5 0.0 collective-permute-done.7.args_22_
  47.5 0.0 collective-permute-done.5.args_20_
  47.5 1.3 %collective-permute-start.11 = (bf16[5,64,256]{2,1,0:T(8,128)(2,1)S(1)}, bf16[5,64,256]{2,1,0:T(8,128)(2,1)S(1)}, u32[]{:S(2)}, u32[]{:S(2)}) collective-permute-start(bf16[5,64,256]{2,1,0:T(8,128)(2,1)S(1)} %get-tuple-element.225), channel_id=1, source_target_pairs={{16,0},{18,2},{20,4},{22,6},{24,8},{26,10},{28,12},{30,14},{17,1},... | collective-permute-start | bytes 491528 | tf_op jit(solution)/shard_map/ppermute | solution.py:1372
  48.8 1.3 %collective-permute-start.12 = (bf16[4,16,256]{2,1,0:T(8,128)(2,1)S(1)}, bf16[4,16,256]{2,1,0:T(8,128)(2,1)S(1)}, u32[]{:S(2)}, u32[]{:S(2)}) collective-permute-start(bf16[4,16,256]{2,1,0:T(8,128)(2,1)S(1)} %get-tuple-element.226.args_30_), channel_id=1, source_target_pairs={{16,2},{18,4},{20,6},{22,8},{24,10},{26,12},{28,14},{30,0},{17,3},... | collective-permute-start | bytes 98312 | tf_op jit(solution)/shard_map/ppermute | solution.py:1373
  50.1 1.3 %collective-permute-start.13 = (bf16[4,16,256]{2,1,0:T(8,128)(2,1)S(1)}, bf16[4,16,256]{2,1,0:T(8,128)(2,1)S(1)}, u32[]{:S(2)}, u32[]{:S(2)}) collective-permute-start(bf16[4,16,256]{2,1,0:T(8,128)(2,1)S(1)} %get-tuple-element.227.args_29_), channel_id=1, source_target_pairs={{18,0},{20,2},{22,4},{24,6},{26,8},{28,10},{30,12},{16,14},{19,1},... | collective-permute-start | bytes 98312 | tf_op jit(solution)/shard_map/ppermute | solution.py:1374
  51.4 9.6 %shard_map.195 = (f32[4,64,256]{2,1,0:T(8,128)S(1)}, bf16[4,64,256]{2,1,0:T(8,128)(2,1)}, bf16[4,16,256]{2,1,0:T(8,128)(2,1)S(1)}, bf16[4,16,256]{2,1,0:T(8,128)...) custom-call(f32[8,256]{1,0:T(8,128)S(1)} %copy-done.7, ...), custom_call_target="tpu_custom_call" | custom-call | tf_op jit(solution)/shard_map/pallas_call | solution.py:682
  60.9 2.1 %collective-permute-done.12.args_21_ = bf16[4,16,256]{2,1,0:T(8,128)(2,1)S(1)} collective-permute-done((bf16[4,16,256]{2,1,0:T(8,128)(2,1)S(1)}, bf16[4,16,256]{2,1,0:T(8,128)(2,1)S(1)}, u32[]{:S(2)}, u32[]{:S(2)}) %collective-permute-start.12) | collective-permute-done | bytes 32800 | tf_op jit(solution)/shard_map/ppermute | solution.py:1373
  63.0 0.0 collective-permute-done.13.args_22_
  63.0 0.0 collective-permute-done.11.args_20_
  63.0 9.4 %shard_map.196 = (f32[4,64,256]{2,1,0:T(8,128)S(1)}, bf16[4,64,256]{2,1,0:T(8,128)(2,1)}, bf16[4,16,256]{2,1,0:T(8,128)(2,1)}, bf16[4,16,256]{2,1,0:T(8,128)(2,1...) custom-call(f32[8,256]{1,0:T(8,128)S(1)} %copy-done.7, ...), custom_call_target="tpu_custom_call" | custom-call | tf_op jit(solution)/shard_map/pallas_call | solution.py:682
  72.4 1.0 shard_map.197
  73.4 0.1 collective-permute-start.14
  73.5 1.3 %collective-permute-start.15 = (f32[2,8,128]{2,1,0:T(8,128)S(1)}, f32[2,8,128]{2,1,0:T(8,128)S(1)}, u32[]{:S(2)}, u32[]{:S(2)}) collective-permute-start(f32[2,8,128]{2,1,0:T(8,128)S(1)} %get-tuple-element.254), channel_id=1, source_target_pairs={{0,16},{2,18},{4,20},{6,22},{8,24},{10,26},{12,28},{14,30},{1,17},... | collective-permute-start | bytes 24584 | tf_op jit(solution)/shard_map/ppermute | solution.py:1389
  74.8 1.3 %collective-permute-done.15.args_5_ = f32[2,8,128]{2,1,0:T(8,128)S(1)} collective-permute-done((f32[2,8,128]{2,1,0:T(8,128)S(1)}, f32[2,8,128]{2,1,0:T(8,128)S(1)}, u32[]{:S(2)}, u32[]{:S(2)}) %collective-permute-start.15) | collective-permute-done | bytes 8224 | tf_op jit(solution)/shard_map/ppermute | solution.py:1389
  76.1 0.2 shard_map.198
  76.3 0.1 collective-permute-start.18
  76.4 2.1 %collective-permute-start.19 = (bf16[384,128]{1,0:T(8,128)(2,1)S(1)}, bf16[384,128]{1,0:T(8,128)(2,1)S(1)}, u32[]{:S(2)}, u32[]{:S(2)}) collective-permute-start(bf16[384,128]{1,0:T(8,128)(2,1)S(1)} %get-tuple-element.268), channel_id=1, source_target_pairs={{0,6},{2,8},{4,10},{6,12},{8,14},{10,0},{12,2},{14,4},{1,7},{3,9},... | collective-permute-start | bytes 294920 | tf_op jit(solution)/shard_map/ppermute | solution.py:1395
  78.6 1.5 %collective-permute-start.16 = (bf16[672,128]{1,0:T(8,128)(2,1)S(1)}, bf16[672,128]{1,0:T(8,128)(2,1)S(1)}, u32[]{:S(2)}, u32[]{:S(2)}) collective-permute-start(bf16[672,128]{1,0:T(8,128)(2,1)S(1)} %get-tuple-element.255), channel_id=1, source_target_pairs={{0,2},{2,4},{4,6},{6,8},{8,10},{10,12},{12,14},{14,0},{1,3},{3,5},... | collective-permute-start | bytes 516104 | tf_op jit(solution)/shard_map/ppermute | solution.py:1395
  80.1 3.2 %collective-permute-start.17 = (bf16[672,128]{1,0:T(8,128)(2,1)S(1)}, bf16[672,128]{1,0:T(8,128)(2,1)S(1)}, u32[]{:S(2)}, u32[]{:S(2)}) collective-permute-start(bf16[672,128]{1,0:T(8,128)(2,1)S(1)} %get-tuple-element.256), channel_id=1, source_target_pairs={{0,14},{2,0},{4,2},{6,4},{8,6},{10,8},{12,10},{14,12},{1,15},{3,1}... | collective-permute-start | bytes 516104 | tf_op jit(solution)/shard_map/ppermute | solution.py:1395
  83.3 0.2 collective-permute-start.20
  83.5 0.4 collective-permute-done.18
  83.9 0.5 collective-permute-start.21
  84.5 8.4 %collective-permute-done.19 = bf16[384,128]{1,0:T(8,128)(2,1)S(1)} collective-permute-done((bf16[384,128]{1,0:T(8,128)(2,1)S(1)}, bf16[384,128]{1,0:T(8,128)(2,1)S(1)}, u32[]{:S(2)}, u32[]{:S(2)}) %collective-permute-start.19) | collective-permute-done | bytes 98336 | tf_op jit(solution)/shard_map/ppermute | solution.py:1395
  92.8 2.8 %collective-permute-done.20 = bf16[384,128]{1,0:T(8,128)(2,1)S(1)} collective-permute-done((bf16[384,128]{1,0:T(8,128)(2,1)S(1)}, bf16[384,128]{1,0:T(8,128)(2,1)S(1)}, u32[]{:S(2)}, u32[]{:S(2)}) %collective-permute-start.20) | collective-permute-done | bytes 98336 | tf_op jit(solution)/shard_map/ppermute | solution.py:1395
  95.6 0.0 collective-permute-done.21
  95.6 3.5 %collective-permute-done.22 = bf16[384,128]{1,0:T(8,128)(2,1)S(1)} collective-permute-done((bf16[384,128]{1,0:T(8,128)(2,1)S(1)}, bf16[384,128]{1,0:T(8,128)(2,1)S(1)}, u32[]{:S(2)}, u32[]{:S(2)}) %collective-permute-start.22) | collective-permute-done | bytes 98336 | tf_op jit(solution)/shard_map/ppermute | solution.py:1395
  99.1 0.1 convert_add_fusion.args_0_
  99.2 0.1 collective-permute-start.23
  99.3 1.0 shard_map.199
  100.3 0.5 collective-permute-done.23.args_1_
  100.7 0.8 shard_map.200
  (17 shorter events, 0.1 us)
Async XLA Ops:
  2.2 9.1 %collective-permute-start = (bf16[9,16,256]{2,1,0:T(8,128)(2,1)}, bf16[9,16,256]{2,1,0:T(8,128)(2,1)S(1)}, u32[]{:S(2)}, u32[]{:S(2)}) collective-permute-start(bf16[9,16,256]{2,1,0:T(8,128)(2,1)} %get-tuple-element.144), channel_id=1, source_target_pairs={{0,2},{2,4},{4,6},{6,8},{8,10},{10,12},{12,14},{14,0},{1,3},{3,5},... | collective-permute-start | bytes 221192 | tf_op jit(solution)/shard_map/ppermute | solution.py:1280
  5.2 6.1 %collective-permute-start.1 = (bf16[9,16,256]{2,1,0:T(8,128)(2,1)}, bf16[9,16,256]{2,1,0:T(8,128)(2,1)S(1)}, u32[]{:S(2)}, u32[]{:S(2)}) collective-permute-start(bf16[9,16,256]{2,1,0:T(8,128)(2,1)} %get-tuple-element.145), channel_id=1, source_target_pairs={{2,0},{4,2},{6,4},{8,6},{10,8},{12,10},{14,12},{0,14},{3,1},{5,3},... | collective-permute-start | bytes 221192 | tf_op jit(solution)/shard_map/ppermute | solution.py:1281
  11.3 11.5 %copy-start = (bf16[1,256,1280]{2,1,0:T(8,128)(2,1)S(1)}, bf16[1,256,1280]{2,1,0:T(8,128)(2,1)}, u32[]{:S(2)}) copy-start(bf16[1,256,1280]{2,1,0:T(8,128)(2,1)} %args_1_.10) | copy-start | bytes 1966084
  11.4 11.5 %copy-start.1 = (bf16[1,256,768]{2,1,0:T(8,128)(2,1)S(1)}, bf16[1,256,768]{2,1,0:T(8,128)(2,1)}, u32[]{:S(2)}) copy-start(bf16[1,256,768]{2,1,0:T(8,128)(2,1)} %args_2_.12) | copy-start | bytes 1179652
  11.4 11.5 %copy-start.2 = (bf16[1,256,768]{2,1,0:T(8,128)(2,1)S(1)}, bf16[1,256,768]{2,1,0:T(8,128)(2,1)}, u32[]{:S(2)}) copy-start(bf16[1,256,768]{2,1,0:T(8,128)(2,1)} %args_4_.12) | copy-start | bytes 1179652
  11.4 11.5 %copy-start.3 = (bf16[32,1024]{1,0:T(8,128)(2,1)S(1)}, bf16[32,1024]{1,0:T(8,128)(2,1)}, u32[]{:S(2)}) copy-start(bf16[32,1024]{1,0:T(8,128)(2,1)} %get-tuple-element.150.args_4_.args_3_) | copy-start | bytes 196612
  11.4 11.5 %copy-start.4 = (bf16[2,1,4,64,256]{4,3,2,1,0:T(8,128)(2,1)S(1)}, bf16[2,1,4,64,256]{4,3,2,1,0:T(8,128)(2,1)}, u32[]{:S(2)}) copy-start(bf16[2,1,4,64,256]{4,3,2,1,0:T(8,128)(2,1)} %args_5_.6) | copy-start | bytes 786436
  11.4 11.5 %copy-start.6 = (f32[2,104,128]{2,1,0:T(8,128)S(1)}, f32[2,104,128]{2,1,0:T(8,128)}, u32[]{:S(2)}) copy-start(f32[2,104,128]{2,1,0:T(8,128)} %get-tuple-element.166.args_3_) | copy-start | bytes 319492
  11.4 11.5 %copy-start.7 = (f32[8,256]{1,0:T(8,128)S(1)}, f32[8,256]{1,0:T(8,128)}, u32[]{:S(2)}) copy-start(f32[8,256]{1,0:T(8,128)} %get-tuple-element.149.args_6_.args_0_) | copy-start | bytes 24580
  11.4 11.5 %copy-start.8 = (f32[2,1,3,64]{3,1,2,0:T(1,128)S(1)}, f32[2,1,3,64]{3,1,2,0:T(1,128)}, u32[]{:S(2)}) copy-start(f32[2,1,3,64]{3,1,2,0:T(1,128)} %param.13) | copy-start | bytes 4612
  11.4 21.6 %copy-start.5 = (bf16[2,1,4,64,256]{4,3,2,1,0:T(8,128)(2,1)S(1)}, bf16[2,1,4,64,256]{4,3,2,1,0:T(8,128)(2,1)}, u32[]{:S(2)}) copy-start(bf16[2,1,4,64,256]{4,3,2,1,0:T(8,128)(2,1)} %args_15_.3) | copy-start | bytes 786436
  18.9 12.8 %collective-permute-start.2 = (bf16[4,64,256]{2,1,0:T(8,128)(2,1)S(1)}, bf16[4,64,256]{2,1,0:T(8,128)(2,1)S(1)}, u32[]{:S(2)}, u32[]{:S(2)}) collective-permute-start(bf16[4,64,256]{2,1,0:T(8,128)(2,1)S(1)} %get-tuple-element.154.args_3_), channel_id=1, source_target_pairs={{0,16},{2,18},{4,20},{6,22},{8,24},{10,26},{12,28},{14,30},{1,17},... | collective-permute-start | bytes 393224 | tf_op jit(solution)/shard_map/ppermute | solution.py:1327
  20.2 12.8 %collective-permute-start.3 = (bf16[4,16,256]{2,1,0:T(8,128)(2,1)S(1)}, bf16[4,16,256]{2,1,0:T(8,128)(2,1)S(1)}, u32[]{:S(2)}, u32[]{:S(2)}) collective-permute-start(bf16[4,16,256]{2,1,0:T(8,128)(2,1)S(1)} %get-tuple-element.163), channel_id=1, source_target_pairs={{0,18},{2,20},{4,22},{6,24},{8,26},{10,28},{12,30},{14,16},{1,19},... | collective-permute-start | bytes 98312 | tf_op jit(solution)/shard_map/ppermute | solution.py:1328
  21.5 11.5 %collective-permute-start.4 = (bf16[4,16,256]{2,1,0:T(8,128)(2,1)S(1)}, bf16[4,16,256]{2,1,0:T(8,128)(2,1)S(1)}, u32[]{:S(2)}, u32[]{:S(2)}) collective-permute-start(bf16[4,16,256]{2,1,0:T(8,128)(2,1)S(1)} %get-tuple-element.164), channel_id=1, source_target_pairs={{2,16},{4,18},{6,20},{8,22},{10,24},{12,26},{14,28},{0,30},{3,17},... | collective-permute-start | bytes 98312 | tf_op jit(solution)/shard_map/ppermute | solution.py:1329
  29.0 8.0 %collective-permute-start.9 = (bf16[4,64,256]{2,1,0:T(8,128)(2,1)S(1)}, bf16[4,64,256]{2,1,0:T(8,128)(2,1)S(1)}, u32[]{:S(2)}, u32[]{:S(2)}) collective-permute-start(bf16[4,64,256]{2,1,0:T(8,128)(2,1)S(1)} %get-tuple-element.195), channel_id=1, source_target_pairs={{0,18},{2,20},{4,22},{6,24},{8,26},{10,28},{12,30},{14,16},{1,19},... | collective-permute-start | bytes 393224 | tf_op jit(solution)/shard_map/ppermute | solution.py:1328
  30.4 14.2 %collective-permute-start.8 = (bf16[4,64,256]{2,1,0:T(8,128)(2,1)S(1)}, bf16[4,64,256]{2,1,0:T(8,128)(2,1)S(1)}, u32[]{:S(2)}, u32[]{:S(2)}) collective-permute-start(bf16[4,64,256]{2,1,0:T(8,128)(2,1)S(1)} %get-tuple-element.194.args_5_), channel_id=1, source_target_pairs={{0,16},{2,18},{4,20},{6,22},{8,24},{10,26},{12,28},{14,30},{1,17},... | collective-permute-start | bytes 393224 | tf_op jit(solution)/shard_map/ppermute | solution.py:1327
  31.7 12.8 %collective-permute-start.10 = (bf16[4,64,256]{2,1,0:T(8,128)(2,1)S(1)}, bf16[4,64,256]{2,1,0:T(8,128)(2,1)S(1)}, u32[]{:S(2)}, u32[]{:S(2)}) collective-permute-start(bf16[4,64,256]{2,1,0:T(8,128)(2,1)S(1)} %get-tuple-element.196), channel_id=1, source_target_pairs={{2,16},{4,18},{6,20},{8,22},{10,24},{12,26},{14,28},{0,30},{3,17},... | collective-permute-start | bytes 393224 | tf_op jit(solution)/shard_map/ppermute | solution.py:1329
  33.2 14.2 %collective-permute-start.5 = (bf16[4,64,256]{2,1,0:T(8,128)(2,1)S(1)}, bf16[4,64,256]{2,1,0:T(8,128)(2,1)S(1)}, u32[]{:S(2)}, u32[]{:S(2)}) collective-permute-start(bf16[4,64,256]{2,1,0:T(8,128)(2,1)S(1)} %get-tuple-element.184), channel_id=1, source_target_pairs={{16,0},{18,2},{20,4},{22,6},{24,8},{26,10},{28,12},{30,14},{17,1},... | collective-permute-start | bytes 393224 | tf_op jit(solution)/shard_map/ppermute | solution.py:1372
  34.5 12.9 %collective-permute-start.6 = (bf16[4,16,256]{2,1,0:T(8,128)(2,1)S(1)}, bf16[4,16,256]{2,1,0:T(8,128)(2,1)S(1)}, u32[]{:S(2)}, u32[]{:S(2)}) collective-permute-start(bf16[4,16,256]{2,1,0:T(8,128)(2,1)S(1)} %get-tuple-element.185.args_27_), channel_id=1, source_target_pairs={{16,2},{18,4},{20,6},{22,8},{24,10},{26,12},{28,14},{30,0},{17,3},... | collective-permute-start | bytes 98312 | tf_op jit(solution)/shard_map/ppermute | solution.py:1373
  37.0 10.4 %collective-permute-start.7 = (bf16[4,16,256]{2,1,0:T(8,128)(2,1)S(1)}, bf16[4,16,256]{2,1,0:T(8,128)(2,1)S(1)}, u32[]{:S(2)}, u32[]{:S(2)}) collective-permute-start(bf16[4,16,256]{2,1,0:T(8,128)(2,1)S(1)} %get-tuple-element.186.args_26_), channel_id=1, source_target_pairs={{18,0},{20,2},{22,4},{24,6},{26,8},{28,10},{30,12},{16,14},{19,1},... | collective-permute-start | bytes 98312 | tf_op jit(solution)/shard_map/ppermute | solution.py:1374
  47.5 15.6 %collective-permute-start.11 = (bf16[5,64,256]{2,1,0:T(8,128)(2,1)S(1)}, bf16[5,64,256]{2,1,0:T(8,128)(2,1)S(1)}, u32[]{:S(2)}, u32[]{:S(2)}) collective-permute-start(bf16[5,64,256]{2,1,0:T(8,128)(2,1)S(1)} %get-tuple-element.225), channel_id=1, source_target_pairs={{16,0},{18,2},{20,4},{22,6},{24,8},{26,10},{28,12},{30,14},{17,1},... | collective-permute-start | bytes 491528 | tf_op jit(solution)/shard_map/ppermute | solution.py:1372
  48.8 14.3 %collective-permute-start.12 = (bf16[4,16,256]{2,1,0:T(8,128)(2,1)S(1)}, bf16[4,16,256]{2,1,0:T(8,128)(2,1)S(1)}, u32[]{:S(2)}, u32[]{:S(2)}) collective-permute-start(bf16[4,16,256]{2,1,0:T(8,128)(2,1)S(1)} %get-tuple-element.226.args_30_), channel_id=1, source_target_pairs={{16,2},{18,4},{20,6},{22,8},{24,10},{26,12},{28,14},{30,0},{17,3},... | collective-permute-start | bytes 98312 | tf_op jit(solution)/shard_map/ppermute | solution.py:1373
  50.1 13.0 %collective-permute-start.13 = (bf16[4,16,256]{2,1,0:T(8,128)(2,1)S(1)}, bf16[4,16,256]{2,1,0:T(8,128)(2,1)S(1)}, u32[]{:S(2)}, u32[]{:S(2)}) collective-permute-start(bf16[4,16,256]{2,1,0:T(8,128)(2,1)S(1)} %get-tuple-element.227.args_29_), channel_id=1, source_target_pairs={{18,0},{20,2},{22,4},{24,6},{26,8},{28,10},{30,12},{16,14},{19,1},... | collective-permute-start | bytes 98312 | tf_op jit(solution)/shard_map/ppermute | solution.py:1374
  73.4 2.7 %collective-permute-start.14 = (bf16[8,384,128]{2,1,0:T(8,128)(2,1)S(1)}, bf16[8,384,128]{2,1,0:T(8,128)(2,1)S(1)}, u32[]{:S(2)}, u32[]{:S(2)}) collective-permute-start(bf16[8,384,128]{2,1,0:T(8,128)(2,1)S(1)} %get-tuple-element.250), channel_id=1, source_target_pairs={{0,1},{1,0},{2,3},{3,2},{4,5},{5,4},{6,7},{7,6},{8,9},{9,8},{10,11... | collective-permute-start | bytes 2359304 | tf_op jit(solution)/shard_map/ppermute | solution.py:1391
  73.5 2.6 %collective-permute-start.15 = (f32[2,8,128]{2,1,0:T(8,128)S(1)}, f32[2,8,128]{2,1,0:T(8,128)S(1)}, u32[]{:S(2)}, u32[]{:S(2)}) collective-permute-start(f32[2,8,128]{2,1,0:T(8,128)S(1)} %get-tuple-element.254), channel_id=1, source_target_pairs={{0,16},{2,18},{4,20},{6,22},{8,24},{10,26},{12,28},{14,30},{1,17},... | collective-permute-start | bytes 24584 | tf_op jit(solution)/shard_map/ppermute | solution.py:1389
  76.3 7.6 %collective-permute-start.18 = (bf16[384,128]{1,0:T(8,128)(2,1)S(1)}, bf16[384,128]{1,0:T(8,128)(2,1)S(1)}, u32[]{:S(2)}, u32[]{:S(2)}) collective-permute-start(bf16[384,128]{1,0:T(8,128)(2,1)S(1)} %get-tuple-element.267), channel_id=1, source_target_pairs={{0,4},{2,6},{4,8},{6,10},{8,12},{10,14},{12,0},{14,2},{1,5},{3,7},... | collective-permute-start | bytes 294920 | tf_op jit(solution)/shard_map/ppermute | solution.py:1395
  76.4 16.4 %collective-permute-start.19 = (bf16[384,128]{1,0:T(8,128)(2,1)S(1)}, bf16[384,128]{1,0:T(8,128)(2,1)S(1)}, u32[]{:S(2)}, u32[]{:S(2)}) collective-permute-start(bf16[384,128]{1,0:T(8,128)(2,1)S(1)} %get-tuple-element.268), channel_id=1, source_target_pairs={{0,6},{2,8},{4,10},{6,12},{8,14},{10,0},{12,2},{14,4},{1,7},{3,9},... | collective-permute-start | bytes 294920 | tf_op jit(solution)/shard_map/ppermute | solution.py:1395
  78.6 20.6 %collective-permute-start.16 = (bf16[672,128]{1,0:T(8,128)(2,1)S(1)}, bf16[672,128]{1,0:T(8,128)(2,1)S(1)}, u32[]{:S(2)}, u32[]{:S(2)}) collective-permute-start(bf16[672,128]{1,0:T(8,128)(2,1)S(1)} %get-tuple-element.255), channel_id=1, source_target_pairs={{0,2},{2,4},{4,6},{6,8},{8,10},{10,12},{12,14},{14,0},{1,3},{3,5},... | collective-permute-start | bytes 516104 | tf_op jit(solution)/shard_map/ppermute | solution.py:1395
  80.1 19.1 %collective-permute-start.17 = (bf16[672,128]{1,0:T(8,128)(2,1)S(1)}, bf16[672,128]{1,0:T(8,128)(2,1)S(1)}, u32[]{:S(2)}, u32[]{:S(2)}) collective-permute-start(bf16[672,128]{1,0:T(8,128)(2,1)S(1)} %get-tuple-element.256), channel_id=1, source_target_pairs={{0,14},{2,0},{4,2},{6,4},{8,6},{10,8},{12,10},{14,12},{1,15},{3,1}... | collective-permute-start | bytes 516104 | tf_op jit(solution)/shard_map/ppermute | solution.py:1395
  83.3 12.3 %collective-permute-start.20 = (bf16[384,128]{1,0:T(8,128)(2,1)S(1)}, bf16[384,128]{1,0:T(8,128)(2,1)S(1)}, u32[]{:S(2)}, u32[]{:S(2)}) collective-permute-start(bf16[384,128]{1,0:T(8,128)(2,1)S(1)} %get-tuple-element.269), channel_id=1, source_target_pairs={{0,8},{2,10},{4,12},{6,14},{8,0},{10,2},{12,4},{14,6},{1,9},{3,11}... | collective-permute-start | bytes 294920 | tf_op jit(solution)/shard_map/ppermute | solution.py:1395
  83.9 11.7 %collective-permute-start.21 = (bf16[384,128]{1,0:T(8,128)(2,1)S(1)}, bf16[384,128]{1,0:T(8,128)(2,1)S(1)}, u32[]{:S(2)}, u32[]{:S(2)}) collective-permute-start(bf16[384,128]{1,0:T(8,128)(2,1)S(1)} %get-tuple-element.270), channel_id=1, source_target_pairs={{0,10},{2,12},{4,14},{6,0},{8,2},{10,4},{12,6},{14,8},{1,11},{3,13... | collective-permute-start | bytes 294920 | tf_op jit(solution)/shard_map/ppermute | solution.py:1395
  92.8 6.3 %collective-permute-start.22 = (bf16[384,128]{1,0:T(8,128)(2,1)S(1)}, bf16[384,128]{1,0:T(8,128)(2,1)S(1)}, u32[]{:S(2)}, u32[]{:S(2)}) collective-permute-start(bf16[384,128]{1,0:T(8,128)(2,1)S(1)} %get-tuple-element.271), channel_id=1, source_target_pairs={{0,12},{2,14},{4,0},{6,2},{8,4},{10,6},{12,8},{14,10},{1,13},{3,15... | collective-permute-start | bytes 294920 | tf_op jit(solution)/shard_map/ppermute | solution.py:1395
  99.2 1.5 %collective-permute-start.23 = (f32[384,128]{1,0:T(8,128)S(1)}, f32[384,128]{1,0:T(8,128)S(1)}, u32[]{:S(2)}, u32[]{:S(2)}) collective-permute-start(f32[384,128]{1,0:T(8,128)S(1)} %convert_add_fusion.args_0_), channel_id=1, source_target_pairs={{0,1},{1,0},{2,3},{3,2},{4,5},{5,4},{6,7},{7,6},{8,9},{9,8},{10,11... | collective-permute-start | bytes 589832 | tf_op jit(solution)/shard_map/ppermute | solution.py:1408

commit v7 on v6

--- a/solution.py
+++ b/solution.py
@@ -668,7 +668,7 @@
 BORDERS = ("rim_low", "rim_high", "gplaces")
 
 
-def call(body, arrays, outs, scratch, role=None, grant_mb=16, place=VMEM):
+def call(body, arrays, outs, scratch, role=None, grant_mb=14, place=VMEM):
     arrays, outs = vars(arrays), vars(outs)
     names = list(arrays) + list(outs) + list(scratch)
 

time: 102 us -> 102 us (level)
  no operation moved by 1% of the time
where the time goes in v7:
time: 102 us; the launch traced here: 101 us
  Pallas kernels  46.3 us (45%)
  starting transfers between devices  30.8 us (30%)
  waiting for transfers between devices  22.9 us (22%)
  between operations  1.05 us (1%)
    pallas_call x14, Pallas kernels, call(): pl.pallas_call(kernel, out_shape=list(outs.values()), in_specs=[spec for...  46.3 us
    ppermute x7, waiting for transfers between devices, on_device(): lax.ppermute(piece, 'space', [(i, (i + hop) % space) for i in range(space)])  15.1 us
    ppermute x7, starting transfers between devices, on_device(): lax.ppermute(piece, 'space', [(i, (i + hop) % space) for i in range(space)])  7.72 us
    ppermute x2, waiting for transfers between devices, on_device(): lax.ppermute(rim_high, both, back_up)  4.83 us
    ppermute x1, starting transfers between devices, on_device(): pack_high = lax.ppermute(borders.down, 'space', down)  3.1 us
    ppermute x1, starting transfers between devices, on_device(): pack_low = lax.ppermute(borders.up, 'space', up)  3.02 us
    ppermute x2, starting transfers between devices, on_device(): lax.ppermute(first.fresh, both, forth)  2.59 us
    ppermute x2, starting transfers between devices, on_device(): lax.ppermute(first.tail, both, forth_up)  2.59 us
  transfers between devices with their start and end apart: 24, of which 9 were waited for; matrix products, arithmetic and copies ran while one was open for 0% of the time, Pallas kernels for 26%

profile of v7, /device:TPU:0, one launch (start us, length us, event | category | flops | bytes accessed | tf_op | source)
XLA Modules:
  0.0 101.2 jit_solution(681107144357741416)
XLA Ops:
  0.6 1.5 %shard_map.187 = (bf16[9,16,256]{2,1,0:T(8,128)(2,1)}, bf16[9,16,256]{2,1,0:T(8,128)(2,1)}) custom-call(bf16[2,1,4,64,256]{4,3,2,1,0:T(8,128)(2,1)} %args_5_.6, f32[2,3,1,64]{3,2,1,0:T(1,128)} %bitcast.5), custom_call_target="tpu_custom_call" | custom-call | tf_op jit(solution)/shard_map/pallas_call | solution.py:682
  2.2 3.0 %collective-permute-start = (bf16[9,16,256]{2,1,0:T(8,128)(2,1)}, bf16[9,16,256]{2,1,0:T(8,128)(2,1)S(1)}, u32[]{:S(2)}, u32[]{:S(2)}) collective-permute-start(bf16[9,16,256]{2,1,0:T(8,128)(2,1)} %get-tuple-element.144), channel_id=1, source_target_pairs={{0,2},{2,4},{4,6},{6,8},{8,10},{10,12},{12,14},{14,0},{1,3},{3,5},... | collective-permute-start | bytes 221192 | tf_op jit(solution)/shard_map/ppermute | solution.py:1280
  5.2 3.1 %collective-permute-start.1 = (bf16[9,16,256]{2,1,0:T(8,128)(2,1)}, bf16[9,16,256]{2,1,0:T(8,128)(2,1)S(1)}, u32[]{:S(2)}, u32[]{:S(2)}) collective-permute-start(bf16[9,16,256]{2,1,0:T(8,128)(2,1)} %get-tuple-element.145), channel_id=1, source_target_pairs={{2,0},{4,2},{6,4},{8,6},{10,8},{12,10},{14,12},{0,14},{3,1},{5,3},... | collective-permute-start | bytes 221192 | tf_op jit(solution)/shard_map/ppermute | solution.py:1281
  8.3 3.0 %shard_map.188 = (f32[2,104,128]{2,1,0:T(8,128)}, f32[8,256]{1,0:T(8,128)}, bf16[32,1024]{1,0:T(8,128)(2,1)}, bf16[20480,1280]{1,0:T(8,128)(2,1)}, f32[51200,256]{1,0:T(8,128)}) custom-call(bf16[2,1,4,64,256]{4,3,2,1,0:T(8,128)(2,1)} %args_5_.6, f32[2,3,1,64]{3,2,1,0:T(1,128)} %bitcast.6, s32[2,1,32,64]{3,2,1,0:T(8,128)} %args_2_.8, ...), custom_call_target="tpu_custom_call" | custom-call | tf_op jit(solution)/shard_map/pallas_call | solution.py:682
  11.3 0.0 collective-permute-done.args_0_
  11.3 0.0 collective-permute-done.1.args_1_
  11.3 0.0 copy-start
  11.4 0.0 copy-start.1
  11.4 0.0 copy-start.2
  11.4 0.0 copy-start.3
  11.4 0.0 copy-start.4
  11.4 0.0 copy-start.6
  11.4 0.0 copy-start.7
  11.4 0.0 copy-start.8
  11.4 0.0 copy-start.5
  11.4 7.5 %shard_map.189 = (bf16[4,64,256]{2,1,0:T(8,128)(2,1)S(1)}, bf16[4,16,256]{2,1,0:T(8,128)(2,1)S(1)}, bf16[4,16,256]{2,1,0:T(8,128)(2,1)S(1)}, bf16[384,256]{1,0:T...) custom-call(bf16[9,16,256]{2,1,0:T(8,128)(2,1)S(1)} %collective-perm, ...), custom_call_target="tpu_custom_call" | custom-call | tf_op jit(solution)/shard_map/pallas_call | solution.py:682
  18.9 1.3 %collective-permute-start.2 = (bf16[4,64,256]{2,1,0:T(8,128)(2,1)S(1)}, bf16[4,64,256]{2,1,0:T(8,128)(2,1)S(1)}, u32[]{:S(2)}, u32[]{:S(2)}) collective-permute-start(bf16[4,64,256]{2,1,0:T(8,128)(2,1)S(1)} %get-tuple-element.154.args_3_), channel_id=1, source_target_pairs={{0,16},{2,18},{4,20},{6,22},{8,24},{10,26},{12,28},{14,30},{1,17},... | collective-permute-start | bytes 393224 | tf_op jit(solution)/shard_map/ppermute | solution.py:1327
  20.2 1.3 %collective-permute-start.3 = (bf16[4,16,256]{2,1,0:T(8,128)(2,1)S(1)}, bf16[4,16,256]{2,1,0:T(8,128)(2,1)S(1)}, u32[]{:S(2)}, u32[]{:S(2)}) collective-permute-start(bf16[4,16,256]{2,1,0:T(8,128)(2,1)S(1)} %get-tuple-element.163), channel_id=1, source_target_pairs={{0,18},{2,20},{4,22},{6,24},{8,26},{10,28},{12,30},{14,16},{1,19},... | collective-permute-start | bytes 98312 | tf_op jit(solution)/shard_map/ppermute | solution.py:1328
  21.5 1.3 %collective-permute-start.4 = (bf16[4,16,256]{2,1,0:T(8,128)(2,1)S(1)}, bf16[4,16,256]{2,1,0:T(8,128)(2,1)S(1)}, u32[]{:S(2)}, u32[]{:S(2)}) collective-permute-start(bf16[4,16,256]{2,1,0:T(8,128)(2,1)S(1)} %get-tuple-element.164), channel_id=1, source_target_pairs={{2,16},{4,18},{6,20},{8,22},{10,24},{12,26},{14,28},{0,30},{3,17},... | collective-permute-start | bytes 98312 | tf_op jit(solution)/shard_map/ppermute | solution.py:1329
  22.9 6.0 %shard_map.190 = (bf16[4,64,256]{2,1,0:T(8,128)(2,1)S(1)}, bf16[4,64,256]{2,1,0:T(8,128)(2,1)S(1)}, bf16[4,64,256]{2,1,0:T(8,128)(2,1)S(1)}, bf16[384,256]{1,0:T...) custom-call(bf16[9,16,256]{2,1,0:T(8,128)(2,1)S(1)} %collective-perm, ...), custom_call_target="tpu_custom_call" | custom-call | tf_op jit(solution)/shard_map/pallas_call | solution.py:682
  28.9 1.3 %collective-permute-start.9 = (bf16[4,64,256]{2,1,0:T(8,128)(2,1)S(1)}, bf16[4,64,256]{2,1,0:T(8,128)(2,1)S(1)}, u32[]{:S(2)}, u32[]{:S(2)}) collective-permute-start(bf16[4,64,256]{2,1,0:T(8,128)(2,1)S(1)} %get-tuple-element.195), channel_id=1, source_target_pairs={{0,18},{2,20},{4,22},{6,24},{8,26},{10,28},{12,30},{14,16},{1,19},... | collective-permute-start | bytes 393224 | tf_op jit(solution)/shard_map/ppermute | solution.py:1328
  30.2 1.3 %collective-permute-start.8 = (bf16[4,64,256]{2,1,0:T(8,128)(2,1)S(1)}, bf16[4,64,256]{2,1,0:T(8,128)(2,1)S(1)}, u32[]{:S(2)}, u32[]{:S(2)}) collective-permute-start(bf16[4,64,256]{2,1,0:T(8,128)(2,1)S(1)} %get-tuple-element.194.args_5_), channel_id=1, source_target_pairs={{0,16},{2,18},{4,20},{6,22},{8,24},{10,26},{12,28},{14,30},{1,17},... | collective-permute-start | bytes 393224 | tf_op jit(solution)/shard_map/ppermute | solution.py:1327
  31.5 0.0 collective-permute-done.2.args_12_
  31.5 1.3 %collective-permute-start.10 = (bf16[4,64,256]{2,1,0:T(8,128)(2,1)S(1)}, bf16[4,64,256]{2,1,0:T(8,128)(2,1)S(1)}, u32[]{:S(2)}, u32[]{:S(2)}) collective-permute-start(bf16[4,64,256]{2,1,0:T(8,128)(2,1)S(1)} %get-tuple-element.196), channel_id=1, source_target_pairs={{2,16},{4,18},{6,20},{8,22},{10,24},{12,26},{14,28},{0,30},{3,17},... | collective-permute-start | bytes 393224 | tf_op jit(solution)/shard_map/ppermute | solution.py:1329
  32.8 0.0 collective-permute-done.3.args_13_
  32.9 0.0 collective-permute-done.4.args_14_
  32.9 0.2 shard_map.192
  33.1 1.3 %collective-permute-start.5 = (bf16[4,64,256]{2,1,0:T(8,128)(2,1)S(1)}, bf16[4,64,256]{2,1,0:T(8,128)(2,1)S(1)}, u32[]{:S(2)}, u32[]{:S(2)}) collective-permute-start(bf16[4,64,256]{2,1,0:T(8,128)(2,1)S(1)} %get-tuple-element.184), channel_id=1, source_target_pairs={{16,0},{18,2},{20,4},{22,6},{24,8},{26,10},{28,12},{30,14},{17,1},... | collective-permute-start | bytes 393224 | tf_op jit(solution)/shard_map/ppermute | solution.py:1372
  34.4 1.3 %collective-permute-start.6 = (bf16[4,16,256]{2,1,0:T(8,128)(2,1)S(1)}, bf16[4,16,256]{2,1,0:T(8,128)(2,1)S(1)}, u32[]{:S(2)}, u32[]{:S(2)}) collective-permute-start(bf16[4,16,256]{2,1,0:T(8,128)(2,1)S(1)} %get-tuple-element.185.args_27_), channel_id=1, source_target_pairs={{16,2},{18,4},{20,6},{22,8},{24,10},{26,12},{28,14},{30,0},{17,3},... | collective-permute-start | bytes 98312 | tf_op jit(solution)/shard_map/ppermute | solution.py:1373
  35.7 1.2 %collective-permute-done.9.args_13_ = bf16[4,64,256]{2,1,0:T(8,128)(2,1)S(1)} collective-permute-done((bf16[4,64,256]{2,1,0:T(8,128)(2,1)S(1)}, bf16[4,64,256]{2,1,0:T(8,128)(2,1)S(1)}, u32[]{:S(2)}, u32[]{:S(2)}) %collective-permute-start.9) | collective-permute-done | bytes 131104 | tf_op jit(solution)/shard_map/ppermute | solution.py:1328
  36.9 1.3 %collective-permute-start.7 = (bf16[4,16,256]{2,1,0:T(8,128)(2,1)S(1)}, bf16[4,16,256]{2,1,0:T(8,128)(2,1)S(1)}, u32[]{:S(2)}, u32[]{:S(2)}) collective-permute-start(bf16[4,16,256]{2,1,0:T(8,128)(2,1)S(1)} %get-tuple-element.186.args_26_), channel_id=1, source_target_pairs={{18,0},{20,2},{22,4},{24,6},{26,8},{28,10},{30,12},{16,14},{19,1},... | collective-permute-start | bytes 98312 | tf_op jit(solution)/shard_map/ppermute | solution.py:1374
  38.2 6.2 %shard_map.193 = (f32[10,8,256]{2,1,0:T(8,128)S(1)}, bf16[8,32,256]{2,1,0:T(8,128)(2,1)S(1)}, bf16[8,256,128]{2,1,0:T(8,128)(2,1)S(1)}, bf16[8,192,256]{2,1,0:T(...) custom-call(bf16[9,16,256]{2,1,0:T(8,128)(2,1)S(1)} %collective-perm, ...), custom_call_target="tpu_custom_call" | custom-call | tf_op jit(solution)/shard_map/pallas_call | solution.py:682
  44.4 0.0 collective-permute-done.8.args_12_
  44.4 2.8 %collective-permute-done.6.args_21_ = bf16[4,16,256]{2,1,0:T(8,128)(2,1)S(1)} collective-permute-done((bf16[4,16,256]{2,1,0:T(8,128)(2,1)S(1)}, bf16[4,16,256]{2,1,0:T(8,128)(2,1)S(1)}, u32[]{:S(2)}, u32[]{:S(2)}) %collective-permute-start.6) | collective-permute-done | bytes 32800 | tf_op jit(solution)/shard_map/ppermute | solution.py:1373
  47.2 0.0 collective-permute-done.7.args_22_
  47.2 1.3 %collective-permute-start.11 = (bf16[5,64,256]{2,1,0:T(8,128)(2,1)S(1)}, bf16[5,64,256]{2,1,0:T(8,128)(2,1)S(1)}, u32[]{:S(2)}, u32[]{:S(2)}) collective-permute-start(bf16[5,64,256]{2,1,0:T(8,128)(2,1)S(1)} %get-tuple-element.225), channel_id=1, source_target_pairs={{16,0},{18,2},{20,4},{22,6},{24,8},{26,10},{28,12},{30,14},{17,1},... | collective-permute-start | bytes 491528 | tf_op jit(solution)/shard_map/ppermute | solution.py:1372
  48.5 1.3 %collective-permute-start.12 = (bf16[4,16,256]{2,1,0:T(8,128)(2,1)S(1)}, bf16[4,16,256]{2,1,0:T(8,128)(2,1)S(1)}, u32[]{:S(2)}, u32[]{:S(2)}) collective-permute-start(bf16[4,16,256]{2,1,0:T(8,128)(2,1)S(1)} %get-tuple-element.226.args_30_), channel_id=1, source_target_pairs={{16,2},{18,4},{20,6},{22,8},{24,10},{26,12},{28,14},{30,0},{17,3},... | collective-permute-start | bytes 98312 | tf_op jit(solution)/shard_map/ppermute | solution.py:1373
  49.8 1.3 %collective-permute-start.13 = (bf16[4,16,256]{2,1,0:T(8,128)(2,1)S(1)}, bf16[4,16,256]{2,1,0:T(8,128)(2,1)S(1)}, u32[]{:S(2)}, u32[]{:S(2)}) collective-permute-start(bf16[4,16,256]{2,1,0:T(8,128)(2,1)S(1)} %get-tuple-element.227.args_29_), channel_id=1, source_target_pairs={{18,0},{20,2},{22,4},{24,6},{26,8},{28,10},{30,12},{16,14},{19,1},... | collective-permute-start | bytes 98312 | tf_op jit(solution)/shard_map/ppermute | solution.py:1374
  51.1 9.6 %shard_map.195 = (f32[4,64,256]{2,1,0:T(8,128)S(1)}, bf16[4,64,256]{2,1,0:T(8,128)(2,1)}, bf16[4,16,256]{2,1,0:T(8,128)(2,1)S(1)}, bf16[4,16,256]{2,1,0:T(8,128)...) custom-call(f32[8,256]{1,0:T(8,128)S(1)} %copy-done.7, ...), custom_call_target="tpu_custom_call" | custom-call | tf_op jit(solution)/shard_map/pallas_call | solution.py:682
  60.7 2.1 %collective-permute-done.12.args_21_ = bf16[4,16,256]{2,1,0:T(8,128)(2,1)S(1)} collective-permute-done((bf16[4,16,256]{2,1,0:T(8,128)(2,1)S(1)}, bf16[4,16,256]{2,1,0:T(8,128)(2,1)S(1)}, u32[]{:S(2)}, u32[]{:S(2)}) %collective-permute-start.12) | collective-permute-done | bytes 32800 | tf_op jit(solution)/shard_map/ppermute | solution.py:1373
  62.7 0.0 collective-permute-done.13.args_22_
  62.7 0.0 collective-permute-done.11.args_20_
  62.7 9.4 %shard_map.196 = (f32[4,64,256]{2,1,0:T(8,128)S(1)}, bf16[4,64,256]{2,1,0:T(8,128)(2,1)}, bf16[4,16,256]{2,1,0:T(8,128)(2,1)}, bf16[4,16,256]{2,1,0:T(8,128)(2,1...) custom-call(f32[8,256]{1,0:T(8,128)S(1)} %copy-done.7, ...), custom_call_target="tpu_custom_call" | custom-call | tf_op jit(solution)/shard_map/pallas_call | solution.py:682
  72.1 1.0 shard_map.197
  73.1 0.1 collective-permute-start.14
  73.2 1.3 %collective-permute-start.15 = (f32[2,8,128]{2,1,0:T(8,128)S(1)}, f32[2,8,128]{2,1,0:T(8,128)S(1)}, u32[]{:S(2)}, u32[]{:S(2)}) collective-permute-start(f32[2,8,128]{2,1,0:T(8,128)S(1)} %get-tuple-element.254), channel_id=1, source_target_pairs={{0,16},{2,18},{4,20},{6,22},{8,24},{10,26},{12,28},{14,30},{1,17},... | collective-permute-start | bytes 24584 | tf_op jit(solution)/shard_map/ppermute | solution.py:1389
  74.5 1.3 %collective-permute-done.15.args_5_ = f32[2,8,128]{2,1,0:T(8,128)S(1)} collective-permute-done((f32[2,8,128]{2,1,0:T(8,128)S(1)}, f32[2,8,128]{2,1,0:T(8,128)S(1)}, u32[]{:S(2)}, u32[]{:S(2)}) %collective-permute-start.15) | collective-permute-done | bytes 8224 | tf_op jit(solution)/shard_map/ppermute | solution.py:1389
  75.8 0.0 collective-permute-done.14.args_1_
  75.8 0.2 shard_map.198
  76.0 0.1 collective-permute-start.18
  76.1 2.2 %collective-permute-start.19 = (bf16[384,128]{1,0:T(8,128)(2,1)S(1)}, bf16[384,128]{1,0:T(8,128)(2,1)S(1)}, u32[]{:S(2)}, u32[]{:S(2)}) collective-permute-start(bf16[384,128]{1,0:T(8,128)(2,1)S(1)} %get-tuple-element.268), channel_id=1, source_target_pairs={{0,6},{2,8},{4,10},{6,12},{8,14},{10,0},{12,2},{14,4},{1,7},{3,9},... | collective-permute-start | bytes 294920 | tf_op jit(solution)/shard_map/ppermute | solution.py:1395
  78.3 1.5 %collective-permute-start.16 = (bf16[672,128]{1,0:T(8,128)(2,1)S(1)}, bf16[672,128]{1,0:T(8,128)(2,1)S(1)}, u32[]{:S(2)}, u32[]{:S(2)}) collective-permute-start(bf16[672,128]{1,0:T(8,128)(2,1)S(1)} %get-tuple-element.255), channel_id=1, source_target_pairs={{0,2},{2,4},{4,6},{6,8},{8,10},{10,12},{12,14},{14,0},{1,3},{3,5},... | collective-permute-start | bytes 516104 | tf_op jit(solution)/shard_map/ppermute | solution.py:1395
  79.7 3.3 %collective-permute-start.17 = (bf16[672,128]{1,0:T(8,128)(2,1)S(1)}, bf16[672,128]{1,0:T(8,128)(2,1)S(1)}, u32[]{:S(2)}, u32[]{:S(2)}) collective-permute-start(bf16[672,128]{1,0:T(8,128)(2,1)S(1)} %get-tuple-element.256), channel_id=1, source_target_pairs={{0,14},{2,0},{4,2},{6,4},{8,6},{10,8},{12,10},{14,12},{1,15},{3,1}... | collective-permute-start | bytes 516104 | tf_op jit(solution)/shard_map/ppermute | solution.py:1395
  83.0 0.2 collective-permute-start.20
  83.2 0.4 collective-permute-done.18
  83.6 0.5 collective-permute-start.21
  84.1 8.4 %collective-permute-done.19 = bf16[384,128]{1,0:T(8,128)(2,1)S(1)} collective-permute-done((bf16[384,128]{1,0:T(8,128)(2,1)S(1)}, bf16[384,128]{1,0:T(8,128)(2,1)S(1)}, u32[]{:S(2)}, u32[]{:S(2)}) %collective-permute-start.19) | collective-permute-done | bytes 98336 | tf_op jit(solution)/shard_map/ppermute | solution.py:1395
  92.5 2.8 %collective-permute-done.20 = bf16[384,128]{1,0:T(8,128)(2,1)S(1)} collective-permute-done((bf16[384,128]{1,0:T(8,128)(2,1)S(1)}, bf16[384,128]{1,0:T(8,128)(2,1)S(1)}, u32[]{:S(2)}, u32[]{:S(2)}) %collective-permute-start.20) | collective-permute-done | bytes 98336 | tf_op jit(solution)/shard_map/ppermute | solution.py:1395
  95.3 3.5 %collective-permute-done.22 = bf16[384,128]{1,0:T(8,128)(2,1)S(1)} collective-permute-done((bf16[384,128]{1,0:T(8,128)(2,1)S(1)}, bf16[384,128]{1,0:T(8,128)(2,1)S(1)}, u32[]{:S(2)}, u32[]{:S(2)}) %collective-permute-start.22) | collective-permute-done | bytes 98336 | tf_op jit(solution)/shard_map/ppermute | solution.py:1395
  98.8 0.1 convert_add_fusion.args_0_
  98.9 0.1 collective-permute-start.23
  99.0 1.0 shard_map.199
  100.0 0.5 collective-permute-done.23.args_1_
  100.4 0.8 shard_map.200
  (17 shorter events, 0.1 us)
Async XLA Ops:
  2.2 9.1 %collective-permute-start = (bf16[9,16,256]{2,1,0:T(8,128)(2,1)}, bf16[9,16,256]{2,1,0:T(8,128)(2,1)S(1)}, u32[]{:S(2)}, u32[]{:S(2)}) collective-permute-start(bf16[9,16,256]{2,1,0:T(8,128)(2,1)} %get-tuple-element.144), channel_id=1, source_target_pairs={{0,2},{2,4},{4,6},{6,8},{8,10},{10,12},{12,14},{14,0},{1,3},{3,5},... | collective-permute-start | bytes 221192 | tf_op jit(solution)/shard_map/ppermute | solution.py:1280
  5.2 6.1 %collective-permute-start.1 = (bf16[9,16,256]{2,1,0:T(8,128)(2,1)}, bf16[9,16,256]{2,1,0:T(8,128)(2,1)S(1)}, u32[]{:S(2)}, u32[]{:S(2)}) collective-permute-start(bf16[9,16,256]{2,1,0:T(8,128)(2,1)} %get-tuple-element.145), channel_id=1, source_target_pairs={{2,0},{4,2},{6,4},{8,6},{10,8},{12,10},{14,12},{0,14},{3,1},{5,3},... | collective-permute-start | bytes 221192 | tf_op jit(solution)/shard_map/ppermute | solution.py:1281
  11.3 11.5 %copy-start = (bf16[1,256,1280]{2,1,0:T(8,128)(2,1)S(1)}, bf16[1,256,1280]{2,1,0:T(8,128)(2,1)}, u32[]{:S(2)}) copy-start(bf16[1,256,1280]{2,1,0:T(8,128)(2,1)} %args_1_.10) | copy-start | bytes 1966084
  11.4 11.5 %copy-start.1 = (bf16[1,256,768]{2,1,0:T(8,128)(2,1)S(1)}, bf16[1,256,768]{2,1,0:T(8,128)(2,1)}, u32[]{:S(2)}) copy-start(bf16[1,256,768]{2,1,0:T(8,128)(2,1)} %args_2_.12) | copy-start | bytes 1179652
  11.4 11.5 %copy-start.2 = (bf16[1,256,768]{2,1,0:T(8,128)(2,1)S(1)}, bf16[1,256,768]{2,1,0:T(8,128)(2,1)}, u32[]{:S(2)}) copy-start(bf16[1,256,768]{2,1,0:T(8,128)(2,1)} %args_4_.12) | copy-start | bytes 1179652
  11.4 11.5 %copy-start.3 = (bf16[32,1024]{1,0:T(8,128)(2,1)S(1)}, bf16[32,1024]{1,0:T(8,128)(2,1)}, u32[]{:S(2)}) copy-start(bf16[32,1024]{1,0:T(8,128)(2,1)} %get-tuple-element.150.args_4_.args_3_) | copy-start | bytes 196612
  11.4 11.5 %copy-start.4 = (bf16[2,1,4,64,256]{4,3,2,1,0:T(8,128)(2,1)S(1)}, bf16[2,1,4,64,256]{4,3,2,1,0:T(8,128)(2,1)}, u32[]{:S(2)}) copy-start(bf16[2,1,4,64,256]{4,3,2,1,0:T(8,128)(2,1)} %args_5_.6) | copy-start | bytes 786436
  11.4 11.5 %copy-start.6 = (f32[2,104,128]{2,1,0:T(8,128)S(1)}, f32[2,104,128]{2,1,0:T(8,128)}, u32[]{:S(2)}) copy-start(f32[2,104,128]{2,1,0:T(8,128)} %get-tuple-element.166.args_3_) | copy-start | bytes 319492
  11.4 11.5 %copy-start.7 = (f32[8,256]{1,0:T(8,128)S(1)}, f32[8,256]{1,0:T(8,128)}, u32[]{:S(2)}) copy-start(f32[8,256]{1,0:T(8,128)} %get-tuple-element.149.args_6_.args_0_) | copy-start | bytes 24580
  11.4 11.5 %copy-start.8 = (f32[2,1,3,64]{3,1,2,0:T(1,128)S(1)}, f32[2,1,3,64]{3,1,2,0:T(1,128)}, u32[]{:S(2)}) copy-start(f32[2,1,3,64]{3,1,2,0:T(1,128)} %param.13) | copy-start | bytes 4612
  11.4 21.4 %copy-start.5 = (bf16[2,1,4,64,256]{4,3,2,1,0:T(8,128)(2,1)S(1)}, bf16[2,1,4,64,256]{4,3,2,1,0:T(8,128)(2,1)}, u32[]{:S(2)}) copy-start(bf16[2,1,4,64,256]{4,3,2,1,0:T(8,128)(2,1)} %args_15_.3) | copy-start | bytes 786436
  18.9 12.6 %collective-permute-start.2 = (bf16[4,64,256]{2,1,0:T(8,128)(2,1)S(1)}, bf16[4,64,256]{2,1,0:T(8,128)(2,1)S(1)}, u32[]{:S(2)}, u32[]{:S(2)}) collective-permute-start(bf16[4,64,256]{2,1,0:T(8,128)(2,1)S(1)} %get-tuple-element.154.args_3_), channel_id=1, source_target_pairs={{0,16},{2,18},{4,20},{6,22},{8,24},{10,26},{12,28},{14,30},{1,17},... | collective-permute-start | bytes 393224 | tf_op jit(solution)/shard_map/ppermute | solution.py:1327
  20.2 12.6 %collective-permute-start.3 = (bf16[4,16,256]{2,1,0:T(8,128)(2,1)S(1)}, bf16[4,16,256]{2,1,0:T(8,128)(2,1)S(1)}, u32[]{:S(2)}, u32[]{:S(2)}) collective-permute-start(bf16[4,16,256]{2,1,0:T(8,128)(2,1)S(1)} %get-tuple-element.163), channel_id=1, source_target_pairs={{0,18},{2,20},{4,22},{6,24},{8,26},{10,28},{12,30},{14,16},{1,19},... | collective-permute-start | bytes 98312 | tf_op jit(solution)/shard_map/ppermute | solution.py:1328
  21.5 11.3 %collective-permute-start.4 = (bf16[4,16,256]{2,1,0:T(8,128)(2,1)S(1)}, bf16[4,16,256]{2,1,0:T(8,128)(2,1)S(1)}, u32[]{:S(2)}, u32[]{:S(2)}) collective-permute-start(bf16[4,16,256]{2,1,0:T(8,128)(2,1)S(1)} %get-tuple-element.164), channel_id=1, source_target_pairs={{2,16},{4,18},{6,20},{8,22},{10,24},{12,26},{14,28},{0,30},{3,17},... | collective-permute-start | bytes 98312 | tf_op jit(solution)/shard_map/ppermute | solution.py:1329
  28.9 8.0 %collective-permute-start.9 = (bf16[4,64,256]{2,1,0:T(8,128)(2,1)S(1)}, bf16[4,64,256]{2,1,0:T(8,128)(2,1)S(1)}, u32[]{:S(2)}, u32[]{:S(2)}) collective-permute-start(bf16[4,64,256]{2,1,0:T(8,128)(2,1)S(1)} %get-tuple-element.195), channel_id=1, source_target_pairs={{0,18},{2,20},{4,22},{6,24},{8,26},{10,28},{12,30},{14,16},{1,19},... | collective-permute-start | bytes 393224 | tf_op jit(solution)/shard_map/ppermute | solution.py:1328
  30.2 14.2 %collective-permute-start.8 = (bf16[4,64,256]{2,1,0:T(8,128)(2,1)S(1)}, bf16[4,64,256]{2,1,0:T(8,128)(2,1)S(1)}, u32[]{:S(2)}, u32[]{:S(2)}) collective-permute-start(bf16[4,64,256]{2,1,0:T(8,128)(2,1)S(1)} %get-tuple-element.194.args_5_), channel_id=1, source_target_pairs={{0,16},{2,18},{4,20},{6,22},{8,24},{10,26},{12,28},{14,30},{1,17},... | collective-permute-start | bytes 393224 | tf_op jit(solution)/shard_map/ppermute | solution.py:1327
  31.5 12.8 %collective-permute-start.10 = (bf16[4,64,256]{2,1,0:T(8,128)(2,1)S(1)}, bf16[4,64,256]{2,1,0:T(8,128)(2,1)S(1)}, u32[]{:S(2)}, u32[]{:S(2)}) collective-permute-start(bf16[4,64,256]{2,1,0:T(8,128)(2,1)S(1)} %get-tuple-element.196), channel_id=1, source_target_pairs={{2,16},{4,18},{6,20},{8,22},{10,24},{12,26},{14,28},{0,30},{3,17},... | collective-permute-start | bytes 393224 | tf_op jit(solution)/shard_map/ppermute | solution.py:1329
  33.1 14.1 %collective-permute-start.5 = (bf16[4,64,256]{2,1,0:T(8,128)(2,1)S(1)}, bf16[4,64,256]{2,1,0:T(8,128)(2,1)S(1)}, u32[]{:S(2)}, u32[]{:S(2)}) collective-permute-start(bf16[4,64,256]{2,1,0:T(8,128)(2,1)S(1)} %get-tuple-element.184), channel_id=1, source_target_pairs={{16,0},{18,2},{20,4},{22,6},{24,8},{26,10},{28,12},{30,14},{17,1},... | collective-permute-start | bytes 393224 | tf_op jit(solution)/shard_map/ppermute | solution.py:1372
  34.4 12.8 %collective-permute-start.6 = (bf16[4,16,256]{2,1,0:T(8,128)(2,1)S(1)}, bf16[4,16,256]{2,1,0:T(8,128)(2,1)S(1)}, u32[]{:S(2)}, u32[]{:S(2)}) collective-permute-start(bf16[4,16,256]{2,1,0:T(8,128)(2,1)S(1)} %get-tuple-element.185.args_27_), channel_id=1, source_target_pairs={{16,2},{18,4},{20,6},{22,8},{24,10},{26,12},{28,14},{30,0},{17,3},... | collective-permute-start | bytes 98312 | tf_op jit(solution)/shard_map/ppermute | solution.py:1373
  36.9 10.3 %collective-permute-start.7 = (bf16[4,16,256]{2,1,0:T(8,128)(2,1)S(1)}, bf16[4,16,256]{2,1,0:T(8,128)(2,1)S(1)}, u32[]{:S(2)}, u32[]{:S(2)}) collective-permute-start(bf16[4,16,256]{2,1,0:T(8,128)(2,1)S(1)} %get-tuple-element.186.args_26_), channel_id=1, source_target_pairs={{18,0},{20,2},{22,4},{24,6},{26,8},{28,10},{30,12},{16,14},{19,1},... | collective-permute-start | bytes 98312 | tf_op jit(solution)/shard_map/ppermute | solution.py:1374
  47.2 15.5 %collective-permute-start.11 = (bf16[5,64,256]{2,1,0:T(8,128)(2,1)S(1)}, bf16[5,64,256]{2,1,0:T(8,128)(2,1)S(1)}, u32[]{:S(2)}, u32[]{:S(2)}) collective-permute-start(bf16[5,64,256]{2,1,0:T(8,128)(2,1)S(1)} %get-tuple-element.225), channel_id=1, source_target_pairs={{16,0},{18,2},{20,4},{22,6},{24,8},{26,10},{28,12},{30,14},{17,1},... | collective-permute-start | bytes 491528 | tf_op jit(solution)/shard_map/ppermute | solution.py:1372
  48.5 14.2 %collective-permute-start.12 = (bf16[4,16,256]{2,1,0:T(8,128)(2,1)S(1)}, bf16[4,16,256]{2,1,0:T(8,128)(2,1)S(1)}, u32[]{:S(2)}, u32[]{:S(2)}) collective-permute-start(bf16[4,16,256]{2,1,0:T(8,128)(2,1)S(1)} %get-tuple-element.226.args_30_), channel_id=1, source_target_pairs={{16,2},{18,4},{20,6},{22,8},{24,10},{26,12},{28,14},{30,0},{17,3},... | collective-permute-start | bytes 98312 | tf_op jit(solution)/shard_map/ppermute | solution.py:1373
  49.8 12.9 %collective-permute-start.13 = (bf16[4,16,256]{2,1,0:T(8,128)(2,1)S(1)}, bf16[4,16,256]{2,1,0:T(8,128)(2,1)S(1)}, u32[]{:S(2)}, u32[]{:S(2)}) collective-permute-start(bf16[4,16,256]{2,1,0:T(8,128)(2,1)S(1)} %get-tuple-element.227.args_29_), channel_id=1, source_target_pairs={{18,0},{20,2},{22,4},{24,6},{26,8},{28,10},{30,12},{16,14},{19,1},... | collective-permute-start | bytes 98312 | tf_op jit(solution)/shard_map/ppermute | solution.py:1374
  73.1 2.7 %collective-permute-start.14 = (bf16[8,384,128]{2,1,0:T(8,128)(2,1)S(1)}, bf16[8,384,128]{2,1,0:T(8,128)(2,1)S(1)}, u32[]{:S(2)}, u32[]{:S(2)}) collective-permute-start(bf16[8,384,128]{2,1,0:T(8,128)(2,1)S(1)} %get-tuple-element.250), channel_id=1, source_target_pairs={{0,1},{1,0},{2,3},{3,2},{4,5},{5,4},{6,7},{7,6},{8,9},{9,8},{10,11... | collective-permute-start | bytes 2359304 | tf_op jit(solution)/shard_map/ppermute | solution.py:1391
  73.2 2.6 %collective-permute-start.15 = (f32[2,8,128]{2,1,0:T(8,128)S(1)}, f32[2,8,128]{2,1,0:T(8,128)S(1)}, u32[]{:S(2)}, u32[]{:S(2)}) collective-permute-start(f32[2,8,128]{2,1,0:T(8,128)S(1)} %get-tuple-element.254), channel_id=1, source_target_pairs={{0,16},{2,18},{4,20},{6,22},{8,24},{10,26},{12,28},{14,30},{1,17},... | collective-permute-start | bytes 24584 | tf_op jit(solution)/shard_map/ppermute | solution.py:1389
  76.0 7.6 %collective-permute-start.18 = (bf16[384,128]{1,0:T(8,128)(2,1)S(1)}, bf16[384,128]{1,0:T(8,128)(2,1)S(1)}, u32[]{:S(2)}, u32[]{:S(2)}) collective-permute-start(bf16[384,128]{1,0:T(8,128)(2,1)S(1)} %get-tuple-element.267), channel_id=1, source_target_pairs={{0,4},{2,6},{4,8},{6,10},{8,12},{10,14},{12,0},{14,2},{1,5},{3,7},... | collective-permute-start | bytes 294920 | tf_op jit(solution)/shard_map/ppermute | solution.py:1395
  76.1 16.4 %collective-permute-start.19 = (bf16[384,128]{1,0:T(8,128)(2,1)S(1)}, bf16[384,128]{1,0:T(8,128)(2,1)S(1)}, u32[]{:S(2)}, u32[]{:S(2)}) collective-permute-start(bf16[384,128]{1,0:T(8,128)(2,1)S(1)} %get-tuple-element.268), channel_id=1, source_target_pairs={{0,6},{2,8},{4,10},{6,12},{8,14},{10,0},{12,2},{14,4},{1,7},{3,9},... | collective-permute-start | bytes 294920 | tf_op jit(solution)/shard_map/ppermute | solution.py:1395
  78.3 20.5 %collective-permute-start.16 = (bf16[672,128]{1,0:T(8,128)(2,1)S(1)}, bf16[672,128]{1,0:T(8,128)(2,1)S(1)}, u32[]{:S(2)}, u32[]{:S(2)}) collective-permute-start(bf16[672,128]{1,0:T(8,128)(2,1)S(1)} %get-tuple-element.255), channel_id=1, source_target_pairs={{0,2},{2,4},{4,6},{6,8},{8,10},{10,12},{12,14},{14,0},{1,3},{3,5},... | collective-permute-start | bytes 516104 | tf_op jit(solution)/shard_map/ppermute | solution.py:1395
  79.7 19.1 %collective-permute-start.17 = (bf16[672,128]{1,0:T(8,128)(2,1)S(1)}, bf16[672,128]{1,0:T(8,128)(2,1)S(1)}, u32[]{:S(2)}, u32[]{:S(2)}) collective-permute-start(bf16[672,128]{1,0:T(8,128)(2,1)S(1)} %get-tuple-element.256), channel_id=1, source_target_pairs={{0,14},{2,0},{4,2},{6,4},{8,6},{10,8},{12,10},{14,12},{1,15},{3,1}... | collective-permute-start | bytes 516104 | tf_op jit(solution)/shard_map/ppermute | solution.py:1395
  83.0 12.3 %collective-permute-start.20 = (bf16[384,128]{1,0:T(8,128)(2,1)S(1)}, bf16[384,128]{1,0:T(8,128)(2,1)S(1)}, u32[]{:S(2)}, u32[]{:S(2)}) collective-permute-start(bf16[384,128]{1,0:T(8,128)(2,1)S(1)} %get-tuple-element.269), channel_id=1, source_target_pairs={{0,8},{2,10},{4,12},{6,14},{8,0},{10,2},{12,4},{14,6},{1,9},{3,11}... | collective-permute-start | bytes 294920 | tf_op jit(solution)/shard_map/ppermute | solution.py:1395
  83.6 11.7 %collective-permute-start.21 = (bf16[384,128]{1,0:T(8,128)(2,1)S(1)}, bf16[384,128]{1,0:T(8,128)(2,1)S(1)}, u32[]{:S(2)}, u32[]{:S(2)}) collective-permute-start(bf16[384,128]{1,0:T(8,128)(2,1)S(1)} %get-tuple-element.270), channel_id=1, source_target_pairs={{0,10},{2,12},{4,14},{6,0},{8,2},{10,4},{12,6},{14,8},{1,11},{3,13... | collective-permute-start | bytes 294920 | tf_op jit(solution)/shard_map/ppermute | solution.py:1395
  92.5 6.3 %collective-permute-start.22 = (bf16[384,128]{1,0:T(8,128)(2,1)S(1)}, bf16[384,128]{1,0:T(8,128)(2,1)S(1)}, u32[]{:S(2)}, u32[]{:S(2)}) collective-permute-start(bf16[384,128]{1,0:T(8,128)(2,1)S(1)} %get-tuple-element.271), channel_id=1, source_target_pairs={{0,12},{2,14},{4,0},{6,2},{8,4},{10,6},{12,8},{14,10},{1,13},{3,15... | collective-permute-start | bytes 294920 | tf_op jit(solution)/shard_map/ppermute | solution.py:1395
  98.9 1.5 %collective-permute-start.23 = (f32[384,128]{1,0:T(8,128)S(1)}, f32[384,128]{1,0:T(8,128)S(1)}, u32[]{:S(2)}, u32[]{:S(2)}) collective-permute-start(f32[384,128]{1,0:T(8,128)S(1)} %convert_add_fusion.args_0_), channel_id=1, source_target_pairs={{0,1},{1,0},{2,3},{3,2},{4,5},{5,4},{6,7},{7,6},{8,9},{9,8},{10,11... | collective-permute-start | bytes 589832 | tf_op jit(solution)/shard_map/ppermute | solution.py:1408
